TPU v7x, 256 devices: a whole 4x4x8 slice. The times are simulated.
256 devices in a mesh: rep: 32 (over z, x), row: 4 (over y), col: 2 (over core).
Axes of the slice: x: 4, y: 4, z: 8, core: 2. Of those that a mesh axis runs over, the one named last changes fastest.
Arguments:
- tokens: bfloat16 [1024, 5120], P(('rep', 'col'), 'row'), may hold values from -6 to 6
- w_in: bfloat16 [5120, 10240], P('row', ('rep', 'col')), may hold values from -0.078125 to 0.078125
- w_out: bfloat16 [10240, 5120], P(('rep', 'col'), 'row'), may hold values from -0.0625 to 0.0625
- cotangent: bfloat16 [1024, 5120], P(('rep', 'col'), 'row'), may hold values from -3 to 3
Outputs:
- output: bfloat16 [1024, 5120], P(('rep', 'col'), 'row')
- input_grad: bfloat16 [1024, 5120], P(('rep', 'col'), 'row')
- grad_in: float32 [5120, 10240], P('row', ('rep', 'col'))
- grad_out: float32 [10240, 5120], P(('rep', 'col'), 'row')
All inputs are finite; a program needn't handle non-finite values.
Results may differ from a plain program's by a relative error of at most 0.0049.
Values may be sent and summed in bfloat16 or wider, within the bound.
No kernel may reach another device: no remote copies, remote signals or barrier semaphores. Data moves between devices by JAX's collectives and lax.ppermute only.
A program may use at most 64 MiB of HBM per device.

v0:
```python
import jax
import jax.numpy as jnp
from jax import lax
from jax.sharding import PartitionSpec as P


def smooth_gate(value):
    return 0.5 * value * (1.0 + jax.scipy.special.erf(value * 0.7071067811865476))


def smooth_slope(value):
    cumul = 0.5 * (1.0 + jax.scipy.special.erf(value * 0.7071067811865476))
    return cumul + value * jnp.exp(-0.5 * value * value) * 0.3989422804014327


def contract_last(left, right):
    return lax.dot_general(
        left, right, (((1,), (1,)), ((), ())), preferred_element_type=jnp.float32
    )


def contract_first(left, right):
    return lax.dot_general(
        left, right, (((0,), (0,)), ((), ())), preferred_element_type=jnp.float32
    )


def on_device(tokens, w_in, w_out, cotangent):
    tok_full = lax.all_gather(tokens, ("rep", "col"), axis=0, tiled=True)
    pre_share = lax.psum_scatter(
        jnp.dot(tok_full, w_in, preferred_element_type=jnp.float32),
        "row",
        scatter_dimension=0,
        tiled=True,
    )
    act_share = smooth_gate(pre_share).astype(jnp.bfloat16)
    act_full = lax.all_gather(act_share, "row", axis=0, tiled=True)
    out_sum = lax.psum_scatter(
        jnp.dot(act_full, w_out, preferred_element_type=jnp.float32),
        ("rep", "col"),
        scatter_dimension=0,
        tiled=True,
    )
    output = out_sum.astype(jnp.bfloat16)
    cot_full = lax.all_gather(cotangent, ("rep", "col"), axis=0, tiled=True)
    grad_act = lax.psum_scatter(
        contract_last(cot_full, w_out), "row", scatter_dimension=0, tiled=True
    )
    grad_share = (grad_act * smooth_slope(pre_share)).astype(jnp.bfloat16)
    grad_full = lax.all_gather(grad_share, "row", axis=0, tiled=True)
    back_sum = lax.psum_scatter(
        contract_last(grad_full, w_in), ("rep", "col"), scatter_dimension=0, tiled=True
    )
    input_grad = back_sum.astype(jnp.bfloat16)
    grad_in = contract_first(tok_full, grad_full)
    grad_out = contract_first(act_full, cot_full)
    return (output, input_grad, grad_in, grad_out)


def solution(mesh):
    placed = (
        P(("rep", "col"), "row"),
        P("row", ("rep", "col")),
        P(("rep", "col"), "row"),
        P(("rep", "col"), "row"),
    )
    return jax.shard_map(
        on_device,
        mesh=mesh,
        in_specs=placed,
        out_specs=(
            P(("rep", "col"), "row"),
            P(("rep", "col"), "row"),
            P("row", ("rep", "col")),
            P(("rep", "col"), "row"),
        ),
        check_vma=False,
    )
```

profile of v0, /device:TPU:2, one launch (start us, length us, event | category | flops | bytes accessed | tf_op | source)
XLA Modules:
  0.0 539.5 jit_solution(10737224420827394745)
XLA Ops:
  7.2 0.0 copy-start
  7.2 0.0 all-gather.5.cloned.1.call-start
  7.2 0.7 all-gather.5.cloned.1.call-update
  7.9 0.0 all-gather.3.cloned.1.call-start
  8.0 0.7 all-gather.3.cloned.1.call-update
  8.7 0.0 copy-start.4
  8.7 0.0 reduce-scatter.9.cloned.1.call-start
  8.7 81.6 %all-gather.5.cloned.1.call-done = bf16[1024,1280]{1,0:T(8,128)(2,1)} async-done(((bf16[16,1280]{1,0:T(8,128)(2,1)}), bf16[1024,1280]{1,0:T(8,128)(2,1)}) %all-gather.5.cloned.1.call-update) | async-done | bytes 2621456 | tf_op jit(solution)/shard_map/all_gather | solution.py:45
  90.3 0.0 copy-done
  90.3 3.6 fusion.8
  93.9 0.0 reduce-scatter.9.cloned.1.call-update
  93.9 0.0 reduce-scatter.5.cloned.1.call-start
  94.0 74.4 %all-gather.3.cloned.1.call-done = bf16[1024,1280]{1,0:T(8,128)(2,1)} async-done(((bf16[16,1280]{1,0:T(8,128)(2,1)}), bf16[1024,1280]{1,0:T(8,128)(2,1)}) %all-gather.3.cloned.1.call-update) | async-done | bytes 2621456 | tf_op jit(solution)/shard_map/all_gather | solution.py:29
  168.4 0.0 copy-done.4
  168.4 3.6 fusion.6
  172.0 0.0 reduce-scatter.5.cloned.1.call-update
  172.0 0.0 reduce-scatter.7.cloned.1.call-start
  172.0 22.6 %reduce-scatter.9.cloned.1.call-done = f32[256,160]{0,1:T(8,128)} async-done(((f32[1024,160]{0,1:T(8,128)}), f32[256,160]{0,1:T(8,128)}) %reduce-scatter.9.cloned.1.call-update) | async-done | bytes 163856 | tf_op jit(solution)/shard_map/reduce_scatter | solution.py:46
  194.7 27.2 %reduce-scatter.5.cloned.1.call-done = f32[256,160]{0,1:T(8,128)} async-done(((f32[1024,160]{0,1:T(8,128)}), f32[256,160]{0,1:T(8,128)}) %reduce-scatter.5.cloned.1.call-update) | async-done | bytes 163856 | tf_op jit(solution)/shard_map/reduce_scatter | solution.py:30
  221.9 1.1 fusion.5
  222.9 12.4 %all_gather.13 = bf16[1024,160]{0,1:T(8,128)(2,1)S(1)} all-gather(bf16[256,160]{0,1:T(8,128)(2,1)S(1)} %get-tuple-element.5), channel_id=1, replica_groups=mesh['rep'=32,'row'=4,'col'=2] {'row'}, dimensions={0}, use_global_device_ids=true | all-gather | bytes 409600 | tf_op jit(solution)/shard_map/all_gather | solution.py:37
  235.3 3.2 fusion.7
  238.5 0.0 reduce-scatter.7.cloned.1.call-update
  238.6 0.0 reduce-scatter.11.cloned.1.call-start
  238.6 12.4 %all_gather.15 = bf16[1024,160]{0,1:T(8,128)(2,1)S(1)} all-gather(bf16[256,160]{0,1:T(8,128)(2,1)S(1)} %get-tuple-element.4), channel_id=1, replica_groups=mesh['rep'=32,'row'=4,'col'=2] {'row'}, dimensions={0}, use_global_device_ids=true | all-gather | bytes 409600 | tf_op jit(solution)/shard_map/all_gather | solution.py:50
  251.0 0.0 copy-start.3
  251.0 0.7 copy-done.3
  251.8 3.2 fusion.9
  255.0 0.0 copy-start.2
  255.0 0.0 reduce-scatter.11.cloned.1.call-update
  255.0 1.8 copy-done.2
  256.8 0.0 copy-start.1
  256.8 2.6 convolution_bitcast_fusion
  259.4 0.0 copy-done.1
  259.4 1.5 fusion.10
  260.9 122.0 %reduce-scatter.7.cloned.1.call-done = f32[16,1280]{1,0:T(8,128)} async-done(((f32[1024,1280]{1,0:T(8,128)}), f32[16,1280]{1,0:T(8,128)}) %reduce-scatter.7.cloned.1.call-update) | async-done | bytes 81936 | tf_op jit(solution)/shard_map/reduce_scatter | solution.py:38
  382.9 1.5 convert_element_type.13
  384.4 146.7 %reduce-scatter.11.cloned.1.call-done = f32[16,1280]{1,0:T(8,128)} async-done(((f32[1024,1280]{1,0:T(8,128)}), f32[16,1280]{1,0:T(8,128)}) %reduce-scatter.11.cloned.1.call-update) | async-done | bytes 81936 | tf_op jit(solution)/shard_map/reduce_scatter | solution.py:51
  531.2 1.5 convert_element_type.15
Async XLA Ops:
  7.2 83.1 %copy-start = (bf16[160,1280]{1,0:T(8,128)(2,1)S(1)}, bf16[160,1280]{1,0:T(8,128)(2,1)}, u32[]{:S(2)}) copy-start(bf16[160,1280]{1,0:T(8,128)(2,1)} %param.6) | copy-start | bytes 1228804
  7.2 83.1 %all-gather.5.cloned.1.call-start = ((), (), s32[]{:S(2)}) async-start(), calls=%async_computation.7 | async-start | bytes 2662400 | tf_op jit(solution)/shard_map/all_gather | solution.py:45
  7.9 160.5 %all-gather.3.cloned.1.call-start = ((), (), s32[]{:S(2)}) async-start(), calls=%async_computation.4 | async-start | bytes 2662400 | tf_op jit(solution)/shard_map/all_gather | solution.py:29
  8.7 159.7 %copy-start.4 = (bf16[1280,160]{0,1:T(8,128)(2,1)S(1)}, bf16[1280,160]{0,1:T(8,128)(2,1)}, u32[]{:S(2)}) copy-start(bf16[1280,160]{0,1:T(8,128)(2,1)} %param.5) | copy-start | bytes 1228804
  8.7 186.0 %reduce-scatter.9.cloned.1.call-start = ((), (), s32[]{:S(2)}) async-start(), calls=%async_computation.8 | async-start | bytes 819200 | tf_op jit(solution)/shard_map/reduce_scatter | solution.py:46
  93.9 127.9 %reduce-scatter.5.cloned.1.call-start = ((), (), s32[]{:S(2)}) async-start(), calls=%async_computation.5 | async-start | bytes 819200 | tf_op jit(solution)/shard_map/reduce_scatter | solution.py:30
  172.0 210.9 %reduce-scatter.7.cloned.1.call-start = ((), (), s32[]{:S(2)}) async-start(), calls=%async_computation.6 | async-start | bytes 5324800 | tf_op jit(solution)/shard_map/reduce_scatter | solution.py:38
  238.6 292.6 %reduce-scatter.11.cloned.1.call-start = ((), (), s32[]{:S(2)}) async-start(), calls=%async_computation.9 | async-start | bytes 5324800 | tf_op jit(solution)/shard_map/reduce_scatter | solution.py:51
  251.0 0.7 copy-start.3
  255.0 1.8 copy-start.2
  256.8 2.6 copy-start.1
Sparse Core Ops, SparseCore 0:
  10.8 79.5 all-gather.4
  93.1 75.2 all-gather.2
  171.5 23.1 reduce-scatter.8
  197.6 24.1 reduce-scatter.4
  238.7 144.2 reduce-scatter.6
  387.5 143.6 reduce-scatter.10
where the time goes:
time: 541 us; the launch traced here: 540 us
  waiting for transfers between devices  476 us (88%)
  blocking collectives  24.8 us (5%)
  matrix products  17.7 us (3%)
  between operations  14.1 us (3%)
    reduce_scatter x1, waiting for transfers between devices, on_device(): lax.psum_scatter(contract_last(grad_full, w_in), ('rep', 'col'), scatter_...  147 us
    reduce_scatter x1, waiting for transfers between devices, on_device(): lax.psum_scatter(jnp.dot(act_full, w_out, preferred_element_type=jnp.floa...  122 us
    all_gather x1, waiting for transfers between devices, on_device(): cot_full = lax.all_gather(cotangent, ('rep', 'col'), axis=0, tiled=True)  81.6 us
    all_gather x1, waiting for transfers between devices, on_device(): tok_full = lax.all_gather(tokens, ('rep', 'col'), axis=0, tiled=True)  74.4 us
    reduce_scatter x1, waiting for transfers between devices, on_device(): lax.psum_scatter(jnp.dot(tok_full, w_in, preferred_element_type=jnp.float...  27.2 us
    reduce_scatter x1, waiting for transfers between devices, on_device(): lax.psum_scatter(contract_last(cot_full, w_out), 'row', scatter_dimension...  22.6 us
    all_gather x1, blocking collectives, on_device(): grad_full = lax.all_gather(grad_share, 'row', axis=0, tiled=True)  12.4 us
    all_gather x1, blocking collectives, on_device(): act_full = lax.all_gather(act_share, 'row', axis=0, tiled=True)  12.4 us
  transfers between devices with their start and end apart: 6, of which 6 were waited for; matrix products, arithmetic and copies ran while one was open for 3% of the time, Pallas kernels for 0%

commit v1 on v0

v1 whole, which is shorter than its diff:
```python
import jax
import jax.numpy as jnp
from jax import lax
from jax.experimental import pallas as pl
from jax.experimental.pallas import tpu as pltpu
from jax.sharding import Mesh, PartitionSpec as P

BF = jnp.bfloat16
F32 = jnp.float32
SIZE = {"z": 8, "x": 4, "row": 4, "col": 2}
ORDER = (0, 1, 7, 2, 6, 3, 5, 4)


def smooth_gate(value):
    return 0.5 * value * (1.0 + lax.erf(value * 0.7071067811865476))


def smooth_slope(value):
    cumul = 0.5 * (1.0 + lax.erf(value * 0.7071067811865476))
    return cumul + value * jnp.exp(-0.5 * value * value) * 0.3989422804014327


def send(value, axis, shift):
    size = SIZE[axis]
    return lax.ppermute(value, axis, [(i, (i + shift) % size) for i in range(size)])


def swap_pair(value):
    return lax.ppermute(value, "x", [(i, i ^ 1) for i in range(4)])


def after(value, other):
    return lax.optimization_barrier((value, other))[0]


def call(body, outs, args, flops=1 << 20, scratch=()):
    specs = [pl.BlockSpec(memory_space=pltpu.SMEM)]
    specs += [pl.BlockSpec(memory_space=pltpu.VMEM)] * (len(args) - 1)
    kernel = pl.pallas_call(
        body,
        out_shape=outs,
        in_specs=specs,
        out_specs=[pl.BlockSpec(memory_space=pltpu.VMEM)] * len(outs),
        scratch_shapes=list(scratch),
        compiler_params=pltpu.CompilerParams(vmem_limit_bytes=40 << 20),
        cost_estimate=pl.CostEstimate(
            flops=flops, bytes_accessed=1 << 20, transcendentals=0
        ),
    )
    return list(kernel(*args))


def cat(values):
    return jnp.concatenate(values, 0)


def dot(a, b, dim_a, dim_b):
    return lax.dot_general(
        a, b, (((dim_a,), (dim_b,)), ((), ())), preferred_element_type=F32
    )


def up_kernel(me, q0, q1, q2, q3, wi, wi2, wo, wo2, tok, cot, p0, p1, p2, p3, whole):
    h = wi.shape[0]
    for a, quarter in enumerate((q0, q1, q2, q3)):
        for j in range(4):
            row = a * 128 + j * 32
            tok[row : row + 32] = quarter[j * 64 : j * 64 + 32]
            cot[row : row + 32] = quarter[j * 64 + 32 : j * 64 + 64]
    for s, (weights, value) in enumerate((((wi, wi2), tok), ((wo, wo2), cot))):
        for i, w in enumerate(weights):
            total = dot(w[...], value[...], 1, 1)
            for a in range(4):
                whole[a, s, i * h : i * h + h] = total[:, a * 128 : a * 128 + 128]
    for k, part in enumerate((p0, p1, p2, p3)):
        part[...] = whole[(me[0] + k) % 4]


def act_kernel(me, p0, p1, p2, p3, out):
    del me
    pre = p0[0] + p1[0] + p2[0] + p3[0]
    grad_act = p0[1] + p1[1] + p2[1] + p3[1]
    out[0] = smooth_gate(pre).astype(BF)
    out[1] = (grad_act * smooth_slope(pre)).astype(BF)


def down_kernel(me, b0, b1, b2, b3, wi, wi2, wo, wo2, own, oth_a, oth_b, full):
    h = wi.shape[0]
    for k, block in enumerate((b0, b1, b2, b3)):
        lane = pl.multiple_of(((me[0] + k) % 4) * 128, 128)
        full[:, :, pl.ds(lane, 128)] = block[...]
    for s, (w, w2) in enumerate(((wo, wo2), (wi, wi2))):
        for half in (1, 0):
            value = dot(full[s, :h, half * 256 : half * 256 + 256], w[...], 0, 0)
            value += dot(full[s, h:, half * 256 : half * 256 + 256], w2[...], 0, 0)
            for j in range(8):
                piece = value[j * 32 : j * 32 + 32]
                row = j * 64 + s * 32
                if half == 0:
                    own[row : row + 32] = piece
                elif j < 4:
                    oth_a[row : row + 32] = piece.astype(BF)
                else:
                    oth_b[row - 256 : row - 224] = piece.astype(BF)


def pair_kernel(me, full, tok, cot, out):
    del me
    h = full.shape[1] // 2
    out[:h] = dot(full[0, h:], cot[...], 1, 0).astype(BF)
    out[h:] = dot(full[1, h:], tok[...], 1, 0).astype(BF)


def own_kernel(me, full, tok, cot, grad_out, grad_in):
    del me
    h = full.shape[1] // 2
    grad_out[...] = dot(full[0, :h], cot[...], 1, 0)
    grad_in[...] = dot(full[1, :h], tok[...], 1, 0)


def on_device(tokens, w_in, w_out, cotangent):
    me = lax.axis_index("row").astype(jnp.int32).reshape(1)
    d, h = w_in.shape
    shape = jax.ShapeDtypeStruct
    flops = 2 * 1024 * d * h

    far = send(cat([tokens, cotangent]), "x", 2)
    z = {0: cat([tokens, far[:16], cotangent, far[16:]])}
    z[1], z[7] = send(z[0], "z", -1), send(z[0], "z", 1)
    w_in_t = w_in.T
    w_in_2 = swap_pair(after(w_in_t, z[0]))
    w_out_2 = swap_pair(after(w_out, z[1]))
    z[2], z[6] = send(z[1], "z", -1), send(z[7], "z", 1)
    own_a = cat([z[k] for k in ORDER[:4]])
    z[3], z[5] = send(z[2], "z", -1), send(z[6], "z", 1)
    oth_a = send(own_a, "col", 1)
    z[4] = cat([send(z[3][:32], "z", -1), send(z[5][32:], "z", 1)])
    own_b = cat([z[k] for k in ORDER[4:]])
    oth_b = send(own_b, "col", 1)

    part = shape((2, 2 * h, 128), F32)
    tok, cot, *parts = call(
        up_kernel,
        [shape((512, d), BF)] * 2 + [part] * 4,
        [me, own_a, own_b, oth_a, oth_b, w_in_t, w_in_2, w_out, w_out_2],
        2 * flops,
        [pltpu.VMEM((4, 2, 2 * h, 128), F32)],
    )
    parts[1:] = [send(parts[k], "row", k) for k in (1, 2, 3)]
    (block,) = call(act_kernel, [shape((2, 2 * h, 128), BF)], [me, *parts])
    blocks = [block] + [send(block, "row", -k) for k in (1, 2, 3)]

    own, oth_a, oth_b, full = call(
        down_kernel,
        [shape((512, d), F32), shape((256, d), BF), shape((256, d), BF), shape((2, 2 * h, 512), BF)],
        [me, *blocks, w_in_t, w_in_2, w_out, w_out_2],
        2 * flops,
    )
    oth_b = send(oth_b, "col", 1)
    oth_a = send(oth_a, "col", 1)
    (pair,) = call(
        pair_kernel, [shape((2 * h, d), BF)], [me, after(full, oth_b), tok, cot], flops
    )
    piece = {}
    for i, k in enumerate(ORDER):
        got = oth_a if i < 4 else oth_b
        got = got[i % 4 * 64 : i % 4 * 64 + 64].astype(F32)
        piece[k] = own[i * 64 : i * 64 + 64] + got
    up = send(piece[4][:32].astype(BF), "z", 1).astype(F32)
    down = send(piece[4][32:].astype(BF), "z", -1).astype(F32)
    pair = swap_pair(pair)
    up = cat([up + piece[3][:32], piece[3][32:]])
    down = cat([piece[5][:32], down + piece[5][32:]])
    up = send(up.astype(BF), "z", 1).astype(F32)
    down = send(down.astype(BF), "z", -1).astype(F32)
    up = send((up + piece[2]).astype(BF), "z", 1).astype(F32)
    down = send((down + piece[6]).astype(BF), "z", -1).astype(F32)
    grad_out, grad_in_t = call(
        own_kernel, [shape((h, d), F32)] * 2, [me, after(full, pair), tok, cot], flops
    )
    up = send((up + piece[1]).astype(BF), "z", 1).astype(F32)
    down = send((down + piece[7]).astype(BF), "z", -1).astype(F32)
    total = piece[0] + up + down
    far = send(cat([total[16:32], total[48:]]).astype(BF), "x", 2).astype(F32)
    output = (total[:16] + far[:16]).astype(BF)
    input_grad = (total[32:48] + far[16:]).astype(BF)
    grad_out = grad_out + pair[:h].astype(F32)
    grad_in_t = grad_in_t + pair[h:].astype(F32)
    return (output, input_grad, grad_in_t.T, grad_out)


def solution(mesh):
    mesh = Mesh(mesh.devices.reshape(8, 4, 4, 2), ("z", "x", "row", "col"))
    whole = ("z", "x", "col")
    placed = (P(whole, "row"), P("row", whole), P(whole, "row"), P(whole, "row"))
    return jax.shard_map(
        on_device,
        mesh=mesh,
        in_specs=placed,
        out_specs=(P(whole, "row"), P(whole, "row"), P("row", whole), P(whole, "row")),
        check_vma=False,
    )
```

time: 541 us -> 155 us (0.29)
  waiting for transfers between devices: 476 us -> 91.3 us
  starting transfers between devices: 0.24 us -> 48.8 us
  blocking collectives: 24.8 us -> 0 us
  matrix products: 17.7 us -> 0 us
  between operations: 14.1 us -> 0.91 us
  Pallas kernels: 0 us -> 7.21 us
    reduce_scatter x4 -> x0, waiting for transfers between devices: 319 us -> none  [the longest x1 147 us: on_device(): lax.psum_scatter(contract_last(grad_full, w_in), ('rep', 'col'), scatter_...]
    all_gather x2 -> x0, waiting for transfers between devices: 156 us -> none  [the longest x1 81.6 us: on_device(): cot_full = lax.all_gather(cotangent, ('rep', 'col'), axis=0, tiled=True)]
    ppermute x0 -> x31, waiting for transfers between devices: none -> 91.3 us  [the longest x28 59.4 us: send(): lax.ppermute(value, axis, [(i, (i + shift) % size) for i in range(size)])]
    ppermute x0 -> x31, starting transfers between devices: none -> 48.8 us  [the longest x28 46 us: send(): lax.ppermute(value, axis, [(i, (i + shift) % size) for i in range(size)])]
    all_gather x2 -> x0, blocking collectives: 24.8 us -> none  [the longest x1 12.4 us: on_device(): grad_full = lax.all_gather(grad_share, 'row', axis=0, tiled=True)]
    dot_general x6 -> x0, matrix products: 17.7 us -> none  [the longest x2 6.82 us: contract_last(): lax.dot_general(left, right, (((1,), (1,)), ((), ())), preferred_element_...]
    pallas_call x0 -> x5, Pallas kernels: none -> 7.21 us  [call(): return list(kernel(*args))]
  transfers between devices with their start and end apart: 6 -> 31, of which waited for: 6 -> 20; matrix products, arithmetic and copies ran while one was open for 3% -> 2% of each run, Pallas kernels for 0% -> 1%
where the time goes in v1:
time: 155 us; the launch traced here: 154 us
  waiting for transfers between devices  91.3 us (59%)
  starting transfers between devices  48.8 us (31%)
  Pallas kernels  7.21 us (5%)
  other arithmetic  4.07 us (3%)
  local copies, waits for them, and re-layouts  1.72 us (1%)
    ppermute x28, waiting for transfers between devices, send(): lax.ppermute(value, axis, [(i, (i + shift) % size) for i in range(size)])  59.4 us
    ppermute x28, starting transfers between devices, send(): lax.ppermute(value, axis, [(i, (i + shift) % size) for i in range(size)])  46 us
    ppermute x3, waiting for transfers between devices, swap_pair(): return lax.ppermute(value, 'x', [(i, i ^ 1) for i in range(4)])  31.9 us
    pallas_call x5, Pallas kernels, call(): return list(kernel(*args))  7.21 us
  transfers between devices with their start and end apart: 31, of which 20 were waited for; matrix products, arithmetic and copies ran while one was open for 2% of the time, Pallas kernels for 1%

profile of v1, /device:TPU:2, one launch (start us, length us, event | category | flops | bytes accessed | tf_op | source)
XLA Modules:
  0.0 154.0 jit_solution(8416077130821432904)
XLA Ops:
  0.7 0.9 pad_maximum_fusion.3
  1.5 2.1 %collective-permute-start = (bf16[32,1280]{1,0:T(8,128)(2,1)S(1)}, bf16[32,1280]{1,0:T(8,128)(2,1)S(1)}, u32[]{:S(2)}, u32[]{:S(2)}) collective-permute-start(bf16[32,1280]{1,0:T(8,128)(2,1)S(1)} %pad_maximum_fusion.3), channel_id=1, source_target_pairs={{0,16},{8,24},{16,0},{24,8},{1,17},{9,25},{17,1},{25,9},{2,18},{10... | collective-permute-start | bytes 245768 | tf_op jit(solution)/shard_map/ppermute | solution.py:25
  3.7 0.8 constant_dynamic-update-slice_fusion.6
  4.4 3.0 %collective-permute-done = bf16[32,1280]{1,0:T(8,128)(2,1)S(1)} collective-permute-done((bf16[32,1280]{1,0:T(8,128)(2,1)S(1)}, bf16[32,1280]{1,0:T(8,128)(2,1)S(1)}, u32[]{:S(2)}, u32[]{:S(2)}) %collective-permute-start) | collective-permute-done | bytes 81952 | tf_op jit(solution)/shard_map/ppermute | solution.py:25
  7.5 0.8 pad_maximum_fusion
  8.3 2.0 %collective-permute-start.2 = (bf16[64,1280]{1,0:T(8,128)(2,1)S(1)}, bf16[64,1280]{1,0:T(8,128)(2,1)S(1)}, u32[]{:S(2)}, u32[]{:S(2)}) collective-permute-start(bf16[64,1280]{1,0:T(8,128)(2,1)S(1)} %pad_maximum_fusion), channel_id=1, source_target_pairs={{0,32},{32,64},{64,96},{96,128},{128,160},{160,192},{192,224},{224... | collective-permute-start | bytes 491528 | tf_op jit(solution)/shard_map/ppermute | solution.py:25
  10.3 4.0 %collective-permute-start.1 = (bf16[64,1280]{1,0:T(8,128)(2,1)S(1)}, bf16[64,1280]{1,0:T(8,128)(2,1)S(1)}, u32[]{:S(2)}, u32[]{:S(2)}) collective-permute-start(bf16[64,1280]{1,0:T(8,128)(2,1)S(1)} %pad_maximum_fusion), channel_id=1, source_target_pairs={{0,224},{32,0},{64,32},{96,64},{128,96},{160,128},{192,160},{224,1... | collective-permute-start | bytes 491528 | tf_op jit(solution)/shard_map/ppermute | solution.py:25
  14.3 0.8 constant_dynamic-update-slice_fusion.4
  15.1 2.4 %collective-permute-done.2 = bf16[64,1280]{1,0:T(8,128)(2,1)S(1)} collective-permute-done((bf16[64,1280]{1,0:T(8,128)(2,1)S(1)}, bf16[64,1280]{1,0:T(8,128)(2,1)S(1)}, u32[]{:S(2)}, u32[]{:S(2)}) %collective-permute-start.2) | collective-permute-done | bytes 163872 | tf_op jit(solution)/shard_map/ppermute | solution.py:25
  17.5 0.0 collective-permute-start.4
  17.5 0.0 collective-permute-done.1
  17.5 3.3 %collective-permute-start.3 = (bf16[64,1280]{1,0:T(8,128)(2,1)S(1)}, bf16[64,1280]{1,0:T(8,128)(2,1)S(1)}, u32[]{:S(2)}, u32[]{:S(2)}) collective-permute-start(bf16[64,1280]{1,0:T(8,128)(2,1)S(1)} %collective-permute-done.1), channel_id=1, source_target_pairs={{0,224},{32,0},{64,32},{96,64},{128,96},{160,128},{192,160},{224,1... | collective-permute-start | bytes 491528 | tf_op jit(solution)/shard_map/ppermute | solution.py:25
  20.9 2.8 %collective-permute-done.3 = bf16[64,1280]{1,0:T(8,128)(2,1)S(1)} collective-permute-done((bf16[64,1280]{1,0:T(8,128)(2,1)S(1)}, bf16[64,1280]{1,0:T(8,128)(2,1)S(1)}, u32[]{:S(2)}, u32[]{:S(2)}) %collective-permute-start.3) | collective-permute-done | bytes 163872 | tf_op jit(solution)/shard_map/ppermute | solution.py:25
  23.7 0.1 collective-permute-start.9
  23.8 3.8 %collective-permute-start.5 = (bf16[64,1280]{1,0:T(8,128)(2,1)S(1)}, bf16[64,1280]{1,0:T(8,128)(2,1)S(1)}, u32[]{:S(2)}, u32[]{:S(2)}) collective-permute-start(bf16[64,1280]{1,0:T(8,128)(2,1)S(1)} %collective-permute-done.3), channel_id=1, source_target_pairs={{0,224},{32,0},{64,32},{96,64},{128,96},{160,128},{192,160},{224,1... | collective-permute-start | bytes 491528 | tf_op jit(solution)/shard_map/ppermute | solution.py:25
  27.6 7.5 %collective-permute-done.6 = bf16[64,1280]{1,0:T(8,128)(2,1)S(1)} collective-permute-done((bf16[64,1280]{1,0:T(8,128)(2,1)S(1)}, bf16[64,1280]{1,0:T(8,128)(2,1)S(1)}, u32[]{:S(2)}, u32[]{:S(2)}) %collective-permute-start.6) | collective-permute-done | bytes 163872 | tf_op jit(solution)/shard_map/ppermute | solution.py:25
  35.1 3.3 %collective-permute-start.7 = (bf16[32,1280]{1,0:T(8,128)(2,1)S(1)}, bf16[32,1280]{1,0:T(8,128)(2,1)S(1)}, u32[]{:S(2)}, u32[]{:S(2)}) collective-permute-start(bf16[32,1280]{1,0:T(8,128)(2,1)S(1)} %slice.144), channel_id=1, source_target_pairs={{0,224},{32,0},{64,32},{96,64},{128,96},{160,128},{192,160},{224,1... | collective-permute-start | bytes 245768 | tf_op jit(solution)/shard_map/ppermute | solution.py:25
  38.4 2.0 %collective-permute-done.7 = bf16[32,1280]{1,0:T(8,128)(2,1)S(1)} collective-permute-done((bf16[32,1280]{1,0:T(8,128)(2,1)S(1)}, bf16[32,1280]{1,0:T(8,128)(2,1)S(1)}, u32[]{:S(2)}, u32[]{:S(2)}) %collective-permute-start.7) | collective-permute-done | bytes 81952 | tf_op jit(solution)/shard_map/ppermute | solution.py:25
  40.5 0.3 collective-permute-done.8
  40.7 0.0 collective-permute-start.10
  40.8 0.6 collective-permute-start.11
  41.4 1.5 collective-permute-start.12
  42.9 10.3 %collective-permute-done.11.wi2 = bf16[160,1280]{1,0:T(8,128)(2,1)} collective-permute-done((bf16[160,1280]{1,0:T(8,128)(2,1)S(1)}, bf16[160,1280]{1,0:T(8,128)(2,1)}, u32[]{:S(2)}, u32[]{:S(2)}) %collective-permute-start.11) | collective-permute-done | bytes 409632 | tf_op jit(solution)/shard_map/ppermute | solution.py:29
  53.2 8.3 %collective-permute-done.12.wo2 = bf16[160,1280]{1,0:T(8,128)(2,1)} collective-permute-done((bf16[160,1280]{1,0:T(8,128)(2,1)S(1)}, bf16[160,1280]{1,0:T(8,128)(2,1)}, u32[]{:S(2)}, u32[]{:S(2)}) %collective-permute-start.12) | collective-permute-done | bytes 409632 | tf_op jit(solution)/shard_map/ppermute | solution.py:29
  61.5 3.1 %shard_map.75 = (bf16[512,1280]{1,0:T(8,128)(2,1)S(1)}, bf16[512,1280]{1,0:T(8,128)(2,1)S(1)}, f32[2,320,128]{2,1,0:T(8,128)S(1)}, f32[2,320,128]{2,1,0:T(8,128)...) custom-call(s32[1]{0:T(128)} %bitcast.me, bf16[256,1280]{1,0:T(8,128)(2,1)S(1)} %constant_dynamic-update-slice_fusion.q0, ...), custom_call_target="tpu_custom_call" | custom-call | flops 838860800 | bytes 1048576 | tf_op jit(solution)/shard_map/pallas_call | solution.py:50
  64.6 1.7 %collective-permute-start.13 = (f32[2,320,128]{2,1,0:T(8,128)S(1)}, f32[2,320,128]{2,1,0:T(8,128)S(1)}, u32[]{:S(2)}, u32[]{:S(2)}) collective-permute-start(f32[2,320,128]{2,1,0:T(8,128)S(1)} %get-tuple-element.23), channel_id=1, source_target_pairs={{0,2},{2,4},{4,6},{6,0},{1,3},{3,5},{5,7},{7,1},{8,10},{10,12},{12... | collective-permute-start | bytes 983048 | tf_op jit(solution)/shard_map/ppermute | solution.py:25
  66.3 2.9 %collective-permute-start.14 = (f32[2,320,128]{2,1,0:T(8,128)S(1)}, f32[2,320,128]{2,1,0:T(8,128)S(1)}, u32[]{:S(2)}, u32[]{:S(2)}) collective-permute-start(f32[2,320,128]{2,1,0:T(8,128)S(1)} %get-tuple-element.24), channel_id=1, source_target_pairs={{0,4},{2,6},{4,0},{6,2},{1,5},{3,7},{5,1},{7,3},{8,12},{10,14},{12... | collective-permute-start | bytes 983048 | tf_op jit(solution)/shard_map/ppermute | solution.py:25
  69.2 1.3 collective-permute-start.15
  70.5 4.9 %collective-permute-done.13.p1 = f32[2,320,128]{2,1,0:T(8,128)S(1)} collective-permute-done((f32[2,320,128]{2,1,0:T(8,128)S(1)}, f32[2,320,128]{2,1,0:T(8,128)S(1)}, u32[]{:S(2)}, u32[]{:S(2)}) %collective-permute-start.13) | collective-permute-done | bytes 327712 | tf_op jit(solution)/shard_map/ppermute | solution.py:25
  75.4 8.0 %collective-permute-done.14.p2 = f32[2,320,128]{2,1,0:T(8,128)S(1)} collective-permute-done((f32[2,320,128]{2,1,0:T(8,128)S(1)}, f32[2,320,128]{2,1,0:T(8,128)S(1)}, u32[]{:S(2)}, u32[]{:S(2)}) %collective-permute-start.14) | collective-permute-done | bytes 327712 | tf_op jit(solution)/shard_map/ppermute | solution.py:25
  83.4 0.1 shard_map.76.b0
  83.6 1.3 collective-permute-start.18
  84.9 2.4 %collective-permute-start.17 = (bf16[2,320,128]{2,1,0:T(8,128)(2,1)S(1)}, bf16[2,320,128]{2,1,0:T(8,128)(2,1)S(1)}, u32[]{:S(2)}, u32[]{:S(2)}) collective-permute-start(bf16[2,320,128]{2,1,0:T(8,128)(2,1)S(1)} %shard_map.76.b0), channel_id=1, source_target_pairs={{0,4},{2,6},{4,0},{6,2},{1,5},{3,7},{5,1},{7,3},{8,12},{10,14},{12... | collective-permute-start | bytes 491528 | tf_op jit(solution)/shard_map/ppermute | solution.py:25
  87.3 1.6 %collective-permute-start.16 = (bf16[2,320,128]{2,1,0:T(8,128)(2,1)S(1)}, bf16[2,320,128]{2,1,0:T(8,128)(2,1)S(1)}, u32[]{:S(2)}, u32[]{:S(2)}) collective-permute-start(bf16[2,320,128]{2,1,0:T(8,128)(2,1)S(1)} %shard_map.76.b0), channel_id=1, source_target_pairs={{0,6},{2,0},{4,2},{6,4},{1,7},{3,1},{5,3},{7,5},{8,14},{10,8},{12,... | collective-permute-start | bytes 491528 | tf_op jit(solution)/shard_map/ppermute | solution.py:25
  88.8 1.3 collective-permute-done.18.b3
  90.2 4.7 %collective-permute-done.17.b2 = bf16[2,320,128]{2,1,0:T(8,128)(2,1)S(1)} collective-permute-done((bf16[2,320,128]{2,1,0:T(8,128)(2,1)S(1)}, bf16[2,320,128]{2,1,0:T(8,128)(2,1)S(1)}, u32[]{:S(2)}, u32[]{:S(2)}) %collective-permute-start.17) | collective-permute-done | bytes 163872 | tf_op jit(solution)/shard_map/ppermute | solution.py:25
  94.9 2.8 %shard_map.77 = (f32[512,1280]{1,0:T(8,128)S(1)}, bf16[256,1280]{1,0:T(8,128)(2,1)S(1)}, bf16[256,1280]{1,0:T(8,128)(2,1)S(1)}, bf16[2,320,512]{2,1,0:T(8,128)(2,1)S(1)}) custom-call(s32[1]{0:T(128)} %bitcast.me, bf16[2,320,128]{2,1,0:T(8,128)(2,1)S(1)} %shard_map.76.b0, bf16[2,320,128]{2,1,0:T(8,128)(2,1)S(1)} %collective-permute-done.16.b1, ...), custom_call_target="tpu_custom_call" | custom-call | flops 838860800 | bytes 1048576 | tf_op jit(solution)/shard_map/pallas_call | solution.py:50
  97.7 0.1 collective-permute-start.20
  97.8 2.1 %collective-permute-done.20 = bf16[256,1280]{1,0:T(8,128)(2,1)S(1)} collective-permute-done((bf16[256,1280]{1,0:T(8,128)(2,1)S(1)}, bf16[256,1280]{1,0:T(8,128)(2,1)S(1)}, u32[]{:S(2)}, u32[]{:S(2)}) %collective-permute-start.20) | collective-permute-done | bytes 655392 | tf_op jit(solution)/shard_map/ppermute | solution.py:25
  99.9 0.1 add_convert_fusion.4
  100.0 3.5 %collective-permute-start.25 = (bf16[32,1280]{1,0:T(8,128)(2,1)S(1)}, bf16[32,1280]{1,0:T(8,128)(2,1)S(1)}, u32[]{:S(2)}, u32[]{:S(2)}) collective-permute-start(bf16[32,1280]{1,0:T(8,128)(2,1)S(1)} %get-tuple-element.51), channel_id=1, source_target_pairs={{0,224},{32,0},{64,32},{96,64},{128,96},{160,128},{192,160},{224,1... | collective-permute-start | bytes 245768 | tf_op jit(solution)/shard_map/ppermute | solution.py:25
  103.5 2.0 %collective-permute-done.25 = bf16[32,1280]{1,0:T(8,128)(2,1)S(1)} collective-permute-done((bf16[32,1280]{1,0:T(8,128)(2,1)S(1)}, bf16[32,1280]{1,0:T(8,128)(2,1)S(1)}, u32[]{:S(2)}, u32[]{:S(2)}) %collective-permute-start.25) | collective-permute-done | bytes 81952 | tf_op jit(solution)/shard_map/ppermute | solution.py:25
  105.5 3.7 %collective-permute-start.26 = (bf16[64,1280]{1,0:T(8,128)(2,1)S(1)}, bf16[64,1280]{1,0:T(8,128)(2,1)S(1)}, u32[]{:S(2)}, u32[]{:S(2)}) collective-permute-start(bf16[64,1280]{1,0:T(8,128)(2,1)S(1)} %pad_maximum_fusion.2), channel_id=1, source_target_pairs={{0,224},{32,0},{64,32},{96,64},{128,96},{160,128},{192,160},{224,1... | collective-permute-start | bytes 491528 | tf_op jit(solution)/shard_map/ppermute | solution.py:25
  109.3 2.9 %collective-permute-done.26 = bf16[64,1280]{1,0:T(8,128)(2,1)S(1)} collective-permute-done((bf16[64,1280]{1,0:T(8,128)(2,1)S(1)}, bf16[64,1280]{1,0:T(8,128)(2,1)S(1)}, u32[]{:S(2)}, u32[]{:S(2)}) %collective-permute-start.26) | collective-permute-done | bytes 163872 | tf_op jit(solution)/shard_map/ppermute | solution.py:25
  112.2 0.1 convert_add_fusion.3
  112.3 3.0 %collective-permute-done.21 = bf16[32,1280]{1,0:T(8,128)(2,1)S(1)} collective-permute-done((bf16[32,1280]{1,0:T(8,128)(2,1)S(1)}, bf16[32,1280]{1,0:T(8,128)(2,1)S(1)}, u32[]{:S(2)}, u32[]{:S(2)}) %collective-permute-start.21) | collective-permute-done | bytes 81952 | tf_op jit(solution)/shard_map/ppermute | solution.py:25
  115.4 0.1 collective-permute-start.22
  115.5 3.2 %collective-permute-start.27 = (bf16[64,1280]{1,0:T(8,128)(2,1)S(1)}, bf16[64,1280]{1,0:T(8,128)(2,1)S(1)}, u32[]{:S(2)}, u32[]{:S(2)}) collective-permute-start(bf16[64,1280]{1,0:T(8,128)(2,1)S(1)} %get-tuple-element.41), channel_id=1, source_target_pairs={{0,224},{32,0},{64,32},{96,64},{128,96},{160,128},{192,160},{224,1... | collective-permute-start | bytes 491528 | tf_op jit(solution)/shard_map/ppermute | solution.py:25
  118.7 3.8 %collective-permute-done.22 = bf16[64,1280]{1,0:T(8,128)(2,1)S(1)} collective-permute-done((bf16[64,1280]{1,0:T(8,128)(2,1)S(1)}, bf16[64,1280]{1,0:T(8,128)(2,1)S(1)}, u32[]{:S(2)}, u32[]{:S(2)}) %collective-permute-start.22) | collective-permute-done | bytes 163872 | tf_op jit(solution)/shard_map/ppermute | solution.py:25
  122.5 0.1 add_convert_fusion.3
  122.5 0.1 collective-permute-start.23
  122.6 6.5 %collective-permute-done.23 = bf16[64,1280]{1,0:T(8,128)(2,1)S(1)} collective-permute-done((bf16[64,1280]{1,0:T(8,128)(2,1)S(1)}, bf16[64,1280]{1,0:T(8,128)(2,1)S(1)}, u32[]{:S(2)}, u32[]{:S(2)}) %collective-permute-start.23) | collective-permute-done | bytes 163872 | tf_op jit(solution)/shard_map/ppermute | solution.py:25
  129.2 0.1 add_convert_fusion.2
  129.3 0.1 collective-permute-start.24
  129.3 3.2 %collective-permute-start.28 = (bf16[64,1280]{1,0:T(8,128)(2,1)S(1)}, bf16[64,1280]{1,0:T(8,128)(2,1)S(1)}, u32[]{:S(2)}, u32[]{:S(2)}) collective-permute-start(bf16[64,1280]{1,0:T(8,128)(2,1)S(1)} %get-tuple-element.39), channel_id=1, source_target_pairs={{0,224},{32,0},{64,32},{96,64},{128,96},{160,128},{192,160},{224,1... | collective-permute-start | bytes 491528 | tf_op jit(solution)/shard_map/ppermute | solution.py:25
  132.6 0.6 shard_map.78
  133.2 0.6 collective-permute-start.30
  133.8 2.1 %collective-permute-done.24 = bf16[64,1280]{1,0:T(8,128)(2,1)S(1)} collective-permute-done((bf16[64,1280]{1,0:T(8,128)(2,1)S(1)}, bf16[64,1280]{1,0:T(8,128)(2,1)S(1)}, u32[]{:S(2)}, u32[]{:S(2)}) %collective-permute-start.24) | collective-permute-done | bytes 163872 | tf_op jit(solution)/shard_map/ppermute | solution.py:25
  135.9 0.1 fusion.4
  136.0 2.2 %collective-permute-start.29 = (bf16[32,1280]{1,0:T(8,128)(2,1)S(1)}, bf16[32,1280]{1,0:T(8,128)(2,1)S(1)}, u32[]{:S(2)}, u32[]{:S(2)}) collective-permute-start(bf16[32,1280]{1,0:T(8,128)(2,1)S(1)} %pad_maximum_fusion.4), channel_id=1, source_target_pairs={{0,16},{8,24},{16,0},{24,8},{1,17},{9,25},{17,1},{25,9},{2,18},{10... | collective-permute-start | bytes 245768 | tf_op jit(solution)/shard_map/ppermute | solution.py:25
  138.2 13.2 %collective-permute-done.30 = bf16[320,1280]{1,0:T(8,128)(2,1)S(1)} collective-permute-done((bf16[320,1280]{1,0:T(8,128)(2,1)S(1)}, bf16[320,1280]{1,0:T(8,128)(2,1)S(1)}, u32[]{:S(2)}, u32[]{:S(2)}) %collective-permute-start.30) | collective-permute-done | bytes 819232 | tf_op jit(solution)/shard_map/ppermute | solution.py:29
  151.4 0.6 shard_map.79
  152.0 1.3 convert_add_fusion
  153.3 0.6 fusion.2
  (40 shorter events, 0.3 us)
Async XLA Ops:
  0.6 40.1 %copy-start = (bf16[1280,160]{0,1:T(8,128)(2,1)S(1)}, bf16[1280,160]{0,1:T(8,128)(2,1)}, u32[]{:S(2)}) copy-start(bf16[1280,160]{0,1:T(8,128)(2,1)} %param.5) | copy-start | bytes 1228804
  0.6 40.7 %copy-start.1 = (bf16[160,1280]{1,0:T(8,128)(2,1)S(1)}, bf16[160,1280]{1,0:T(8,128)(2,1)}, u32[]{:S(2)}) copy-start(bf16[160,1280]{1,0:T(8,128)(2,1)} %wo.3) | copy-start | bytes 1228804
  1.5 5.9 %collective-permute-start = (bf16[32,1280]{1,0:T(8,128)(2,1)S(1)}, bf16[32,1280]{1,0:T(8,128)(2,1)S(1)}, u32[]{:S(2)}, u32[]{:S(2)}) collective-permute-start(bf16[32,1280]{1,0:T(8,128)(2,1)S(1)} %pad_maximum_fusion.3), channel_id=1, source_target_pairs={{0,16},{8,24},{16,0},{24,8},{1,17},{9,25},{17,1},{25,9},{2,18},{10... | collective-permute-start | bytes 245768 | tf_op jit(solution)/shard_map/ppermute | solution.py:25
  8.3 9.2 %collective-permute-start.2 = (bf16[64,1280]{1,0:T(8,128)(2,1)S(1)}, bf16[64,1280]{1,0:T(8,128)(2,1)S(1)}, u32[]{:S(2)}, u32[]{:S(2)}) collective-permute-start(bf16[64,1280]{1,0:T(8,128)(2,1)S(1)} %pad_maximum_fusion), channel_id=1, source_target_pairs={{0,32},{32,64},{64,96},{96,128},{128,160},{160,192},{192,224},{224... | collective-permute-start | bytes 491528 | tf_op jit(solution)/shard_map/ppermute | solution.py:25
  10.3 7.2 %collective-permute-start.1 = (bf16[64,1280]{1,0:T(8,128)(2,1)S(1)}, bf16[64,1280]{1,0:T(8,128)(2,1)S(1)}, u32[]{:S(2)}, u32[]{:S(2)}) collective-permute-start(bf16[64,1280]{1,0:T(8,128)(2,1)S(1)} %pad_maximum_fusion), channel_id=1, source_target_pairs={{0,224},{32,0},{64,32},{96,64},{128,96},{160,128},{192,160},{224,1... | collective-permute-start | bytes 491528 | tf_op jit(solution)/shard_map/ppermute | solution.py:25
  17.5 10.0 %collective-permute-start.4 = (bf16[64,1280]{1,0:T(8,128)(2,1)S(1)}, bf16[64,1280]{1,0:T(8,128)(2,1)S(1)}, u32[]{:S(2)}, u32[]{:S(2)}) collective-permute-start(bf16[64,1280]{1,0:T(8,128)(2,1)S(1)} %collective-permute-done.2), channel_id=1, source_target_pairs={{0,32},{32,64},{64,96},{96,128},{128,160},{160,192},{192,224},{224... | collective-permute-start | bytes 491528 | tf_op jit(solution)/shard_map/ppermute | solution.py:25
  17.5 6.2 %collective-permute-start.3 = (bf16[64,1280]{1,0:T(8,128)(2,1)S(1)}, bf16[64,1280]{1,0:T(8,128)(2,1)S(1)}, u32[]{:S(2)}, u32[]{:S(2)}) collective-permute-start(bf16[64,1280]{1,0:T(8,128)(2,1)S(1)} %collective-permute-done.1), channel_id=1, source_target_pairs={{0,224},{32,0},{64,32},{96,64},{128,96},{160,128},{192,160},{224,1... | collective-permute-start | bytes 491528 | tf_op jit(solution)/shard_map/ppermute | solution.py:25
  23.7 37.8 %collective-permute-start.9 = (bf16[256,1280]{1,0:T(8,128)(2,1)S(1)}, bf16[256,1280]{1,0:T(8,128)(2,1)S(1)}, u32[]{:S(2)}, u32[]{:S(2)}) collective-permute-start(bf16[256,1280]{1,0:T(8,128)(2,1)S(1)} %constant_dynamic-update-slice_fusion.q0), channel_id=1, source_target_pairs={{0,1},{1,0},{2,3},{3,2},{4,5},{5,4},{6,7},{7,6},{8,9},{9,8},{10,11... | collective-permute-start | bytes 1966088 | tf_op jit(solution)/shard_map/ppermute | solution.py:25
  23.8 11.3 %collective-permute-start.5 = (bf16[64,1280]{1,0:T(8,128)(2,1)S(1)}, bf16[64,1280]{1,0:T(8,128)(2,1)S(1)}, u32[]{:S(2)}, u32[]{:S(2)}) collective-permute-start(bf16[64,1280]{1,0:T(8,128)(2,1)S(1)} %collective-permute-done.3), channel_id=1, source_target_pairs={{0,224},{32,0},{64,32},{96,64},{128,96},{160,128},{192,160},{224,1... | collective-permute-start | bytes 491528 | tf_op jit(solution)/shard_map/ppermute | solution.py:25
  27.6 7.5 %collective-permute-start.6 = (bf16[64,1280]{1,0:T(8,128)(2,1)S(1)}, bf16[64,1280]{1,0:T(8,128)(2,1)S(1)}, u32[]{:S(2)}, u32[]{:S(2)}) collective-permute-start(bf16[64,1280]{1,0:T(8,128)(2,1)S(1)} %collective-permute-done.4), channel_id=1, source_target_pairs={{0,32},{32,64},{64,96},{96,128},{128,160},{160,192},{192,224},{224... | collective-permute-start | bytes 491528 | tf_op jit(solution)/shard_map/ppermute | solution.py:25
  35.1 5.7 %collective-permute-start.8 = (bf16[32,1280]{1,0:T(8,128)(2,1)S(1)}, bf16[32,1280]{1,0:T(8,128)(2,1)S(1)}, u32[]{:S(2)}, u32[]{:S(2)}) collective-permute-start(bf16[32,1280]{1,0:T(8,128)(2,1)S(1)} %slice.145), channel_id=1, source_target_pairs={{0,32},{32,64},{64,96},{96,128},{128,160},{160,192},{192,224},{224... | collective-permute-start | bytes 245768 | tf_op jit(solution)/shard_map/ppermute | solution.py:25
  35.1 5.4 %collective-permute-start.7 = (bf16[32,1280]{1,0:T(8,128)(2,1)S(1)}, bf16[32,1280]{1,0:T(8,128)(2,1)S(1)}, u32[]{:S(2)}, u32[]{:S(2)}) collective-permute-start(bf16[32,1280]{1,0:T(8,128)(2,1)S(1)} %slice.144), channel_id=1, source_target_pairs={{0,224},{32,0},{64,32},{96,64},{128,96},{160,128},{192,160},{224,1... | collective-permute-start | bytes 245768 | tf_op jit(solution)/shard_map/ppermute | solution.py:25
  40.7 20.8 %collective-permute-start.10 = (bf16[256,1280]{1,0:T(8,128)(2,1)S(1)}, bf16[256,1280]{1,0:T(8,128)(2,1)S(1)}, u32[]{:S(2)}, u32[]{:S(2)}) collective-permute-start(bf16[256,1280]{1,0:T(8,128)(2,1)S(1)} %constant_dynamic-update-slice_fusion.7.q1), channel_id=1, source_target_pairs={{0,1},{1,0},{2,3},{3,2},{4,5},{5,4},{6,7},{7,6},{8,9},{9,8},{10,11... | collective-permute-start | bytes 1966088 | tf_op jit(solution)/shard_map/ppermute | solution.py:25
  40.8 12.5 %collective-permute-start.11 = (bf16[160,1280]{1,0:T(8,128)(2,1)S(1)}, bf16[160,1280]{1,0:T(8,128)(2,1)}, u32[]{:S(2)}, u32[]{:S(2)}) collective-permute-start(bf16[160,1280]{1,0:T(8,128)(2,1)S(1)} %bitcast.4), channel_id=1, source_target_pairs={{0,8},{8,0},{16,24},{24,16},{1,9},{9,1},{17,25},{25,17},{2,10},{10... | collective-permute-start | bytes 1228808 | tf_op jit(solution)/shard_map/ppermute | solution.py:29
  41.4 20.1 %collective-permute-start.12 = (bf16[160,1280]{1,0:T(8,128)(2,1)S(1)}, bf16[160,1280]{1,0:T(8,128)(2,1)}, u32[]{:S(2)}, u32[]{:S(2)}) collective-permute-start(bf16[160,1280]{1,0:T(8,128)(2,1)S(1)} %copy-done.1), channel_id=1, source_target_pairs={{0,8},{8,0},{16,24},{24,16},{1,9},{9,1},{17,25},{25,17},{2,10},{10... | collective-permute-start | bytes 1228808 | tf_op jit(solution)/shard_map/ppermute | solution.py:29
  64.6 10.8 %collective-permute-start.13 = (f32[2,320,128]{2,1,0:T(8,128)S(1)}, f32[2,320,128]{2,1,0:T(8,128)S(1)}, u32[]{:S(2)}, u32[]{:S(2)}) collective-permute-start(f32[2,320,128]{2,1,0:T(8,128)S(1)} %get-tuple-element.23), channel_id=1, source_target_pairs={{0,2},{2,4},{4,6},{6,0},{1,3},{3,5},{5,7},{7,1},{8,10},{10,12},{12... | collective-permute-start | bytes 983048 | tf_op jit(solution)/shard_map/ppermute | solution.py:25
  66.3 17.1 %collective-permute-start.14 = (f32[2,320,128]{2,1,0:T(8,128)S(1)}, f32[2,320,128]{2,1,0:T(8,128)S(1)}, u32[]{:S(2)}, u32[]{:S(2)}) collective-permute-start(f32[2,320,128]{2,1,0:T(8,128)S(1)} %get-tuple-element.24), channel_id=1, source_target_pairs={{0,4},{2,6},{4,0},{6,2},{1,5},{3,7},{5,1},{7,3},{8,12},{10,14},{12... | collective-permute-start | bytes 983048 | tf_op jit(solution)/shard_map/ppermute | solution.py:25
  69.2 14.3 %collective-permute-start.15 = (f32[2,320,128]{2,1,0:T(8,128)S(1)}, f32[2,320,128]{2,1,0:T(8,128)S(1)}, u32[]{:S(2)}, u32[]{:S(2)}) collective-permute-start(f32[2,320,128]{2,1,0:T(8,128)S(1)} %get-tuple-element.25), channel_id=1, source_target_pairs={{0,6},{2,0},{4,2},{6,4},{1,7},{3,1},{5,3},{7,5},{8,14},{10,8},{12,... | collective-permute-start | bytes 983048 | tf_op jit(solution)/shard_map/ppermute | solution.py:25
  83.6 6.6 %collective-permute-start.18 = (bf16[2,320,128]{2,1,0:T(8,128)(2,1)S(1)}, bf16[2,320,128]{2,1,0:T(8,128)(2,1)S(1)}, u32[]{:S(2)}, u32[]{:S(2)}) collective-permute-start(bf16[2,320,128]{2,1,0:T(8,128)(2,1)S(1)} %shard_map.76.b0), channel_id=1, source_target_pairs={{0,2},{2,4},{4,6},{6,0},{1,3},{3,5},{5,7},{7,1},{8,10},{10,12},{12... | collective-permute-start | bytes 491528 | tf_op jit(solution)/shard_map/ppermute | solution.py:25
  84.9 10.0 %collective-permute-start.17 = (bf16[2,320,128]{2,1,0:T(8,128)(2,1)S(1)}, bf16[2,320,128]{2,1,0:T(8,128)(2,1)S(1)}, u32[]{:S(2)}, u32[]{:S(2)}) collective-permute-start(bf16[2,320,128]{2,1,0:T(8,128)(2,1)S(1)} %shard_map.76.b0), channel_id=1, source_target_pairs={{0,4},{2,6},{4,0},{6,2},{1,5},{3,7},{5,1},{7,3},{8,12},{10,14},{12... | collective-permute-start | bytes 491528 | tf_op jit(solution)/shard_map/ppermute | solution.py:25
  87.3 7.6 %collective-permute-start.16 = (bf16[2,320,128]{2,1,0:T(8,128)(2,1)S(1)}, bf16[2,320,128]{2,1,0:T(8,128)(2,1)S(1)}, u32[]{:S(2)}, u32[]{:S(2)}) collective-permute-start(bf16[2,320,128]{2,1,0:T(8,128)(2,1)S(1)} %shard_map.76.b0), channel_id=1, source_target_pairs={{0,6},{2,0},{4,2},{6,4},{1,7},{3,1},{5,3},{7,5},{8,14},{10,8},{12,... | collective-permute-start | bytes 491528 | tf_op jit(solution)/shard_map/ppermute | solution.py:25
  97.7 2.2 %collective-permute-start.20 = (bf16[256,1280]{1,0:T(8,128)(2,1)S(1)}, bf16[256,1280]{1,0:T(8,128)(2,1)S(1)}, u32[]{:S(2)}, u32[]{:S(2)}) collective-permute-start(bf16[256,1280]{1,0:T(8,128)(2,1)S(1)} %get-tuple-element.28), channel_id=1, source_target_pairs={{0,1},{1,0},{2,3},{3,2},{4,5},{5,4},{6,7},{7,6},{8,9},{9,8},{10,11... | collective-permute-start | bytes 1966088 | tf_op jit(solution)/shard_map/ppermute | solution.py:25
  100.0 5.5 %collective-permute-start.25 = (bf16[32,1280]{1,0:T(8,128)(2,1)S(1)}, bf16[32,1280]{1,0:T(8,128)(2,1)S(1)}, u32[]{:S(2)}, u32[]{:S(2)}) collective-permute-start(bf16[32,1280]{1,0:T(8,128)(2,1)S(1)} %get-tuple-element.51), channel_id=1, source_target_pairs={{0,224},{32,0},{64,32},{96,64},{128,96},{160,128},{192,160},{224,1... | collective-permute-start | bytes 245768 | tf_op jit(solution)/shard_map/ppermute | solution.py:25
  105.5 6.6 %collective-permute-start.26 = (bf16[64,1280]{1,0:T(8,128)(2,1)S(1)}, bf16[64,1280]{1,0:T(8,128)(2,1)S(1)}, u32[]{:S(2)}, u32[]{:S(2)}) collective-permute-start(bf16[64,1280]{1,0:T(8,128)(2,1)S(1)} %pad_maximum_fusion.2), channel_id=1, source_target_pairs={{0,224},{32,0},{64,32},{96,64},{128,96},{160,128},{192,160},{224,1... | collective-permute-start | bytes 491528 | tf_op jit(solution)/shard_map/ppermute | solution.py:25
  109.3 9.4 %collective-permute-start.19 = (bf16[256,1280]{1,0:T(8,128)(2,1)S(1)}, bf16[256,1280]{1,0:T(8,128)(2,1)S(1)}, u32[]{:S(2)}, u32[]{:S(2)}) collective-permute-start(bf16[256,1280]{1,0:T(8,128)(2,1)S(1)} %get-tuple-element.27), channel_id=1, source_target_pairs={{0,1},{1,0},{2,3},{3,2},{4,5},{5,4},{6,7},{7,6},{8,9},{9,8},{10,11... | collective-permute-start | bytes 1966088 | tf_op jit(solution)/shard_map/ppermute | solution.py:25
  109.3 6.1 %collective-permute-start.21 = (bf16[32,1280]{1,0:T(8,128)(2,1)S(1)}, bf16[32,1280]{1,0:T(8,128)(2,1)S(1)}, u32[]{:S(2)}, u32[]{:S(2)}) collective-permute-start(bf16[32,1280]{1,0:T(8,128)(2,1)S(1)} %get-tuple-element.50), channel_id=1, source_target_pairs={{0,32},{32,64},{64,96},{96,128},{128,160},{160,192},{192,224},{224... | collective-permute-start | bytes 245768 | tf_op jit(solution)/shard_map/ppermute | solution.py:25
  115.4 7.1 %collective-permute-start.22 = (bf16[64,1280]{1,0:T(8,128)(2,1)S(1)}, bf16[64,1280]{1,0:T(8,128)(2,1)S(1)}, u32[]{:S(2)}, u32[]{:S(2)}) collective-permute-start(bf16[64,1280]{1,0:T(8,128)(2,1)S(1)} %pad_maximum_fusion.1), channel_id=1, source_target_pairs={{0,32},{32,64},{64,96},{96,128},{128,160},{160,192},{192,224},{224... | collective-permute-start | bytes 491528 | tf_op jit(solution)/shard_map/ppermute | solution.py:25
  115.5 7.2 %collective-permute-start.27 = (bf16[64,1280]{1,0:T(8,128)(2,1)S(1)}, bf16[64,1280]{1,0:T(8,128)(2,1)S(1)}, u32[]{:S(2)}, u32[]{:S(2)}) collective-permute-start(bf16[64,1280]{1,0:T(8,128)(2,1)S(1)} %get-tuple-element.41), channel_id=1, source_target_pairs={{0,224},{32,0},{64,32},{96,64},{128,96},{160,128},{192,160},{224,1... | collective-permute-start | bytes 491528 | tf_op jit(solution)/shard_map/ppermute | solution.py:25
  122.5 6.6 %collective-permute-start.23 = (bf16[64,1280]{1,0:T(8,128)(2,1)S(1)}, bf16[64,1280]{1,0:T(8,128)(2,1)S(1)}, u32[]{:S(2)}, u32[]{:S(2)}) collective-permute-start(bf16[64,1280]{1,0:T(8,128)(2,1)S(1)} %add_convert_fusion.3), channel_id=1, source_target_pairs={{0,32},{32,64},{64,96},{96,128},{128,160},{160,192},{192,224},{224... | collective-permute-start | bytes 491528 | tf_op jit(solution)/shard_map/ppermute | solution.py:25
  129.3 6.6 %collective-permute-start.24 = (bf16[64,1280]{1,0:T(8,128)(2,1)S(1)}, bf16[64,1280]{1,0:T(8,128)(2,1)S(1)}, u32[]{:S(2)}, u32[]{:S(2)}) collective-permute-start(bf16[64,1280]{1,0:T(8,128)(2,1)S(1)} %get-tuple-element.38), channel_id=1, source_target_pairs={{0,32},{32,64},{64,96},{96,128},{128,160},{160,192},{192,224},{224... | collective-permute-start | bytes 491528 | tf_op jit(solution)/shard_map/ppermute | solution.py:25
  129.3 6.5 %collective-permute-start.28 = (bf16[64,1280]{1,0:T(8,128)(2,1)S(1)}, bf16[64,1280]{1,0:T(8,128)(2,1)S(1)}, u32[]{:S(2)}, u32[]{:S(2)}) collective-permute-start(bf16[64,1280]{1,0:T(8,128)(2,1)S(1)} %get-tuple-element.39), channel_id=1, source_target_pairs={{0,224},{32,0},{64,32},{96,64},{128,96},{160,128},{192,160},{224,1... | collective-permute-start | bytes 491528 | tf_op jit(solution)/shard_map/ppermute | solution.py:25
  133.2 18.2 %collective-permute-start.30 = (bf16[320,1280]{1,0:T(8,128)(2,1)S(1)}, bf16[320,1280]{1,0:T(8,128)(2,1)S(1)}, u32[]{:S(2)}, u32[]{:S(2)}) collective-permute-start(bf16[320,1280]{1,0:T(8,128)(2,1)S(1)} %shard_map.78), channel_id=1, source_target_pairs={{0,8},{8,0},{16,24},{24,16},{1,9},{9,1},{17,25},{25,17},{2,10},{10... | collective-permute-start | bytes 2457608 | tf_op jit(solution)/shard_map/ppermute | solution.py:29
  136.0 17.3 %collective-permute-start.29 = (bf16[32,1280]{1,0:T(8,128)(2,1)S(1)}, bf16[32,1280]{1,0:T(8,128)(2,1)S(1)}, u32[]{:S(2)}, u32[]{:S(2)}) collective-permute-start(bf16[32,1280]{1,0:T(8,128)(2,1)S(1)} %pad_maximum_fusion.4), channel_id=1, source_target_pairs={{0,16},{8,24},{16,0},{24,8},{1,17},{9,25},{17,1},{25,9},{2,18},{10... | collective-permute-start | bytes 245768 | tf_op jit(solution)/shard_map/ppermute | solution.py:25

commit v2 on v1

v2 whole, which is shorter than its diff:
```python
import functools

import jax
import jax.numpy as jnp
from jax import lax
from jax.experimental import pallas as pl
from jax.experimental.pallas import tpu as pltpu
from jax.sharding import Mesh, PartitionSpec as P

BF = jnp.bfloat16
F32 = jnp.float32
SIZE = {"z": 8, "x": 4, "row": 4, "col": 2}
ORDER = (0, 1, 7, 2, 6, 3, 5, 4)
HEAD = 5


def smooth_gate(value):
    return 0.5 * value * (1.0 + lax.erf(value * 0.7071067811865476))


def smooth_slope(value):
    cumul = 0.5 * (1.0 + lax.erf(value * 0.7071067811865476))
    return cumul + value * jnp.exp(-0.5 * value * value) * 0.3989422804014327


def send(value, axis, shift):
    size = SIZE[axis]
    return lax.ppermute(value, axis, [(i, (i + shift) % size) for i in range(size)])


def token_pair(value):
    return lax.ppermute(value, "x", [(0, 1), (1, 0), (2, 3), (3, 2)])


def weight_pair(value):
    return lax.ppermute(value, "x", [(0, 3), (3, 0), (1, 2), (2, 1)])


def after(value, other):
    return lax.optimization_barrier((value, other))[0]


def call(body, outs, args, flops=1 << 20, scratch=()):
    specs = [pl.BlockSpec(memory_space=pltpu.SMEM)]
    specs += [pl.BlockSpec(memory_space=pltpu.VMEM)] * (len(args) - 1)
    kernel = pl.pallas_call(
        body,
        out_shape=outs,
        in_specs=specs,
        out_specs=[pl.BlockSpec(memory_space=pltpu.VMEM)] * len(outs),
        scratch_shapes=list(scratch),
        compiler_params=pltpu.CompilerParams(vmem_limit_bytes=40 << 20),
        cost_estimate=pl.CostEstimate(
            flops=flops, bytes_accessed=1 << 20, transcendentals=0
        ),
    )
    return list(kernel(*args))


def cat(values):
    return jnp.concatenate(values, 0)


def dot(a, b, dim_a, dim_b):
    return lax.dot_general(
        a, b, (((dim_a,), (dim_b,)), ((), ())), preferred_element_type=F32
    )


def up_kernel(me, *refs):
    quarters, weights = refs[:8], (refs[8:10], refs[10:12])
    tok, cot, parts, whole = refs[12], refs[13], refs[14:18], refs[18]
    h = weights[0][0].shape[0]
    for q in range(4):
        for j in range(8):
            ref, i = (quarters[2 * q], j) if j < HEAD else (quarters[2 * q + 1], j - HEAD)
            row = q * 128 + j * 16
            tok[row : row + 16] = ref[i * 32 : i * 32 + 16]
            cot[row : row + 16] = ref[i * 32 + 16 : i * 32 + 32]
    for s, value in enumerate((tok, cot)):
        for i, w in enumerate(weights[s]):
            total = dot(w[...], value[...], 1, 1)
            for q in range(4):
                whole[q, s, i * h : i * h + h] = total[:, q * 128 : q * 128 + 128]
    for k, part in enumerate(parts):
        part[...] = whole[(me[0] + k) % 4]


def act_kernel(me, p0, p1, p2, p3, out):
    del me
    pre = p0[0] + p1[0] + p2[0] + p3[0]
    grad_act = p0[1] + p1[1] + p2[1] + p3[1]
    out[0] = smooth_gate(pre).astype(BF)
    out[1] = (grad_act * smooth_slope(pre)).astype(BF)


def down_kernel(me, b0, b1, b2, b3, wi, wi2, wo, wo2, near, far, head, tail, full):
    h = wi.shape[0]
    for k, block in enumerate((b0, b1, b2, b3)):
        lane = pl.multiple_of(((me[0] + k) % 4) * 128, 128)
        full[:, :, pl.ds(lane, 128)] = block[...]
    for s, (w, w2) in enumerate(((wo, wo2), (wi, wi2))):
        value = dot(full[s, :h], w[...], 0, 0) + dot(full[s, h:], w2[...], 0, 0)
        for q in range(4):
            for j in range(8):
                piece = value[q * 128 + j * 16 : q * 128 + j * 16 + 16]
                row = j * 32 + s * 16
                if q < 2:
                    (near, far)[q][row : row + 16] = piece
                elif j < HEAD:
                    row += (3 - q) * HEAD * 32
                    head[row : row + 16] = piece.astype(BF)
                else:
                    row += (3 - q) * (8 - HEAD) * 32 - HEAD * 32
                    tail[row : row + 16] = piece.astype(BF)


def pair_kernel(me, full, tok, cot, out, back):
    del me
    h = full.shape[1] // 2
    out[...] = dot(full[0, h:], cot[...], 1, 0).astype(BF)
    back[...] = dot(full[1, h:], tok[...], 1, 0).astype(BF)


def own_kernel(s, me, full, value, other, grad):
    del me
    h = full.shape[1] // 2
    grad[...] = dot(full[s, :h], value[...], 1, 0) + other[...].astype(F32)


def on_device(tokens, w_in, w_out, cotangent):
    me = lax.axis_index("row").astype(jnp.int32).reshape(1)
    d, h = w_in.shape
    shape = jax.ShapeDtypeStruct
    flops = 2 * 1024 * d * h

    z = {0: cat([tokens, cotangent])}
    z[1], z[7] = send(z[0], "z", -1), send(z[0], "z", 1)
    w_in_t = w_in.T
    w_in_2 = weight_pair(after(w_in_t, z[0]))
    z[2], z[6] = send(z[1], "z", -1), send(z[7], "z", 1)
    near_h = cat([z[k] for k in ORDER[:HEAD]])
    ring = after((z[2], z[6]), w_in_2)
    w_out_2 = weight_pair(after(w_out, z[2]))
    far_h = token_pair(near_h)
    z[3], z[5] = send(ring[0], "z", -1), send(ring[1], "z", 1)
    ring = after((z[3], z[5]), w_out_2)
    z[4] = cat([send(ring[0][:16], "z", -1), send(ring[1][16:], "z", 1)])
    near_t = cat([z[k] for k in ORDER[HEAD:]])
    far_t = token_pair(near_t)
    quarters = [near_h, near_t, far_h, far_t]
    quarters += [send(value, "col", 1) for value in quarters]

    part = shape((2, 2 * h, 128), F32)
    tok, cot, *parts = call(
        up_kernel,
        [shape((512, d), BF)] * 2 + [part] * 4,
        [me, *quarters, w_in_t, w_in_2, w_out, w_out_2],
        2 * flops,
        [pltpu.VMEM((4, 2, 2 * h, 128), F32)],
    )
    parts[1:] = [send(parts[k], "row", k) for k in (1, 2, 3)]
    (block,) = call(act_kernel, [shape((2, 2 * h, 128), BF)], [me, *parts])
    blocks = [block] + [send(block, "row", -k) for k in (1, 2, 3)]

    sums = shape((256, d), F32)
    near, far, head, tail, full = call(
        down_kernel,
        [sums, sums, shape((HEAD * 64, d), BF), shape(((8 - HEAD) * 64, d), BF), shape((2, 2 * h, 512), BF)],
        [me, *blocks, w_in_t, w_in_2, w_out, w_out_2],
        2 * flops,
    )
    cut, rest = HEAD * 32, (8 - HEAD) * 32
    tail = send(tail, "col", 1).astype(F32)
    far_t = token_pair((far[cut:] + tail[:rest]).astype(BF)).astype(F32)
    near_t = near[cut:] + tail[rest:] + far_t
    head = send(head, "col", 1).astype(F32)
    far_h = token_pair((far[:cut] + head[:cut]).astype(BF)).astype(F32)
    near_h = near[:cut] + head[cut:] + far_h
    piece = {}
    for i, k in enumerate(ORDER):
        piece[k] = near_h[i * 32 : i * 32 + 32] if i < HEAD else near_t[(i - HEAD) * 32 : (i - HEAD) * 32 + 32]
    pair_out, pair_in = call(
        pair_kernel, [shape((h, d), BF)] * 2, [me, after(full, tail), tok, cot], flops
    )
    pair_out, pair_in = weight_pair(pair_out), weight_pair(pair_in)
    up = send(piece[4][:16].astype(BF), "z", 1).astype(F32)
    down = send(piece[4][16:].astype(BF), "z", -1).astype(F32)
    up = cat([up + piece[3][:16], piece[3][16:]]).astype(BF)
    down = cat([piece[5][:16], down + piece[5][16:]]).astype(BF)
    up, down = after((up, down), pair_out)
    up, down = send(up, "z", 1).astype(F32), send(down, "z", -1).astype(F32)
    up, down = (up + piece[2]).astype(BF), (down + piece[6]).astype(BF)
    up, down = after((up, down), pair_in)
    up, down = send(up, "z", 1).astype(F32), send(down, "z", -1).astype(F32)
    weight = [shape((h, d), F32)]
    (grad_out,) = call(functools.partial(own_kernel, 0), weight, [me, full, cot, pair_out], flops)
    (grad_in_t,) = call(functools.partial(own_kernel, 1), weight, [me, full, tok, pair_in], flops)
    up, down = (up + piece[1]).astype(BF), (down + piece[7]).astype(BF)
    up, down = send(up, "z", 1).astype(F32), send(down, "z", -1).astype(F32)
    total = (piece[0] + up + down).astype(BF)
    output, input_grad = total[:16], total[16:]
    return (output, input_grad, grad_in_t.T, grad_out)


def solution(mesh):
    mesh = Mesh(mesh.devices.reshape(8, 4, 4, 2), ("z", "x", "row", "col"))
    whole = ("z", "x", "col")
    placed = (P(whole, "row"), P("row", whole), P(whole, "row"), P(whole, "row"))
    return jax.shard_map(
        on_device,
        mesh=mesh,
        in_specs=placed,
        out_specs=(P(whole, "row"), P(whole, "row"), P("row", whole), P(whole, "row")),
        check_vma=False,
    )
```

time: 155 us -> 118 us (0.76)
  waiting for transfers between devices: 91.3 us -> 56.1 us
  other arithmetic: 4.07 us -> 0.6 us
    ppermute x28, waiting for transfers between devices: 59.4 us -> 38.5 us  [send(): lax.ppermute(value, axis, [(i, (i + shift) % size) for i in range(size)])]
    ppermute x3 -> x8, waiting for transfers between devices: 31.9 us -> 17.6 us  [the longest x4 10.6 us: token_pair(): return lax.ppermute(value, 'x', [(0, 1), (1, 0), (2, 3), (3, 2)])]
    ppermute x3 -> x8, starting transfers between devices: 2.74 us -> 11 us  [the longest x4 5.71 us: token_pair(): return lax.ppermute(value, 'x', [(0, 1), (1, 0), (2, 3), (3, 2)])]
    ppermute x28, starting transfers between devices: 46 us -> 38 us  [send(): lax.ppermute(value, axis, [(i, (i + shift) % size) for i in range(size)])]
    concatenate x5 -> x1, other arithmetic: 1.73 us -> 0.01 us  [cat(): return jnp.concatenate(values, 0)]
    pallas_call x5 -> x6, Pallas kernels: 7.21 us -> 8.12 us  [call(): return list(kernel(*args))]
  transfers between devices with their start and end apart: 31 -> 36, of which waited for: 20 -> 21; matrix products, arithmetic and copies ran while one was open for 2% -> 0% of each run, Pallas kernels for 1% -> 3%
where the time goes in v2:
time: 118 us; the launch traced here: 117 us
  waiting for transfers between devices  56.1 us (48%)
  starting transfers between devices  49.1 us (42%)
  Pallas kernels  8.12 us (7%)
  local copies, waits for them, and re-layouts  2.36 us (2%)
    ppermute x28, waiting for transfers between devices, send(): lax.ppermute(value, axis, [(i, (i + shift) % size) for i in range(size)])  38.5 us
    ppermute x28, starting transfers between devices, send(): lax.ppermute(value, axis, [(i, (i + shift) % size) for i in range(size)])  38 us
    ppermute x4, waiting for transfers between devices, token_pair(): return lax.ppermute(value, 'x', [(0, 1), (1, 0), (2, 3), (3, 2)])  10.6 us
    pallas_call x6, Pallas kernels, call(): return list(kernel(*args))  8.12 us
    ppermute x4, waiting for transfers between devices, weight_pair(): return lax.ppermute(value, 'x', [(0, 3), (3, 0), (1, 2), (2, 1)])  7.01 us
    ppermute x4, starting transfers between devices, token_pair(): return lax.ppermute(value, 'x', [(0, 1), (1, 0), (2, 3), (3, 2)])  5.71 us
    ppermute x4, starting transfers between devices, weight_pair(): return lax.ppermute(value, 'x', [(0, 3), (3, 0), (1, 2), (2, 1)])  5.32 us
  transfers between devices with their start and end apart: 36, of which 21 were waited for; matrix products, arithmetic and copies ran while one was open for 0% of the time, Pallas kernels for 3%

profile of v2, /device:TPU:2, one launch (start us, length us, event | category | flops | bytes accessed | tf_op | source)
XLA Modules:
  0.0 117.1 jit_solution(9031102490606939781)
XLA Ops:
  0.7 0.9 constant_dynamic-update-slice_fusion.1
  1.5 0.8 constant_dynamic-update-slice_fusion
  2.3 1.9 %collective-permute-start.1 = (bf16[32,1280]{1,0:T(8,128)(2,1)S(1)}, bf16[32,1280]{1,0:T(8,128)(2,1)S(1)}, u32[]{:S(2)}, u32[]{:S(2)}) collective-permute-start(bf16[32,1280]{1,0:T(8,128)(2,1)S(1)} %get-tuple-element.66), channel_id=1, source_target_pairs={{0,32},{32,64},{64,96},{96,128},{128,160},{160,192},{192,224},{224... | collective-permute-start | bytes 245768 | tf_op jit(solution)/shard_map/ppermute | solution.py:28
  4.2 4.0 %collective-permute-start = (bf16[32,1280]{1,0:T(8,128)(2,1)S(1)}, bf16[32,1280]{1,0:T(8,128)(2,1)S(1)}, u32[]{:S(2)}, u32[]{:S(2)}) collective-permute-start(bf16[32,1280]{1,0:T(8,128)(2,1)S(1)} %get-tuple-element.66), channel_id=1, source_target_pairs={{0,224},{32,0},{64,32},{96,64},{128,96},{160,128},{192,160},{224,1... | collective-permute-start | bytes 245768 | tf_op jit(solution)/shard_map/ppermute | solution.py:28
  8.2 1.5 %collective-permute-start.4 = (bf16[160,1280]{1,0:T(8,128)(2,1)}, bf16[160,1280]{1,0:T(8,128)(2,1)S(1)}, u32[]{:S(2)}, u32[]{:S(2)}) collective-permute-start(bf16[160,1280]{1,0:T(8,128)(2,1)} %bitcast.3), channel_id=1, source_target_pairs={{0,24},{24,0},{8,16},{16,8},{1,25},{25,1},{9,17},{17,9},{2,26},{26... | collective-permute-start | bytes 1228808 | tf_op jit(solution)/shard_map/ppermute | solution.py:36
  9.7 0.9 collective-permute-done.1
  10.6 3.3 %collective-permute-start.2 = (bf16[32,1280]{1,0:T(8,128)(2,1)S(1)}, bf16[32,1280]{1,0:T(8,128)(2,1)S(1)}, u32[]{:S(2)}, u32[]{:S(2)}) collective-permute-start(bf16[32,1280]{1,0:T(8,128)(2,1)S(1)} %collective-permute-done), channel_id=1, source_target_pairs={{0,224},{32,0},{64,32},{96,64},{128,96},{160,128},{192,160},{224,1... | collective-permute-start | bytes 245768 | tf_op jit(solution)/shard_map/ppermute | solution.py:28
  13.9 2.0 %collective-permute-done.2 = bf16[32,1280]{1,0:T(8,128)(2,1)S(1)} collective-permute-done((bf16[32,1280]{1,0:T(8,128)(2,1)S(1)}, bf16[32,1280]{1,0:T(8,128)(2,1)S(1)}, u32[]{:S(2)}, u32[]{:S(2)}) %collective-permute-start.2) | collective-permute-done | bytes 81952 | tf_op jit(solution)/shard_map/ppermute | solution.py:28
  15.9 1.5 %collective-permute-start.7 = (bf16[160,1280]{1,0:T(8,128)(2,1)}, bf16[160,1280]{1,0:T(8,128)(2,1)S(1)}, u32[]{:S(2)}, u32[]{:S(2)}) collective-permute-start(bf16[160,1280]{1,0:T(8,128)(2,1)} %wo.1), channel_id=1, source_target_pairs={{0,24},{24,0},{8,16},{16,8},{1,25},{25,1},{9,17},{17,9},{2,26},{26... | collective-permute-start | bytes 1228808 | tf_op jit(solution)/shard_map/ppermute | solution.py:36
  17.5 3.4 %collective-permute-done.4.refs_9_.wi2 = bf16[160,1280]{1,0:T(8,128)(2,1)S(1)} collective-permute-done((bf16[160,1280]{1,0:T(8,128)(2,1)}, bf16[160,1280]{1,0:T(8,128)(2,1)S(1)}, u32[]{:S(2)}, u32[]{:S(2)}) %collective-permute-start.4) | collective-permute-done | bytes 409632 | tf_op jit(solution)/shard_map/ppermute | solution.py:36
  20.8 1.0 collective-permute-start.5
  21.9 1.1 collective-permute-start.10
  22.9 1.7 %collective-permute-start.6 = (bf16[32,1280]{1,0:T(8,128)(2,1)S(1)}, bf16[32,1280]{1,0:T(8,128)(2,1)S(1)}, u32[]{:S(2)}, u32[]{:S(2)}) collective-permute-start(bf16[32,1280]{1,0:T(8,128)(2,1)S(1)} %collective-permute-done.3), channel_id=1, source_target_pairs={{0,32},{32,64},{64,96},{96,128},{128,160},{160,192},{192,224},{224... | collective-permute-start | bytes 245768 | tf_op jit(solution)/shard_map/ppermute | solution.py:28
  24.6 0.7 collective-permute-done.5
  25.3 3.3 %collective-permute-done.6 = bf16[32,1280]{1,0:T(8,128)(2,1)S(1)} collective-permute-done((bf16[32,1280]{1,0:T(8,128)(2,1)S(1)}, bf16[32,1280]{1,0:T(8,128)(2,1)S(1)}, u32[]{:S(2)}, u32[]{:S(2)}) %collective-permute-start.6) | collective-permute-done | bytes 81952 | tf_op jit(solution)/shard_map/ppermute | solution.py:28
  28.6 1.5 %collective-permute-start.8 = (bf16[16,1280]{1,0:T(8,128)(2,1)S(1)}, bf16[16,1280]{1,0:T(8,128)(2,1)S(1)}, u32[]{:S(2)}, u32[]{:S(2)}) collective-permute-start(bf16[16,1280]{1,0:T(8,128)(2,1)S(1)} %slice.82), channel_id=1, source_target_pairs={{0,224},{32,0},{64,32},{96,64},{128,96},{160,128},{192,160},{224,1... | collective-permute-start | bytes 122888 | tf_op jit(solution)/shard_map/ppermute | solution.py:28
  30.1 0.7 collective-permute-start.9
  30.8 1.9 %collective-permute-done.8 = bf16[16,1280]{1,0:T(8,128)(2,1)S(1)} collective-permute-done((bf16[16,1280]{1,0:T(8,128)(2,1)S(1)}, bf16[16,1280]{1,0:T(8,128)(2,1)S(1)}, u32[]{:S(2)}, u32[]{:S(2)}) %collective-permute-start.8) | collective-permute-done | bytes 40992 | tf_op jit(solution)/shard_map/ppermute | solution.py:28
  32.7 2.7 %collective-permute-done.9 = bf16[16,1280]{1,0:T(8,128)(2,1)S(1)} collective-permute-done((bf16[16,1280]{1,0:T(8,128)(2,1)S(1)}, bf16[16,1280]{1,0:T(8,128)(2,1)S(1)}, u32[]{:S(2)}, u32[]{:S(2)}) %collective-permute-start.9) | collective-permute-done | bytes 40992 | tf_op jit(solution)/shard_map/ppermute | solution.py:28
  35.4 1.5 %collective-permute-start.11 = (bf16[96,1280]{1,0:T(8,128)(2,1)S(1)}, bf16[96,1280]{1,0:T(8,128)(2,1)}, u32[]{:S(2)}, u32[]{:S(2)}) collective-permute-start(bf16[96,1280]{1,0:T(8,128)(2,1)S(1)} %constant_dynamic-update-slice_fusion.8.refs_1_), channel_id=1, source_target_pairs={{0,8},{8,0},{16,24},{24,16},{1,9},{9,1},{17,25},{25,17},{2,10},{10... | collective-permute-start | bytes 737288 | tf_op jit(solution)/shard_map/ppermute | solution.py:32
  36.9 0.5 collective-permute-start.14
  37.4 4.3 %collective-permute-done.11.refs_3_ = bf16[96,1280]{1,0:T(8,128)(2,1)} collective-permute-done((bf16[96,1280]{1,0:T(8,128)(2,1)S(1)}, bf16[96,1280]{1,0:T(8,128)(2,1)}, u32[]{:S(2)}, u32[]{:S(2)}) %collective-permute-start.11) | collective-permute-done | bytes 245792 | tf_op jit(solution)/shard_map/ppermute | solution.py:32
  41.7 1.8 %collective-permute-done.15.refs_7_ = bf16[96,1280]{1,0:T(8,128)(2,1)} collective-permute-done((bf16[96,1280]{1,0:T(8,128)(2,1)}, bf16[96,1280]{1,0:T(8,128)(2,1)}, u32[]{:S(2)}, u32[]{:S(2)}) %collective-permute-start.15) | collective-permute-done | bytes 245792 | tf_op jit(solution)/shard_map/ppermute | solution.py:28
  43.5 3.1 %shard_map.75 = (bf16[512,1280]{1,0:T(8,128)(2,1)S(1)}, bf16[512,1280]{1,0:T(8,128)(2,1)S(1)}, f32[2,320,128]{2,1,0:T(8,128)S(1)}, f32[2,320,128]{2,1,0:T(8,128)...) custom-call(s32[1]{0:T(128)} %bitcast.me, ...), custom_call_target="tpu_custom_call" | custom-call | flops 838860800 | bytes 1048576 | tf_op jit(solution)/shard_map/pallas_call | solution.py:57
  46.7 1.8 %collective-permute-start.16 = (f32[2,320,128]{2,1,0:T(8,128)S(1)}, f32[2,320,128]{2,1,0:T(8,128)S(1)}, u32[]{:S(2)}, u32[]{:S(2)}) collective-permute-start(f32[2,320,128]{2,1,0:T(8,128)S(1)} %get-tuple-element.35), channel_id=1, source_target_pairs={{0,2},{2,4},{4,6},{6,0},{1,3},{3,5},{5,7},{7,1},{8,10},{10,12},{12... | collective-permute-start | bytes 983048 | tf_op jit(solution)/shard_map/ppermute | solution.py:28
  48.5 2.9 %collective-permute-start.17 = (f32[2,320,128]{2,1,0:T(8,128)S(1)}, f32[2,320,128]{2,1,0:T(8,128)S(1)}, u32[]{:S(2)}, u32[]{:S(2)}) collective-permute-start(f32[2,320,128]{2,1,0:T(8,128)S(1)} %get-tuple-element.36), channel_id=1, source_target_pairs={{0,4},{2,6},{4,0},{6,2},{1,5},{3,7},{5,1},{7,3},{8,12},{10,14},{12... | collective-permute-start | bytes 983048 | tf_op jit(solution)/shard_map/ppermute | solution.py:28
  51.4 1.3 %collective-permute-start.18 = (f32[2,320,128]{2,1,0:T(8,128)S(1)}, f32[2,320,128]{2,1,0:T(8,128)S(1)}, u32[]{:S(2)}, u32[]{:S(2)}) collective-permute-start(f32[2,320,128]{2,1,0:T(8,128)S(1)} %get-tuple-element.37), channel_id=1, source_target_pairs={{0,6},{2,0},{4,2},{6,4},{1,7},{3,1},{5,3},{7,5},{8,14},{10,8},{12,... | collective-permute-start | bytes 983048 | tf_op jit(solution)/shard_map/ppermute | solution.py:28
  52.8 5.2 %collective-permute-done.16.p1 = f32[2,320,128]{2,1,0:T(8,128)S(1)} collective-permute-done((f32[2,320,128]{2,1,0:T(8,128)S(1)}, f32[2,320,128]{2,1,0:T(8,128)S(1)}, u32[]{:S(2)}, u32[]{:S(2)}) %collective-permute-start.16) | collective-permute-done | bytes 327712 | tf_op jit(solution)/shard_map/ppermute | solution.py:28
  58.0 8.2 %collective-permute-done.17.p2 = f32[2,320,128]{2,1,0:T(8,128)S(1)} collective-permute-done((f32[2,320,128]{2,1,0:T(8,128)S(1)}, f32[2,320,128]{2,1,0:T(8,128)S(1)}, u32[]{:S(2)}, u32[]{:S(2)}) %collective-permute-start.17) | collective-permute-done | bytes 327712 | tf_op jit(solution)/shard_map/ppermute | solution.py:28
  66.2 0.1 shard_map.76.b0
  66.3 1.3 %collective-permute-start.21 = (bf16[2,320,128]{2,1,0:T(8,128)(2,1)S(1)}, bf16[2,320,128]{2,1,0:T(8,128)(2,1)S(1)}, u32[]{:S(2)}, u32[]{:S(2)}) collective-permute-start(bf16[2,320,128]{2,1,0:T(8,128)(2,1)S(1)} %shard_map.76.b0), channel_id=1, source_target_pairs={{0,2},{2,4},{4,6},{6,0},{1,3},{3,5},{5,7},{7,1},{8,10},{10,12},{12... | collective-permute-start | bytes 491528 | tf_op jit(solution)/shard_map/ppermute | solution.py:28
  67.6 2.4 %collective-permute-start.20 = (bf16[2,320,128]{2,1,0:T(8,128)(2,1)S(1)}, bf16[2,320,128]{2,1,0:T(8,128)(2,1)S(1)}, u32[]{:S(2)}, u32[]{:S(2)}) collective-permute-start(bf16[2,320,128]{2,1,0:T(8,128)(2,1)S(1)} %shard_map.76.b0), channel_id=1, source_target_pairs={{0,4},{2,6},{4,0},{6,2},{1,5},{3,7},{5,1},{7,3},{8,12},{10,14},{12... | collective-permute-start | bytes 491528 | tf_op jit(solution)/shard_map/ppermute | solution.py:28
  70.0 1.6 %collective-permute-start.19 = (bf16[2,320,128]{2,1,0:T(8,128)(2,1)S(1)}, bf16[2,320,128]{2,1,0:T(8,128)(2,1)S(1)}, u32[]{:S(2)}, u32[]{:S(2)}) collective-permute-start(bf16[2,320,128]{2,1,0:T(8,128)(2,1)S(1)} %shard_map.76.b0), channel_id=1, source_target_pairs={{0,6},{2,0},{4,2},{6,4},{1,7},{3,1},{5,3},{7,5},{8,14},{10,8},{12,... | collective-permute-start | bytes 491528 | tf_op jit(solution)/shard_map/ppermute | solution.py:28
  71.6 1.4 %collective-permute-done.21.b3 = bf16[2,320,128]{2,1,0:T(8,128)(2,1)S(1)} collective-permute-done((bf16[2,320,128]{2,1,0:T(8,128)(2,1)S(1)}, bf16[2,320,128]{2,1,0:T(8,128)(2,1)S(1)}, u32[]{:S(2)}, u32[]{:S(2)}) %collective-permute-start.21) | collective-permute-done | bytes 163872 | tf_op jit(solution)/shard_map/ppermute | solution.py:28
  73.0 4.6 %collective-permute-done.20.b2 = bf16[2,320,128]{2,1,0:T(8,128)(2,1)S(1)} collective-permute-done((bf16[2,320,128]{2,1,0:T(8,128)(2,1)S(1)}, bf16[2,320,128]{2,1,0:T(8,128)(2,1)S(1)}, u32[]{:S(2)}, u32[]{:S(2)}) %collective-permute-start.20) | collective-permute-done | bytes 163872 | tf_op jit(solution)/shard_map/ppermute | solution.py:28
  77.6 1.7 %shard_map.77 = (f32[256,1280]{1,0:T(8,128)S(1)}, f32[256,1280]{1,0:T(8,128)S(1)}, bf16[320,1280]{1,0:T(8,128)(2,1)S(1)}, bf16[192,1280]{1,0:T(8,128)(2,1)S(1)}, bf16[2,320,512]{2,1,0:T(8,128)(2,1)S(1)}) custom-call(s32[1]{0:T(128)} %bitcast.me, bf16[2,320,128]{2,1,0:T(8,128)(2,1)S(1)} %shard_map.76.b0, bf16[2,320,128]{2,1,0:T(8,128)(2,1)S(1)} %collective-permute-done.19.b1, ...), custom_call_target="tpu_custom_call" | custom-call | flops 838860800 | bytes 1048576 | tf_op jit(solution)/shard_map/pallas_call | solution.py:57
  79.3 0.1 collective-permute-start.24
  79.4 1.9 %collective-permute-done.24 = bf16[192,1280]{1,0:T(8,128)(2,1)S(1)} collective-permute-done((bf16[192,1280]{1,0:T(8,128)(2,1)S(1)}, bf16[192,1280]{1,0:T(8,128)(2,1)S(1)}, u32[]{:S(2)}, u32[]{:S(2)}) %collective-permute-start.24) | collective-permute-done | bytes 491552 | tf_op jit(solution)/shard_map/ppermute | solution.py:28
  81.3 0.1 convert_element_type.64
  81.4 1.6 %collective-permute-start.25 = (bf16[96,1280]{1,0:T(8,128)(2,1)S(1)}, bf16[96,1280]{1,0:T(8,128)(2,1)S(1)}, u32[]{:S(2)}, u32[]{:S(2)}) collective-permute-start(bf16[96,1280]{1,0:T(8,128)(2,1)S(1)} %fusion.2), channel_id=1, source_target_pairs={{0,8},{8,0},{16,24},{24,16},{1,9},{9,1},{17,25},{25,17},{2,10},{10... | collective-permute-start | bytes 737288 | tf_op jit(solution)/shard_map/ppermute | solution.py:32
  83.0 0.6 shard_map.78
  83.6 2.2 %collective-permute-start.28 = (bf16[160,1280]{1,0:T(8,128)(2,1)S(1)}, bf16[160,1280]{1,0:T(8,128)(2,1)S(1)}, u32[]{:S(2)}, u32[]{:S(2)}) collective-permute-start(bf16[160,1280]{1,0:T(8,128)(2,1)S(1)} %get-tuple-element.46), channel_id=1, source_target_pairs={{0,24},{24,0},{8,16},{16,8},{1,25},{25,1},{9,17},{17,9},{2,26},{26... | collective-permute-start | bytes 1228808 | tf_op jit(solution)/shard_map/ppermute | solution.py:36
  85.8 0.1 collective-permute-start.31
  85.9 3.6 %collective-permute-done.25 = bf16[96,1280]{1,0:T(8,128)(2,1)S(1)} collective-permute-done((bf16[96,1280]{1,0:T(8,128)(2,1)S(1)}, bf16[96,1280]{1,0:T(8,128)(2,1)S(1)}, u32[]{:S(2)}, u32[]{:S(2)}) %collective-permute-start.25) | collective-permute-done | bytes 245792 | tf_op jit(solution)/shard_map/ppermute | solution.py:32
  89.5 0.1 fusion.12
  89.6 0.1 collective-permute-start.27
  89.7 2.0 %collective-permute-start.26 = (bf16[16,1280]{1,0:T(8,128)(2,1)S(1)}, bf16[16,1280]{1,0:T(8,128)(2,1)S(1)}, u32[]{:S(2)}, u32[]{:S(2)}) collective-permute-start(bf16[16,1280]{1,0:T(8,128)(2,1)S(1)} %get-tuple-element.63), channel_id=1, source_target_pairs={{0,32},{32,64},{64,96},{96,128},{128,160},{160,192},{192,224},{224... | collective-permute-start | bytes 122888 | tf_op jit(solution)/shard_map/ppermute | solution.py:28
  91.7 0.1 convert_element_type.61
  91.8 0.1 fusion
  91.9 1.6 %collective-permute-start.23 = (bf16[160,1280]{1,0:T(8,128)(2,1)S(1)}, bf16[160,1280]{1,0:T(8,128)(2,1)S(1)}, u32[]{:S(2)}, u32[]{:S(2)}) collective-permute-start(bf16[160,1280]{1,0:T(8,128)(2,1)S(1)} %fusion), channel_id=1, source_target_pairs={{0,8},{8,0},{16,24},{24,16},{1,9},{9,1},{17,25},{25,17},{2,10},{10... | collective-permute-start | bytes 1228808 | tf_op jit(solution)/shard_map/ppermute | solution.py:32
  93.5 0.2 collective-permute-done.27
  93.7 1.3 %collective-permute-done.26 = bf16[16,1280]{1,0:T(8,128)(2,1)S(1)} collective-permute-done((bf16[16,1280]{1,0:T(8,128)(2,1)S(1)}, bf16[16,1280]{1,0:T(8,128)(2,1)S(1)}, u32[]{:S(2)}, u32[]{:S(2)}) %collective-permute-start.26) | collective-permute-done | bytes 40992 | tf_op jit(solution)/shard_map/ppermute | solution.py:28
  95.0 1.1 collective-permute-done.28.other
  96.2 3.2 %collective-permute-start.30 = (bf16[32,1280]{1,0:T(8,128)(2,1)S(1)}, bf16[32,1280]{1,0:T(8,128)(2,1)S(1)}, u32[]{:S(2)}, u32[]{:S(2)}) collective-permute-start(bf16[32,1280]{1,0:T(8,128)(2,1)S(1)} %get-tuple-element.48), channel_id=1, source_target_pairs={{0,224},{32,0},{64,32},{96,64},{128,96},{160,128},{192,160},{224,1... | collective-permute-start | bytes 245768 | tf_op jit(solution)/shard_map/ppermute | solution.py:28
  99.4 2.7 %collective-permute-done.23 = bf16[160,1280]{1,0:T(8,128)(2,1)S(1)} collective-permute-done((bf16[160,1280]{1,0:T(8,128)(2,1)S(1)}, bf16[160,1280]{1,0:T(8,128)(2,1)S(1)}, u32[]{:S(2)}, u32[]{:S(2)}) %collective-permute-start.23) | collective-permute-done | bytes 409632 | tf_op jit(solution)/shard_map/ppermute | solution.py:32
  102.1 0.1 fusion.1
  102.3 2.5 %collective-permute-done.31.other = bf16[160,1280]{1,0:T(8,128)(2,1)S(1)} collective-permute-done((bf16[160,1280]{1,0:T(8,128)(2,1)S(1)}, bf16[160,1280]{1,0:T(8,128)(2,1)S(1)}, u32[]{:S(2)}, u32[]{:S(2)}) %collective-permute-start.31) | collective-permute-done | bytes 409632 | tf_op jit(solution)/shard_map/ppermute | solution.py:36
  104.8 3.2 %collective-permute-start.34 = (bf16[32,1280]{1,0:T(8,128)(2,1)S(1)}, bf16[32,1280]{1,0:T(8,128)(2,1)S(1)}, u32[]{:S(2)}, u32[]{:S(2)}) collective-permute-start(bf16[32,1280]{1,0:T(8,128)(2,1)S(1)} %get-tuple-element.51), channel_id=1, source_target_pairs={{0,224},{32,0},{64,32},{96,64},{128,96},{160,128},{192,160},{224,1... | collective-permute-start | bytes 245768 | tf_op jit(solution)/shard_map/ppermute | solution.py:28
  108.0 2.4 %collective-permute-done.32 = bf16[32,1280]{1,0:T(8,128)(2,1)S(1)} collective-permute-done((bf16[32,1280]{1,0:T(8,128)(2,1)S(1)}, bf16[32,1280]{1,0:T(8,128)(2,1)S(1)}, u32[]{:S(2)}, u32[]{:S(2)}) %collective-permute-start.32) | collective-permute-done | bytes 81952 | tf_op jit(solution)/shard_map/ppermute | solution.py:28
  110.4 0.1 collective-permute-start.33
  110.5 3.3 %collective-permute-start.35 = (bf16[32,1280]{1,0:T(8,128)(2,1)S(1)}, bf16[32,1280]{1,0:T(8,128)(2,1)S(1)}, u32[]{:S(2)}, u32[]{:S(2)}) collective-permute-start(bf16[32,1280]{1,0:T(8,128)(2,1)S(1)} %get-tuple-element.55), channel_id=1, source_target_pairs={{0,224},{32,0},{64,32},{96,64},{128,96},{160,128},{192,160},{224,1... | collective-permute-start | bytes 245768 | tf_op jit(solution)/shard_map/ppermute | solution.py:28
  113.8 1.3 %shard_map.80 = f32[160,1280]{1,0:T(8,128)} custom-call(s32[1]{0:T(128)} %bitcast.me, bf16[2,320,512]{2,1,0:T(8,128)(2,1)S(1)} %get-tuple-element.43.full, bf16[512,1280]{1,0:T(8,128)(2,1)S(1)} %get-tuple-element.45.cot.value, bf16[160,1280]{1,0:T(8,128)(2,1)S(1)} %collective-permute-done.28.other), custom_call_target="tpu_custom_call" | custom-call | flops 419430400 | bytes 1048576 | tf_op jit(solution)/shard_map/pallas_call | solution.py:57
  115.1 1.3 %shard_map.79 = f32[160,1280]{1,0:T(8,128)} custom-call(s32[1]{0:T(128)} %bitcast.me, bf16[2,320,512]{2,1,0:T(8,128)(2,1)S(1)} %get-tuple-element.43.full, bf16[512,1280]{1,0:T(8,128)(2,1)S(1)} %get-tuple-element.44.tok.value, bf16[160,1280]{1,0:T(8,128)(2,1)S(1)} %collective-permute-done.31.other), custom_call_target="tpu_custom_call" | custom-call | flops 419430400 | bytes 1048576 | tf_op jit(solution)/shard_map/pallas_call | solution.py:57
  116.4 0.6 fusion.15
  (43 shorter events, 0.3 us)
Async XLA Ops:
  0.6 42.9 %copy-start = (bf16[1280,160]{0,1:T(8,128)(2,1)S(1)}, bf16[1280,160]{0,1:T(8,128)(2,1)}, u32[]{:S(2)}) copy-start(bf16[1280,160]{0,1:T(8,128)(2,1)} %param.5) | copy-start | bytes 1228804
  0.6 42.9 %copy-start.1 = (bf16[160,1280]{1,0:T(8,128)(2,1)S(1)}, bf16[160,1280]{1,0:T(8,128)(2,1)}, u32[]{:S(2)}) copy-start(bf16[160,1280]{1,0:T(8,128)(2,1)} %wo.1) | copy-start | bytes 1228804
  2.3 8.3 %collective-permute-start.1 = (bf16[32,1280]{1,0:T(8,128)(2,1)S(1)}, bf16[32,1280]{1,0:T(8,128)(2,1)S(1)}, u32[]{:S(2)}, u32[]{:S(2)}) collective-permute-start(bf16[32,1280]{1,0:T(8,128)(2,1)S(1)} %get-tuple-element.66), channel_id=1, source_target_pairs={{0,32},{32,64},{64,96},{96,128},{128,160},{160,192},{192,224},{224... | collective-permute-start | bytes 245768 | tf_op jit(solution)/shard_map/ppermute | solution.py:28
  4.2 6.4 %collective-permute-start = (bf16[32,1280]{1,0:T(8,128)(2,1)S(1)}, bf16[32,1280]{1,0:T(8,128)(2,1)S(1)}, u32[]{:S(2)}, u32[]{:S(2)}) collective-permute-start(bf16[32,1280]{1,0:T(8,128)(2,1)S(1)} %get-tuple-element.66), channel_id=1, source_target_pairs={{0,224},{32,0},{64,32},{96,64},{128,96},{160,128},{192,160},{224,1... | collective-permute-start | bytes 245768 | tf_op jit(solution)/shard_map/ppermute | solution.py:28
  8.2 12.6 %collective-permute-start.4 = (bf16[160,1280]{1,0:T(8,128)(2,1)}, bf16[160,1280]{1,0:T(8,128)(2,1)S(1)}, u32[]{:S(2)}, u32[]{:S(2)}) collective-permute-start(bf16[160,1280]{1,0:T(8,128)(2,1)} %bitcast.3), channel_id=1, source_target_pairs={{0,24},{24,0},{8,16},{16,8},{1,25},{25,1},{9,17},{17,9},{2,26},{26... | collective-permute-start | bytes 1228808 | tf_op jit(solution)/shard_map/ppermute | solution.py:36
  10.6 6.9 %collective-permute-start.3 = (bf16[32,1280]{1,0:T(8,128)(2,1)S(1)}, bf16[32,1280]{1,0:T(8,128)(2,1)S(1)}, u32[]{:S(2)}, u32[]{:S(2)}) collective-permute-start(bf16[32,1280]{1,0:T(8,128)(2,1)S(1)} %collective-permute-done.1), channel_id=1, source_target_pairs={{0,32},{32,64},{64,96},{96,128},{128,160},{160,192},{192,224},{224... | collective-permute-start | bytes 245768 | tf_op jit(solution)/shard_map/ppermute | solution.py:28
  10.6 5.3 %collective-permute-start.2 = (bf16[32,1280]{1,0:T(8,128)(2,1)S(1)}, bf16[32,1280]{1,0:T(8,128)(2,1)S(1)}, u32[]{:S(2)}, u32[]{:S(2)}) collective-permute-start(bf16[32,1280]{1,0:T(8,128)(2,1)S(1)} %collective-permute-done), channel_id=1, source_target_pairs={{0,224},{32,0},{64,32},{96,64},{128,96},{160,128},{192,160},{224,1... | collective-permute-start | bytes 245768 | tf_op jit(solution)/shard_map/ppermute | solution.py:28
  15.9 12.6 %collective-permute-start.7 = (bf16[160,1280]{1,0:T(8,128)(2,1)}, bf16[160,1280]{1,0:T(8,128)(2,1)S(1)}, u32[]{:S(2)}, u32[]{:S(2)}) collective-permute-start(bf16[160,1280]{1,0:T(8,128)(2,1)} %wo.1), channel_id=1, source_target_pairs={{0,24},{24,0},{8,16},{16,8},{1,25},{25,1},{9,17},{17,9},{2,26},{26... | collective-permute-start | bytes 1228808 | tf_op jit(solution)/shard_map/ppermute | solution.py:36
  20.8 4.4 %collective-permute-start.5 = (bf16[32,1280]{1,0:T(8,128)(2,1)S(1)}, bf16[32,1280]{1,0:T(8,128)(2,1)S(1)}, u32[]{:S(2)}, u32[]{:S(2)}) collective-permute-start(bf16[32,1280]{1,0:T(8,128)(2,1)S(1)} %collective-permute-done.2), channel_id=1, source_target_pairs={{0,224},{32,0},{64,32},{96,64},{128,96},{160,128},{192,160},{224,1... | collective-permute-start | bytes 245768 | tf_op jit(solution)/shard_map/ppermute | solution.py:28
  21.9 15.0 %collective-permute-start.10 = (bf16[160,1280]{1,0:T(8,128)(2,1)S(1)}, bf16[160,1280]{1,0:T(8,128)(2,1)S(1)}, u32[]{:S(2)}, u32[]{:S(2)}) collective-permute-start(bf16[160,1280]{1,0:T(8,128)(2,1)S(1)} %constant_dynamic-update-slice_fusion.2.refs_0_), channel_id=1, source_target_pairs={{0,8},{8,0},{16,24},{24,16},{1,9},{9,1},{17,25},{25,17},{2,10},{10... | collective-permute-start | bytes 1228808 | tf_op jit(solution)/shard_map/ppermute | solution.py:32
  22.9 5.7 %collective-permute-start.6 = (bf16[32,1280]{1,0:T(8,128)(2,1)S(1)}, bf16[32,1280]{1,0:T(8,128)(2,1)S(1)}, u32[]{:S(2)}, u32[]{:S(2)}) collective-permute-start(bf16[32,1280]{1,0:T(8,128)(2,1)S(1)} %collective-permute-done.3), channel_id=1, source_target_pairs={{0,32},{32,64},{64,96},{96,128},{128,160},{160,192},{192,224},{224... | collective-permute-start | bytes 245768 | tf_op jit(solution)/shard_map/ppermute | solution.py:28
  28.6 4.1 %collective-permute-start.8 = (bf16[16,1280]{1,0:T(8,128)(2,1)S(1)}, bf16[16,1280]{1,0:T(8,128)(2,1)S(1)}, u32[]{:S(2)}, u32[]{:S(2)}) collective-permute-start(bf16[16,1280]{1,0:T(8,128)(2,1)S(1)} %slice.82), channel_id=1, source_target_pairs={{0,224},{32,0},{64,32},{96,64},{128,96},{160,128},{192,160},{224,1... | collective-permute-start | bytes 122888 | tf_op jit(solution)/shard_map/ppermute | solution.py:28
  30.1 5.3 %collective-permute-start.9 = (bf16[16,1280]{1,0:T(8,128)(2,1)S(1)}, bf16[16,1280]{1,0:T(8,128)(2,1)S(1)}, u32[]{:S(2)}, u32[]{:S(2)}) collective-permute-start(bf16[16,1280]{1,0:T(8,128)(2,1)S(1)} %slice.83), channel_id=1, source_target_pairs={{0,32},{32,64},{64,96},{96,128},{128,160},{160,192},{192,224},{224... | collective-permute-start | bytes 122888 | tf_op jit(solution)/shard_map/ppermute | solution.py:28
  35.4 6.3 %collective-permute-start.11 = (bf16[96,1280]{1,0:T(8,128)(2,1)S(1)}, bf16[96,1280]{1,0:T(8,128)(2,1)}, u32[]{:S(2)}, u32[]{:S(2)}) collective-permute-start(bf16[96,1280]{1,0:T(8,128)(2,1)S(1)} %constant_dynamic-update-slice_fusion.8.refs_1_), channel_id=1, source_target_pairs={{0,8},{8,0},{16,24},{24,16},{1,9},{9,1},{17,25},{25,17},{2,10},{10... | collective-permute-start | bytes 737288 | tf_op jit(solution)/shard_map/ppermute | solution.py:32
  36.9 4.8 %collective-permute-start.12 = (bf16[160,1280]{1,0:T(8,128)(2,1)S(1)}, bf16[160,1280]{1,0:T(8,128)(2,1)S(1)}, u32[]{:S(2)}, u32[]{:S(2)}) collective-permute-start(bf16[160,1280]{1,0:T(8,128)(2,1)S(1)} %constant_dynamic-update-slice_fusion.2.refs_0_), channel_id=1, source_target_pairs={{0,1},{1,0},{2,3},{3,2},{4,5},{5,4},{6,7},{7,6},{8,9},{9,8},{10,11... | collective-permute-start | bytes 1228808 | tf_op jit(solution)/shard_map/ppermute | solution.py:28
  36.9 4.8 %collective-permute-start.14 = (bf16[160,1280]{1,0:T(8,128)(2,1)S(1)}, bf16[160,1280]{1,0:T(8,128)(2,1)S(1)}, u32[]{:S(2)}, u32[]{:S(2)}) collective-permute-start(bf16[160,1280]{1,0:T(8,128)(2,1)S(1)} %collective-permute-done.10.refs_2_), channel_id=1, source_target_pairs={{0,1},{1,0},{2,3},{3,2},{4,5},{5,4},{6,7},{7,6},{8,9},{9,8},{10,11... | collective-permute-start | bytes 1228808 | tf_op jit(solution)/shard_map/ppermute | solution.py:28
  37.4 4.3 %collective-permute-start.13 = (bf16[96,1280]{1,0:T(8,128)(2,1)S(1)}, bf16[96,1280]{1,0:T(8,128)(2,1)}, u32[]{:S(2)}, u32[]{:S(2)}) collective-permute-start(bf16[96,1280]{1,0:T(8,128)(2,1)S(1)} %constant_dynamic-update-slice_fusion.8.refs_1_), channel_id=1, source_target_pairs={{0,1},{1,0},{2,3},{3,2},{4,5},{5,4},{6,7},{7,6},{8,9},{9,8},{10,11... | collective-permute-start | bytes 737288 | tf_op jit(solution)/shard_map/ppermute | solution.py:28
  41.7 1.9 %collective-permute-start.15 = (bf16[96,1280]{1,0:T(8,128)(2,1)}, bf16[96,1280]{1,0:T(8,128)(2,1)}, u32[]{:S(2)}, u32[]{:S(2)}) collective-permute-start(bf16[96,1280]{1,0:T(8,128)(2,1)} %collective-permute-done.11.refs_3_), channel_id=1, source_target_pairs={{0,1},{1,0},{2,3},{3,2},{4,5},{5,4},{6,7},{7,6},{8,9},{9,8},{10,11... | collective-permute-start | bytes 737288 | tf_op jit(solution)/shard_map/ppermute | solution.py:28
  46.7 11.3 %collective-permute-start.16 = (f32[2,320,128]{2,1,0:T(8,128)S(1)}, f32[2,320,128]{2,1,0:T(8,128)S(1)}, u32[]{:S(2)}, u32[]{:S(2)}) collective-permute-start(f32[2,320,128]{2,1,0:T(8,128)S(1)} %get-tuple-element.35), channel_id=1, source_target_pairs={{0,2},{2,4},{4,6},{6,0},{1,3},{3,5},{5,7},{7,1},{8,10},{10,12},{12... | collective-permute-start | bytes 983048 | tf_op jit(solution)/shard_map/ppermute | solution.py:28
  48.5 17.6 %collective-permute-start.17 = (f32[2,320,128]{2,1,0:T(8,128)S(1)}, f32[2,320,128]{2,1,0:T(8,128)S(1)}, u32[]{:S(2)}, u32[]{:S(2)}) collective-permute-start(f32[2,320,128]{2,1,0:T(8,128)S(1)} %get-tuple-element.36), channel_id=1, source_target_pairs={{0,4},{2,6},{4,0},{6,2},{1,5},{3,7},{5,1},{7,3},{8,12},{10,14},{12... | collective-permute-start | bytes 983048 | tf_op jit(solution)/shard_map/ppermute | solution.py:28
  51.4 14.7 %collective-permute-start.18 = (f32[2,320,128]{2,1,0:T(8,128)S(1)}, f32[2,320,128]{2,1,0:T(8,128)S(1)}, u32[]{:S(2)}, u32[]{:S(2)}) collective-permute-start(f32[2,320,128]{2,1,0:T(8,128)S(1)} %get-tuple-element.37), channel_id=1, source_target_pairs={{0,6},{2,0},{4,2},{6,4},{1,7},{3,1},{5,3},{7,5},{8,14},{10,8},{12,... | collective-permute-start | bytes 983048 | tf_op jit(solution)/shard_map/ppermute | solution.py:28
  66.3 6.7 %collective-permute-start.21 = (bf16[2,320,128]{2,1,0:T(8,128)(2,1)S(1)}, bf16[2,320,128]{2,1,0:T(8,128)(2,1)S(1)}, u32[]{:S(2)}, u32[]{:S(2)}) collective-permute-start(bf16[2,320,128]{2,1,0:T(8,128)(2,1)S(1)} %shard_map.76.b0), channel_id=1, source_target_pairs={{0,2},{2,4},{4,6},{6,0},{1,3},{3,5},{5,7},{7,1},{8,10},{10,12},{12... | collective-permute-start | bytes 491528 | tf_op jit(solution)/shard_map/ppermute | solution.py:28
  67.6 10.0 %collective-permute-start.20 = (bf16[2,320,128]{2,1,0:T(8,128)(2,1)S(1)}, bf16[2,320,128]{2,1,0:T(8,128)(2,1)S(1)}, u32[]{:S(2)}, u32[]{:S(2)}) collective-permute-start(bf16[2,320,128]{2,1,0:T(8,128)(2,1)S(1)} %shard_map.76.b0), channel_id=1, source_target_pairs={{0,4},{2,6},{4,0},{6,2},{1,5},{3,7},{5,1},{7,3},{8,12},{10,14},{12... | collective-permute-start | bytes 491528 | tf_op jit(solution)/shard_map/ppermute | solution.py:28
  70.0 7.6 %collective-permute-start.19 = (bf16[2,320,128]{2,1,0:T(8,128)(2,1)S(1)}, bf16[2,320,128]{2,1,0:T(8,128)(2,1)S(1)}, u32[]{:S(2)}, u32[]{:S(2)}) collective-permute-start(bf16[2,320,128]{2,1,0:T(8,128)(2,1)S(1)} %shard_map.76.b0), channel_id=1, source_target_pairs={{0,6},{2,0},{4,2},{6,4},{1,7},{3,1},{5,3},{7,5},{8,14},{10,8},{12,... | collective-permute-start | bytes 491528 | tf_op jit(solution)/shard_map/ppermute | solution.py:28
  79.3 2.0 %collective-permute-start.24 = (bf16[192,1280]{1,0:T(8,128)(2,1)S(1)}, bf16[192,1280]{1,0:T(8,128)(2,1)S(1)}, u32[]{:S(2)}, u32[]{:S(2)}) collective-permute-start(bf16[192,1280]{1,0:T(8,128)(2,1)S(1)} %get-tuple-element.41), channel_id=1, source_target_pairs={{0,1},{1,0},{2,3},{3,2},{4,5},{5,4},{6,7},{7,6},{8,9},{9,8},{10,11... | collective-permute-start | bytes 1474568 | tf_op jit(solution)/shard_map/ppermute | solution.py:28
  81.4 8.1 %collective-permute-start.25 = (bf16[96,1280]{1,0:T(8,128)(2,1)S(1)}, bf16[96,1280]{1,0:T(8,128)(2,1)S(1)}, u32[]{:S(2)}, u32[]{:S(2)}) collective-permute-start(bf16[96,1280]{1,0:T(8,128)(2,1)S(1)} %fusion.2), channel_id=1, source_target_pairs={{0,8},{8,0},{16,24},{24,16},{1,9},{9,1},{17,25},{25,17},{2,10},{10... | collective-permute-start | bytes 737288 | tf_op jit(solution)/shard_map/ppermute | solution.py:32
  83.0 8.7 %collective-permute-start.22 = (bf16[320,1280]{1,0:T(8,128)(2,1)S(1)}, bf16[320,1280]{1,0:T(8,128)(2,1)S(1)}, u32[]{:S(2)}, u32[]{:S(2)}) collective-permute-start(bf16[320,1280]{1,0:T(8,128)(2,1)S(1)} %get-tuple-element.39), channel_id=1, source_target_pairs={{0,1},{1,0},{2,3},{3,2},{4,5},{5,4},{6,7},{7,6},{8,9},{9,8},{10,11... | collective-permute-start | bytes 2457608 | tf_op jit(solution)/shard_map/ppermute | solution.py:28
  83.6 12.6 %collective-permute-start.28 = (bf16[160,1280]{1,0:T(8,128)(2,1)S(1)}, bf16[160,1280]{1,0:T(8,128)(2,1)S(1)}, u32[]{:S(2)}, u32[]{:S(2)}) collective-permute-start(bf16[160,1280]{1,0:T(8,128)(2,1)S(1)} %get-tuple-element.46), channel_id=1, source_target_pairs={{0,24},{24,0},{8,16},{16,8},{1,25},{25,1},{9,17},{17,9},{2,26},{26... | collective-permute-start | bytes 1228808 | tf_op jit(solution)/shard_map/ppermute | solution.py:36
  85.8 18.9 %collective-permute-start.31 = (bf16[160,1280]{1,0:T(8,128)(2,1)S(1)}, bf16[160,1280]{1,0:T(8,128)(2,1)S(1)}, u32[]{:S(2)}, u32[]{:S(2)}) collective-permute-start(bf16[160,1280]{1,0:T(8,128)(2,1)S(1)} %get-tuple-element.49), channel_id=1, source_target_pairs={{0,24},{24,0},{8,16},{16,8},{1,25},{25,1},{9,17},{17,9},{2,26},{26... | collective-permute-start | bytes 1228808 | tf_op jit(solution)/shard_map/ppermute | solution.py:36
  89.6 4.1 %collective-permute-start.27 = (bf16[16,1280]{1,0:T(8,128)(2,1)S(1)}, bf16[16,1280]{1,0:T(8,128)(2,1)S(1)}, u32[]{:S(2)}, u32[]{:S(2)}) collective-permute-start(bf16[16,1280]{1,0:T(8,128)(2,1)S(1)} %get-tuple-element.61), channel_id=1, source_target_pairs={{0,224},{32,0},{64,32},{96,64},{128,96},{160,128},{192,160},{224,1... | collective-permute-start | bytes 122888 | tf_op jit(solution)/shard_map/ppermute | solution.py:28
  89.7 5.3 %collective-permute-start.26 = (bf16[16,1280]{1,0:T(8,128)(2,1)S(1)}, bf16[16,1280]{1,0:T(8,128)(2,1)S(1)}, u32[]{:S(2)}, u32[]{:S(2)}) collective-permute-start(bf16[16,1280]{1,0:T(8,128)(2,1)S(1)} %get-tuple-element.63), channel_id=1, source_target_pairs={{0,32},{32,64},{64,96},{96,128},{128,160},{160,192},{192,224},{224... | collective-permute-start | bytes 122888 | tf_op jit(solution)/shard_map/ppermute | solution.py:28
  91.9 10.2 %collective-permute-start.23 = (bf16[160,1280]{1,0:T(8,128)(2,1)S(1)}, bf16[160,1280]{1,0:T(8,128)(2,1)S(1)}, u32[]{:S(2)}, u32[]{:S(2)}) collective-permute-start(bf16[160,1280]{1,0:T(8,128)(2,1)S(1)} %fusion), channel_id=1, source_target_pairs={{0,8},{8,0},{16,24},{24,16},{1,9},{9,1},{17,25},{25,17},{2,10},{10... | collective-permute-start | bytes 1228808 | tf_op jit(solution)/shard_map/ppermute | solution.py:32
  96.2 6.1 %collective-permute-start.29 = (bf16[32,1280]{1,0:T(8,128)(2,1)S(1)}, bf16[32,1280]{1,0:T(8,128)(2,1)S(1)}, u32[]{:S(2)}, u32[]{:S(2)}) collective-permute-start(bf16[32,1280]{1,0:T(8,128)(2,1)S(1)} %get-tuple-element.47), channel_id=1, source_target_pairs={{0,32},{32,64},{64,96},{96,128},{128,160},{160,192},{192,224},{224... | collective-permute-start | bytes 245768 | tf_op jit(solution)/shard_map/ppermute | solution.py:28
  96.2 6.1 %collective-permute-start.30 = (bf16[32,1280]{1,0:T(8,128)(2,1)S(1)}, bf16[32,1280]{1,0:T(8,128)(2,1)S(1)}, u32[]{:S(2)}, u32[]{:S(2)}) collective-permute-start(bf16[32,1280]{1,0:T(8,128)(2,1)S(1)} %get-tuple-element.48), channel_id=1, source_target_pairs={{0,224},{32,0},{64,32},{96,64},{128,96},{160,128},{192,160},{224,1... | collective-permute-start | bytes 245768 | tf_op jit(solution)/shard_map/ppermute | solution.py:28
  104.8 5.7 %collective-permute-start.32 = (bf16[32,1280]{1,0:T(8,128)(2,1)S(1)}, bf16[32,1280]{1,0:T(8,128)(2,1)S(1)}, u32[]{:S(2)}, u32[]{:S(2)}) collective-permute-start(bf16[32,1280]{1,0:T(8,128)(2,1)S(1)} %get-tuple-element.50), channel_id=1, source_target_pairs={{0,32},{32,64},{64,96},{96,128},{128,160},{160,192},{192,224},{224... | collective-permute-start | bytes 245768 | tf_op jit(solution)/shard_map/ppermute | solution.py:28
  104.8 5.7 %collective-permute-start.34 = (bf16[32,1280]{1,0:T(8,128)(2,1)S(1)}, bf16[32,1280]{1,0:T(8,128)(2,1)S(1)}, u32[]{:S(2)}, u32[]{:S(2)}) collective-permute-start(bf16[32,1280]{1,0:T(8,128)(2,1)S(1)} %get-tuple-element.51), channel_id=1, source_target_pairs={{0,224},{32,0},{64,32},{96,64},{128,96},{160,128},{192,160},{224,1... | collective-permute-start | bytes 245768 | tf_op jit(solution)/shard_map/ppermute | solution.py:28
  110.4 6.0 %collective-permute-start.33 = (bf16[32,1280]{1,0:T(8,128)(2,1)S(1)}, bf16[32,1280]{1,0:T(8,128)(2,1)S(1)}, u32[]{:S(2)}, u32[]{:S(2)}) collective-permute-start(bf16[32,1280]{1,0:T(8,128)(2,1)S(1)} %get-tuple-element.54), channel_id=1, source_target_pairs={{0,32},{32,64},{64,96},{96,128},{128,160},{160,192},{192,224},{224... | collective-permute-start | bytes 245768 | tf_op jit(solution)/shard_map/ppermute | solution.py:28
  110.5 5.9 %collective-permute-start.35 = (bf16[32,1280]{1,0:T(8,128)(2,1)S(1)}, bf16[32,1280]{1,0:T(8,128)(2,1)S(1)}, u32[]{:S(2)}, u32[]{:S(2)}) collective-permute-start(bf16[32,1280]{1,0:T(8,128)(2,1)S(1)} %get-tuple-element.55), channel_id=1, source_target_pairs={{0,224},{32,0},{64,32},{96,64},{128,96},{160,128},{192,160},{224,1... | collective-permute-start | bytes 245768 | tf_op jit(solution)/shard_map/ppermute | solution.py:28

commit v3 on v2

--- a/solution.py
+++ b/solution.py
@@ -83,13 +83,15 @@
             for q in range(4):
                 whole[q, s, i * h : i * h + h] = total[:, q * 128 : q * 128 + 128]
     for k, part in enumerate(parts):
-        part[...] = whole[(me[0] + k) % 4]
+        part[...] = whole[(me[0] + k) % 4].astype(part.dtype)
 
 
 def act_kernel(me, p0, p1, p2, p3, out):
     del me
-    pre = p0[0] + p1[0] + p2[0] + p3[0]
-    grad_act = p0[1] + p1[1] + p2[1] + p3[1]
+    pre, grad_act = p0[0], p0[1]
+    for part in (p1, p2, p3):
+        pre += part[0].astype(F32)
+        grad_act += part[1].astype(F32)
     out[0] = smooth_gate(pre).astype(BF)
     out[1] = (grad_act * smooth_slope(pre)).astype(BF)
 
@@ -151,16 +153,16 @@
     quarters = [near_h, near_t, far_h, far_t]
     quarters += [send(value, "col", 1) for value in quarters]
 
-    part = shape((2, 2 * h, 128), F32)
+    part, rounded = shape((2, 2 * h, 128), F32), shape((2, 2 * h, 128), BF)
     tok, cot, *parts = call(
         up_kernel,
-        [shape((512, d), BF)] * 2 + [part] * 4,
+        [shape((512, d), BF)] * 2 + [part] + [rounded] * 3,
         [me, *quarters, w_in_t, w_in_2, w_out, w_out_2],
         2 * flops,
         [pltpu.VMEM((4, 2, 2 * h, 128), F32)],
     )
     parts[1:] = [send(parts[k], "row", k) for k in (1, 2, 3)]
-    (block,) = call(act_kernel, [shape((2, 2 * h, 128), BF)], [me, *parts])
+    (block,) = call(act_kernel, [rounded], [me, *parts])
     blocks = [block] + [send(block, "row", -k) for k in (1, 2, 3)]
 
     sums = shape((256, d), F32)
@@ -175,7 +177,9 @@
     far_t = token_pair((far[cut:] + tail[:rest]).astype(BF)).astype(F32)
     near_t = near[cut:] + tail[rest:] + far_t
     head = send(head, "col", 1).astype(F32)
-    far_h = token_pair((far[:cut] + head[:cut]).astype(BF)).astype(F32)
+    far_h = (far[:cut] + head[:cut]).astype(BF)
+    first = after(near_t[-32:], far_h)
+    far_h = token_pair(far_h).astype(F32)
     near_h = near[:cut] + head[cut:] + far_h
     piece = {}
     for i, k in enumerate(ORDER):
@@ -184,8 +188,8 @@
         pair_kernel, [shape((h, d), BF)] * 2, [me, after(full, tail), tok, cot], flops
     )
     pair_out, pair_in = weight_pair(pair_out), weight_pair(pair_in)
-    up = send(piece[4][:16].astype(BF), "z", 1).astype(F32)
-    down = send(piece[4][16:].astype(BF), "z", -1).astype(F32)
+    up = send(first[:16].astype(BF), "z", 1).astype(F32)
+    down = send(first[16:].astype(BF), "z", -1).astype(F32)
     up = cat([up + piece[3][:16], piece[3][16:]]).astype(BF)
     down = cat([piece[5][:16], down + piece[5][16:]]).astype(BF)
     up, down = after((up, down), pair_out)
@@ -196,8 +200,8 @@
     weight = [shape((h, d), F32)]
     (grad_out,) = call(functools.partial(own_kernel, 0), weight, [me, full, cot, pair_out], flops)
     (grad_in_t,) = call(functools.partial(own_kernel, 1), weight, [me, full, tok, pair_in], flops)
-    up, down = (up + piece[1]).astype(BF), (down + piece[7]).astype(BF)
-    up, down = send(up, "z", 1).astype(F32), send(down, "z", -1).astype(F32)
+    up, down = after((up + piece[1], down + piece[7]), grad_out)
+    up, down = send(up, "z", 1), send(down, "z", -1)
     total = (piece[0] + up + down).astype(BF)
     output, input_grad = total[:16], total[16:]
     return (output, input_grad, grad_in_t.T, grad_out)

time: 118 us -> 111 us (0.941)
  waiting for transfers between devices: 56.1 us -> 48.3 us
    ppermute x28, waiting for transfers between devices: 38.5 us -> 31.6 us  [send(): lax.ppermute(value, axis, [(i, (i + shift) % size) for i in range(size)])]
  transfers between devices with their start and end apart: 36 -> 36, of which waited for: 21 -> 22; matrix products, arithmetic and copies ran while one was open for 0% -> 1% of each run, Pallas kernels for 3% -> 3%
where the time goes in v3:
time: 111 us; the launch traced here: 110 us
  starting transfers between devices  49.6 us (45%)
  waiting for transfers between devices  48.3 us (44%)
  Pallas kernels  8.13 us (7%)
  local copies, waits for them, and re-layouts  2.37 us (2%)
    ppermute x28, starting transfers between devices, send(): lax.ppermute(value, axis, [(i, (i + shift) % size) for i in range(size)])  38.5 us
    ppermute x28, waiting for transfers between devices, send(): lax.ppermute(value, axis, [(i, (i + shift) % size) for i in range(size)])  31.6 us
    ppermute x4, waiting for transfers between devices, token_pair(): return lax.ppermute(value, 'x', [(0, 1), (1, 0), (2, 3), (3, 2)])  10.4 us
    pallas_call x6, Pallas kernels, call(): return list(kernel(*args))  8.13 us
    ppermute x4, waiting for transfers between devices, weight_pair(): return lax.ppermute(value, 'x', [(0, 3), (3, 0), (1, 2), (2, 1)])  6.27 us
    ppermute x4, starting transfers between devices, token_pair(): return lax.ppermute(value, 'x', [(0, 1), (1, 0), (2, 3), (3, 2)])  5.75 us
    ppermute x4, starting transfers between devices, weight_pair(): return lax.ppermute(value, 'x', [(0, 3), (3, 0), (1, 2), (2, 1)])  5.32 us
  transfers between devices with their start and end apart: 36, of which 22 were waited for; matrix products, arithmetic and copies ran while one was open for 1% of the time, Pallas kernels for 3%

profile of v3, /device:TPU:2, one launch (start us, length us, event | category | flops | bytes accessed | tf_op | source)
XLA Modules:
  0.0 109.8 jit_solution(8764780932275311722)
XLA Ops:
  0.7 0.9 constant_dynamic-update-slice_fusion.1
  1.5 0.8 constant_dynamic-update-slice_fusion
  2.3 1.9 %collective-permute-start.1 = (bf16[32,1280]{1,0:T(8,128)(2,1)S(1)}, bf16[32,1280]{1,0:T(8,128)(2,1)S(1)}, u32[]{:S(2)}, u32[]{:S(2)}) collective-permute-start(bf16[32,1280]{1,0:T(8,128)(2,1)S(1)} %get-tuple-element.72), channel_id=1, source_target_pairs={{0,32},{32,64},{64,96},{96,128},{128,160},{160,192},{192,224},{224... | collective-permute-start | bytes 245768 | tf_op jit(solution)/shard_map/ppermute | solution.py:28
  4.2 4.0 %collective-permute-start = (bf16[32,1280]{1,0:T(8,128)(2,1)S(1)}, bf16[32,1280]{1,0:T(8,128)(2,1)S(1)}, u32[]{:S(2)}, u32[]{:S(2)}) collective-permute-start(bf16[32,1280]{1,0:T(8,128)(2,1)S(1)} %get-tuple-element.72), channel_id=1, source_target_pairs={{0,224},{32,0},{64,32},{96,64},{128,96},{160,128},{192,160},{224,1... | collective-permute-start | bytes 245768 | tf_op jit(solution)/shard_map/ppermute | solution.py:28
  8.2 1.5 %collective-permute-start.4 = (bf16[160,1280]{1,0:T(8,128)(2,1)}, bf16[160,1280]{1,0:T(8,128)(2,1)S(1)}, u32[]{:S(2)}, u32[]{:S(2)}) collective-permute-start(bf16[160,1280]{1,0:T(8,128)(2,1)} %bitcast.3), channel_id=1, source_target_pairs={{0,24},{24,0},{8,16},{16,8},{1,25},{25,1},{9,17},{17,9},{2,26},{26... | collective-permute-start | bytes 1228808 | tf_op jit(solution)/shard_map/ppermute | solution.py:36
  9.7 0.9 collective-permute-done.1
  10.6 3.3 %collective-permute-start.2 = (bf16[32,1280]{1,0:T(8,128)(2,1)S(1)}, bf16[32,1280]{1,0:T(8,128)(2,1)S(1)}, u32[]{:S(2)}, u32[]{:S(2)}) collective-permute-start(bf16[32,1280]{1,0:T(8,128)(2,1)S(1)} %collective-permute-done), channel_id=1, source_target_pairs={{0,224},{32,0},{64,32},{96,64},{128,96},{160,128},{192,160},{224,1... | collective-permute-start | bytes 245768 | tf_op jit(solution)/shard_map/ppermute | solution.py:28
  13.9 2.0 %collective-permute-done.2 = bf16[32,1280]{1,0:T(8,128)(2,1)S(1)} collective-permute-done((bf16[32,1280]{1,0:T(8,128)(2,1)S(1)}, bf16[32,1280]{1,0:T(8,128)(2,1)S(1)}, u32[]{:S(2)}, u32[]{:S(2)}) %collective-permute-start.2) | collective-permute-done | bytes 81952 | tf_op jit(solution)/shard_map/ppermute | solution.py:28
  15.9 1.5 %collective-permute-start.7 = (bf16[160,1280]{1,0:T(8,128)(2,1)}, bf16[160,1280]{1,0:T(8,128)(2,1)S(1)}, u32[]{:S(2)}, u32[]{:S(2)}) collective-permute-start(bf16[160,1280]{1,0:T(8,128)(2,1)} %wo.1), channel_id=1, source_target_pairs={{0,24},{24,0},{8,16},{16,8},{1,25},{25,1},{9,17},{17,9},{2,26},{26... | collective-permute-start | bytes 1228808 | tf_op jit(solution)/shard_map/ppermute | solution.py:36
  17.5 3.4 %collective-permute-done.4.refs_9_.wi2 = bf16[160,1280]{1,0:T(8,128)(2,1)S(1)} collective-permute-done((bf16[160,1280]{1,0:T(8,128)(2,1)}, bf16[160,1280]{1,0:T(8,128)(2,1)S(1)}, u32[]{:S(2)}, u32[]{:S(2)}) %collective-permute-start.4) | collective-permute-done | bytes 409632 | tf_op jit(solution)/shard_map/ppermute | solution.py:36
  20.8 1.0 collective-permute-start.5
  21.9 1.1 collective-permute-start.10
  22.9 1.7 %collective-permute-start.6 = (bf16[32,1280]{1,0:T(8,128)(2,1)S(1)}, bf16[32,1280]{1,0:T(8,128)(2,1)S(1)}, u32[]{:S(2)}, u32[]{:S(2)}) collective-permute-start(bf16[32,1280]{1,0:T(8,128)(2,1)S(1)} %collective-permute-done.3), channel_id=1, source_target_pairs={{0,32},{32,64},{64,96},{96,128},{128,160},{160,192},{192,224},{224... | collective-permute-start | bytes 245768 | tf_op jit(solution)/shard_map/ppermute | solution.py:28
  24.6 0.7 collective-permute-done.5
  25.3 3.3 %collective-permute-done.6 = bf16[32,1280]{1,0:T(8,128)(2,1)S(1)} collective-permute-done((bf16[32,1280]{1,0:T(8,128)(2,1)S(1)}, bf16[32,1280]{1,0:T(8,128)(2,1)S(1)}, u32[]{:S(2)}, u32[]{:S(2)}) %collective-permute-start.6) | collective-permute-done | bytes 81952 | tf_op jit(solution)/shard_map/ppermute | solution.py:28
  28.6 1.5 %collective-permute-start.8 = (bf16[16,1280]{1,0:T(8,128)(2,1)S(1)}, bf16[16,1280]{1,0:T(8,128)(2,1)S(1)}, u32[]{:S(2)}, u32[]{:S(2)}) collective-permute-start(bf16[16,1280]{1,0:T(8,128)(2,1)S(1)} %slice.82), channel_id=1, source_target_pairs={{0,224},{32,0},{64,32},{96,64},{128,96},{160,128},{192,160},{224,1... | collective-permute-start | bytes 122888 | tf_op jit(solution)/shard_map/ppermute | solution.py:28
  30.1 0.7 collective-permute-start.9
  30.8 1.9 %collective-permute-done.8 = bf16[16,1280]{1,0:T(8,128)(2,1)S(1)} collective-permute-done((bf16[16,1280]{1,0:T(8,128)(2,1)S(1)}, bf16[16,1280]{1,0:T(8,128)(2,1)S(1)}, u32[]{:S(2)}, u32[]{:S(2)}) %collective-permute-start.8) | collective-permute-done | bytes 40992 | tf_op jit(solution)/shard_map/ppermute | solution.py:28
  32.7 2.7 %collective-permute-done.9 = bf16[16,1280]{1,0:T(8,128)(2,1)S(1)} collective-permute-done((bf16[16,1280]{1,0:T(8,128)(2,1)S(1)}, bf16[16,1280]{1,0:T(8,128)(2,1)S(1)}, u32[]{:S(2)}, u32[]{:S(2)}) %collective-permute-start.9) | collective-permute-done | bytes 40992 | tf_op jit(solution)/shard_map/ppermute | solution.py:28
  35.4 1.5 %collective-permute-start.11 = (bf16[96,1280]{1,0:T(8,128)(2,1)S(1)}, bf16[96,1280]{1,0:T(8,128)(2,1)}, u32[]{:S(2)}, u32[]{:S(2)}) collective-permute-start(bf16[96,1280]{1,0:T(8,128)(2,1)S(1)} %constant_dynamic-update-slice_fusion.8.refs_1_), channel_id=1, source_target_pairs={{0,8},{8,0},{16,24},{24,16},{1,9},{9,1},{17,25},{25,17},{2,10},{10... | collective-permute-start | bytes 737288 | tf_op jit(solution)/shard_map/ppermute | solution.py:32
  36.9 0.5 collective-permute-start.14
  37.4 4.3 %collective-permute-done.11.refs_3_ = bf16[96,1280]{1,0:T(8,128)(2,1)} collective-permute-done((bf16[96,1280]{1,0:T(8,128)(2,1)S(1)}, bf16[96,1280]{1,0:T(8,128)(2,1)}, u32[]{:S(2)}, u32[]{:S(2)}) %collective-permute-start.11) | collective-permute-done | bytes 245792 | tf_op jit(solution)/shard_map/ppermute | solution.py:32
  41.7 1.8 %collective-permute-done.15.refs_7_ = bf16[96,1280]{1,0:T(8,128)(2,1)} collective-permute-done((bf16[96,1280]{1,0:T(8,128)(2,1)}, bf16[96,1280]{1,0:T(8,128)(2,1)}, u32[]{:S(2)}, u32[]{:S(2)}) %collective-permute-start.15) | collective-permute-done | bytes 245792 | tf_op jit(solution)/shard_map/ppermute | solution.py:28
  43.5 3.1 %shard_map.75 = (bf16[512,1280]{1,0:T(8,128)(2,1)S(1)}, bf16[512,1280]{1,0:T(8,128)(2,1)S(1)}, f32[2,320,128]{2,1,0:T(8,128)S(1)}, bf16[2,320,128]{2,1,0:T(8,128...) custom-call(s32[1]{0:T(128)} %bitcast.me, ...), custom_call_target="tpu_custom_call" | custom-call | flops 838860800 | bytes 1048576 | tf_op jit(solution)/shard_map/pallas_call | solution.py:57
  46.7 1.8 %collective-permute-start.16 = (bf16[2,320,128]{2,1,0:T(8,128)(2,1)S(1)}, bf16[2,320,128]{2,1,0:T(8,128)(2,1)S(1)}, u32[]{:S(2)}, u32[]{:S(2)}) collective-permute-start(bf16[2,320,128]{2,1,0:T(8,128)(2,1)S(1)} %get-tuple-element.38), channel_id=1, source_target_pairs={{0,2},{2,4},{4,6},{6,0},{1,3},{3,5},{5,7},{7,1},{8,10},{10,12},{12... | collective-permute-start | bytes 491528 | tf_op jit(solution)/shard_map/ppermute | solution.py:28
  48.5 2.9 %collective-permute-start.17 = (bf16[2,320,128]{2,1,0:T(8,128)(2,1)S(1)}, bf16[2,320,128]{2,1,0:T(8,128)(2,1)S(1)}, u32[]{:S(2)}, u32[]{:S(2)}) collective-permute-start(bf16[2,320,128]{2,1,0:T(8,128)(2,1)S(1)} %get-tuple-element.39), channel_id=1, source_target_pairs={{0,4},{2,6},{4,0},{6,2},{1,5},{3,7},{5,1},{7,3},{8,12},{10,14},{12... | collective-permute-start | bytes 491528 | tf_op jit(solution)/shard_map/ppermute | solution.py:28
  51.4 1.3 %collective-permute-start.18 = (bf16[2,320,128]{2,1,0:T(8,128)(2,1)S(1)}, bf16[2,320,128]{2,1,0:T(8,128)(2,1)S(1)}, u32[]{:S(2)}, u32[]{:S(2)}) collective-permute-start(bf16[2,320,128]{2,1,0:T(8,128)(2,1)S(1)} %get-tuple-element.40), channel_id=1, source_target_pairs={{0,6},{2,0},{4,2},{6,4},{1,7},{3,1},{5,3},{7,5},{8,14},{10,8},{12,... | collective-permute-start | bytes 491528 | tf_op jit(solution)/shard_map/ppermute | solution.py:28
  52.8 1.7 %collective-permute-done.16.p1 = bf16[2,320,128]{2,1,0:T(8,128)(2,1)S(1)} collective-permute-done((bf16[2,320,128]{2,1,0:T(8,128)(2,1)S(1)}, bf16[2,320,128]{2,1,0:T(8,128)(2,1)S(1)}, u32[]{:S(2)}, u32[]{:S(2)}) %collective-permute-start.16) | collective-permute-done | bytes 163872 | tf_op jit(solution)/shard_map/ppermute | solution.py:28
  54.4 4.7 %collective-permute-done.17.p2 = bf16[2,320,128]{2,1,0:T(8,128)(2,1)S(1)} collective-permute-done((bf16[2,320,128]{2,1,0:T(8,128)(2,1)S(1)}, bf16[2,320,128]{2,1,0:T(8,128)(2,1)S(1)}, u32[]{:S(2)}, u32[]{:S(2)}) %collective-permute-start.17) | collective-permute-done | bytes 163872 | tf_op jit(solution)/shard_map/ppermute | solution.py:28
  59.1 0.2 shard_map.76.b0
  59.3 1.3 %collective-permute-start.21 = (bf16[2,320,128]{2,1,0:T(8,128)(2,1)S(1)}, bf16[2,320,128]{2,1,0:T(8,128)(2,1)S(1)}, u32[]{:S(2)}, u32[]{:S(2)}) collective-permute-start(bf16[2,320,128]{2,1,0:T(8,128)(2,1)S(1)} %shard_map.76.b0), channel_id=1, source_target_pairs={{0,2},{2,4},{4,6},{6,0},{1,3},{3,5},{5,7},{7,1},{8,10},{10,12},{12... | collective-permute-start | bytes 491528 | tf_op jit(solution)/shard_map/ppermute | solution.py:28
  60.6 2.4 %collective-permute-start.20 = (bf16[2,320,128]{2,1,0:T(8,128)(2,1)S(1)}, bf16[2,320,128]{2,1,0:T(8,128)(2,1)S(1)}, u32[]{:S(2)}, u32[]{:S(2)}) collective-permute-start(bf16[2,320,128]{2,1,0:T(8,128)(2,1)S(1)} %shard_map.76.b0), channel_id=1, source_target_pairs={{0,4},{2,6},{4,0},{6,2},{1,5},{3,7},{5,1},{7,3},{8,12},{10,14},{12... | collective-permute-start | bytes 491528 | tf_op jit(solution)/shard_map/ppermute | solution.py:28
  63.0 1.6 %collective-permute-start.19 = (bf16[2,320,128]{2,1,0:T(8,128)(2,1)S(1)}, bf16[2,320,128]{2,1,0:T(8,128)(2,1)S(1)}, u32[]{:S(2)}, u32[]{:S(2)}) collective-permute-start(bf16[2,320,128]{2,1,0:T(8,128)(2,1)S(1)} %shard_map.76.b0), channel_id=1, source_target_pairs={{0,6},{2,0},{4,2},{6,4},{1,7},{3,1},{5,3},{7,5},{8,14},{10,8},{12,... | collective-permute-start | bytes 491528 | tf_op jit(solution)/shard_map/ppermute | solution.py:28
  64.6 1.9 %collective-permute-done.21.b3 = bf16[2,320,128]{2,1,0:T(8,128)(2,1)S(1)} collective-permute-done((bf16[2,320,128]{2,1,0:T(8,128)(2,1)S(1)}, bf16[2,320,128]{2,1,0:T(8,128)(2,1)S(1)}, u32[]{:S(2)}, u32[]{:S(2)}) %collective-permute-start.21) | collective-permute-done | bytes 163872 | tf_op jit(solution)/shard_map/ppermute | solution.py:28
  66.5 3.8 %collective-permute-done.20.b2 = bf16[2,320,128]{2,1,0:T(8,128)(2,1)S(1)} collective-permute-done((bf16[2,320,128]{2,1,0:T(8,128)(2,1)S(1)}, bf16[2,320,128]{2,1,0:T(8,128)(2,1)S(1)}, u32[]{:S(2)}, u32[]{:S(2)}) %collective-permute-start.20) | collective-permute-done | bytes 163872 | tf_op jit(solution)/shard_map/ppermute | solution.py:28
  70.3 1.7 %shard_map.77 = (f32[256,1280]{1,0:T(8,128)S(1)}, f32[256,1280]{1,0:T(8,128)S(1)}, bf16[320,1280]{1,0:T(8,128)(2,1)S(1)}, bf16[192,1280]{1,0:T(8,128)(2,1)S(1)}, bf16[2,320,512]{2,1,0:T(8,128)(2,1)S(1)}) custom-call(s32[1]{0:T(128)} %bitcast.me, bf16[2,320,128]{2,1,0:T(8,128)(2,1)S(1)} %shard_map.76.b0, bf16[2,320,128]{2,1,0:T(8,128)(2,1)S(1)} %collective-permute-done.19.b1, ...), custom_call_target="tpu_custom_call" | custom-call | flops 838860800 | bytes 1048576 | tf_op jit(solution)/shard_map/pallas_call | solution.py:57
  72.0 0.1 collective-permute-start.24
  72.1 0.5 collective-permute-start.22
  72.6 1.4 %collective-permute-done.24 = bf16[192,1280]{1,0:T(8,128)(2,1)S(1)} collective-permute-done((bf16[192,1280]{1,0:T(8,128)(2,1)S(1)}, bf16[192,1280]{1,0:T(8,128)(2,1)S(1)}, u32[]{:S(2)}, u32[]{:S(2)}) %collective-permute-start.24) | collective-permute-done | bytes 491552 | tf_op jit(solution)/shard_map/ppermute | solution.py:28
  74.1 1.6 %collective-permute-start.25 = (bf16[96,1280]{1,0:T(8,128)(2,1)S(1)}, bf16[96,1280]{1,0:T(8,128)(2,1)S(1)}, u32[]{:S(2)}, u32[]{:S(2)}) collective-permute-start(bf16[96,1280]{1,0:T(8,128)(2,1)S(1)} %fusion.2), channel_id=1, source_target_pairs={{0,8},{8,0},{16,24},{24,16},{1,9},{9,1},{17,25},{25,17},{2,10},{10... | collective-permute-start | bytes 737288 | tf_op jit(solution)/shard_map/ppermute | solution.py:32
  75.7 0.6 shard_map.78
  76.3 2.2 %collective-permute-start.28 = (bf16[160,1280]{1,0:T(8,128)(2,1)S(1)}, bf16[160,1280]{1,0:T(8,128)(2,1)S(1)}, u32[]{:S(2)}, u32[]{:S(2)}) collective-permute-start(bf16[160,1280]{1,0:T(8,128)(2,1)S(1)} %get-tuple-element.50), channel_id=1, source_target_pairs={{0,24},{24,0},{8,16},{16,8},{1,25},{25,1},{9,17},{17,9},{2,26},{26... | collective-permute-start | bytes 1228808 | tf_op jit(solution)/shard_map/ppermute | solution.py:36
  78.6 0.1 collective-permute-start.31
  78.7 3.5 %collective-permute-done.25 = bf16[96,1280]{1,0:T(8,128)(2,1)S(1)} collective-permute-done((bf16[96,1280]{1,0:T(8,128)(2,1)S(1)}, bf16[96,1280]{1,0:T(8,128)(2,1)S(1)}, u32[]{:S(2)}, u32[]{:S(2)}) %collective-permute-start.25) | collective-permute-done | bytes 245792 | tf_op jit(solution)/shard_map/ppermute | solution.py:32
  82.3 0.1 convert_element_type.49
  82.4 0.1 fusion
  82.5 0.1 collective-permute-start.27
  82.6 2.0 %collective-permute-start.26 = (bf16[16,1280]{1,0:T(8,128)(2,1)S(1)}, bf16[16,1280]{1,0:T(8,128)(2,1)S(1)}, u32[]{:S(2)}, u32[]{:S(2)}) collective-permute-start(bf16[16,1280]{1,0:T(8,128)(2,1)S(1)} %get-tuple-element.71), channel_id=1, source_target_pairs={{0,32},{32,64},{64,96},{96,128},{128,160},{160,192},{192,224},{224... | collective-permute-start | bytes 122888 | tf_op jit(solution)/shard_map/ppermute | solution.py:28
  84.6 1.6 %collective-permute-start.23 = (bf16[160,1280]{1,0:T(8,128)(2,1)S(1)}, bf16[160,1280]{1,0:T(8,128)(2,1)S(1)}, u32[]{:S(2)}, u32[]{:S(2)}) collective-permute-start(bf16[160,1280]{1,0:T(8,128)(2,1)S(1)} %fusion), channel_id=1, source_target_pairs={{0,8},{8,0},{16,24},{24,16},{1,9},{9,1},{17,25},{25,17},{2,10},{10... | collective-permute-start | bytes 1228808 | tf_op jit(solution)/shard_map/ppermute | solution.py:32
  86.2 0.4 collective-permute-done.27
  86.6 1.3 %collective-permute-done.26 = bf16[16,1280]{1,0:T(8,128)(2,1)S(1)} collective-permute-done((bf16[16,1280]{1,0:T(8,128)(2,1)S(1)}, bf16[16,1280]{1,0:T(8,128)(2,1)S(1)}, u32[]{:S(2)}, u32[]{:S(2)}) %collective-permute-start.26) | collective-permute-done | bytes 40992 | tf_op jit(solution)/shard_map/ppermute | solution.py:28
  87.9 0.9 collective-permute-done.28.other
  88.9 3.2 %collective-permute-start.30 = (bf16[32,1280]{1,0:T(8,128)(2,1)S(1)}, bf16[32,1280]{1,0:T(8,128)(2,1)S(1)}, u32[]{:S(2)}, u32[]{:S(2)}) collective-permute-start(bf16[32,1280]{1,0:T(8,128)(2,1)S(1)} %get-tuple-element.52), channel_id=1, source_target_pairs={{0,224},{32,0},{64,32},{96,64},{128,96},{160,128},{192,160},{224,1... | collective-permute-start | bytes 245768 | tf_op jit(solution)/shard_map/ppermute | solution.py:28
  92.1 2.6 %collective-permute-done.23 = bf16[160,1280]{1,0:T(8,128)(2,1)S(1)} collective-permute-done((bf16[160,1280]{1,0:T(8,128)(2,1)S(1)}, bf16[160,1280]{1,0:T(8,128)(2,1)S(1)}, u32[]{:S(2)}, u32[]{:S(2)}) %collective-permute-start.23) | collective-permute-done | bytes 409632 | tf_op jit(solution)/shard_map/ppermute | solution.py:32
  94.7 0.1 fusion.1
  94.9 1.9 %collective-permute-done.31.other = bf16[160,1280]{1,0:T(8,128)(2,1)S(1)} collective-permute-done((bf16[160,1280]{1,0:T(8,128)(2,1)S(1)}, bf16[160,1280]{1,0:T(8,128)(2,1)S(1)}, u32[]{:S(2)}, u32[]{:S(2)}) %collective-permute-start.31) | collective-permute-done | bytes 409632 | tf_op jit(solution)/shard_map/ppermute | solution.py:36
  96.8 3.2 %collective-permute-start.33 = (bf16[32,1280]{1,0:T(8,128)(2,1)S(1)}, bf16[32,1280]{1,0:T(8,128)(2,1)S(1)}, u32[]{:S(2)}, u32[]{:S(2)}) collective-permute-start(bf16[32,1280]{1,0:T(8,128)(2,1)S(1)} %get-tuple-element.55), channel_id=1, source_target_pairs={{0,224},{32,0},{64,32},{96,64},{128,96},{160,128},{192,160},{224,1... | collective-permute-start | bytes 245768 | tf_op jit(solution)/shard_map/ppermute | solution.py:28
  100.1 1.3 %shard_map.79 = f32[160,1280]{1,0:T(8,128)} custom-call(s32[1]{0:T(128)} %bitcast.me, bf16[2,320,512]{2,1,0:T(8,128)(2,1)S(1)} %get-tuple-element.47.full, bf16[512,1280]{1,0:T(8,128)(2,1)S(1)} %get-tuple-element.49.cot.value, bf16[160,1280]{1,0:T(8,128)(2,1)S(1)} %collective-permute-done.28.other), custom_call_target="tpu_custom_call" | custom-call | flops 419430400 | bytes 1048576 | tf_op jit(solution)/shard_map/pallas_call | solution.py:57
  101.4 1.1 %collective-permute-done.32 = bf16[32,1280]{1,0:T(8,128)(2,1)S(1)} collective-permute-done((bf16[32,1280]{1,0:T(8,128)(2,1)S(1)}, bf16[32,1280]{1,0:T(8,128)(2,1)S(1)}, u32[]{:S(2)}, u32[]{:S(2)}) %collective-permute-start.32) | collective-permute-done | bytes 81952 | tf_op jit(solution)/shard_map/ppermute | solution.py:28
  102.5 0.2 collective-permute-start.34
  102.7 3.2 %collective-permute-start.35 = (f32[32,1280]{1,0:T(8,128)S(1)}, f32[32,1280]{1,0:T(8,128)S(1)}, u32[]{:S(2)}, u32[]{:S(2)}) collective-permute-start(f32[32,1280]{1,0:T(8,128)S(1)} %get-tuple-element.57), channel_id=1, source_target_pairs={{0,224},{32,0},{64,32},{96,64},{128,96},{160,128},{192,160},{224,1... | collective-permute-start | bytes 491528 | tf_op jit(solution)/shard_map/ppermute | solution.py:28
  105.9 1.3 %shard_map.80 = f32[160,1280]{1,0:T(8,128)} custom-call(s32[1]{0:T(128)} %bitcast.me, bf16[2,320,512]{2,1,0:T(8,128)(2,1)S(1)} %get-tuple-element.47.full, bf16[512,1280]{1,0:T(8,128)(2,1)S(1)} %get-tuple-element.48.tok.value, bf16[160,1280]{1,0:T(8,128)(2,1)S(1)} %collective-permute-done.31.other), custom_call_target="tpu_custom_call" | custom-call | flops 419430400 | bytes 1048576 | tf_op jit(solution)/shard_map/pallas_call | solution.py:57
  107.2 1.9 %collective-permute-done.34 = f32[32,1280]{1,0:T(8,128)S(1)} collective-permute-done((f32[32,1280]{1,0:T(8,128)S(1)}, f32[32,1280]{1,0:T(8,128)S(1)}, u32[]{:S(2)}, u32[]{:S(2)}) %collective-permute-start.34) | collective-permute-done | bytes 163872 | tf_op jit(solution)/shard_map/ppermute | solution.py:28
  109.2 0.6 fusion.13
  (45 shorter events, 0.4 us)
Async XLA Ops:
  0.6 42.9 %copy-start = (bf16[1280,160]{0,1:T(8,128)(2,1)S(1)}, bf16[1280,160]{0,1:T(8,128)(2,1)}, u32[]{:S(2)}) copy-start(bf16[1280,160]{0,1:T(8,128)(2,1)} %param.5) | copy-start | bytes 1228804
  0.6 42.9 %copy-start.1 = (bf16[160,1280]{1,0:T(8,128)(2,1)S(1)}, bf16[160,1280]{1,0:T(8,128)(2,1)}, u32[]{:S(2)}) copy-start(bf16[160,1280]{1,0:T(8,128)(2,1)} %wo.1) | copy-start | bytes 1228804
  2.3 8.3 %collective-permute-start.1 = (bf16[32,1280]{1,0:T(8,128)(2,1)S(1)}, bf16[32,1280]{1,0:T(8,128)(2,1)S(1)}, u32[]{:S(2)}, u32[]{:S(2)}) collective-permute-start(bf16[32,1280]{1,0:T(8,128)(2,1)S(1)} %get-tuple-element.72), channel_id=1, source_target_pairs={{0,32},{32,64},{64,96},{96,128},{128,160},{160,192},{192,224},{224... | collective-permute-start | bytes 245768 | tf_op jit(solution)/shard_map/ppermute | solution.py:28
  4.2 6.4 %collective-permute-start = (bf16[32,1280]{1,0:T(8,128)(2,1)S(1)}, bf16[32,1280]{1,0:T(8,128)(2,1)S(1)}, u32[]{:S(2)}, u32[]{:S(2)}) collective-permute-start(bf16[32,1280]{1,0:T(8,128)(2,1)S(1)} %get-tuple-element.72), channel_id=1, source_target_pairs={{0,224},{32,0},{64,32},{96,64},{128,96},{160,128},{192,160},{224,1... | collective-permute-start | bytes 245768 | tf_op jit(solution)/shard_map/ppermute | solution.py:28
  8.2 12.6 %collective-permute-start.4 = (bf16[160,1280]{1,0:T(8,128)(2,1)}, bf16[160,1280]{1,0:T(8,128)(2,1)S(1)}, u32[]{:S(2)}, u32[]{:S(2)}) collective-permute-start(bf16[160,1280]{1,0:T(8,128)(2,1)} %bitcast.3), channel_id=1, source_target_pairs={{0,24},{24,0},{8,16},{16,8},{1,25},{25,1},{9,17},{17,9},{2,26},{26... | collective-permute-start | bytes 1228808 | tf_op jit(solution)/shard_map/ppermute | solution.py:36
  10.6 6.9 %collective-permute-start.3 = (bf16[32,1280]{1,0:T(8,128)(2,1)S(1)}, bf16[32,1280]{1,0:T(8,128)(2,1)S(1)}, u32[]{:S(2)}, u32[]{:S(2)}) collective-permute-start(bf16[32,1280]{1,0:T(8,128)(2,1)S(1)} %collective-permute-done.1), channel_id=1, source_target_pairs={{0,32},{32,64},{64,96},{96,128},{128,160},{160,192},{192,224},{224... | collective-permute-start | bytes 245768 | tf_op jit(solution)/shard_map/ppermute | solution.py:28
  10.6 5.3 %collective-permute-start.2 = (bf16[32,1280]{1,0:T(8,128)(2,1)S(1)}, bf16[32,1280]{1,0:T(8,128)(2,1)S(1)}, u32[]{:S(2)}, u32[]{:S(2)}) collective-permute-start(bf16[32,1280]{1,0:T(8,128)(2,1)S(1)} %collective-permute-done), channel_id=1, source_target_pairs={{0,224},{32,0},{64,32},{96,64},{128,96},{160,128},{192,160},{224,1... | collective-permute-start | bytes 245768 | tf_op jit(solution)/shard_map/ppermute | solution.py:28
  15.9 12.6 %collective-permute-start.7 = (bf16[160,1280]{1,0:T(8,128)(2,1)}, bf16[160,1280]{1,0:T(8,128)(2,1)S(1)}, u32[]{:S(2)}, u32[]{:S(2)}) collective-permute-start(bf16[160,1280]{1,0:T(8,128)(2,1)} %wo.1), channel_id=1, source_target_pairs={{0,24},{24,0},{8,16},{16,8},{1,25},{25,1},{9,17},{17,9},{2,26},{26... | collective-permute-start | bytes 1228808 | tf_op jit(solution)/shard_map/ppermute | solution.py:36
  20.8 4.4 %collective-permute-start.5 = (bf16[32,1280]{1,0:T(8,128)(2,1)S(1)}, bf16[32,1280]{1,0:T(8,128)(2,1)S(1)}, u32[]{:S(2)}, u32[]{:S(2)}) collective-permute-start(bf16[32,1280]{1,0:T(8,128)(2,1)S(1)} %collective-permute-done.2), channel_id=1, source_target_pairs={{0,224},{32,0},{64,32},{96,64},{128,96},{160,128},{192,160},{224,1... | collective-permute-start | bytes 245768 | tf_op jit(solution)/shard_map/ppermute | solution.py:28
  21.9 15.0 %collective-permute-start.10 = (bf16[160,1280]{1,0:T(8,128)(2,1)S(1)}, bf16[160,1280]{1,0:T(8,128)(2,1)S(1)}, u32[]{:S(2)}, u32[]{:S(2)}) collective-permute-start(bf16[160,1280]{1,0:T(8,128)(2,1)S(1)} %constant_dynamic-update-slice_fusion.2.refs_0_), channel_id=1, source_target_pairs={{0,8},{8,0},{16,24},{24,16},{1,9},{9,1},{17,25},{25,17},{2,10},{10... | collective-permute-start | bytes 1228808 | tf_op jit(solution)/shard_map/ppermute | solution.py:32
  22.9 5.7 %collective-permute-start.6 = (bf16[32,1280]{1,0:T(8,128)(2,1)S(1)}, bf16[32,1280]{1,0:T(8,128)(2,1)S(1)}, u32[]{:S(2)}, u32[]{:S(2)}) collective-permute-start(bf16[32,1280]{1,0:T(8,128)(2,1)S(1)} %collective-permute-done.3), channel_id=1, source_target_pairs={{0,32},{32,64},{64,96},{96,128},{128,160},{160,192},{192,224},{224... | collective-permute-start | bytes 245768 | tf_op jit(solution)/shard_map/ppermute | solution.py:28
  28.6 4.1 %collective-permute-start.8 = (bf16[16,1280]{1,0:T(8,128)(2,1)S(1)}, bf16[16,1280]{1,0:T(8,128)(2,1)S(1)}, u32[]{:S(2)}, u32[]{:S(2)}) collective-permute-start(bf16[16,1280]{1,0:T(8,128)(2,1)S(1)} %slice.82), channel_id=1, source_target_pairs={{0,224},{32,0},{64,32},{96,64},{128,96},{160,128},{192,160},{224,1... | collective-permute-start | bytes 122888 | tf_op jit(solution)/shard_map/ppermute | solution.py:28
  30.1 5.3 %collective-permute-start.9 = (bf16[16,1280]{1,0:T(8,128)(2,1)S(1)}, bf16[16,1280]{1,0:T(8,128)(2,1)S(1)}, u32[]{:S(2)}, u32[]{:S(2)}) collective-permute-start(bf16[16,1280]{1,0:T(8,128)(2,1)S(1)} %slice.83), channel_id=1, source_target_pairs={{0,32},{32,64},{64,96},{96,128},{128,160},{160,192},{192,224},{224... | collective-permute-start | bytes 122888 | tf_op jit(solution)/shard_map/ppermute | solution.py:28
  35.4 6.3 %collective-permute-start.11 = (bf16[96,1280]{1,0:T(8,128)(2,1)S(1)}, bf16[96,1280]{1,0:T(8,128)(2,1)}, u32[]{:S(2)}, u32[]{:S(2)}) collective-permute-start(bf16[96,1280]{1,0:T(8,128)(2,1)S(1)} %constant_dynamic-update-slice_fusion.8.refs_1_), channel_id=1, source_target_pairs={{0,8},{8,0},{16,24},{24,16},{1,9},{9,1},{17,25},{25,17},{2,10},{10... | collective-permute-start | bytes 737288 | tf_op jit(solution)/shard_map/ppermute | solution.py:32
  36.9 4.8 %collective-permute-start.12 = (bf16[160,1280]{1,0:T(8,128)(2,1)S(1)}, bf16[160,1280]{1,0:T(8,128)(2,1)S(1)}, u32[]{:S(2)}, u32[]{:S(2)}) collective-permute-start(bf16[160,1280]{1,0:T(8,128)(2,1)S(1)} %constant_dynamic-update-slice_fusion.2.refs_0_), channel_id=1, source_target_pairs={{0,1},{1,0},{2,3},{3,2},{4,5},{5,4},{6,7},{7,6},{8,9},{9,8},{10,11... | collective-permute-start | bytes 1228808 | tf_op jit(solution)/shard_map/ppermute | solution.py:28
  36.9 4.8 %collective-permute-start.14 = (bf16[160,1280]{1,0:T(8,128)(2,1)S(1)}, bf16[160,1280]{1,0:T(8,128)(2,1)S(1)}, u32[]{:S(2)}, u32[]{:S(2)}) collective-permute-start(bf16[160,1280]{1,0:T(8,128)(2,1)S(1)} %collective-permute-done.10.refs_2_), channel_id=1, source_target_pairs={{0,1},{1,0},{2,3},{3,2},{4,5},{5,4},{6,7},{7,6},{8,9},{9,8},{10,11... | collective-permute-start | bytes 1228808 | tf_op jit(solution)/shard_map/ppermute | solution.py:28
  37.4 4.3 %collective-permute-start.13 = (bf16[96,1280]{1,0:T(8,128)(2,1)S(1)}, bf16[96,1280]{1,0:T(8,128)(2,1)}, u32[]{:S(2)}, u32[]{:S(2)}) collective-permute-start(bf16[96,1280]{1,0:T(8,128)(2,1)S(1)} %constant_dynamic-update-slice_fusion.8.refs_1_), channel_id=1, source_target_pairs={{0,1},{1,0},{2,3},{3,2},{4,5},{5,4},{6,7},{7,6},{8,9},{9,8},{10,11... | collective-permute-start | bytes 737288 | tf_op jit(solution)/shard_map/ppermute | solution.py:28
  41.7 1.9 %collective-permute-start.15 = (bf16[96,1280]{1,0:T(8,128)(2,1)}, bf16[96,1280]{1,0:T(8,128)(2,1)}, u32[]{:S(2)}, u32[]{:S(2)}) collective-permute-start(bf16[96,1280]{1,0:T(8,128)(2,1)} %collective-permute-done.11.refs_3_), channel_id=1, source_target_pairs={{0,1},{1,0},{2,3},{3,2},{4,5},{5,4},{6,7},{7,6},{8,9},{9,8},{10,11... | collective-permute-start | bytes 737288 | tf_op jit(solution)/shard_map/ppermute | solution.py:28
  46.7 7.8 %collective-permute-start.16 = (bf16[2,320,128]{2,1,0:T(8,128)(2,1)S(1)}, bf16[2,320,128]{2,1,0:T(8,128)(2,1)S(1)}, u32[]{:S(2)}, u32[]{:S(2)}) collective-permute-start(bf16[2,320,128]{2,1,0:T(8,128)(2,1)S(1)} %get-tuple-element.38), channel_id=1, source_target_pairs={{0,2},{2,4},{4,6},{6,0},{1,3},{3,5},{5,7},{7,1},{8,10},{10,12},{12... | collective-permute-start | bytes 491528 | tf_op jit(solution)/shard_map/ppermute | solution.py:28
  48.5 10.6 %collective-permute-start.17 = (bf16[2,320,128]{2,1,0:T(8,128)(2,1)S(1)}, bf16[2,320,128]{2,1,0:T(8,128)(2,1)S(1)}, u32[]{:S(2)}, u32[]{:S(2)}) collective-permute-start(bf16[2,320,128]{2,1,0:T(8,128)(2,1)S(1)} %get-tuple-element.39), channel_id=1, source_target_pairs={{0,4},{2,6},{4,0},{6,2},{1,5},{3,7},{5,1},{7,3},{8,12},{10,14},{12... | collective-permute-start | bytes 491528 | tf_op jit(solution)/shard_map/ppermute | solution.py:28
  51.4 7.7 %collective-permute-start.18 = (bf16[2,320,128]{2,1,0:T(8,128)(2,1)S(1)}, bf16[2,320,128]{2,1,0:T(8,128)(2,1)S(1)}, u32[]{:S(2)}, u32[]{:S(2)}) collective-permute-start(bf16[2,320,128]{2,1,0:T(8,128)(2,1)S(1)} %get-tuple-element.40), channel_id=1, source_target_pairs={{0,6},{2,0},{4,2},{6,4},{1,7},{3,1},{5,3},{7,5},{8,14},{10,8},{12,... | collective-permute-start | bytes 491528 | tf_op jit(solution)/shard_map/ppermute | solution.py:28
  59.3 7.2 %collective-permute-start.21 = (bf16[2,320,128]{2,1,0:T(8,128)(2,1)S(1)}, bf16[2,320,128]{2,1,0:T(8,128)(2,1)S(1)}, u32[]{:S(2)}, u32[]{:S(2)}) collective-permute-start(bf16[2,320,128]{2,1,0:T(8,128)(2,1)S(1)} %shard_map.76.b0), channel_id=1, source_target_pairs={{0,2},{2,4},{4,6},{6,0},{1,3},{3,5},{5,7},{7,1},{8,10},{10,12},{12... | collective-permute-start | bytes 491528 | tf_op jit(solution)/shard_map/ppermute | solution.py:28
  60.6 9.7 %collective-permute-start.20 = (bf16[2,320,128]{2,1,0:T(8,128)(2,1)S(1)}, bf16[2,320,128]{2,1,0:T(8,128)(2,1)S(1)}, u32[]{:S(2)}, u32[]{:S(2)}) collective-permute-start(bf16[2,320,128]{2,1,0:T(8,128)(2,1)S(1)} %shard_map.76.b0), channel_id=1, source_target_pairs={{0,4},{2,6},{4,0},{6,2},{1,5},{3,7},{5,1},{7,3},{8,12},{10,14},{12... | collective-permute-start | bytes 491528 | tf_op jit(solution)/shard_map/ppermute | solution.py:28
  63.0 7.3 %collective-permute-start.19 = (bf16[2,320,128]{2,1,0:T(8,128)(2,1)S(1)}, bf16[2,320,128]{2,1,0:T(8,128)(2,1)S(1)}, u32[]{:S(2)}, u32[]{:S(2)}) collective-permute-start(bf16[2,320,128]{2,1,0:T(8,128)(2,1)S(1)} %shard_map.76.b0), channel_id=1, source_target_pairs={{0,6},{2,0},{4,2},{6,4},{1,7},{3,1},{5,3},{7,5},{8,14},{10,8},{12,... | collective-permute-start | bytes 491528 | tf_op jit(solution)/shard_map/ppermute | solution.py:28
  72.0 2.0 %collective-permute-start.24 = (bf16[192,1280]{1,0:T(8,128)(2,1)S(1)}, bf16[192,1280]{1,0:T(8,128)(2,1)S(1)}, u32[]{:S(2)}, u32[]{:S(2)}) collective-permute-start(bf16[192,1280]{1,0:T(8,128)(2,1)S(1)} %get-tuple-element.44), channel_id=1, source_target_pairs={{0,1},{1,0},{2,3},{3,2},{4,5},{5,4},{6,7},{7,6},{8,9},{9,8},{10,11... | collective-permute-start | bytes 1474568 | tf_op jit(solution)/shard_map/ppermute | solution.py:28
  72.1 10.2 %collective-permute-start.22 = (bf16[320,1280]{1,0:T(8,128)(2,1)S(1)}, bf16[320,1280]{1,0:T(8,128)(2,1)S(1)}, u32[]{:S(2)}, u32[]{:S(2)}) collective-permute-start(bf16[320,1280]{1,0:T(8,128)(2,1)S(1)} %get-tuple-element.42), channel_id=1, source_target_pairs={{0,1},{1,0},{2,3},{3,2},{4,5},{5,4},{6,7},{7,6},{8,9},{9,8},{10,11... | collective-permute-start | bytes 2457608 | tf_op jit(solution)/shard_map/ppermute | solution.py:28
  74.1 8.1 %collective-permute-start.25 = (bf16[96,1280]{1,0:T(8,128)(2,1)S(1)}, bf16[96,1280]{1,0:T(8,128)(2,1)S(1)}, u32[]{:S(2)}, u32[]{:S(2)}) collective-permute-start(bf16[96,1280]{1,0:T(8,128)(2,1)S(1)} %fusion.2), channel_id=1, source_target_pairs={{0,8},{8,0},{16,24},{24,16},{1,9},{9,1},{17,25},{25,17},{2,10},{10... | collective-permute-start | bytes 737288 | tf_op jit(solution)/shard_map/ppermute | solution.py:32
  76.3 12.5 %collective-permute-start.28 = (bf16[160,1280]{1,0:T(8,128)(2,1)S(1)}, bf16[160,1280]{1,0:T(8,128)(2,1)S(1)}, u32[]{:S(2)}, u32[]{:S(2)}) collective-permute-start(bf16[160,1280]{1,0:T(8,128)(2,1)S(1)} %get-tuple-element.50), channel_id=1, source_target_pairs={{0,24},{24,0},{8,16},{16,8},{1,25},{25,1},{9,17},{17,9},{2,26},{26... | collective-permute-start | bytes 1228808 | tf_op jit(solution)/shard_map/ppermute | solution.py:36
  78.6 18.3 %collective-permute-start.31 = (bf16[160,1280]{1,0:T(8,128)(2,1)S(1)}, bf16[160,1280]{1,0:T(8,128)(2,1)S(1)}, u32[]{:S(2)}, u32[]{:S(2)}) collective-permute-start(bf16[160,1280]{1,0:T(8,128)(2,1)S(1)} %get-tuple-element.53), channel_id=1, source_target_pairs={{0,24},{24,0},{8,16},{16,8},{1,25},{25,1},{9,17},{17,9},{2,26},{26... | collective-permute-start | bytes 1228808 | tf_op jit(solution)/shard_map/ppermute | solution.py:36
  82.5 4.1 %collective-permute-start.27 = (bf16[16,1280]{1,0:T(8,128)(2,1)S(1)}, bf16[16,1280]{1,0:T(8,128)(2,1)S(1)}, u32[]{:S(2)}, u32[]{:S(2)}) collective-permute-start(bf16[16,1280]{1,0:T(8,128)(2,1)S(1)} %get-tuple-element.70), channel_id=1, source_target_pairs={{0,224},{32,0},{64,32},{96,64},{128,96},{160,128},{192,160},{224,1... | collective-permute-start | bytes 122888 | tf_op jit(solution)/shard_map/ppermute | solution.py:28
  82.6 5.2 %collective-permute-start.26 = (bf16[16,1280]{1,0:T(8,128)(2,1)S(1)}, bf16[16,1280]{1,0:T(8,128)(2,1)S(1)}, u32[]{:S(2)}, u32[]{:S(2)}) collective-permute-start(bf16[16,1280]{1,0:T(8,128)(2,1)S(1)} %get-tuple-element.71), channel_id=1, source_target_pairs={{0,32},{32,64},{64,96},{96,128},{128,160},{160,192},{192,224},{224... | collective-permute-start | bytes 122888 | tf_op jit(solution)/shard_map/ppermute | solution.py:28
  84.6 10.1 %collective-permute-start.23 = (bf16[160,1280]{1,0:T(8,128)(2,1)S(1)}, bf16[160,1280]{1,0:T(8,128)(2,1)S(1)}, u32[]{:S(2)}, u32[]{:S(2)}) collective-permute-start(bf16[160,1280]{1,0:T(8,128)(2,1)S(1)} %fusion), channel_id=1, source_target_pairs={{0,8},{8,0},{16,24},{24,16},{1,9},{9,1},{17,25},{25,17},{2,10},{10... | collective-permute-start | bytes 1228808 | tf_op jit(solution)/shard_map/ppermute | solution.py:32
  88.9 6.0 %collective-permute-start.29 = (bf16[32,1280]{1,0:T(8,128)(2,1)S(1)}, bf16[32,1280]{1,0:T(8,128)(2,1)S(1)}, u32[]{:S(2)}, u32[]{:S(2)}) collective-permute-start(bf16[32,1280]{1,0:T(8,128)(2,1)S(1)} %get-tuple-element.51), channel_id=1, source_target_pairs={{0,32},{32,64},{64,96},{96,128},{128,160},{160,192},{192,224},{224... | collective-permute-start | bytes 245768 | tf_op jit(solution)/shard_map/ppermute | solution.py:28
  88.9 6.0 %collective-permute-start.30 = (bf16[32,1280]{1,0:T(8,128)(2,1)S(1)}, bf16[32,1280]{1,0:T(8,128)(2,1)S(1)}, u32[]{:S(2)}, u32[]{:S(2)}) collective-permute-start(bf16[32,1280]{1,0:T(8,128)(2,1)S(1)} %get-tuple-element.52), channel_id=1, source_target_pairs={{0,224},{32,0},{64,32},{96,64},{128,96},{160,128},{192,160},{224,1... | collective-permute-start | bytes 245768 | tf_op jit(solution)/shard_map/ppermute | solution.py:28
  96.8 5.7 %collective-permute-start.32 = (bf16[32,1280]{1,0:T(8,128)(2,1)S(1)}, bf16[32,1280]{1,0:T(8,128)(2,1)S(1)}, u32[]{:S(2)}, u32[]{:S(2)}) collective-permute-start(bf16[32,1280]{1,0:T(8,128)(2,1)S(1)} %get-tuple-element.54), channel_id=1, source_target_pairs={{0,32},{32,64},{64,96},{96,128},{128,160},{160,192},{192,224},{224... | collective-permute-start | bytes 245768 | tf_op jit(solution)/shard_map/ppermute | solution.py:28
  96.8 5.7 %collective-permute-start.33 = (bf16[32,1280]{1,0:T(8,128)(2,1)S(1)}, bf16[32,1280]{1,0:T(8,128)(2,1)S(1)}, u32[]{:S(2)}, u32[]{:S(2)}) collective-permute-start(bf16[32,1280]{1,0:T(8,128)(2,1)S(1)} %get-tuple-element.55), channel_id=1, source_target_pairs={{0,224},{32,0},{64,32},{96,64},{128,96},{160,128},{192,160},{224,1... | collective-permute-start | bytes 245768 | tf_op jit(solution)/shard_map/ppermute | solution.py:28
  102.5 6.6 %collective-permute-start.34 = (f32[32,1280]{1,0:T(8,128)S(1)}, f32[32,1280]{1,0:T(8,128)S(1)}, u32[]{:S(2)}, u32[]{:S(2)}) collective-permute-start(f32[32,1280]{1,0:T(8,128)S(1)} %get-tuple-element.56), channel_id=1, source_target_pairs={{0,32},{32,64},{64,96},{96,128},{128,160},{160,192},{192,224},{224... | collective-permute-start | bytes 491528 | tf_op jit(solution)/shard_map/ppermute | solution.py:28
  102.7 6.4 %collective-permute-start.35 = (f32[32,1280]{1,0:T(8,128)S(1)}, f32[32,1280]{1,0:T(8,128)S(1)}, u32[]{:S(2)}, u32[]{:S(2)}) collective-permute-start(f32[32,1280]{1,0:T(8,128)S(1)} %get-tuple-element.57), channel_id=1, source_target_pairs={{0,224},{32,0},{64,32},{96,64},{128,96},{160,128},{192,160},{224,1... | collective-permute-start | bytes 491528 | tf_op jit(solution)/shard_map/ppermute | solution.py:28

commit v4 on v3

v4 whole, which is shorter than its diff:
```python
import functools

import jax
import jax.numpy as jnp
from jax import lax
from jax.experimental import pallas as pl
from jax.experimental.pallas import tpu as pltpu
from jax.sharding import Mesh, PartitionSpec as P

BF = jnp.bfloat16
F32 = jnp.float32
SIZE = {"z": 8, "x": 4, "row": 4, "col": 2}
CUT, REST = 160, 96


def smooth_gate(value):
    return 0.5 * value * (1.0 + lax.erf(value * 0.7071067811865476))


def smooth_slope(value):
    cumul = 0.5 * (1.0 + lax.erf(value * 0.7071067811865476))
    return cumul + value * jnp.exp(-0.5 * value * value) * 0.3989422804014327


def send(value, axis, shift):
    size = SIZE[axis]
    return lax.ppermute(value, axis, [(i, (i + shift) % size) for i in range(size)])


def along(value):
    pairs = [(2 * i + c, (i + 1 - 2 * c) % 8 * 2 + c) for i in range(8) for c in range(2)]
    return lax.ppermute(value, ("z", "col"), pairs)


def token_pair(value):
    return lax.ppermute(value, "x", [(0, 1), (1, 0), (2, 3), (3, 2)])


def weight_pair(value):
    return lax.ppermute(value, "x", [(0, 3), (3, 0), (1, 2), (2, 1)])


def after(value, other):
    return lax.optimization_barrier((value, other))[0]


def call(body, outs, args, flops=1 << 20, scratch=()):
    specs = [pl.BlockSpec(memory_space=pltpu.SMEM)]
    specs += [pl.BlockSpec(memory_space=pltpu.VMEM)] * (len(args) - 1)
    kernel = pl.pallas_call(
        body,
        out_shape=outs,
        in_specs=specs,
        out_specs=[pl.BlockSpec(memory_space=pltpu.VMEM)] * len(outs),
        scratch_shapes=list(scratch),
        compiler_params=pltpu.CompilerParams(vmem_limit_bytes=40 << 20),
        cost_estimate=pl.CostEstimate(
            flops=flops, bytes_accessed=1 << 20, transcendentals=0
        ),
    )
    return list(kernel(*args))


def cat(values):
    return jnp.concatenate(values, 0)


def dot(a, b, dim_a, dim_b):
    return lax.dot_general(
        a, b, (((dim_a,), (dim_b,)), ((), ())), preferred_element_type=F32
    )


def blocks(core, sign):
    out = [(0, core, 0)]
    for step in (1, 2, 3):
        z = (8 + sign * (1 - 2 * core) * step) % 8
        out += [(64 * step - 32, core, z), (64 * step, 1 - core, z)]
    return out + [(224, core, 4)]


def place(chip, core, z):
    return pl.ds(pl.multiple_of(chip * 256 + core * 128 + z * 16, 16), 16)


def up_kernel(me, *refs):
    held, weights = refs[:8], (refs[8:10], refs[10:12])
    tok, cot, parts, whole = refs[12], refs[13], refs[14:18], refs[18]
    h = weights[0][0].shape[0]
    for group in range(2):
        mine = me[1] if group == 0 else 1 - me[1]
        for chip in range(2):
            pair = held[group * 4 + chip * 2 : group * 4 + chip * 2 + 2]
            for row, core, z in blocks(mine, -1):
                ref, row = (pair[0], row) if row < CUT else (pair[1], row - CUT)
                tok[place(chip, core, z)] = ref[row : row + 16]
                cot[place(chip, core, z)] = ref[row + 16 : row + 32]
    for s, value in enumerate((tok, cot)):
        for i, w in enumerate(weights[s]):
            total = dot(w[...], value[...], 1, 1)
            for q in range(4):
                whole[q, s, i * h : i * h + h] = total[:, q * 128 : q * 128 + 128]
    for k, part in enumerate(parts):
        part[...] = whole[(me[0] + k) % 4].astype(part.dtype)


def act_kernel(me, p0, p1, p2, p3, out):
    del me
    pre, grad_act = p0[0], p0[1]
    for part in (p1, p2, p3):
        pre += part[0].astype(F32)
        grad_act += part[1].astype(F32)
    out[0] = smooth_gate(pre).astype(BF)
    out[1] = (grad_act * smooth_slope(pre)).astype(BF)


def down_kernel(me, b0, b1, b2, b3, wi, wi2, wo, wo2, near, far, head, tail, full, whole):
    h = wi.shape[0]
    for k, block in enumerate((b0, b1, b2, b3)):
        lane = pl.multiple_of(((me[0] + k) % 4) * 128, 128)
        full[:, :, pl.ds(lane, 128)] = block[...]
    for s, (w, w2) in enumerate(((wo, wo2), (wi, wi2))):
        whole[...] = dot(full[s, :h], w[...], 0, 0) + dot(full[s, h:], w2[...], 0, 0)
        for chip in range(2):
            for row, core, z in blocks(1 - me[1], 1):
                value = whole[place(chip, core, z)].astype(BF)
                if row < CUT:
                    row += (1 - chip) * CUT + s * 16
                    head[row : row + 16] = value
                else:
                    row += (1 - chip) * REST - CUT + s * 16
                    tail[row : row + 16] = value
            for row, core, z in blocks(me[1], 1):
                (near, far)[chip][row + s * 16 : row + s * 16 + 16] = whole[place(chip, core, z)]


def pair_kernel(me, full, tok, cot, out, back):
    del me
    h = full.shape[1] // 2
    out[...] = dot(full[0, h:], cot[...], 1, 0).astype(BF)
    back[...] = dot(full[1, h:], tok[...], 1, 0).astype(BF)


def own_kernel(s, me, full, value, other, grad):
    del me
    h = full.shape[1] // 2
    grad[...] = dot(full[s, :h], value[...], 1, 0) + other[...].astype(F32)


def on_device(tokens, w_in, w_out, cotangent):
    me = jnp.stack([lax.axis_index("row"), lax.axis_index("col")]).astype(jnp.int32)
    d, h = w_in.shape
    shape = jax.ShapeDtypeStruct
    flops = 2 * 1024 * d * h

    base = cat([tokens, cotangent])
    first = along(cat([base, send(base, "col", 1)]))
    w_in_t = w_in.T
    w_in_2 = weight_pair(after(w_in_t, base))
    second = along(first)
    near_h = cat([base, first, second])
    third = after(second, w_in_2)
    w_out_2 = weight_pair(after(w_out, second))
    far_h = token_pair(near_h)
    third = along(third)
    near_t = cat([third, along(after(third, w_out_2)[:32])])
    far_t = token_pair(near_t)
    quarters = [near_h, near_t, far_h, far_t]
    quarters += [send(value, "col", 1) for value in quarters]

    part, rounded = shape((2, 2 * h, 128), F32), shape((2, 2 * h, 128), BF)
    tok, cot, *parts = call(
        up_kernel,
        [shape((512, d), BF)] * 2 + [part] + [rounded] * 3,
        [me, *quarters, w_in_t, w_in_2, w_out, w_out_2],
        2 * flops,
        [pltpu.VMEM((4, 2, 2 * h, 128), F32)],
    )
    parts[1:] = [send(parts[k], "row", k) for k in (1, 2, 3)]
    (block,) = call(act_kernel, [rounded], [me, *parts])
    shared = [block] + [send(block, "row", -k) for k in (1, 2, 3)]

    sums = shape((256, d), F32)
    near, far, head, tail, full = call(
        down_kernel,
        [sums, sums, shape((2 * CUT, d), BF), shape((2 * REST, d), BF), shape((2, 2 * h, 512), BF)],
        [me, *shared, w_in_t, w_in_2, w_out, w_out_2],
        2 * flops,
        [pltpu.VMEM((512, d), F32)],
    )
    tail = send(tail, "col", 1).astype(F32)
    far_t = token_pair((far[CUT:] + tail[:REST]).astype(BF)).astype(F32)
    near_t = near[CUT:] + tail[REST:] + far_t
    head = send(head, "col", 1).astype(F32)
    far_h = (far[:CUT] + head[:CUT]).astype(BF)
    chain = after(near_t[64:], far_h)
    near_h = near[:CUT] + head[CUT:] + token_pair(far_h).astype(F32)
    pair_out, pair_in = call(
        pair_kernel, [shape((h, d), BF)] * 2, [me, after(full, tail), tok, cot], flops
    )
    pair_out, pair_in = weight_pair(pair_out), weight_pair(pair_in)
    chain = along(chain.astype(BF)).astype(F32)
    chain = cat([near_t[:32] + chain, near_t[32:64]]).astype(BF)
    chain = along(after(chain, pair_out)).astype(F32)
    chain = (near_h[96:160] + chain).astype(BF)
    chain = along(after(chain, pair_in)).astype(F32)
    weight = [shape((h, d), F32)]
    (grad_out,) = call(functools.partial(own_kernel, 0), weight, [me, full, cot, pair_out], flops)
    (grad_in_t,) = call(functools.partial(own_kernel, 1), weight, [me, full, tok, pair_in], flops)
    chain = along(after(near_h[32:96] + chain, grad_out))
    total = near_h[:32] + chain[:32] + send(after(chain[32:], grad_in_t), "col", 1)
    output, input_grad = total[:16].astype(BF), total[16:].astype(BF)
    return (output, input_grad, grad_in_t.T, grad_out)


def solution(mesh):
    mesh = Mesh(mesh.devices.reshape(8, 4, 4, 2), ("z", "x", "row", "col"))
    whole = ("z", "x", "col")
    placed = (P(whole, "row"), P("row", whole), P(whole, "row"), P(whole, "row"))
    return jax.shard_map(
        on_device,
        mesh=mesh,
        in_specs=placed,
        out_specs=(P(whole, "row"), P(whole, "row"), P("row", whole), P(whole, "row")),
        check_vma=False,
    )
```

time: 111 us -> 127 us (1.14)
  the two profiles are of different devices: /device:TPU:2 before, /device:TPU:1 now
where the time goes in v4:
time: 127 us
  waiting for transfers between devices  58.1 us (46%)
  starting transfers between devices  52.6 us (41%)
  Pallas kernels  11.3 us (9%)
  local copies, waits for them, and re-layouts  2.37 us (2%)
  other arithmetic  1.48 us (1%)
    ppermute x14, starting transfers between devices, send(): lax.ppermute(value, axis, [(i, (i + shift) % size) for i in range(size)])  23.5 us
    ppermute x8, starting transfers between devices, along(): return lax.ppermute(value, ('z', 'col'), pairs)  21.1 us
    ppermute x14, waiting for transfers between devices, send(): lax.ppermute(value, axis, [(i, (i + shift) % size) for i in range(size)])  17.6 us
    ppermute x8, waiting for transfers between devices, along(): return lax.ppermute(value, ('z', 'col'), pairs)  15.8 us
    ppermute x4, waiting for transfers between devices, weight_pair(): return lax.ppermute(value, 'x', [(0, 3), (3, 0), (1, 2), (2, 1)])  14.2 us
    pallas_call x6, Pallas kernels, call(): return list(kernel(*args))  11.3 us
    ppermute x4, waiting for transfers between devices, token_pair(): return lax.ppermute(value, 'x', [(0, 1), (1, 0), (2, 3), (3, 2)])  10.5 us
    ppermute x4, starting transfers between devices, weight_pair(): return lax.ppermute(value, 'x', [(0, 3), (3, 0), (1, 2), (2, 1)])  7.72 us
  transfers between devices with their start and end apart: 30, of which 20 were waited for; matrix products, arithmetic and copies ran while one was open for 0% of the time, Pallas kernels for 4%

profile of v4, /device:TPU:1, one launch (start us, length us, event | category | flops | bytes accessed | tf_op | source)
XLA Modules:
  0.0 126.6 jit_solution(4069566367250998463)
XLA Ops:
  0.6 0.0 copy-start
  0.7 0.9 constant_dynamic-update-slice_fusion.1
  1.5 0.8 constant_dynamic-update-slice_fusion
  2.3 3.2 %collective-permute-start = (bf16[32,1280]{1,0:T(8,128)(2,1)S(1)}, bf16[32,1280]{1,0:T(8,128)(2,1)S(1)}, u32[]{:S(2)}, u32[]{:S(2)}) collective-permute-start(bf16[32,1280]{1,0:T(8,128)(2,1)S(1)} %get-tuple-element.54), channel_id=1, source_target_pairs={{0,1},{1,0},{2,3},{3,2},{4,5},{5,4},{6,7},{7,6},{8,9},{9,8},{10,11... | collective-permute-start | bytes 245768 | tf_op jit(solution)/shard_map/ppermute | solution.py:27
  5.5 0.9 collective-permute-done
  6.5 0.8 pad_maximum_fusion
  7.3 3.9 %collective-permute-start.1 = (bf16[64,1280]{1,0:T(8,128)(2,1)S(1)}, bf16[64,1280]{1,0:T(8,128)(2,1)S(1)}, u32[]{:S(2)}, u32[]{:S(2)}) collective-permute-start(bf16[64,1280]{1,0:T(8,128)(2,1)S(1)} %pad_maximum_fusion), channel_id=1, source_target_pairs={{0,32},{1,225},{32,64},{33,1},{64,96},{65,33},{96,128},{97,65},{12... | collective-permute-start | bytes 491528 | tf_op jit(solution)/shard_map/ppermute | solution.py:32
  11.2 2.5 %collective-permute-start.3 = (bf16[160,1280]{1,0:T(8,128)(2,1)}, bf16[160,1280]{1,0:T(8,128)(2,1)S(1)}, u32[]{:S(2)}, u32[]{:S(2)}) collective-permute-start(bf16[160,1280]{1,0:T(8,128)(2,1)} %bitcast.4), channel_id=1, source_target_pairs={{0,24},{24,0},{8,16},{16,8},{1,25},{25,1},{9,17},{17,9},{2,26},{26... | collective-permute-start | bytes 1228808 | tf_op jit(solution)/shard_map/ppermute | solution.py:40
  13.7 3.2 %collective-permute-start.2 = (bf16[64,1280]{1,0:T(8,128)(2,1)S(1)}, bf16[64,1280]{1,0:T(8,128)(2,1)S(1)}, u32[]{:S(2)}, u32[]{:S(2)}) collective-permute-start(bf16[64,1280]{1,0:T(8,128)(2,1)S(1)} %collective-permute-done.1), channel_id=1, source_target_pairs={{0,32},{1,225},{32,64},{33,1},{64,96},{65,33},{96,128},{97,65},{12... | collective-permute-start | bytes 491528 | tf_op jit(solution)/shard_map/ppermute | solution.py:32
  16.9 2.3 %collective-permute-done.2 = bf16[64,1280]{1,0:T(8,128)(2,1)S(1)} collective-permute-done((bf16[64,1280]{1,0:T(8,128)(2,1)S(1)}, bf16[64,1280]{1,0:T(8,128)(2,1)S(1)}, u32[]{:S(2)}, u32[]{:S(2)}) %collective-permute-start.2) | collective-permute-done | bytes 163872 | tf_op jit(solution)/shard_map/ppermute | solution.py:32
  19.1 2.5 %collective-permute-start.5 = (bf16[160,1280]{1,0:T(8,128)(2,1)}, bf16[160,1280]{1,0:T(8,128)(2,1)S(1)}, u32[]{:S(2)}, u32[]{:S(2)}) collective-permute-start(bf16[160,1280]{1,0:T(8,128)(2,1)} %wo.1), channel_id=1, source_target_pairs={{0,24},{24,0},{8,16},{16,8},{1,25},{25,1},{9,17},{17,9},{2,26},{26... | collective-permute-start | bytes 1228808 | tf_op jit(solution)/shard_map/ppermute | solution.py:40
  21.6 3.5 %collective-permute-start.4 = (bf16[64,1280]{1,0:T(8,128)(2,1)S(1)}, bf16[64,1280]{1,0:T(8,128)(2,1)S(1)}, u32[]{:S(2)}, u32[]{:S(2)}) collective-permute-start(bf16[64,1280]{1,0:T(8,128)(2,1)S(1)} %collective-permute-done.2), channel_id=1, source_target_pairs={{0,32},{1,225},{32,64},{33,1},{64,96},{65,33},{96,128},{97,65},{12... | collective-permute-start | bytes 491528 | tf_op jit(solution)/shard_map/ppermute | solution.py:32
  25.1 0.1 collective-permute-start.7
  25.2 2.1 %collective-permute-done.4 = bf16[64,1280]{1,0:T(8,128)(2,1)S(1)} collective-permute-done((bf16[64,1280]{1,0:T(8,128)(2,1)S(1)}, bf16[64,1280]{1,0:T(8,128)(2,1)S(1)}, u32[]{:S(2)}, u32[]{:S(2)}) %collective-permute-start.4) | collective-permute-done | bytes 163872 | tf_op jit(solution)/shard_map/ppermute | solution.py:32
  27.4 1.6 %collective-permute-done.5.refs_11_.wo2 = bf16[160,1280]{1,0:T(8,128)(2,1)S(1)} collective-permute-done((bf16[160,1280]{1,0:T(8,128)(2,1)}, bf16[160,1280]{1,0:T(8,128)(2,1)S(1)}, u32[]{:S(2)}, u32[]{:S(2)}) %collective-permute-start.5) | collective-permute-done | bytes 409632 | tf_op jit(solution)/shard_map/ppermute | solution.py:40
  29.0 6.4 %collective-permute-start.6 = (bf16[32,1280]{1,0:T(8,128)(2,1)S(1)}, bf16[32,1280]{1,0:T(8,128)(2,1)S(1)}, u32[]{:S(2)}, u32[]{:S(2)}) collective-permute-start(bf16[32,1280]{1,0:T(8,128)(2,1)S(1)} %slice.60), channel_id=1, source_target_pairs={{0,32},{1,225},{32,64},{33,1},{64,96},{65,33},{96,128},{97,65},{12... | collective-permute-start | bytes 245768 | tf_op jit(solution)/shard_map/ppermute | solution.py:32
  35.4 1.5 %collective-permute-done.6 = bf16[32,1280]{1,0:T(8,128)(2,1)S(1)} collective-permute-done((bf16[32,1280]{1,0:T(8,128)(2,1)S(1)}, bf16[32,1280]{1,0:T(8,128)(2,1)S(1)}, u32[]{:S(2)}, u32[]{:S(2)}) %collective-permute-start.6) | collective-permute-done | bytes 81952 | tf_op jit(solution)/shard_map/ppermute | solution.py:32
  36.9 1.8 %collective-permute-start.9 = (bf16[160,1280]{1,0:T(8,128)(2,1)S(1)}, bf16[160,1280]{1,0:T(8,128)(2,1)S(1)}, u32[]{:S(2)}, u32[]{:S(2)}) collective-permute-start(bf16[160,1280]{1,0:T(8,128)(2,1)S(1)} %constant_dynamic-update-slice_fusion.2.refs_0_), channel_id=1, source_target_pairs={{0,1},{1,0},{2,3},{3,2},{4,5},{5,4},{6,7},{7,6},{8,9},{9,8},{10,11... | collective-permute-start | bytes 1228808 | tf_op jit(solution)/shard_map/ppermute | solution.py:27
  38.7 0.1 collective-permute-start.11
  38.8 0.4 collective-permute-start.10
  39.2 3.5 %collective-permute-done.8.refs_3_ = bf16[96,1280]{1,0:T(8,128)(2,1)} collective-permute-done((bf16[96,1280]{1,0:T(8,128)(2,1)S(1)}, bf16[96,1280]{1,0:T(8,128)(2,1)}, u32[]{:S(2)}, u32[]{:S(2)}) %collective-permute-start.8) | collective-permute-done | bytes 245792 | tf_op jit(solution)/shard_map/ppermute | solution.py:36
  42.7 2.6 %collective-permute-start.12 = (bf16[96,1280]{1,0:T(8,128)(2,1)}, bf16[96,1280]{1,0:T(8,128)(2,1)}, u32[]{:S(2)}, u32[]{:S(2)}) collective-permute-start(bf16[96,1280]{1,0:T(8,128)(2,1)} %collective-permute-done.8.refs_3_), channel_id=1, source_target_pairs={{0,1},{1,0},{2,3},{3,2},{4,5},{5,4},{6,7},{7,6},{8,9},{9,8},{10,11... | collective-permute-start | bytes 737288 | tf_op jit(solution)/shard_map/ppermute | solution.py:27
  45.3 0.1 pad_add_fusion.me
  45.4 1.4 %collective-permute-done.12.refs_7_ = bf16[96,1280]{1,0:T(8,128)(2,1)} collective-permute-done((bf16[96,1280]{1,0:T(8,128)(2,1)}, bf16[96,1280]{1,0:T(8,128)(2,1)}, u32[]{:S(2)}, u32[]{:S(2)}) %collective-permute-start.12) | collective-permute-done | bytes 245792 | tf_op jit(solution)/shard_map/ppermute | solution.py:27
  46.8 3.2 %shard_map.75 = (bf16[512,1280]{1,0:T(8,128)(2,1)S(1)}, bf16[512,1280]{1,0:T(8,128)(2,1)S(1)}, f32[2,320,128]{2,1,0:T(8,128)S(1)}, bf16[2,320,128]{2,1,0:T(8,128...) custom-call(s32[2]{0:T(128)S(1)} %pad_add_fusion.me, ...), custom_call_target="tpu_custom_call" | custom-call | flops 838860800 | bytes 1048576 | tf_op jit(solution)/shard_map/pallas_call | solution.py:61
  50.0 1.4 %collective-permute-start.13 = (bf16[2,320,128]{2,1,0:T(8,128)(2,1)S(1)}, bf16[2,320,128]{2,1,0:T(8,128)(2,1)S(1)}, u32[]{:S(2)}, u32[]{:S(2)}) collective-permute-start(bf16[2,320,128]{2,1,0:T(8,128)(2,1)S(1)} %get-tuple-element.32), channel_id=1, source_target_pairs={{0,2},{2,4},{4,6},{6,0},{1,3},{3,5},{5,7},{7,1},{8,10},{10,12},{12... | collective-permute-start | bytes 491528 | tf_op jit(solution)/shard_map/ppermute | solution.py:27
  51.4 2.6 %collective-permute-start.14 = (bf16[2,320,128]{2,1,0:T(8,128)(2,1)S(1)}, bf16[2,320,128]{2,1,0:T(8,128)(2,1)S(1)}, u32[]{:S(2)}, u32[]{:S(2)}) collective-permute-start(bf16[2,320,128]{2,1,0:T(8,128)(2,1)S(1)} %get-tuple-element.33), channel_id=1, source_target_pairs={{0,4},{2,6},{4,0},{6,2},{1,5},{3,7},{5,1},{7,3},{8,12},{10,14},{12... | collective-permute-start | bytes 491528 | tf_op jit(solution)/shard_map/ppermute | solution.py:27
  54.0 1.1 collective-permute-start.15
  55.1 1.8 %collective-permute-done.13.p1 = bf16[2,320,128]{2,1,0:T(8,128)(2,1)S(1)} collective-permute-done((bf16[2,320,128]{2,1,0:T(8,128)(2,1)S(1)}, bf16[2,320,128]{2,1,0:T(8,128)(2,1)S(1)}, u32[]{:S(2)}, u32[]{:S(2)}) %collective-permute-start.13) | collective-permute-done | bytes 163872 | tf_op jit(solution)/shard_map/ppermute | solution.py:27
  56.9 4.6 %collective-permute-done.14.p2 = bf16[2,320,128]{2,1,0:T(8,128)(2,1)S(1)} collective-permute-done((bf16[2,320,128]{2,1,0:T(8,128)(2,1)S(1)}, bf16[2,320,128]{2,1,0:T(8,128)(2,1)S(1)}, u32[]{:S(2)}, u32[]{:S(2)}) %collective-permute-start.14) | collective-permute-done | bytes 163872 | tf_op jit(solution)/shard_map/ppermute | solution.py:27
  61.5 0.7 shard_map.76.b0
  62.2 1.2 collective-permute-start.18
  63.4 2.5 %collective-permute-start.17 = (bf16[2,320,128]{2,1,0:T(8,128)(2,1)S(1)}, bf16[2,320,128]{2,1,0:T(8,128)(2,1)S(1)}, u32[]{:S(2)}, u32[]{:S(2)}) collective-permute-start(bf16[2,320,128]{2,1,0:T(8,128)(2,1)S(1)} %shard_map.76.b0), channel_id=1, source_target_pairs={{0,4},{2,6},{4,0},{6,2},{1,5},{3,7},{5,1},{7,3},{8,12},{10,14},{12... | collective-permute-start | bytes 491528 | tf_op jit(solution)/shard_map/ppermute | solution.py:27
  65.9 0.6 collective-permute-start.16
  66.5 1.6 %collective-permute-done.18.b3 = bf16[2,320,128]{2,1,0:T(8,128)(2,1)S(1)} collective-permute-done((bf16[2,320,128]{2,1,0:T(8,128)(2,1)S(1)}, bf16[2,320,128]{2,1,0:T(8,128)(2,1)S(1)}, u32[]{:S(2)}, u32[]{:S(2)}) %collective-permute-start.18) | collective-permute-done | bytes 163872 | tf_op jit(solution)/shard_map/ppermute | solution.py:27
  68.2 4.7 %collective-permute-done.17.b2 = bf16[2,320,128]{2,1,0:T(8,128)(2,1)S(1)} collective-permute-done((bf16[2,320,128]{2,1,0:T(8,128)(2,1)S(1)}, bf16[2,320,128]{2,1,0:T(8,128)(2,1)S(1)}, u32[]{:S(2)}, u32[]{:S(2)}) %collective-permute-start.17) | collective-permute-done | bytes 163872 | tf_op jit(solution)/shard_map/ppermute | solution.py:27
  72.9 2.6 %shard_map.77 = (f32[256,1280]{1,0:T(8,128)S(1)}, f32[256,1280]{1,0:T(8,128)S(1)}, bf16[320,1280]{1,0:T(8,128)(2,1)S(1)}, bf16[192,1280]{1,0:T(8,128)(2,1)S(1)}, bf16[2,320,512]{2,1,0:T(8,128)(2,1)S(1)}) custom-call(s32[2]{0:T(128)S(1)} %pad_add_fusion.me, bf16[2,320,128]{2,1,0:T(8,128)(2,1)S(1)} %shard_map.76.b0, ...), custom_call_target="tpu_custom_call" | custom-call | flops 838860800 | bytes 1048576 | tf_op jit(solution)/shard_map/pallas_call | solution.py:61
  75.5 1.8 %collective-permute-start.21 = (bf16[192,1280]{1,0:T(8,128)(2,1)S(1)}, bf16[192,1280]{1,0:T(8,128)(2,1)S(1)}, u32[]{:S(2)}, u32[]{:S(2)}) collective-permute-start(bf16[192,1280]{1,0:T(8,128)(2,1)S(1)} %get-tuple-element.38), channel_id=1, source_target_pairs={{0,1},{1,0},{2,3},{3,2},{4,5},{5,4},{6,7},{7,6},{8,9},{9,8},{10,11... | collective-permute-start | bytes 1474568 | tf_op jit(solution)/shard_map/ppermute | solution.py:27
  77.3 1.5 %collective-permute-done.21 = bf16[192,1280]{1,0:T(8,128)(2,1)S(1)} collective-permute-done((bf16[192,1280]{1,0:T(8,128)(2,1)S(1)}, bf16[192,1280]{1,0:T(8,128)(2,1)S(1)}, u32[]{:S(2)}, u32[]{:S(2)}) %collective-permute-start.21) | collective-permute-done | bytes 491552 | tf_op jit(solution)/shard_map/ppermute | solution.py:27
  78.8 0.1 convert_element_type.39
  78.8 0.1 fusion.2
  78.9 0.2 collective-permute-start.22
  79.0 0.7 collective-permute-start.19
  79.7 6.4 %collective-permute-done.22 = bf16[96,1280]{1,0:T(8,128)(2,1)S(1)} collective-permute-done((bf16[96,1280]{1,0:T(8,128)(2,1)S(1)}, bf16[96,1280]{1,0:T(8,128)(2,1)S(1)}, u32[]{:S(2)}, u32[]{:S(2)}) %collective-permute-start.22) | collective-permute-done | bytes 245792 | tf_op jit(solution)/shard_map/ppermute | solution.py:36
  86.1 0.1 fusion.3
  86.2 0.1 convert_element_type.36
  86.4 0.1 fusion
  86.4 3.1 %collective-permute-start.23 = (bf16[32,1280]{1,0:T(8,128)(2,1)S(1)}, bf16[32,1280]{1,0:T(8,128)(2,1)S(1)}, u32[]{:S(2)}, u32[]{:S(2)}) collective-permute-start(bf16[32,1280]{1,0:T(8,128)(2,1)S(1)} %get-tuple-element.39), channel_id=1, source_target_pairs={{0,32},{1,225},{32,64},{33,1},{64,96},{65,33},{96,128},{97,65},{12... | collective-permute-start | bytes 245768 | tf_op jit(solution)/shard_map/ppermute | solution.py:32
  89.6 1.1 shard_map.78
  90.7 2.5 %collective-permute-start.24 = (bf16[160,1280]{1,0:T(8,128)(2,1)S(1)}, bf16[160,1280]{1,0:T(8,128)(2,1)S(1)}, u32[]{:S(2)}, u32[]{:S(2)}) collective-permute-start(bf16[160,1280]{1,0:T(8,128)(2,1)S(1)} %get-tuple-element.44), channel_id=1, source_target_pairs={{0,24},{24,0},{8,16},{16,8},{1,25},{25,1},{9,17},{17,9},{2,26},{26... | collective-permute-start | bytes 1228808 | tf_op jit(solution)/shard_map/ppermute | solution.py:40
  93.2 0.3 collective-permute-start.26
  93.5 10.0 %collective-permute-done.24.other = bf16[160,1280]{1,0:T(8,128)(2,1)S(1)} collective-permute-done((bf16[160,1280]{1,0:T(8,128)(2,1)S(1)}, bf16[160,1280]{1,0:T(8,128)(2,1)S(1)}, u32[]{:S(2)}, u32[]{:S(2)}) %collective-permute-start.24) | collective-permute-done | bytes 409632 | tf_op jit(solution)/shard_map/ppermute | solution.py:40
  103.6 0.6 collective-permute-done.20
  104.1 0.1 fusion.1
  104.3 3.8 %collective-permute-done.25 = bf16[64,1280]{1,0:T(8,128)(2,1)S(1)} collective-permute-done((bf16[64,1280]{1,0:T(8,128)(2,1)S(1)}, bf16[64,1280]{1,0:T(8,128)(2,1)S(1)}, u32[]{:S(2)}, u32[]{:S(2)}) %collective-permute-start.25) | collective-permute-done | bytes 163872 | tf_op jit(solution)/shard_map/ppermute | solution.py:32
  108.1 2.5 %collective-permute-done.26.other = bf16[160,1280]{1,0:T(8,128)(2,1)S(1)} collective-permute-done((bf16[160,1280]{1,0:T(8,128)(2,1)S(1)}, bf16[160,1280]{1,0:T(8,128)(2,1)S(1)}, u32[]{:S(2)}, u32[]{:S(2)}) %collective-permute-start.26) | collective-permute-done | bytes 409632 | tf_op jit(solution)/shard_map/ppermute | solution.py:40
  110.6 1.8 %shard_map.79 = f32[160,1280]{1,0:T(8,128)} custom-call(s32[2]{0:T(128)S(1)} %pad_add_fusion.me, bf16[2,320,512]{2,1,0:T(8,128)(2,1)S(1)} %get-tuple-element.41.full, bf16[512,1280]{1,0:T(8,128)(2,1)S(1)} %get-tuple-element.43.cot.value, bf16[160,1280]{1,0:T(8,128)(2,1)S(1)} %collective-permute-done.24.other), custom_call_target="tpu_custom_call" | custom-call | flops 419430400 | bytes 1048576 | tf_op jit(solution)/shard_map/pallas_call | solution.py:61
  112.4 2.6 %collective-permute-done.27 = bf16[64,1280]{1,0:T(8,128)(2,1)S(1)} collective-permute-done((bf16[64,1280]{1,0:T(8,128)(2,1)S(1)}, bf16[64,1280]{1,0:T(8,128)(2,1)S(1)}, u32[]{:S(2)}, u32[]{:S(2)}) %collective-permute-start.27) | collective-permute-done | bytes 163872 | tf_op jit(solution)/shard_map/ppermute | solution.py:32
  115.1 1.0 collective-permute-start.28
  116.1 1.8 %shard_map.80 = f32[160,1280]{1,0:T(8,128)} custom-call(s32[2]{0:T(128)S(1)} %pad_add_fusion.me, bf16[2,320,512]{2,1,0:T(8,128)(2,1)S(1)} %get-tuple-element.41.full, bf16[512,1280]{1,0:T(8,128)(2,1)S(1)} %get-tuple-element.42.tok.value, bf16[160,1280]{1,0:T(8,128)(2,1)S(1)} %collective-permute-done.26.other), custom_call_target="tpu_custom_call" | custom-call | flops 419430400 | bytes 1048576 | tf_op jit(solution)/shard_map/pallas_call | solution.py:61
  117.9 3.5 %collective-permute-done.28 = f32[64,1280]{1,0:T(8,128)S(1)} collective-permute-done((f32[64,1280]{1,0:T(8,128)S(1)}, f32[64,1280]{1,0:T(8,128)S(1)}, u32[]{:S(2)}, u32[]{:S(2)}) %collective-permute-start.28) | collective-permute-done | bytes 327712 | tf_op jit(solution)/shard_map/ppermute | solution.py:32
  121.4 3.5 %collective-permute-start.29 = (f32[32,1280]{1,0:T(8,128)S(1)}, f32[32,1280]{1,0:T(8,128)S(1)}, u32[]{:S(2)}, u32[]{:S(2)}) collective-permute-start(f32[32,1280]{1,0:T(8,128)S(1)} %slice.90), channel_id=1, source_target_pairs={{0,1},{1,0},{2,3},{3,2},{4,5},{5,4},{6,7},{7,6},{8,9},{9,8},{10,11... | collective-permute-start | bytes 491528 | tf_op jit(solution)/shard_map/ppermute | solution.py:27
  124.9 1.0 collective-permute-done.29
  125.9 0.6 fusion.9
  (29 shorter events, 0.2 us)
Async XLA Ops:
  0.6 46.2 %copy-start = (bf16[1280,160]{0,1:T(8,128)(2,1)S(1)}, bf16[1280,160]{0,1:T(8,128)(2,1)}, u32[]{:S(2)}) copy-start(bf16[1280,160]{0,1:T(8,128)(2,1)} %param.5) | copy-start | bytes 1228804
  0.6 46.2 %copy-start.1 = (bf16[160,1280]{1,0:T(8,128)(2,1)S(1)}, bf16[160,1280]{1,0:T(8,128)(2,1)}, u32[]{:S(2)}) copy-start(bf16[160,1280]{1,0:T(8,128)(2,1)} %wo.1) | copy-start | bytes 1228804
  2.3 4.2 %collective-permute-start = (bf16[32,1280]{1,0:T(8,128)(2,1)S(1)}, bf16[32,1280]{1,0:T(8,128)(2,1)S(1)}, u32[]{:S(2)}, u32[]{:S(2)}) collective-permute-start(bf16[32,1280]{1,0:T(8,128)(2,1)S(1)} %get-tuple-element.54), channel_id=1, source_target_pairs={{0,1},{1,0},{2,3},{3,2},{4,5},{5,4},{6,7},{7,6},{8,9},{9,8},{10,11... | collective-permute-start | bytes 245768 | tf_op jit(solution)/shard_map/ppermute | solution.py:27
  7.3 6.4 %collective-permute-start.1 = (bf16[64,1280]{1,0:T(8,128)(2,1)S(1)}, bf16[64,1280]{1,0:T(8,128)(2,1)S(1)}, u32[]{:S(2)}, u32[]{:S(2)}) collective-permute-start(bf16[64,1280]{1,0:T(8,128)(2,1)S(1)} %pad_maximum_fusion), channel_id=1, source_target_pairs={{0,32},{1,225},{32,64},{33,1},{64,96},{65,33},{96,128},{97,65},{12... | collective-permute-start | bytes 491528 | tf_op jit(solution)/shard_map/ppermute | solution.py:32
  11.2 10.4 %collective-permute-start.3 = (bf16[160,1280]{1,0:T(8,128)(2,1)}, bf16[160,1280]{1,0:T(8,128)(2,1)S(1)}, u32[]{:S(2)}, u32[]{:S(2)}) collective-permute-start(bf16[160,1280]{1,0:T(8,128)(2,1)} %bitcast.4), channel_id=1, source_target_pairs={{0,24},{24,0},{8,16},{16,8},{1,25},{25,1},{9,17},{17,9},{2,26},{26... | collective-permute-start | bytes 1228808 | tf_op jit(solution)/shard_map/ppermute | solution.py:40
  13.7 5.5 %collective-permute-start.2 = (bf16[64,1280]{1,0:T(8,128)(2,1)S(1)}, bf16[64,1280]{1,0:T(8,128)(2,1)S(1)}, u32[]{:S(2)}, u32[]{:S(2)}) collective-permute-start(bf16[64,1280]{1,0:T(8,128)(2,1)S(1)} %collective-permute-done.1), channel_id=1, source_target_pairs={{0,32},{1,225},{32,64},{33,1},{64,96},{65,33},{96,128},{97,65},{12... | collective-permute-start | bytes 491528 | tf_op jit(solution)/shard_map/ppermute | solution.py:32
  19.1 9.9 %collective-permute-start.5 = (bf16[160,1280]{1,0:T(8,128)(2,1)}, bf16[160,1280]{1,0:T(8,128)(2,1)S(1)}, u32[]{:S(2)}, u32[]{:S(2)}) collective-permute-start(bf16[160,1280]{1,0:T(8,128)(2,1)} %wo.1), channel_id=1, source_target_pairs={{0,24},{24,0},{8,16},{16,8},{1,25},{25,1},{9,17},{17,9},{2,26},{26... | collective-permute-start | bytes 1228808 | tf_op jit(solution)/shard_map/ppermute | solution.py:40
  21.6 5.8 %collective-permute-start.4 = (bf16[64,1280]{1,0:T(8,128)(2,1)S(1)}, bf16[64,1280]{1,0:T(8,128)(2,1)S(1)}, u32[]{:S(2)}, u32[]{:S(2)}) collective-permute-start(bf16[64,1280]{1,0:T(8,128)(2,1)S(1)} %collective-permute-done.2), channel_id=1, source_target_pairs={{0,32},{1,225},{32,64},{33,1},{64,96},{65,33},{96,128},{97,65},{12... | collective-permute-start | bytes 491528 | tf_op jit(solution)/shard_map/ppermute | solution.py:32
  25.1 13.5 %collective-permute-start.7 = (bf16[160,1280]{1,0:T(8,128)(2,1)S(1)}, bf16[160,1280]{1,0:T(8,128)(2,1)S(1)}, u32[]{:S(2)}, u32[]{:S(2)}) collective-permute-start(bf16[160,1280]{1,0:T(8,128)(2,1)S(1)} %constant_dynamic-update-slice_fusion.2.refs_0_), channel_id=1, source_target_pairs={{0,8},{8,0},{16,24},{24,16},{1,9},{9,1},{17,25},{25,17},{2,10},{10... | collective-permute-start | bytes 1228808 | tf_op jit(solution)/shard_map/ppermute | solution.py:36
  29.0 7.8 %collective-permute-start.6 = (bf16[32,1280]{1,0:T(8,128)(2,1)S(1)}, bf16[32,1280]{1,0:T(8,128)(2,1)S(1)}, u32[]{:S(2)}, u32[]{:S(2)}) collective-permute-start(bf16[32,1280]{1,0:T(8,128)(2,1)S(1)} %slice.60), channel_id=1, source_target_pairs={{0,32},{1,225},{32,64},{33,1},{64,96},{65,33},{96,128},{97,65},{12... | collective-permute-start | bytes 245768 | tf_op jit(solution)/shard_map/ppermute | solution.py:32
  36.8 5.8 %collective-permute-start.8 = (bf16[96,1280]{1,0:T(8,128)(2,1)S(1)}, bf16[96,1280]{1,0:T(8,128)(2,1)}, u32[]{:S(2)}, u32[]{:S(2)}) collective-permute-start(bf16[96,1280]{1,0:T(8,128)(2,1)S(1)} %constant_dynamic-update-slice_fusion.6.refs_1_), channel_id=1, source_target_pairs={{0,8},{8,0},{16,24},{24,16},{1,9},{9,1},{17,25},{25,17},{2,10},{10... | collective-permute-start | bytes 737288 | tf_op jit(solution)/shard_map/ppermute | solution.py:36
  36.9 8.5 %collective-permute-start.9 = (bf16[160,1280]{1,0:T(8,128)(2,1)S(1)}, bf16[160,1280]{1,0:T(8,128)(2,1)S(1)}, u32[]{:S(2)}, u32[]{:S(2)}) collective-permute-start(bf16[160,1280]{1,0:T(8,128)(2,1)S(1)} %constant_dynamic-update-slice_fusion.2.refs_0_), channel_id=1, source_target_pairs={{0,1},{1,0},{2,3},{3,2},{4,5},{5,4},{6,7},{7,6},{8,9},{9,8},{10,11... | collective-permute-start | bytes 1228808 | tf_op jit(solution)/shard_map/ppermute | solution.py:27
  38.7 6.7 %collective-permute-start.11 = (bf16[160,1280]{1,0:T(8,128)(2,1)S(1)}, bf16[160,1280]{1,0:T(8,128)(2,1)S(1)}, u32[]{:S(2)}, u32[]{:S(2)}) collective-permute-start(bf16[160,1280]{1,0:T(8,128)(2,1)S(1)} %collective-permute-done.7.refs_2_), channel_id=1, source_target_pairs={{0,1},{1,0},{2,3},{3,2},{4,5},{5,4},{6,7},{7,6},{8,9},{9,8},{10,11... | collective-permute-start | bytes 1228808 | tf_op jit(solution)/shard_map/ppermute | solution.py:27
  38.8 6.6 %collective-permute-start.10 = (bf16[96,1280]{1,0:T(8,128)(2,1)S(1)}, bf16[96,1280]{1,0:T(8,128)(2,1)}, u32[]{:S(2)}, u32[]{:S(2)}) collective-permute-start(bf16[96,1280]{1,0:T(8,128)(2,1)S(1)} %constant_dynamic-update-slice_fusion.6.refs_1_), channel_id=1, source_target_pairs={{0,1},{1,0},{2,3},{3,2},{4,5},{5,4},{6,7},{7,6},{8,9},{9,8},{10,11... | collective-permute-start | bytes 737288 | tf_op jit(solution)/shard_map/ppermute | solution.py:27
  42.7 4.1 %collective-permute-start.12 = (bf16[96,1280]{1,0:T(8,128)(2,1)}, bf16[96,1280]{1,0:T(8,128)(2,1)}, u32[]{:S(2)}, u32[]{:S(2)}) collective-permute-start(bf16[96,1280]{1,0:T(8,128)(2,1)} %collective-permute-done.8.refs_3_), channel_id=1, source_target_pairs={{0,1},{1,0},{2,3},{3,2},{4,5},{5,4},{6,7},{7,6},{8,9},{9,8},{10,11... | collective-permute-start | bytes 737288 | tf_op jit(solution)/shard_map/ppermute | solution.py:27
  50.0 6.8 %collective-permute-start.13 = (bf16[2,320,128]{2,1,0:T(8,128)(2,1)S(1)}, bf16[2,320,128]{2,1,0:T(8,128)(2,1)S(1)}, u32[]{:S(2)}, u32[]{:S(2)}) collective-permute-start(bf16[2,320,128]{2,1,0:T(8,128)(2,1)S(1)} %get-tuple-element.32), channel_id=1, source_target_pairs={{0,2},{2,4},{4,6},{6,0},{1,3},{3,5},{5,7},{7,1},{8,10},{10,12},{12... | collective-permute-start | bytes 491528 | tf_op jit(solution)/shard_map/ppermute | solution.py:27
  51.4 10.1 %collective-permute-start.14 = (bf16[2,320,128]{2,1,0:T(8,128)(2,1)S(1)}, bf16[2,320,128]{2,1,0:T(8,128)(2,1)S(1)}, u32[]{:S(2)}, u32[]{:S(2)}) collective-permute-start(bf16[2,320,128]{2,1,0:T(8,128)(2,1)S(1)} %get-tuple-element.33), channel_id=1, source_target_pairs={{0,4},{2,6},{4,0},{6,2},{1,5},{3,7},{5,1},{7,3},{8,12},{10,14},{12... | collective-permute-start | bytes 491528 | tf_op jit(solution)/shard_map/ppermute | solution.py:27
  54.0 7.5 %collective-permute-start.15 = (bf16[2,320,128]{2,1,0:T(8,128)(2,1)S(1)}, bf16[2,320,128]{2,1,0:T(8,128)(2,1)S(1)}, u32[]{:S(2)}, u32[]{:S(2)}) collective-permute-start(bf16[2,320,128]{2,1,0:T(8,128)(2,1)S(1)} %get-tuple-element.34), channel_id=1, source_target_pairs={{0,6},{2,0},{4,2},{6,4},{1,7},{3,1},{5,3},{7,5},{8,14},{10,8},{12,... | collective-permute-start | bytes 491528 | tf_op jit(solution)/shard_map/ppermute | solution.py:27
  62.2 6.0 %collective-permute-start.18 = (bf16[2,320,128]{2,1,0:T(8,128)(2,1)S(1)}, bf16[2,320,128]{2,1,0:T(8,128)(2,1)S(1)}, u32[]{:S(2)}, u32[]{:S(2)}) collective-permute-start(bf16[2,320,128]{2,1,0:T(8,128)(2,1)S(1)} %shard_map.76.b0), channel_id=1, source_target_pairs={{0,2},{2,4},{4,6},{6,0},{1,3},{3,5},{5,7},{7,1},{8,10},{10,12},{12... | collective-permute-start | bytes 491528 | tf_op jit(solution)/shard_map/ppermute | solution.py:27
  63.4 9.5 %collective-permute-start.17 = (bf16[2,320,128]{2,1,0:T(8,128)(2,1)S(1)}, bf16[2,320,128]{2,1,0:T(8,128)(2,1)S(1)}, u32[]{:S(2)}, u32[]{:S(2)}) collective-permute-start(bf16[2,320,128]{2,1,0:T(8,128)(2,1)S(1)} %shard_map.76.b0), channel_id=1, source_target_pairs={{0,4},{2,6},{4,0},{6,2},{1,5},{3,7},{5,1},{7,3},{8,12},{10,14},{12... | collective-permute-start | bytes 491528 | tf_op jit(solution)/shard_map/ppermute | solution.py:27
  65.9 7.0 %collective-permute-start.16 = (bf16[2,320,128]{2,1,0:T(8,128)(2,1)S(1)}, bf16[2,320,128]{2,1,0:T(8,128)(2,1)S(1)}, u32[]{:S(2)}, u32[]{:S(2)}) collective-permute-start(bf16[2,320,128]{2,1,0:T(8,128)(2,1)S(1)} %shard_map.76.b0), channel_id=1, source_target_pairs={{0,6},{2,0},{4,2},{6,4},{1,7},{3,1},{5,3},{7,5},{8,14},{10,8},{12,... | collective-permute-start | bytes 491528 | tf_op jit(solution)/shard_map/ppermute | solution.py:27
  75.5 3.3 %collective-permute-start.21 = (bf16[192,1280]{1,0:T(8,128)(2,1)S(1)}, bf16[192,1280]{1,0:T(8,128)(2,1)S(1)}, u32[]{:S(2)}, u32[]{:S(2)}) collective-permute-start(bf16[192,1280]{1,0:T(8,128)(2,1)S(1)} %get-tuple-element.38), channel_id=1, source_target_pairs={{0,1},{1,0},{2,3},{3,2},{4,5},{5,4},{6,7},{7,6},{8,9},{9,8},{10,11... | collective-permute-start | bytes 1474568 | tf_op jit(solution)/shard_map/ppermute | solution.py:27
  78.9 7.3 %collective-permute-start.22 = (bf16[96,1280]{1,0:T(8,128)(2,1)S(1)}, bf16[96,1280]{1,0:T(8,128)(2,1)S(1)}, u32[]{:S(2)}, u32[]{:S(2)}) collective-permute-start(bf16[96,1280]{1,0:T(8,128)(2,1)S(1)} %fusion.2), channel_id=1, source_target_pairs={{0,8},{8,0},{16,24},{24,16},{1,9},{9,1},{17,25},{25,17},{2,10},{10... | collective-permute-start | bytes 737288 | tf_op jit(solution)/shard_map/ppermute | solution.py:36
  79.0 7.2 %collective-permute-start.19 = (bf16[320,1280]{1,0:T(8,128)(2,1)S(1)}, bf16[320,1280]{1,0:T(8,128)(2,1)S(1)}, u32[]{:S(2)}, u32[]{:S(2)}) collective-permute-start(bf16[320,1280]{1,0:T(8,128)(2,1)S(1)} %get-tuple-element.36), channel_id=1, source_target_pairs={{0,1},{1,0},{2,3},{3,2},{4,5},{5,4},{6,7},{7,6},{8,9},{9,8},{10,11... | collective-permute-start | bytes 2457608 | tf_op jit(solution)/shard_map/ppermute | solution.py:27
  86.4 7.1 %collective-permute-start.23 = (bf16[32,1280]{1,0:T(8,128)(2,1)S(1)}, bf16[32,1280]{1,0:T(8,128)(2,1)S(1)}, u32[]{:S(2)}, u32[]{:S(2)}) collective-permute-start(bf16[32,1280]{1,0:T(8,128)(2,1)S(1)} %get-tuple-element.39), channel_id=1, source_target_pairs={{0,32},{1,225},{32,64},{33,1},{64,96},{65,33},{96,128},{97,65},{12... | collective-permute-start | bytes 245768 | tf_op jit(solution)/shard_map/ppermute | solution.py:32
  90.7 12.8 %collective-permute-start.24 = (bf16[160,1280]{1,0:T(8,128)(2,1)S(1)}, bf16[160,1280]{1,0:T(8,128)(2,1)S(1)}, u32[]{:S(2)}, u32[]{:S(2)}) collective-permute-start(bf16[160,1280]{1,0:T(8,128)(2,1)S(1)} %get-tuple-element.44), channel_id=1, source_target_pairs={{0,24},{24,0},{8,16},{16,8},{1,25},{25,1},{9,17},{17,9},{2,26},{26... | collective-permute-start | bytes 1228808 | tf_op jit(solution)/shard_map/ppermute | solution.py:40
  93.2 17.4 %collective-permute-start.26 = (bf16[160,1280]{1,0:T(8,128)(2,1)S(1)}, bf16[160,1280]{1,0:T(8,128)(2,1)S(1)}, u32[]{:S(2)}, u32[]{:S(2)}) collective-permute-start(bf16[160,1280]{1,0:T(8,128)(2,1)S(1)} %get-tuple-element.46), channel_id=1, source_target_pairs={{0,24},{24,0},{8,16},{16,8},{1,25},{25,1},{9,17},{17,9},{2,26},{26... | collective-permute-start | bytes 1228808 | tf_op jit(solution)/shard_map/ppermute | solution.py:40
  93.5 10.7 %collective-permute-start.20 = (bf16[160,1280]{1,0:T(8,128)(2,1)S(1)}, bf16[160,1280]{1,0:T(8,128)(2,1)S(1)}, u32[]{:S(2)}, u32[]{:S(2)}) collective-permute-start(bf16[160,1280]{1,0:T(8,128)(2,1)S(1)} %fusion), channel_id=1, source_target_pairs={{0,8},{8,0},{16,24},{24,16},{1,9},{9,1},{17,25},{25,17},{2,10},{10... | collective-permute-start | bytes 1228808 | tf_op jit(solution)/shard_map/ppermute | solution.py:36
  103.6 4.5 %collective-permute-start.25 = (bf16[64,1280]{1,0:T(8,128)(2,1)S(1)}, bf16[64,1280]{1,0:T(8,128)(2,1)S(1)}, u32[]{:S(2)}, u32[]{:S(2)}) collective-permute-start(bf16[64,1280]{1,0:T(8,128)(2,1)S(1)} %pad_maximum_fusion.1), channel_id=1, source_target_pairs={{0,32},{1,225},{32,64},{33,1},{64,96},{65,33},{96,128},{97,65},{12... | collective-permute-start | bytes 491528 | tf_op jit(solution)/shard_map/ppermute | solution.py:32
  110.6 4.5 %collective-permute-start.27 = (bf16[64,1280]{1,0:T(8,128)(2,1)S(1)}, bf16[64,1280]{1,0:T(8,128)(2,1)S(1)}, u32[]{:S(2)}, u32[]{:S(2)}) collective-permute-start(bf16[64,1280]{1,0:T(8,128)(2,1)S(1)} %fusion.4), channel_id=1, source_target_pairs={{0,32},{1,225},{32,64},{33,1},{64,96},{65,33},{96,128},{97,65},{12... | collective-permute-start | bytes 491528 | tf_op jit(solution)/shard_map/ppermute | solution.py:32
  115.1 6.3 %collective-permute-start.28 = (f32[64,1280]{1,0:T(8,128)S(1)}, f32[64,1280]{1,0:T(8,128)S(1)}, u32[]{:S(2)}, u32[]{:S(2)}) collective-permute-start(f32[64,1280]{1,0:T(8,128)S(1)} %slice_add_fusion.5), channel_id=1, source_target_pairs={{0,32},{1,225},{32,64},{33,1},{64,96},{65,33},{96,128},{97,65},{12... | collective-permute-start | bytes 983048 | tf_op jit(solution)/shard_map/ppermute | solution.py:32
  121.4 4.5 %collective-permute-start.29 = (f32[32,1280]{1,0:T(8,128)S(1)}, f32[32,1280]{1,0:T(8,128)S(1)}, u32[]{:S(2)}, u32[]{:S(2)}) collective-permute-start(f32[32,1280]{1,0:T(8,128)S(1)} %slice.90), channel_id=1, source_target_pairs={{0,1},{1,0},{2,3},{3,2},{4,5},{5,4},{6,7},{7,6},{8,9},{9,8},{10,11... | collective-permute-start | bytes 491528 | tf_op jit(solution)/shard_map/ppermute | solution.py:27

commit v5 on v3

--- a/solution.py
+++ b/solution.py
@@ -1,5 +1,3 @@
-import functools
-
 import jax
 import jax.numpy as jnp
 from jax import lax
@@ -96,11 +94,9 @@
     out[1] = (grad_act * smooth_slope(pre)).astype(BF)
 
 
-def down_kernel(me, b0, b1, b2, b3, wi, wi2, wo, wo2, near, far, head, tail, full):
+def down_kernel(me, full, wi, wi2, wo, wo2, near, far, head, tail):
+    del me
     h = wi.shape[0]
-    for k, block in enumerate((b0, b1, b2, b3)):
-        lane = pl.multiple_of(((me[0] + k) % 4) * 128, 128)
-        full[:, :, pl.ds(lane, 128)] = block[...]
     for s, (w, w2) in enumerate(((wo, wo2), (wi, wi2))):
         value = dot(full[s, :h], w[...], 0, 0) + dot(full[s, h:], w2[...], 0, 0)
         for q in range(4):
@@ -117,17 +113,20 @@
                     tail[row : row + 16] = piece.astype(BF)
 
 
-def pair_kernel(me, full, tok, cot, out, back):
+def pair_kernel(me, b0, b1, b2, b3, tok, cot, full, out, back):
+    h = full.shape[1] // 2
+    for k, block in enumerate((b0, b1, b2, b3)):
+        lane = pl.multiple_of(((me[0] + k) % 4) * 128, 128)
+        full[:, :, pl.ds(lane, 128)] = block[...]
+    out[...] = dot(full[0, h:], cot[...], 1, 0).astype(BF)
+    back[...] = dot(full[1, h:], tok[...], 1, 0).astype(BF)
+
+
+def own_kernel(me, full, tok, cot, grad_out, grad_in):
     del me
     h = full.shape[1] // 2
-    out[...] = dot(full[0, h:], cot[...], 1, 0).astype(BF)
-    back[...] = dot(full[1, h:], tok[...], 1, 0).astype(BF)
-
-
-def own_kernel(s, me, full, value, other, grad):
-    del me
-    h = full.shape[1] // 2
-    grad[...] = dot(full[s, :h], value[...], 1, 0) + other[...].astype(F32)
+    grad_out[...] = dot(full[0, :h], cot[...], 1, 0)
+    grad_in[...] = dot(full[1, :h], tok[...], 1, 0)
 
 
 def on_device(tokens, w_in, w_out, cotangent):
@@ -136,20 +135,20 @@
     shape = jax.ShapeDtypeStruct
     flops = 2 * 1024 * d * h
 
-    z = {0: cat([tokens, cotangent])}
-    z[1], z[7] = send(z[0], "z", -1), send(z[0], "z", 1)
+    base = cat([tokens, cotangent])
+    z = {0: base}
+    z[2], z[6] = send(base, "z", -2), send(base, "z", 2)
+    z[1], z[7] = send(base, "z", -1), send(base, "z", 1)
     w_in_t = w_in.T
-    w_in_2 = weight_pair(after(w_in_t, z[0]))
-    z[2], z[6] = send(z[1], "z", -1), send(z[7], "z", 1)
+    w_in_2 = weight_pair(after(w_in_t, base))
+    z[3], z[5] = send(z[2], "z", -1), send(z[6], "z", 1)
+    z[4] = cat([send(z[2][:16], "z", -2), send(z[6][16:], "z", 2)])
+    w_out_2 = weight_pair(after(w_out, (z[2], z[6])))
     near_h = cat([z[k] for k in ORDER[:HEAD]])
-    ring = after((z[2], z[6]), w_in_2)
-    w_out_2 = weight_pair(after(w_out, z[2]))
     far_h = token_pair(near_h)
-    z[3], z[5] = send(ring[0], "z", -1), send(ring[1], "z", 1)
-    ring = after((z[3], z[5]), w_out_2)
-    z[4] = cat([send(ring[0][:16], "z", -1), send(ring[1][16:], "z", 1)])
     near_t = cat([z[k] for k in ORDER[HEAD:]])
-    far_t = token_pair(near_t)
+    far_t = token_pair(after(near_t, w_in_2))
+    far_h = after(far_h, w_out_2)
     quarters = [near_h, near_t, far_h, far_t]
     quarters += [send(value, "col", 1) for value in quarters]
 
@@ -166,44 +165,49 @@
     blocks = [block] + [send(block, "row", -k) for k in (1, 2, 3)]
 
     sums = shape((256, d), F32)
-    near, far, head, tail, full = call(
+    full, pair_out, pair_in = call(
+        pair_kernel,
+        [shape((2, 2 * h, 512), BF)] + [shape((h, d), BF)] * 2,
+        [me, *blocks, tok, cot],
+        flops,
+    )
+    near, far, head, tail = call(
         down_kernel,
-        [sums, sums, shape((HEAD * 64, d), BF), shape(((8 - HEAD) * 64, d), BF), shape((2, 2 * h, 512), BF)],
-        [me, *blocks, w_in_t, w_in_2, w_out, w_out_2],
+        [sums, sums, shape((HEAD * 64, d), BF), shape(((8 - HEAD) * 64, d), BF)],
+        [me, full, w_in_t, w_in_2, w_out, w_out_2],
         2 * flops,
     )
     cut, rest = HEAD * 32, (8 - HEAD) * 32
     tail = send(tail, "col", 1).astype(F32)
-    far_t = token_pair((far[cut:] + tail[:rest]).astype(BF)).astype(F32)
-    near_t = near[cut:] + tail[rest:] + far_t
     head = send(head, "col", 1).astype(F32)
-    far_h = (far[:cut] + head[:cut]).astype(BF)
-    first = after(near_t[-32:], far_h)
-    far_h = token_pair(far_h).astype(F32)
-    near_h = near[:cut] + head[cut:] + far_h
-    piece = {}
-    for i, k in enumerate(ORDER):
-        piece[k] = near_h[i * 32 : i * 32 + 32] if i < HEAD else near_t[(i - HEAD) * 32 : (i - HEAD) * 32 + 32]
-    pair_out, pair_in = call(
-        pair_kernel, [shape((h, d), BF)] * 2, [me, after(full, tail), tok, cot], flops
-    )
+    far_t = (far[cut:] + tail[:rest]).astype(BF)
+    far_2 = (far[96:cut] + head[96:cut]).astype(BF)
+    far_1 = (far[:96] + head[:96]).astype(BF)
+    pair_out, pair_in = after((pair_out, pair_in), far_t)
     pair_out, pair_in = weight_pair(pair_out), weight_pair(pair_in)
-    up = send(first[:16].astype(BF), "z", 1).astype(F32)
-    down = send(first[16:].astype(BF), "z", -1).astype(F32)
-    up = cat([up + piece[3][:16], piece[3][16:]]).astype(BF)
-    down = cat([piece[5][:16], down + piece[5][16:]]).astype(BF)
-    up, down = after((up, down), pair_out)
-    up, down = send(up, "z", 1).astype(F32), send(down, "z", -1).astype(F32)
-    up, down = (up + piece[2]).astype(BF), (down + piece[6]).astype(BF)
-    up, down = after((up, down), pair_in)
-    up, down = send(up, "z", 1).astype(F32), send(down, "z", -1).astype(F32)
-    weight = [shape((h, d), F32)]
-    (grad_out,) = call(functools.partial(own_kernel, 0), weight, [me, full, cot, pair_out], flops)
-    (grad_in_t,) = call(functools.partial(own_kernel, 1), weight, [me, full, tok, pair_in], flops)
-    up, down = after((up + piece[1], down + piece[7]), grad_out)
-    up, down = send(up, "z", 1), send(down, "z", -1)
-    total = (piece[0] + up + down).astype(BF)
-    output, input_grad = total[:16], total[16:]
+    grad_out, grad_in_t = call(
+        own_kernel, [shape((h, d), F32)] * 2, [me, full, after(tok, far_t), cot], flops
+    )
+    far_t, far_2 = token_pair(far_t), token_pair(after(far_2, grad_out))
+    third = (near[cut:] + tail[rest:] + far_t.astype(F32)).astype(BF)
+    near, head = after((near, head), third)
+    far_1 = token_pair(after(far_1, third))
+    near_2 = near[96:cut] + head[96 + cut :] + far_2.astype(F32)
+    third = after(third, grad_out)
+    up, down = send(third[:32], "z", 1), send(third[32:64], "z", -1)
+    up_2, down_2 = send(third[64:80], "z", 2), send(third[80:], "z", -2)
+    up, down = up.astype(F32), down.astype(F32)
+    up = cat([up[:16] + up_2.astype(F32), up[16:]]) + near_2[:32]
+    down = cat([down[:16], down[16:] + down_2.astype(F32)]) + near_2[32:]
+    up, down = after((up.astype(BF), down.astype(BF)), pair_out)
+    near, head = after((near, head), up)
+    near_1 = near[:96] + head[cut : 96 + cut] + far_1.astype(F32)
+    total = near_1[:32] + send(up, "z", 2).astype(F32) + send(down, "z", -2).astype(F32)
+    up, down = after((near_1[32:64].astype(BF), near_1[64:].astype(BF)), (up, down))
+    total += send(up, "z", 1).astype(F32) + send(down, "z", -1).astype(F32)
+    output, input_grad = total[:16].astype(BF), total[16:].astype(BF)
+    grad_out = grad_out + pair_out.astype(F32)
+    grad_in_t = grad_in_t + pair_in.astype(F32)
     return (output, input_grad, grad_in_t.T, grad_out)
 
 

time: 111 us -> 105 us (0.946)
  waiting for transfers between devices: 48.3 us -> 37.9 us
  starting transfers between devices: 49.6 us -> 53.4 us
  Pallas kernels: 8.13 us -> 6.14 us
  other arithmetic: 0.59 us -> 2.53 us
    ppermute x4 -> x5, waiting for transfers between devices: 10.4 us -> 3.9 us  [token_pair(): return lax.ppermute(value, 'x', [(0, 1), (1, 0), (2, 3), (3, 2)])]
    ppermute x4 -> x5, starting transfers between devices: 5.75 us -> 8.23 us  [token_pair(): return lax.ppermute(value, 'x', [(0, 1), (1, 0), (2, 3), (3, 2)])]
    ppermute x28, waiting for transfers between devices: 31.6 us -> 29.3 us  [send(): lax.ppermute(value, axis, [(i, (i + shift) % size) for i in range(size)])]
    pallas_call x6 -> x5, Pallas kernels: 8.13 us -> 6.14 us  [call(): return list(kernel(*args))]
    ppermute x4, waiting for transfers between devices: 6.27 us -> 4.73 us  [weight_pair(): return lax.ppermute(value, 'x', [(0, 3), (3, 0), (1, 2), (2, 1)])]
    ppermute x28, starting transfers between devices: 38.5 us -> 40.1 us  [send(): lax.ppermute(value, axis, [(i, (i + shift) % size) for i in range(size)])]
  transfers between devices with their start and end apart: 36 -> 37, of which waited for: 22 -> 17; matrix products, arithmetic and copies ran while one was open for 1% -> 2% of each run, Pallas kernels for 3% -> 1%
where the time goes in v5:
time: 105 us; the launch traced here: 103 us
  starting transfers between devices  53.4 us (51%)
  waiting for transfers between devices  37.9 us (36%)
  Pallas kernels  6.14 us (6%)
  other arithmetic  2.53 us (2%)
  local copies, waits for them, and re-layouts  2.4 us (2%)
    ppermute x28, starting transfers between devices, send(): lax.ppermute(value, axis, [(i, (i + shift) % size) for i in range(size)])  40.1 us
    ppermute x28, waiting for transfers between devices, send(): lax.ppermute(value, axis, [(i, (i + shift) % size) for i in range(size)])  29.3 us
    ppermute x5, starting transfers between devices, token_pair(): return lax.ppermute(value, 'x', [(0, 1), (1, 0), (2, 3), (3, 2)])  8.23 us
    pallas_call x5, Pallas kernels, call(): return list(kernel(*args))  6.14 us
    ppermute x4, starting transfers between devices, weight_pair(): return lax.ppermute(value, 'x', [(0, 3), (3, 0), (1, 2), (2, 1)])  5.09 us
    ppermute x4, waiting for transfers between devices, weight_pair(): return lax.ppermute(value, 'x', [(0, 3), (3, 0), (1, 2), (2, 1)])  4.73 us
    ppermute x5, waiting for transfers between devices, token_pair(): return lax.ppermute(value, 'x', [(0, 1), (1, 0), (2, 3), (3, 2)])  3.9 us
  transfers between devices with their start and end apart: 37, of which 17 were waited for; matrix products, arithmetic and copies ran while one was open for 2% of the time, Pallas kernels for 1%

profile of v5, /device:TPU:2, one launch (start us, length us, event | category | flops | bytes accessed | tf_op | source)
XLA Modules:
  0.0 103.3 jit_solution(14147712528882248137)
XLA Ops:
  0.7 0.9 constant_dynamic-update-slice_fusion.1
  1.5 0.8 constant_dynamic-update-slice_fusion
  2.3 3.3 %collective-permute-start.3 = (bf16[32,1280]{1,0:T(8,128)(2,1)S(1)}, bf16[32,1280]{1,0:T(8,128)(2,1)S(1)}, u32[]{:S(2)}, u32[]{:S(2)}) collective-permute-start(bf16[32,1280]{1,0:T(8,128)(2,1)S(1)} %get-tuple-element.84), channel_id=1, source_target_pairs={{0,64},{32,96},{64,128},{96,160},{128,192},{160,224},{192,0},{224,... | collective-permute-start | bytes 245768 | tf_op jit(solution)/shard_map/ppermute | solution.py:26
  5.6 3.1 %collective-permute-start.2 = (bf16[32,1280]{1,0:T(8,128)(2,1)S(1)}, bf16[32,1280]{1,0:T(8,128)(2,1)S(1)}, u32[]{:S(2)}, u32[]{:S(2)}) collective-permute-start(bf16[32,1280]{1,0:T(8,128)(2,1)S(1)} %get-tuple-element.84), channel_id=1, source_target_pairs={{0,192},{32,224},{64,0},{96,32},{128,64},{160,96},{192,128},{224,1... | collective-permute-start | bytes 245768 | tf_op jit(solution)/shard_map/ppermute | solution.py:26
  8.7 2.4 %collective-permute-start = (bf16[32,1280]{1,0:T(8,128)(2,1)S(1)}, bf16[32,1280]{1,0:T(8,128)(2,1)S(1)}, u32[]{:S(2)}, u32[]{:S(2)}) collective-permute-start(bf16[32,1280]{1,0:T(8,128)(2,1)S(1)} %get-tuple-element.84), channel_id=1, source_target_pairs={{0,224},{32,0},{64,32},{96,64},{128,96},{160,128},{192,160},{224,1... | collective-permute-start | bytes 245768 | tf_op jit(solution)/shard_map/ppermute | solution.py:26
  11.1 1.5 %collective-permute-start.10 = (bf16[160,1280]{1,0:T(8,128)(2,1)}, bf16[160,1280]{1,0:T(8,128)(2,1)S(1)}, u32[]{:S(2)}, u32[]{:S(2)}) collective-permute-start(bf16[160,1280]{1,0:T(8,128)(2,1)} %bitcast.4), channel_id=1, source_target_pairs={{0,24},{24,0},{8,16},{16,8},{1,25},{25,1},{9,17},{17,9},{2,26},{26... | collective-permute-start | bytes 1228808 | tf_op jit(solution)/shard_map/ppermute | solution.py:34
  12.6 1.0 collective-permute-start.7
  13.6 1.0 collective-permute-done.2
  14.5 2.9 %collective-permute-start.6 = (bf16[16,1280]{1,0:T(8,128)(2,1)S(1)}, bf16[16,1280]{1,0:T(8,128)(2,1)S(1)}, u32[]{:S(2)}, u32[]{:S(2)}) collective-permute-start(bf16[16,1280]{1,0:T(8,128)(2,1)S(1)} %slice.120), channel_id=1, source_target_pairs={{0,192},{32,224},{64,0},{96,32},{128,64},{160,96},{192,128},{224,1... | collective-permute-start | bytes 122888 | tf_op jit(solution)/shard_map/ppermute | solution.py:26
  17.4 1.3 %collective-permute-start.4 = (bf16[32,1280]{1,0:T(8,128)(2,1)S(1)}, bf16[32,1280]{1,0:T(8,128)(2,1)S(1)}, u32[]{:S(2)}, u32[]{:S(2)}) collective-permute-start(bf16[32,1280]{1,0:T(8,128)(2,1)S(1)} %collective-permute-done.2), channel_id=1, source_target_pairs={{0,224},{32,0},{64,32},{96,64},{128,96},{160,128},{192,160},{224,1... | collective-permute-start | bytes 245768 | tf_op jit(solution)/shard_map/ppermute | solution.py:26
  18.8 1.9 %collective-permute-start.8 = (bf16[160,1280]{1,0:T(8,128)(2,1)S(1)}, bf16[160,1280]{1,0:T(8,128)(2,1)S(1)}, u32[]{:S(2)}, u32[]{:S(2)}) collective-permute-start(bf16[160,1280]{1,0:T(8,128)(2,1)S(1)} %constant_dynamic-update-slice_fusion.2.refs_0_), channel_id=1, source_target_pairs={{0,8},{8,0},{16,24},{24,16},{1,9},{9,1},{17,25},{25,17},{2,10},{10... | collective-permute-start | bytes 1228808 | tf_op jit(solution)/shard_map/ppermute | solution.py:30
  20.7 1.3 %collective-permute-done.4 = bf16[32,1280]{1,0:T(8,128)(2,1)S(1)} collective-permute-done((bf16[32,1280]{1,0:T(8,128)(2,1)S(1)}, bf16[32,1280]{1,0:T(8,128)(2,1)S(1)}, u32[]{:S(2)}, u32[]{:S(2)}) %collective-permute-start.4) | collective-permute-done | bytes 81952 | tf_op jit(solution)/shard_map/ppermute | solution.py:26
  22.0 0.6 collective-permute-start.5
  22.6 5.1 %collective-permute-done.5 = bf16[32,1280]{1,0:T(8,128)(2,1)S(1)} collective-permute-done((bf16[32,1280]{1,0:T(8,128)(2,1)S(1)}, bf16[32,1280]{1,0:T(8,128)(2,1)S(1)}, u32[]{:S(2)}, u32[]{:S(2)}) %collective-permute-start.5) | collective-permute-done | bytes 81952 | tf_op jit(solution)/shard_map/ppermute | solution.py:26
  27.7 1.5 %collective-permute-start.9 = (bf16[160,1280]{1,0:T(8,128)(2,1)}, bf16[160,1280]{1,0:T(8,128)(2,1)S(1)}, u32[]{:S(2)}, u32[]{:S(2)}) collective-permute-start(bf16[160,1280]{1,0:T(8,128)(2,1)} %wo.1), channel_id=1, source_target_pairs={{0,24},{24,0},{8,16},{16,8},{1,25},{25,1},{9,17},{17,9},{2,26},{26... | collective-permute-start | bytes 1228808 | tf_op jit(solution)/shard_map/ppermute | solution.py:34
  29.2 1.9 %collective-permute-start.11 = (bf16[96,1280]{1,0:T(8,128)(2,1)S(1)}, bf16[96,1280]{1,0:T(8,128)(2,1)}, u32[]{:S(2)}, u32[]{:S(2)}) collective-permute-start(bf16[96,1280]{1,0:T(8,128)(2,1)S(1)} %constant_dynamic-update-slice_fusion.8.refs_1_), channel_id=1, source_target_pairs={{0,8},{8,0},{16,24},{24,16},{1,9},{9,1},{17,25},{25,17},{2,10},{10... | collective-permute-start | bytes 737288 | tf_op jit(solution)/shard_map/ppermute | solution.py:30
  31.1 4.7 %collective-permute-done.9.refs_11_.wo2 = bf16[160,1280]{1,0:T(8,128)(2,1)S(1)} collective-permute-done((bf16[160,1280]{1,0:T(8,128)(2,1)}, bf16[160,1280]{1,0:T(8,128)(2,1)S(1)}, u32[]{:S(2)}, u32[]{:S(2)}) %collective-permute-start.9) | collective-permute-done | bytes 409632 | tf_op jit(solution)/shard_map/ppermute | solution.py:34
  35.8 0.5 collective-permute-start.13
  36.3 1.7 %collective-permute-done.13.refs_5_ = bf16[96,1280]{1,0:T(8,128)(2,1)} collective-permute-done((bf16[96,1280]{1,0:T(8,128)(2,1)S(1)}, bf16[96,1280]{1,0:T(8,128)(2,1)}, u32[]{:S(2)}, u32[]{:S(2)}) %collective-permute-start.13) | collective-permute-done | bytes 245792 | tf_op jit(solution)/shard_map/ppermute | solution.py:26
  38.0 0.1 collective-permute-done.14.refs_6_
  38.1 0.5 collective-permute-done.15.refs_7_
  38.6 3.1 %shard_map.75 = (bf16[512,1280]{1,0:T(8,128)(2,1)S(1)}, bf16[512,1280]{1,0:T(8,128)(2,1)S(1)}, f32[2,320,128]{2,1,0:T(8,128)S(1)}, bf16[2,320,128]{2,1,0:T(8,128...) custom-call(s32[1]{0:T(128)} %bitcast.me, ...), custom_call_target="tpu_custom_call" | custom-call | flops 838860800 | bytes 1048576 | tf_op jit(solution)/shard_map/pallas_call | solution.py:55
  41.7 1.8 %collective-permute-start.16 = (bf16[2,320,128]{2,1,0:T(8,128)(2,1)S(1)}, bf16[2,320,128]{2,1,0:T(8,128)(2,1)S(1)}, u32[]{:S(2)}, u32[]{:S(2)}) collective-permute-start(bf16[2,320,128]{2,1,0:T(8,128)(2,1)S(1)} %get-tuple-element.42), channel_id=1, source_target_pairs={{0,2},{2,4},{4,6},{6,0},{1,3},{3,5},{5,7},{7,1},{8,10},{10,12},{12... | collective-permute-start | bytes 491528 | tf_op jit(solution)/shard_map/ppermute | solution.py:26
  43.6 2.9 %collective-permute-start.17 = (bf16[2,320,128]{2,1,0:T(8,128)(2,1)S(1)}, bf16[2,320,128]{2,1,0:T(8,128)(2,1)S(1)}, u32[]{:S(2)}, u32[]{:S(2)}) collective-permute-start(bf16[2,320,128]{2,1,0:T(8,128)(2,1)S(1)} %get-tuple-element.43), channel_id=1, source_target_pairs={{0,4},{2,6},{4,0},{6,2},{1,5},{3,7},{5,1},{7,3},{8,12},{10,14},{12... | collective-permute-start | bytes 491528 | tf_op jit(solution)/shard_map/ppermute | solution.py:26
  46.5 1.3 %collective-permute-start.18 = (bf16[2,320,128]{2,1,0:T(8,128)(2,1)S(1)}, bf16[2,320,128]{2,1,0:T(8,128)(2,1)S(1)}, u32[]{:S(2)}, u32[]{:S(2)}) collective-permute-start(bf16[2,320,128]{2,1,0:T(8,128)(2,1)S(1)} %get-tuple-element.44), channel_id=1, source_target_pairs={{0,6},{2,0},{4,2},{6,4},{1,7},{3,1},{5,3},{7,5},{8,14},{10,8},{12,... | collective-permute-start | bytes 491528 | tf_op jit(solution)/shard_map/ppermute | solution.py:26
  47.8 1.7 %collective-permute-done.16.p1 = bf16[2,320,128]{2,1,0:T(8,128)(2,1)S(1)} collective-permute-done((bf16[2,320,128]{2,1,0:T(8,128)(2,1)S(1)}, bf16[2,320,128]{2,1,0:T(8,128)(2,1)S(1)}, u32[]{:S(2)}, u32[]{:S(2)}) %collective-permute-start.16) | collective-permute-done | bytes 163872 | tf_op jit(solution)/shard_map/ppermute | solution.py:26
  49.5 4.7 %collective-permute-done.17.p2 = bf16[2,320,128]{2,1,0:T(8,128)(2,1)S(1)} collective-permute-done((bf16[2,320,128]{2,1,0:T(8,128)(2,1)S(1)}, bf16[2,320,128]{2,1,0:T(8,128)(2,1)S(1)}, u32[]{:S(2)}, u32[]{:S(2)}) %collective-permute-start.17) | collective-permute-done | bytes 163872 | tf_op jit(solution)/shard_map/ppermute | solution.py:26
  54.2 0.2 shard_map.76.b0
  54.4 1.3 %collective-permute-start.21 = (bf16[2,320,128]{2,1,0:T(8,128)(2,1)S(1)}, bf16[2,320,128]{2,1,0:T(8,128)(2,1)S(1)}, u32[]{:S(2)}, u32[]{:S(2)}) collective-permute-start(bf16[2,320,128]{2,1,0:T(8,128)(2,1)S(1)} %shard_map.76.b0), channel_id=1, source_target_pairs={{0,2},{2,4},{4,6},{6,0},{1,3},{3,5},{5,7},{7,1},{8,10},{10,12},{12... | collective-permute-start | bytes 491528 | tf_op jit(solution)/shard_map/ppermute | solution.py:26
  55.7 2.4 %collective-permute-start.20 = (bf16[2,320,128]{2,1,0:T(8,128)(2,1)S(1)}, bf16[2,320,128]{2,1,0:T(8,128)(2,1)S(1)}, u32[]{:S(2)}, u32[]{:S(2)}) collective-permute-start(bf16[2,320,128]{2,1,0:T(8,128)(2,1)S(1)} %shard_map.76.b0), channel_id=1, source_target_pairs={{0,4},{2,6},{4,0},{6,2},{1,5},{3,7},{5,1},{7,3},{8,12},{10,14},{12... | collective-permute-start | bytes 491528 | tf_op jit(solution)/shard_map/ppermute | solution.py:26
  58.1 1.6 %collective-permute-start.19 = (bf16[2,320,128]{2,1,0:T(8,128)(2,1)S(1)}, bf16[2,320,128]{2,1,0:T(8,128)(2,1)S(1)}, u32[]{:S(2)}, u32[]{:S(2)}) collective-permute-start(bf16[2,320,128]{2,1,0:T(8,128)(2,1)S(1)} %shard_map.76.b0), channel_id=1, source_target_pairs={{0,6},{2,0},{4,2},{6,4},{1,7},{3,1},{5,3},{7,5},{8,14},{10,8},{12,... | collective-permute-start | bytes 491528 | tf_op jit(solution)/shard_map/ppermute | solution.py:26
  59.6 1.8 %collective-permute-done.21.b3 = bf16[2,320,128]{2,1,0:T(8,128)(2,1)S(1)} collective-permute-done((bf16[2,320,128]{2,1,0:T(8,128)(2,1)S(1)}, bf16[2,320,128]{2,1,0:T(8,128)(2,1)S(1)}, u32[]{:S(2)}, u32[]{:S(2)}) %collective-permute-start.21) | collective-permute-done | bytes 163872 | tf_op jit(solution)/shard_map/ppermute | solution.py:26
  61.4 4.0 %collective-permute-done.20.b2 = bf16[2,320,128]{2,1,0:T(8,128)(2,1)S(1)} collective-permute-done((bf16[2,320,128]{2,1,0:T(8,128)(2,1)S(1)}, bf16[2,320,128]{2,1,0:T(8,128)(2,1)S(1)}, u32[]{:S(2)}, u32[]{:S(2)}) %collective-permute-start.20) | collective-permute-done | bytes 163872 | tf_op jit(solution)/shard_map/ppermute | solution.py:26
  65.4 0.7 shard_map.77
  66.1 1.6 %shard_map.78 = (f32[256,1280]{1,0:T(8,128)S(1)}, f32[256,1280]{1,0:T(8,128)S(1)}, bf16[320,1280]{1,0:T(8,128)(2,1)S(1)}, bf16[192,1280]{1,0:T(8,128)(2,1)S(1)}) custom-call(s32[1]{0:T(128)} %bitcast.me, bf16[2,320,512]{2,1,0:T(8,128)(2,1)S(1)} %get-tuple-element.47.full, bf16[160,1280]{1,0:T(8,128)(2,1)S(1)} %bitcast.6, ...), custom_call_target="tpu_custom_call" | custom-call | flops 838860800 | bytes 1048576 | tf_op jit(solution)/shard_map/pallas_call | solution.py:55
  67.7 0.1 collective-permute-start.22
  67.8 0.5 collective-permute-start.23
  68.3 2.5 %collective-permute-done.23 = bf16[192,1280]{1,0:T(8,128)(2,1)S(1)} collective-permute-done((bf16[192,1280]{1,0:T(8,128)(2,1)S(1)}, bf16[192,1280]{1,0:T(8,128)(2,1)S(1)}, u32[]{:S(2)}, u32[]{:S(2)}) %collective-permute-start.23) | collective-permute-done | bytes 491552 | tf_op jit(solution)/shard_map/ppermute | solution.py:26
  70.8 0.1 convert_element_type.68
  70.9 0.1 convert_element_type.67
  71.0 0.1 fusion.1
  71.1 2.2 %collective-permute-start.24 = (bf16[96,1280]{1,0:T(8,128)(2,1)S(1)}, bf16[96,1280]{1,0:T(8,128)(2,1)S(1)}, u32[]{:S(2)}, u32[]{:S(2)}) collective-permute-start(bf16[96,1280]{1,0:T(8,128)(2,1)S(1)} %get-tuple-element.72), channel_id=1, source_target_pairs={{0,8},{8,0},{16,24},{24,16},{1,9},{9,1},{17,25},{25,17},{2,10},{10... | collective-permute-start | bytes 737288 | tf_op jit(solution)/shard_map/ppermute | solution.py:30
  73.4 0.6 shard_map.79
  74.0 0.1 collective-permute-start.27
  74.1 1.9 %collective-permute-start.30 = (bf16[160,1280]{1,0:T(8,128)(2,1)S(1)}, bf16[160,1280]{1,0:T(8,128)(2,1)S(1)}, u32[]{:S(2)}, u32[]{:S(2)}) collective-permute-start(bf16[160,1280]{1,0:T(8,128)(2,1)S(1)} %get-tuple-element.60), channel_id=1, source_target_pairs={{0,24},{24,0},{8,16},{16,8},{1,25},{25,1},{9,17},{17,9},{2,26},{26... | collective-permute-start | bytes 1228808 | tf_op jit(solution)/shard_map/ppermute | solution.py:34
  75.9 0.2 collective-permute-start.36
  76.2 3.9 %collective-permute-done.24 = bf16[96,1280]{1,0:T(8,128)(2,1)S(1)} collective-permute-done((bf16[96,1280]{1,0:T(8,128)(2,1)S(1)}, bf16[96,1280]{1,0:T(8,128)(2,1)S(1)}, u32[]{:S(2)}, u32[]{:S(2)}) %collective-permute-start.24) | collective-permute-done | bytes 245792 | tf_op jit(solution)/shard_map/ppermute | solution.py:30
  80.2 1.5 %collective-permute-start.29 = (bf16[16,1280]{1,0:T(8,128)(2,1)S(1)}, bf16[16,1280]{1,0:T(8,128)(2,1)S(1)}, u32[]{:S(2)}, u32[]{:S(2)}) collective-permute-start(bf16[16,1280]{1,0:T(8,128)(2,1)S(1)} %get-tuple-element.78), channel_id=1, source_target_pairs={{0,192},{32,224},{64,0},{96,32},{128,64},{160,96},{192,128},{224,1... | collective-permute-start | bytes 122888 | tf_op jit(solution)/shard_map/ppermute | solution.py:26
  81.7 2.0 %collective-permute-start.28 = (bf16[32,1280]{1,0:T(8,128)(2,1)S(1)}, bf16[32,1280]{1,0:T(8,128)(2,1)S(1)}, u32[]{:S(2)}, u32[]{:S(2)}) collective-permute-start(bf16[32,1280]{1,0:T(8,128)(2,1)S(1)} %get-tuple-element.80), channel_id=1, source_target_pairs={{0,224},{32,0},{64,32},{96,64},{128,96},{160,128},{192,160},{224,1... | collective-permute-start | bytes 245768 | tf_op jit(solution)/shard_map/ppermute | solution.py:26
  83.8 1.8 %collective-permute-start.26 = (bf16[16,1280]{1,0:T(8,128)(2,1)S(1)}, bf16[16,1280]{1,0:T(8,128)(2,1)S(1)}, u32[]{:S(2)}, u32[]{:S(2)}) collective-permute-start(bf16[16,1280]{1,0:T(8,128)(2,1)S(1)} %get-tuple-element.79), channel_id=1, source_target_pairs={{0,64},{32,96},{64,128},{96,160},{128,192},{160,224},{192,0},{224,... | collective-permute-start | bytes 122888 | tf_op jit(solution)/shard_map/ppermute | solution.py:26
  85.5 1.2 %collective-permute-done.28 = bf16[32,1280]{1,0:T(8,128)(2,1)S(1)} collective-permute-done((bf16[32,1280]{1,0:T(8,128)(2,1)S(1)}, bf16[32,1280]{1,0:T(8,128)(2,1)S(1)}, u32[]{:S(2)}, u32[]{:S(2)}) %collective-permute-start.28) | collective-permute-done | bytes 81952 | tf_op jit(solution)/shard_map/ppermute | solution.py:26
  86.8 1.4 %collective-permute-start.25 = (bf16[32,1280]{1,0:T(8,128)(2,1)S(1)}, bf16[32,1280]{1,0:T(8,128)(2,1)S(1)}, u32[]{:S(2)}, u32[]{:S(2)}) collective-permute-start(bf16[32,1280]{1,0:T(8,128)(2,1)S(1)} %get-tuple-element.81), channel_id=1, source_target_pairs={{0,32},{32,64},{64,96},{96,128},{128,160},{160,192},{192,224},{224... | collective-permute-start | bytes 245768 | tf_op jit(solution)/shard_map/ppermute | solution.py:26
  88.2 2.1 %collective-permute-start.31 = (bf16[96,1280]{1,0:T(8,128)(2,1)S(1)}, bf16[96,1280]{1,0:T(8,128)(2,1)S(1)}, u32[]{:S(2)}, u32[]{:S(2)}) collective-permute-start(bf16[96,1280]{1,0:T(8,128)(2,1)S(1)} %get-tuple-element.64), channel_id=1, source_target_pairs={{0,8},{8,0},{16,24},{24,16},{1,9},{9,1},{17,25},{25,17},{2,10},{10... | collective-permute-start | bytes 737288 | tf_op jit(solution)/shard_map/ppermute | solution.py:30
  90.4 2.0 %collective-permute-done.25 = bf16[32,1280]{1,0:T(8,128)(2,1)S(1)} collective-permute-done((bf16[32,1280]{1,0:T(8,128)(2,1)S(1)}, bf16[32,1280]{1,0:T(8,128)(2,1)S(1)}, u32[]{:S(2)}, u32[]{:S(2)}) %collective-permute-start.25) | collective-permute-done | bytes 81952 | tf_op jit(solution)/shard_map/ppermute | solution.py:26
  92.5 2.0 %collective-permute-start.33 = (bf16[32,1280]{1,0:T(8,128)(2,1)S(1)}, bf16[32,1280]{1,0:T(8,128)(2,1)S(1)}, u32[]{:S(2)}, u32[]{:S(2)}) collective-permute-start(bf16[32,1280]{1,0:T(8,128)(2,1)S(1)} %get-tuple-element.65), channel_id=1, source_target_pairs={{0,192},{32,224},{64,0},{96,32},{128,64},{160,96},{192,128},{224,1... | collective-permute-start | bytes 245768 | tf_op jit(solution)/shard_map/ppermute | solution.py:26
  94.5 1.0 collective-permute-start.32
  95.5 1.0 convert_add_fusion
  96.5 0.1 fusion.10
  96.6 0.3 collective-permute-start.34
  96.9 3.0 %collective-permute-start.35 = (bf16[32,1280]{1,0:T(8,128)(2,1)S(1)}, bf16[32,1280]{1,0:T(8,128)(2,1)S(1)}, u32[]{:S(2)}, u32[]{:S(2)}) collective-permute-start(bf16[32,1280]{1,0:T(8,128)(2,1)S(1)} %get-tuple-element.67), channel_id=1, source_target_pairs={{0,224},{32,0},{64,32},{96,64},{128,96},{160,128},{192,160},{224,1... | collective-permute-start | bytes 245768 | tf_op jit(solution)/shard_map/ppermute | solution.py:26
  99.9 1.0 add_bitcast_fusion
  100.9 0.8 collective-permute-done.32
  101.7 0.9 collective-permute-done.34
  102.6 0.6 fusion.14
  (52 shorter events, 0.5 us)
Async XLA Ops:
  0.6 38.0 %copy-start = (bf16[1280,160]{0,1:T(8,128)(2,1)S(1)}, bf16[1280,160]{0,1:T(8,128)(2,1)}, u32[]{:S(2)}) copy-start(bf16[1280,160]{0,1:T(8,128)(2,1)} %param.5) | copy-start | bytes 1228804
  0.6 38.0 %copy-start.1 = (bf16[160,1280]{1,0:T(8,128)(2,1)S(1)}, bf16[160,1280]{1,0:T(8,128)(2,1)}, u32[]{:S(2)}) copy-start(bf16[160,1280]{1,0:T(8,128)(2,1)} %wo.1) | copy-start | bytes 1228804
  2.3 10.3 %collective-permute-start.3 = (bf16[32,1280]{1,0:T(8,128)(2,1)S(1)}, bf16[32,1280]{1,0:T(8,128)(2,1)S(1)}, u32[]{:S(2)}, u32[]{:S(2)}) collective-permute-start(bf16[32,1280]{1,0:T(8,128)(2,1)S(1)} %get-tuple-element.84), channel_id=1, source_target_pairs={{0,64},{32,96},{64,128},{96,160},{128,192},{160,224},{192,0},{224,... | collective-permute-start | bytes 245768 | tf_op jit(solution)/shard_map/ppermute | solution.py:26
  5.6 9.0 %collective-permute-start.2 = (bf16[32,1280]{1,0:T(8,128)(2,1)S(1)}, bf16[32,1280]{1,0:T(8,128)(2,1)S(1)}, u32[]{:S(2)}, u32[]{:S(2)}) collective-permute-start(bf16[32,1280]{1,0:T(8,128)(2,1)S(1)} %get-tuple-element.84), channel_id=1, source_target_pairs={{0,192},{32,224},{64,0},{96,32},{128,64},{160,96},{192,128},{224,1... | collective-permute-start | bytes 245768 | tf_op jit(solution)/shard_map/ppermute | solution.py:26
  8.7 8.7 %collective-permute-start = (bf16[32,1280]{1,0:T(8,128)(2,1)S(1)}, bf16[32,1280]{1,0:T(8,128)(2,1)S(1)}, u32[]{:S(2)}, u32[]{:S(2)}) collective-permute-start(bf16[32,1280]{1,0:T(8,128)(2,1)S(1)} %get-tuple-element.84), channel_id=1, source_target_pairs={{0,224},{32,0},{64,32},{96,64},{128,96},{160,128},{192,160},{224,1... | collective-permute-start | bytes 245768 | tf_op jit(solution)/shard_map/ppermute | solution.py:26
  11.1 7.7 %collective-permute-start.1 = (bf16[32,1280]{1,0:T(8,128)(2,1)S(1)}, bf16[32,1280]{1,0:T(8,128)(2,1)S(1)}, u32[]{:S(2)}, u32[]{:S(2)}) collective-permute-start(bf16[32,1280]{1,0:T(8,128)(2,1)S(1)} %get-tuple-element.84), channel_id=1, source_target_pairs={{0,32},{32,64},{64,96},{96,128},{128,160},{160,192},{192,224},{224... | collective-permute-start | bytes 245768 | tf_op jit(solution)/shard_map/ppermute | solution.py:26
  11.1 18.1 %collective-permute-start.10 = (bf16[160,1280]{1,0:T(8,128)(2,1)}, bf16[160,1280]{1,0:T(8,128)(2,1)S(1)}, u32[]{:S(2)}, u32[]{:S(2)}) collective-permute-start(bf16[160,1280]{1,0:T(8,128)(2,1)} %bitcast.4), channel_id=1, source_target_pairs={{0,24},{24,0},{8,16},{16,8},{1,25},{25,1},{9,17},{17,9},{2,26},{26... | collective-permute-start | bytes 1228808 | tf_op jit(solution)/shard_map/ppermute | solution.py:34
  12.6 16.6 %collective-permute-start.7 = (bf16[16,1280]{1,0:T(8,128)(2,1)S(1)}, bf16[16,1280]{1,0:T(8,128)(2,1)S(1)}, u32[]{:S(2)}, u32[]{:S(2)}) collective-permute-start(bf16[16,1280]{1,0:T(8,128)(2,1)S(1)} %slice.121), channel_id=1, source_target_pairs={{0,64},{32,96},{64,128},{96,160},{128,192},{160,224},{192,0},{224,... | collective-permute-start | bytes 122888 | tf_op jit(solution)/shard_map/ppermute | solution.py:26
  14.5 14.6 %collective-permute-start.6 = (bf16[16,1280]{1,0:T(8,128)(2,1)S(1)}, bf16[16,1280]{1,0:T(8,128)(2,1)S(1)}, u32[]{:S(2)}, u32[]{:S(2)}) collective-permute-start(bf16[16,1280]{1,0:T(8,128)(2,1)S(1)} %slice.120), channel_id=1, source_target_pairs={{0,192},{32,224},{64,0},{96,32},{128,64},{160,96},{192,128},{224,1... | collective-permute-start | bytes 122888 | tf_op jit(solution)/shard_map/ppermute | solution.py:26
  17.4 4.6 %collective-permute-start.4 = (bf16[32,1280]{1,0:T(8,128)(2,1)S(1)}, bf16[32,1280]{1,0:T(8,128)(2,1)S(1)}, u32[]{:S(2)}, u32[]{:S(2)}) collective-permute-start(bf16[32,1280]{1,0:T(8,128)(2,1)S(1)} %collective-permute-done.2), channel_id=1, source_target_pairs={{0,224},{32,0},{64,32},{96,64},{128,96},{160,128},{192,160},{224,1... | collective-permute-start | bytes 245768 | tf_op jit(solution)/shard_map/ppermute | solution.py:26
  18.8 12.3 %collective-permute-start.8 = (bf16[160,1280]{1,0:T(8,128)(2,1)S(1)}, bf16[160,1280]{1,0:T(8,128)(2,1)S(1)}, u32[]{:S(2)}, u32[]{:S(2)}) collective-permute-start(bf16[160,1280]{1,0:T(8,128)(2,1)S(1)} %constant_dynamic-update-slice_fusion.2.refs_0_), channel_id=1, source_target_pairs={{0,8},{8,0},{16,24},{24,16},{1,9},{9,1},{17,25},{25,17},{2,10},{10... | collective-permute-start | bytes 1228808 | tf_op jit(solution)/shard_map/ppermute | solution.py:30
  22.0 5.7 %collective-permute-start.5 = (bf16[32,1280]{1,0:T(8,128)(2,1)S(1)}, bf16[32,1280]{1,0:T(8,128)(2,1)S(1)}, u32[]{:S(2)}, u32[]{:S(2)}) collective-permute-start(bf16[32,1280]{1,0:T(8,128)(2,1)S(1)} %collective-permute-done.3), channel_id=1, source_target_pairs={{0,32},{32,64},{64,96},{96,128},{128,160},{160,192},{192,224},{224... | collective-permute-start | bytes 245768 | tf_op jit(solution)/shard_map/ppermute | solution.py:26
  27.7 8.2 %collective-permute-start.9 = (bf16[160,1280]{1,0:T(8,128)(2,1)}, bf16[160,1280]{1,0:T(8,128)(2,1)S(1)}, u32[]{:S(2)}, u32[]{:S(2)}) collective-permute-start(bf16[160,1280]{1,0:T(8,128)(2,1)} %wo.1), channel_id=1, source_target_pairs={{0,24},{24,0},{8,16},{16,8},{1,25},{25,1},{9,17},{17,9},{2,26},{26... | collective-permute-start | bytes 1228808 | tf_op jit(solution)/shard_map/ppermute | solution.py:34
  29.2 7.1 %collective-permute-start.11 = (bf16[96,1280]{1,0:T(8,128)(2,1)S(1)}, bf16[96,1280]{1,0:T(8,128)(2,1)}, u32[]{:S(2)}, u32[]{:S(2)}) collective-permute-start(bf16[96,1280]{1,0:T(8,128)(2,1)S(1)} %constant_dynamic-update-slice_fusion.8.refs_1_), channel_id=1, source_target_pairs={{0,8},{8,0},{16,24},{24,16},{1,9},{9,1},{17,25},{25,17},{2,10},{10... | collective-permute-start | bytes 737288 | tf_op jit(solution)/shard_map/ppermute | solution.py:30
  31.1 6.9 %collective-permute-start.12 = (bf16[160,1280]{1,0:T(8,128)(2,1)S(1)}, bf16[160,1280]{1,0:T(8,128)(2,1)S(1)}, u32[]{:S(2)}, u32[]{:S(2)}) collective-permute-start(bf16[160,1280]{1,0:T(8,128)(2,1)S(1)} %constant_dynamic-update-slice_fusion.2.refs_0_), channel_id=1, source_target_pairs={{0,1},{1,0},{2,3},{3,2},{4,5},{5,4},{6,7},{7,6},{8,9},{9,8},{10,11... | collective-permute-start | bytes 1228808 | tf_op jit(solution)/shard_map/ppermute | solution.py:26
  35.8 2.3 %collective-permute-start.14 = (bf16[160,1280]{1,0:T(8,128)(2,1)S(1)}, bf16[160,1280]{1,0:T(8,128)(2,1)S(1)}, u32[]{:S(2)}, u32[]{:S(2)}) collective-permute-start(bf16[160,1280]{1,0:T(8,128)(2,1)S(1)} %collective-permute-done.8.refs_2_), channel_id=1, source_target_pairs={{0,1},{1,0},{2,3},{3,2},{4,5},{5,4},{6,7},{7,6},{8,9},{9,8},{10,11... | collective-permute-start | bytes 1228808 | tf_op jit(solution)/shard_map/ppermute | solution.py:26
  35.8 2.2 %collective-permute-start.13 = (bf16[96,1280]{1,0:T(8,128)(2,1)S(1)}, bf16[96,1280]{1,0:T(8,128)(2,1)}, u32[]{:S(2)}, u32[]{:S(2)}) collective-permute-start(bf16[96,1280]{1,0:T(8,128)(2,1)S(1)} %constant_dynamic-update-slice_fusion.8.refs_1_), channel_id=1, source_target_pairs={{0,1},{1,0},{2,3},{3,2},{4,5},{5,4},{6,7},{7,6},{8,9},{9,8},{10,11... | collective-permute-start | bytes 737288 | tf_op jit(solution)/shard_map/ppermute | solution.py:26
  36.3 2.3 %collective-permute-start.15 = (bf16[96,1280]{1,0:T(8,128)(2,1)}, bf16[96,1280]{1,0:T(8,128)(2,1)}, u32[]{:S(2)}, u32[]{:S(2)}) collective-permute-start(bf16[96,1280]{1,0:T(8,128)(2,1)} %collective-permute-done.11.refs_3_), channel_id=1, source_target_pairs={{0,1},{1,0},{2,3},{3,2},{4,5},{5,4},{6,7},{7,6},{8,9},{9,8},{10,11... | collective-permute-start | bytes 737288 | tf_op jit(solution)/shard_map/ppermute | solution.py:26
  41.7 7.8 %collective-permute-start.16 = (bf16[2,320,128]{2,1,0:T(8,128)(2,1)S(1)}, bf16[2,320,128]{2,1,0:T(8,128)(2,1)S(1)}, u32[]{:S(2)}, u32[]{:S(2)}) collective-permute-start(bf16[2,320,128]{2,1,0:T(8,128)(2,1)S(1)} %get-tuple-element.42), channel_id=1, source_target_pairs={{0,2},{2,4},{4,6},{6,0},{1,3},{3,5},{5,7},{7,1},{8,10},{10,12},{12... | collective-permute-start | bytes 491528 | tf_op jit(solution)/shard_map/ppermute | solution.py:26
  43.6 10.6 %collective-permute-start.17 = (bf16[2,320,128]{2,1,0:T(8,128)(2,1)S(1)}, bf16[2,320,128]{2,1,0:T(8,128)(2,1)S(1)}, u32[]{:S(2)}, u32[]{:S(2)}) collective-permute-start(bf16[2,320,128]{2,1,0:T(8,128)(2,1)S(1)} %get-tuple-element.43), channel_id=1, source_target_pairs={{0,4},{2,6},{4,0},{6,2},{1,5},{3,7},{5,1},{7,3},{8,12},{10,14},{12... | collective-permute-start | bytes 491528 | tf_op jit(solution)/shard_map/ppermute | solution.py:26
  46.5 7.7 %collective-permute-start.18 = (bf16[2,320,128]{2,1,0:T(8,128)(2,1)S(1)}, bf16[2,320,128]{2,1,0:T(8,128)(2,1)S(1)}, u32[]{:S(2)}, u32[]{:S(2)}) collective-permute-start(bf16[2,320,128]{2,1,0:T(8,128)(2,1)S(1)} %get-tuple-element.44), channel_id=1, source_target_pairs={{0,6},{2,0},{4,2},{6,4},{1,7},{3,1},{5,3},{7,5},{8,14},{10,8},{12,... | collective-permute-start | bytes 491528 | tf_op jit(solution)/shard_map/ppermute | solution.py:26
  54.4 7.1 %collective-permute-start.21 = (bf16[2,320,128]{2,1,0:T(8,128)(2,1)S(1)}, bf16[2,320,128]{2,1,0:T(8,128)(2,1)S(1)}, u32[]{:S(2)}, u32[]{:S(2)}) collective-permute-start(bf16[2,320,128]{2,1,0:T(8,128)(2,1)S(1)} %shard_map.76.b0), channel_id=1, source_target_pairs={{0,2},{2,4},{4,6},{6,0},{1,3},{3,5},{5,7},{7,1},{8,10},{10,12},{12... | collective-permute-start | bytes 491528 | tf_op jit(solution)/shard_map/ppermute | solution.py:26
  55.7 9.7 %collective-permute-start.20 = (bf16[2,320,128]{2,1,0:T(8,128)(2,1)S(1)}, bf16[2,320,128]{2,1,0:T(8,128)(2,1)S(1)}, u32[]{:S(2)}, u32[]{:S(2)}) collective-permute-start(bf16[2,320,128]{2,1,0:T(8,128)(2,1)S(1)} %shard_map.76.b0), channel_id=1, source_target_pairs={{0,4},{2,6},{4,0},{6,2},{1,5},{3,7},{5,1},{7,3},{8,12},{10,14},{12... | collective-permute-start | bytes 491528 | tf_op jit(solution)/shard_map/ppermute | solution.py:26
  58.1 7.4 %collective-permute-start.19 = (bf16[2,320,128]{2,1,0:T(8,128)(2,1)S(1)}, bf16[2,320,128]{2,1,0:T(8,128)(2,1)S(1)}, u32[]{:S(2)}, u32[]{:S(2)}) collective-permute-start(bf16[2,320,128]{2,1,0:T(8,128)(2,1)S(1)} %shard_map.76.b0), channel_id=1, source_target_pairs={{0,6},{2,0},{4,2},{6,4},{1,7},{3,1},{5,3},{7,5},{8,14},{10,8},{12,... | collective-permute-start | bytes 491528 | tf_op jit(solution)/shard_map/ppermute | solution.py:26
  67.7 3.2 %collective-permute-start.22 = (bf16[320,1280]{1,0:T(8,128)(2,1)S(1)}, bf16[320,1280]{1,0:T(8,128)(2,1)S(1)}, u32[]{:S(2)}, u32[]{:S(2)}) collective-permute-start(bf16[320,1280]{1,0:T(8,128)(2,1)S(1)} %get-tuple-element.49), channel_id=1, source_target_pairs={{0,1},{1,0},{2,3},{3,2},{4,5},{5,4},{6,7},{7,6},{8,9},{9,8},{10,11... | collective-permute-start | bytes 2457608 | tf_op jit(solution)/shard_map/ppermute | solution.py:26
  67.8 3.0 %collective-permute-start.23 = (bf16[192,1280]{1,0:T(8,128)(2,1)S(1)}, bf16[192,1280]{1,0:T(8,128)(2,1)S(1)}, u32[]{:S(2)}, u32[]{:S(2)}) collective-permute-start(bf16[192,1280]{1,0:T(8,128)(2,1)S(1)} %get-tuple-element.50), channel_id=1, source_target_pairs={{0,1},{1,0},{2,3},{3,2},{4,5},{5,4},{6,7},{7,6},{8,9},{9,8},{10,11... | collective-permute-start | bytes 1474568 | tf_op jit(solution)/shard_map/ppermute | solution.py:26
  71.1 8.9 %collective-permute-start.24 = (bf16[96,1280]{1,0:T(8,128)(2,1)S(1)}, bf16[96,1280]{1,0:T(8,128)(2,1)S(1)}, u32[]{:S(2)}, u32[]{:S(2)}) collective-permute-start(bf16[96,1280]{1,0:T(8,128)(2,1)S(1)} %get-tuple-element.72), channel_id=1, source_target_pairs={{0,8},{8,0},{16,24},{24,16},{1,9},{9,1},{17,25},{25,17},{2,10},{10... | collective-permute-start | bytes 737288 | tf_op jit(solution)/shard_map/ppermute | solution.py:30
  74.0 9.8 %collective-permute-start.27 = (bf16[64,1280]{1,0:T(8,128)(2,1)S(1)}, bf16[64,1280]{1,0:T(8,128)(2,1)S(1)}, u32[]{:S(2)}, u32[]{:S(2)}) collective-permute-start(bf16[64,1280]{1,0:T(8,128)(2,1)S(1)} %fusion.4), channel_id=1, source_target_pairs={{0,8},{8,0},{16,24},{24,16},{1,9},{9,1},{17,25},{25,17},{2,10},{10... | collective-permute-start | bytes 491528 | tf_op jit(solution)/shard_map/ppermute | solution.py:30
  74.1 18.5 %collective-permute-start.30 = (bf16[160,1280]{1,0:T(8,128)(2,1)S(1)}, bf16[160,1280]{1,0:T(8,128)(2,1)S(1)}, u32[]{:S(2)}, u32[]{:S(2)}) collective-permute-start(bf16[160,1280]{1,0:T(8,128)(2,1)S(1)} %get-tuple-element.60), channel_id=1, source_target_pairs={{0,24},{24,0},{8,16},{16,8},{1,25},{25,1},{9,17},{17,9},{2,26},{26... | collective-permute-start | bytes 1228808 | tf_op jit(solution)/shard_map/ppermute | solution.py:34
  75.9 24.0 %collective-permute-start.36 = (bf16[160,1280]{1,0:T(8,128)(2,1)S(1)}, bf16[160,1280]{1,0:T(8,128)(2,1)S(1)}, u32[]{:S(2)}, u32[]{:S(2)}) collective-permute-start(bf16[160,1280]{1,0:T(8,128)(2,1)S(1)} %get-tuple-element.69), channel_id=1, source_target_pairs={{0,24},{24,0},{8,16},{16,8},{1,25},{25,1},{9,17},{17,9},{2,26},{26... | collective-permute-start | bytes 1228808 | tf_op jit(solution)/shard_map/ppermute | solution.py:34
  80.2 8.0 %collective-permute-start.29 = (bf16[16,1280]{1,0:T(8,128)(2,1)S(1)}, bf16[16,1280]{1,0:T(8,128)(2,1)S(1)}, u32[]{:S(2)}, u32[]{:S(2)}) collective-permute-start(bf16[16,1280]{1,0:T(8,128)(2,1)S(1)} %get-tuple-element.78), channel_id=1, source_target_pairs={{0,192},{32,224},{64,0},{96,32},{128,64},{160,96},{192,128},{224,1... | collective-permute-start | bytes 122888 | tf_op jit(solution)/shard_map/ppermute | solution.py:26
  81.7 5.1 %collective-permute-start.28 = (bf16[32,1280]{1,0:T(8,128)(2,1)S(1)}, bf16[32,1280]{1,0:T(8,128)(2,1)S(1)}, u32[]{:S(2)}, u32[]{:S(2)}) collective-permute-start(bf16[32,1280]{1,0:T(8,128)(2,1)S(1)} %get-tuple-element.80), channel_id=1, source_target_pairs={{0,224},{32,0},{64,32},{96,64},{128,96},{160,128},{192,160},{224,1... | collective-permute-start | bytes 245768 | tf_op jit(solution)/shard_map/ppermute | solution.py:26
  83.8 8.7 %collective-permute-start.26 = (bf16[16,1280]{1,0:T(8,128)(2,1)S(1)}, bf16[16,1280]{1,0:T(8,128)(2,1)S(1)}, u32[]{:S(2)}, u32[]{:S(2)}) collective-permute-start(bf16[16,1280]{1,0:T(8,128)(2,1)S(1)} %get-tuple-element.79), channel_id=1, source_target_pairs={{0,64},{32,96},{64,128},{96,160},{128,192},{160,224},{192,0},{224,... | collective-permute-start | bytes 122888 | tf_op jit(solution)/shard_map/ppermute | solution.py:26
  86.8 5.7 %collective-permute-start.25 = (bf16[32,1280]{1,0:T(8,128)(2,1)S(1)}, bf16[32,1280]{1,0:T(8,128)(2,1)S(1)}, u32[]{:S(2)}, u32[]{:S(2)}) collective-permute-start(bf16[32,1280]{1,0:T(8,128)(2,1)S(1)} %get-tuple-element.81), channel_id=1, source_target_pairs={{0,32},{32,64},{64,96},{96,128},{128,160},{160,192},{192,224},{224... | collective-permute-start | bytes 245768 | tf_op jit(solution)/shard_map/ppermute | solution.py:26
  88.2 8.3 %collective-permute-start.31 = (bf16[96,1280]{1,0:T(8,128)(2,1)S(1)}, bf16[96,1280]{1,0:T(8,128)(2,1)S(1)}, u32[]{:S(2)}, u32[]{:S(2)}) collective-permute-start(bf16[96,1280]{1,0:T(8,128)(2,1)S(1)} %get-tuple-element.64), channel_id=1, source_target_pairs={{0,8},{8,0},{16,24},{24,16},{1,9},{9,1},{17,25},{25,17},{2,10},{10... | collective-permute-start | bytes 737288 | tf_op jit(solution)/shard_map/ppermute | solution.py:30
  92.5 8.3 %collective-permute-start.33 = (bf16[32,1280]{1,0:T(8,128)(2,1)S(1)}, bf16[32,1280]{1,0:T(8,128)(2,1)S(1)}, u32[]{:S(2)}, u32[]{:S(2)}) collective-permute-start(bf16[32,1280]{1,0:T(8,128)(2,1)S(1)} %get-tuple-element.65), channel_id=1, source_target_pairs={{0,192},{32,224},{64,0},{96,32},{128,64},{160,96},{192,128},{224,1... | collective-permute-start | bytes 245768 | tf_op jit(solution)/shard_map/ppermute | solution.py:26
  94.5 7.2 %collective-permute-start.32 = (bf16[32,1280]{1,0:T(8,128)(2,1)S(1)}, bf16[32,1280]{1,0:T(8,128)(2,1)S(1)}, u32[]{:S(2)}, u32[]{:S(2)}) collective-permute-start(bf16[32,1280]{1,0:T(8,128)(2,1)S(1)} %get-tuple-element.61), channel_id=1, source_target_pairs={{0,64},{32,96},{64,128},{96,160},{128,192},{160,224},{192,0},{224,... | collective-permute-start | bytes 245768 | tf_op jit(solution)/shard_map/ppermute | solution.py:26
  96.6 6.0 %collective-permute-start.34 = (bf16[32,1280]{1,0:T(8,128)(2,1)S(1)}, bf16[32,1280]{1,0:T(8,128)(2,1)S(1)}, u32[]{:S(2)}, u32[]{:S(2)}) collective-permute-start(bf16[32,1280]{1,0:T(8,128)(2,1)S(1)} %get-tuple-element.66), channel_id=1, source_target_pairs={{0,32},{32,64},{64,96},{96,128},{128,160},{160,192},{192,224},{224... | collective-permute-start | bytes 245768 | tf_op jit(solution)/shard_map/ppermute | solution.py:26
  96.9 5.7 %collective-permute-start.35 = (bf16[32,1280]{1,0:T(8,128)(2,1)S(1)}, bf16[32,1280]{1,0:T(8,128)(2,1)S(1)}, u32[]{:S(2)}, u32[]{:S(2)}) collective-permute-start(bf16[32,1280]{1,0:T(8,128)(2,1)S(1)} %get-tuple-element.67), channel_id=1, source_target_pairs={{0,224},{32,0},{64,32},{96,64},{128,96},{160,128},{192,160},{224,1... | collective-permute-start | bytes 245768 | tf_op jit(solution)/shard_map/ppermute | solution.py:26

commit v6 on v5

--- a/solution.py
+++ b/solution.py
@@ -66,18 +66,18 @@
 
 
 def up_kernel(me, *refs):
-    quarters, weights = refs[:8], (refs[8:10], refs[10:12])
-    tok, cot, parts, whole = refs[12], refs[13], refs[14:18], refs[18]
-    h = weights[0][0].shape[0]
+    quarters, wi, wo, w_pair = refs[:8], refs[8], refs[9], refs[10]
+    tok, cot, parts, whole = refs[11], refs[12], refs[13:17], refs[17]
+    h = wi.shape[0]
     for q in range(4):
         for j in range(8):
             ref, i = (quarters[2 * q], j) if j < HEAD else (quarters[2 * q + 1], j - HEAD)
             row = q * 128 + j * 16
             tok[row : row + 16] = ref[i * 32 : i * 32 + 16]
             cot[row : row + 16] = ref[i * 32 + 16 : i * 32 + 32]
-    for s, value in enumerate((tok, cot)):
-        for i, w in enumerate(weights[s]):
-            total = dot(w[...], value[...], 1, 1)
+    for s, (w, value) in enumerate(((wi, tok), (wo, cot))):
+        for i, left in enumerate((w[...], w_pair[s * h : s * h + h])):
+            total = dot(left, value[...], 1, 1)
             for q in range(4):
                 whole[q, s, i * h : i * h + h] = total[:, q * 128 : q * 128 + 128]
     for k, part in enumerate(parts):
@@ -94,11 +94,12 @@
     out[1] = (grad_act * smooth_slope(pre)).astype(BF)
 
 
-def down_kernel(me, full, wi, wi2, wo, wo2, near, far, head, tail):
+def down_kernel(me, full, wi, wo, w_pair, near, far, head, tail):
     del me
     h = wi.shape[0]
-    for s, (w, w2) in enumerate(((wo, wo2), (wi, wi2))):
-        value = dot(full[s, :h], w[...], 0, 0) + dot(full[s, h:], w2[...], 0, 0)
+    for s, w in enumerate((wo, wi)):
+        value = dot(full[s, :h], w[...], 0, 0)
+        value += dot(full[s, h:], w_pair[(1 - s) * h : (2 - s) * h], 0, 0)
         for q in range(4):
             for j in range(8):
                 piece = value[q * 128 + j * 16 : q * 128 + j * 16 + 16]
@@ -113,13 +114,13 @@
                     tail[row : row + 16] = piece.astype(BF)
 
 
-def pair_kernel(me, b0, b1, b2, b3, tok, cot, full, out, back):
+def pair_kernel(me, b0, b1, b2, b3, tok, cot, full, out):
     h = full.shape[1] // 2
     for k, block in enumerate((b0, b1, b2, b3)):
         lane = pl.multiple_of(((me[0] + k) % 4) * 128, 128)
         full[:, :, pl.ds(lane, 128)] = block[...]
-    out[...] = dot(full[0, h:], cot[...], 1, 0).astype(BF)
-    back[...] = dot(full[1, h:], tok[...], 1, 0).astype(BF)
+    out[:h] = dot(full[0, h:], cot[...], 1, 0).astype(BF)
+    out[h:] = dot(full[1, h:], tok[...], 1, 0).astype(BF)
 
 
 def own_kernel(me, full, tok, cot, grad_out, grad_in):
@@ -140,15 +141,14 @@
     z[2], z[6] = send(base, "z", -2), send(base, "z", 2)
     z[1], z[7] = send(base, "z", -1), send(base, "z", 1)
     w_in_t = w_in.T
-    w_in_2 = weight_pair(after(w_in_t, base))
+    w_pair = weight_pair(after(cat([w_in_t, w_out]), base))
     z[3], z[5] = send(z[2], "z", -1), send(z[6], "z", 1)
-    z[4] = cat([send(z[2][:16], "z", -2), send(z[6][16:], "z", 2)])
-    w_out_2 = weight_pair(after(w_out, (z[2], z[6])))
     near_h = cat([z[k] for k in ORDER[:HEAD]])
     far_h = token_pair(near_h)
+    z[4] = send(after(z[6], near_h), "z", 2)
     near_t = cat([z[k] for k in ORDER[HEAD:]])
-    far_t = token_pair(after(near_t, w_in_2))
-    far_h = after(far_h, w_out_2)
+    far_t = token_pair(near_t)
+    far_h = after(far_h, w_pair)
     quarters = [near_h, near_t, far_h, far_t]
     quarters += [send(value, "col", 1) for value in quarters]
 
@@ -156,7 +156,7 @@
     tok, cot, *parts = call(
         up_kernel,
         [shape((512, d), BF)] * 2 + [part] + [rounded] * 3,
-        [me, *quarters, w_in_t, w_in_2, w_out, w_out_2],
+        [me, *quarters, w_in_t, w_out, w_pair],
         2 * flops,
         [pltpu.VMEM((4, 2, 2 * h, 128), F32)],
     )
@@ -165,49 +165,44 @@
     blocks = [block] + [send(block, "row", -k) for k in (1, 2, 3)]
 
     sums = shape((256, d), F32)
-    full, pair_out, pair_in = call(
+    full, pair = call(
         pair_kernel,
-        [shape((2, 2 * h, 512), BF)] + [shape((h, d), BF)] * 2,
+        [shape((2, 2 * h, 512), BF), shape((2 * h, d), BF)],
         [me, *blocks, tok, cot],
         flops,
     )
     near, far, head, tail = call(
         down_kernel,
         [sums, sums, shape((HEAD * 64, d), BF), shape(((8 - HEAD) * 64, d), BF)],
-        [me, full, w_in_t, w_in_2, w_out, w_out_2],
+        [me, full, w_in_t, w_out, w_pair],
         2 * flops,
     )
     cut, rest = HEAD * 32, (8 - HEAD) * 32
-    tail = send(tail, "col", 1).astype(F32)
-    head = send(head, "col", 1).astype(F32)
+    tail = send(tail, "col", 1)
+    head = send(after(head, tail), "col", 1).astype(F32)
+    tail = tail.astype(F32)
     far_t = (far[cut:] + tail[:rest]).astype(BF)
-    far_2 = (far[96:cut] + head[96:cut]).astype(BF)
-    far_1 = (far[:96] + head[:96]).astype(BF)
-    pair_out, pair_in = after((pair_out, pair_in), far_t)
-    pair_out, pair_in = weight_pair(pair_out), weight_pair(pair_in)
+    far = after(far, far_t)
+    pair = weight_pair(after(pair, far_t))
     grad_out, grad_in_t = call(
         own_kernel, [shape((h, d), F32)] * 2, [me, full, after(tok, far_t), cot], flops
     )
-    far_t, far_2 = token_pair(far_t), token_pair(after(far_2, grad_out))
+    far_t = token_pair(far_t)
+    far_h = token_pair(after((far[:cut] + head[:cut]).astype(BF), grad_out))
     third = (near[cut:] + tail[rest:] + far_t.astype(F32)).astype(BF)
-    near, head = after((near, head), third)
-    far_1 = token_pair(after(far_1, third))
-    near_2 = near[96:cut] + head[96 + cut :] + far_2.astype(F32)
-    third = after(third, grad_out)
+    near, head, far_h = after((near, head, far_h), third)
     up, down = send(third[:32], "z", 1), send(third[32:64], "z", -1)
-    up_2, down_2 = send(third[64:80], "z", 2), send(third[80:], "z", -2)
-    up, down = up.astype(F32), down.astype(F32)
-    up = cat([up[:16] + up_2.astype(F32), up[16:]]) + near_2[:32]
-    down = cat([down[:16], down[16:] + down_2.astype(F32)]) + near_2[32:]
-    up, down = after((up.astype(BF), down.astype(BF)), pair_out)
-    near, head = after((near, head), up)
-    near_1 = near[:96] + head[cut : 96 + cut] + far_1.astype(F32)
-    total = near_1[:32] + send(up, "z", 2).astype(F32) + send(down, "z", -2).astype(F32)
-    up, down = after((near_1[32:64].astype(BF), near_1[64:].astype(BF)), (up, down))
-    total += send(up, "z", 1).astype(F32) + send(down, "z", -1).astype(F32)
+    up_2 = send(third[64:], "z", 2)
+    near_h = near[:cut] + head[cut:] + far_h.astype(F32)
+    up = up.astype(F32) + up_2.astype(F32) + near_h[96:128]
+    down = down.astype(F32) + near_h[128:]
+    up, down = up.astype(BF), down.astype(BF)
+    near_h, near_1 = after((near_h, near_h[32:96].astype(BF)), (up, pair))
+    total = near_h[:32] + send(up, "z", 2).astype(F32) + send(down, "z", -2).astype(F32)
+    total += send(near_1[:32], "z", 1).astype(F32) + send(near_1[32:], "z", -1).astype(F32)
     output, input_grad = total[:16].astype(BF), total[16:].astype(BF)
-    grad_out = grad_out + pair_out.astype(F32)
-    grad_in_t = grad_in_t + pair_in.astype(F32)
+    grad_out = grad_out + pair[:h].astype(F32)
+    grad_in_t = grad_in_t + pair[h:].astype(F32)
     return (output, input_grad, grad_in_t.T, grad_out)
 
 

time: 105 us -> 101 us (0.962)
  starting transfers between devices: 53.4 us -> 42.4 us
  waiting for transfers between devices: 37.9 us -> 45.5 us
    ppermute x5 -> x4, waiting for transfers between devices: 3.9 us -> 13.5 us  [token_pair(): return lax.ppermute(value, 'x', [(0, 1), (1, 0), (2, 3), (3, 2)])]
    ppermute x28 -> x26, starting transfers between devices: 40.1 us -> 32.5 us  [send(): lax.ppermute(value, axis, [(i, (i + shift) % size) for i in range(size)])]
    ppermute x4 -> x2, waiting for transfers between devices: 4.73 us -> 2.54 us  [weight_pair(): return lax.ppermute(value, 'x', [(0, 3), (3, 0), (1, 2), (2, 1)])]
    ppermute x4 -> x2, starting transfers between devices: 5.09 us -> 2.97 us  [weight_pair(): return lax.ppermute(value, 'x', [(0, 3), (3, 0), (1, 2), (2, 1)])]
    ppermute x5 -> x4, starting transfers between devices: 8.23 us -> 6.83 us  [token_pair(): return lax.ppermute(value, 'x', [(0, 1), (1, 0), (2, 3), (3, 2)])]
    concatenate x0 -> x1, other arithmetic: none -> 1.25 us  [cat(): return jnp.concatenate(values, 0)]
    ppermute x28 -> x26, waiting for transfers between devices: 29.3 us -> 29.5 us  [send(): lax.ppermute(value, axis, [(i, (i + shift) % size) for i in range(size)])]
  transfers between devices with their start and end apart: 37 -> 32, of which waited for: 17 -> 17; matrix products, arithmetic and copies ran while one was open for 2% -> 3% of each run, Pallas kernels for 1% -> 1%
where the time goes in v6:
time: 101 us; the launch traced here: 100 us
  waiting for transfers between devices  45.5 us (45%)
  starting transfers between devices  42.4 us (42%)
  Pallas kernels  6.14 us (6%)
  other arithmetic  3.11 us (3%)
  local copies, waits for them, and re-layouts  2.31 us (2%)
    ppermute x26, starting transfers between devices, send(): lax.ppermute(value, axis, [(i, (i + shift) % size) for i in range(size)])  32.5 us
    ppermute x26, waiting for transfers between devices, send(): lax.ppermute(value, axis, [(i, (i + shift) % size) for i in range(size)])  29.5 us
    ppermute x4, waiting for transfers between devices, token_pair(): return lax.ppermute(value, 'x', [(0, 1), (1, 0), (2, 3), (3, 2)])  13.5 us
    ppermute x4, starting transfers between devices, token_pair(): return lax.ppermute(value, 'x', [(0, 1), (1, 0), (2, 3), (3, 2)])  6.83 us
    pallas_call x5, Pallas kernels, call(): return list(kernel(*args))  6.14 us
    ppermute x2, starting transfers between devices, weight_pair(): return lax.ppermute(value, 'x', [(0, 3), (3, 0), (1, 2), (2, 1)])  2.97 us
    ppermute x2, waiting for transfers between devices, weight_pair(): return lax.ppermute(value, 'x', [(0, 3), (3, 0), (1, 2), (2, 1)])  2.54 us
  transfers between devices with their start and end apart: 32, of which 17 were waited for; matrix products, arithmetic and copies ran while one was open for 3% of the time, Pallas kernels for 1%

profile of v6, /device:TPU:2, one launch (start us, length us, event | category | flops | bytes accessed | tf_op | source)
XLA Modules:
  0.0 100.3 jit_solution(13156720370108450191)
XLA Ops:
  0.6 0.8 constant_dynamic-update-slice_fusion.1
  1.4 0.8 constant_dynamic-update-slice_fusion
  2.2 5.9 %collective-permute-start = (bf16[32,1280]{1,0:T(8,128)(2,1)S(1)}, bf16[32,1280]{1,0:T(8,128)(2,1)S(1)}, u32[]{:S(2)}, u32[]{:S(2)}) collective-permute-start(bf16[32,1280]{1,0:T(8,128)(2,1)S(1)} %get-tuple-element.69), channel_id=1, source_target_pairs={{0,224},{32,0},{64,32},{96,64},{128,96},{160,128},{192,160},{224,1... | collective-permute-start | bytes 245768 | tf_op jit(solution)/shard_map/ppermute | solution.py:26
  8.1 0.0 collective-permute-start.1
  8.1 2.5 %collective-permute-start.2 = (bf16[32,1280]{1,0:T(8,128)(2,1)S(1)}, bf16[32,1280]{1,0:T(8,128)(2,1)S(1)}, u32[]{:S(2)}, u32[]{:S(2)}) collective-permute-start(bf16[32,1280]{1,0:T(8,128)(2,1)S(1)} %get-tuple-element.69), channel_id=1, source_target_pairs={{0,192},{32,224},{64,0},{96,32},{128,64},{160,96},{192,128},{224,1... | collective-permute-start | bytes 245768 | tf_op jit(solution)/shard_map/ppermute | solution.py:26
  10.5 0.5 collective-permute-start.3
  11.0 1.3 %pad_maximum_fusion = bf16[320,1280]{1,0:T(8,128)(2,1)S(1)} fusion(bf16[160,1280]{1,0:T(8,128)(2,1)} %wo.1, bf16[160,1280]{1,0:T(8,128)(2,1)} %bitcast.4), kind=kLoop, calls=%fused_computation.2 | loop fusion | flops 1638400 | bytes 1638400 | tf_op jit(solution)/shard_map/concatenate | solution.py:59
  12.2 1.6 %collective-permute-start.8 = (bf16[320,1280]{1,0:T(8,128)(2,1)S(1)}, bf16[320,1280]{1,0:T(8,128)(2,1)S(1)}, u32[]{:S(2)}, u32[]{:S(2)}) collective-permute-start(bf16[320,1280]{1,0:T(8,128)(2,1)S(1)} %pad_maximum_fusion), channel_id=1, source_target_pairs={{0,24},{24,0},{8,16},{16,8},{1,25},{25,1},{9,17},{17,9},{2,26},{26... | collective-permute-start | bytes 2457608 | tf_op jit(solution)/shard_map/ppermute | solution.py:34
  13.8 0.0 collective-permute-done.2
  13.8 4.4 %collective-permute-start.4 = (bf16[32,1280]{1,0:T(8,128)(2,1)S(1)}, bf16[32,1280]{1,0:T(8,128)(2,1)S(1)}, u32[]{:S(2)}, u32[]{:S(2)}) collective-permute-start(bf16[32,1280]{1,0:T(8,128)(2,1)S(1)} %collective-permute-done.2), channel_id=1, source_target_pairs={{0,224},{32,0},{64,32},{96,64},{128,96},{160,128},{192,160},{224,1... | collective-permute-start | bytes 245768 | tf_op jit(solution)/shard_map/ppermute | solution.py:26
  18.3 0.0 collective-permute-done
  18.4 1.9 %collective-permute-start.7 = (bf16[160,1280]{1,0:T(8,128)(2,1)S(1)}, bf16[160,1280]{1,0:T(8,128)(2,1)S(1)}, u32[]{:S(2)}, u32[]{:S(2)}) collective-permute-start(bf16[160,1280]{1,0:T(8,128)(2,1)S(1)} %constant_dynamic-update-slice_fusion.2.refs_0_), channel_id=1, source_target_pairs={{0,8},{8,0},{16,24},{24,16},{1,9},{9,1},{17,25},{25,17},{2,10},{10... | collective-permute-start | bytes 1228808 | tf_op jit(solution)/shard_map/ppermute | solution.py:30
  20.2 0.0 collective-permute-start.6
  20.2 0.1 collective-permute-start.5
  20.3 0.0 collective-permute-done.4
  20.3 6.8 %collective-permute-done.5 = bf16[32,1280]{1,0:T(8,128)(2,1)S(1)} collective-permute-done((bf16[32,1280]{1,0:T(8,128)(2,1)S(1)}, bf16[32,1280]{1,0:T(8,128)(2,1)S(1)}, u32[]{:S(2)}, u32[]{:S(2)}) %collective-permute-start.5) | collective-permute-done | bytes 81952 | tf_op jit(solution)/shard_map/ppermute | solution.py:26
  27.1 0.0 collective-permute-done.6
  27.2 1.6 %collective-permute-start.9 = (bf16[96,1280]{1,0:T(8,128)(2,1)S(1)}, bf16[96,1280]{1,0:T(8,128)(2,1)}, u32[]{:S(2)}, u32[]{:S(2)}) collective-permute-start(bf16[96,1280]{1,0:T(8,128)(2,1)S(1)} %constant_dynamic-update-slice_fusion.8.refs_1_), channel_id=1, source_target_pairs={{0,8},{8,0},{16,24},{24,16},{1,9},{9,1},{17,25},{25,17},{2,10},{10... | collective-permute-start | bytes 737288 | tf_op jit(solution)/shard_map/ppermute | solution.py:30
  28.8 1.2 %collective-permute-done.7.refs_2_ = bf16[160,1280]{1,0:T(8,128)(2,1)S(1)} collective-permute-done((bf16[160,1280]{1,0:T(8,128)(2,1)S(1)}, bf16[160,1280]{1,0:T(8,128)(2,1)S(1)}, u32[]{:S(2)}, u32[]{:S(2)}) %collective-permute-start.7) | collective-permute-done | bytes 409632 | tf_op jit(solution)/shard_map/ppermute | solution.py:30
  30.0 1.5 %collective-permute-done.8.refs_10_.w_pair = bf16[320,1280]{1,0:T(8,128)(2,1)S(1)} collective-permute-done((bf16[320,1280]{1,0:T(8,128)(2,1)S(1)}, bf16[320,1280]{1,0:T(8,128)(2,1)S(1)}, u32[]{:S(2)}, u32[]{:S(2)}) %collective-permute-start.8) | collective-permute-done | bytes 819232 | tf_op jit(solution)/shard_map/ppermute | solution.py:34
  31.5 0.5 collective-permute-start.11
  32.0 1.6 %collective-permute-done.9.refs_3_ = bf16[96,1280]{1,0:T(8,128)(2,1)} collective-permute-done((bf16[96,1280]{1,0:T(8,128)(2,1)S(1)}, bf16[96,1280]{1,0:T(8,128)(2,1)}, u32[]{:S(2)}, u32[]{:S(2)}) %collective-permute-start.9) | collective-permute-done | bytes 245792 | tf_op jit(solution)/shard_map/ppermute | solution.py:30
  33.6 0.0 collective-permute-start.13
  33.6 1.8 %collective-permute-done.13.refs_7_ = bf16[96,1280]{1,0:T(8,128)(2,1)} collective-permute-done((bf16[96,1280]{1,0:T(8,128)(2,1)}, bf16[96,1280]{1,0:T(8,128)(2,1)}, u32[]{:S(2)}, u32[]{:S(2)}) %collective-permute-start.13) | collective-permute-done | bytes 245792 | tf_op jit(solution)/shard_map/ppermute | solution.py:26
  35.4 3.1 %shard_map.75 = (bf16[512,1280]{1,0:T(8,128)(2,1)S(1)}, bf16[512,1280]{1,0:T(8,128)(2,1)S(1)}, f32[2,320,128]{2,1,0:T(8,128)S(1)}, bf16[2,320,128]{2,1,0:T(8,128...) custom-call(s32[1]{0:T(128)} %bitcast.me, ...), custom_call_target="tpu_custom_call" | custom-call | flops 838860800 | bytes 1048576 | tf_op jit(solution)/shard_map/pallas_call | solution.py:55
  38.6 1.7 %collective-permute-start.14 = (bf16[2,320,128]{2,1,0:T(8,128)(2,1)S(1)}, bf16[2,320,128]{2,1,0:T(8,128)(2,1)S(1)}, u32[]{:S(2)}, u32[]{:S(2)}) collective-permute-start(bf16[2,320,128]{2,1,0:T(8,128)(2,1)S(1)} %get-tuple-element.35), channel_id=1, source_target_pairs={{0,2},{2,4},{4,6},{6,0},{1,3},{3,5},{5,7},{7,1},{8,10},{10,12},{12... | collective-permute-start | bytes 491528 | tf_op jit(solution)/shard_map/ppermute | solution.py:26
  40.2 2.9 %collective-permute-start.15 = (bf16[2,320,128]{2,1,0:T(8,128)(2,1)S(1)}, bf16[2,320,128]{2,1,0:T(8,128)(2,1)S(1)}, u32[]{:S(2)}, u32[]{:S(2)}) collective-permute-start(bf16[2,320,128]{2,1,0:T(8,128)(2,1)S(1)} %get-tuple-element.36), channel_id=1, source_target_pairs={{0,4},{2,6},{4,0},{6,2},{1,5},{3,7},{5,1},{7,3},{8,12},{10,14},{12... | collective-permute-start | bytes 491528 | tf_op jit(solution)/shard_map/ppermute | solution.py:26
  43.1 1.3 %collective-permute-start.16 = (bf16[2,320,128]{2,1,0:T(8,128)(2,1)S(1)}, bf16[2,320,128]{2,1,0:T(8,128)(2,1)S(1)}, u32[]{:S(2)}, u32[]{:S(2)}) collective-permute-start(bf16[2,320,128]{2,1,0:T(8,128)(2,1)S(1)} %get-tuple-element.37), channel_id=1, source_target_pairs={{0,6},{2,0},{4,2},{6,4},{1,7},{3,1},{5,3},{7,5},{8,14},{10,8},{12,... | collective-permute-start | bytes 491528 | tf_op jit(solution)/shard_map/ppermute | solution.py:26
  44.5 1.7 %collective-permute-done.14.p1 = bf16[2,320,128]{2,1,0:T(8,128)(2,1)S(1)} collective-permute-done((bf16[2,320,128]{2,1,0:T(8,128)(2,1)S(1)}, bf16[2,320,128]{2,1,0:T(8,128)(2,1)S(1)}, u32[]{:S(2)}, u32[]{:S(2)}) %collective-permute-start.14) | collective-permute-done | bytes 163872 | tf_op jit(solution)/shard_map/ppermute | solution.py:26
  46.1 4.7 %collective-permute-done.15.p2 = bf16[2,320,128]{2,1,0:T(8,128)(2,1)S(1)} collective-permute-done((bf16[2,320,128]{2,1,0:T(8,128)(2,1)S(1)}, bf16[2,320,128]{2,1,0:T(8,128)(2,1)S(1)}, u32[]{:S(2)}, u32[]{:S(2)}) %collective-permute-start.15) | collective-permute-done | bytes 163872 | tf_op jit(solution)/shard_map/ppermute | solution.py:26
  50.8 0.2 shard_map.76.b0
  51.0 2.2 %collective-permute-start.17 = (bf16[2,320,128]{2,1,0:T(8,128)(2,1)S(1)}, bf16[2,320,128]{2,1,0:T(8,128)(2,1)S(1)}, u32[]{:S(2)}, u32[]{:S(2)}) collective-permute-start(bf16[2,320,128]{2,1,0:T(8,128)(2,1)S(1)} %shard_map.76.b0), channel_id=1, source_target_pairs={{0,6},{2,0},{4,2},{6,4},{1,7},{3,1},{5,3},{7,5},{8,14},{10,8},{12,... | collective-permute-start | bytes 491528 | tf_op jit(solution)/shard_map/ppermute | solution.py:26
  53.2 1.1 %collective-permute-start.18 = (bf16[2,320,128]{2,1,0:T(8,128)(2,1)S(1)}, bf16[2,320,128]{2,1,0:T(8,128)(2,1)S(1)}, u32[]{:S(2)}, u32[]{:S(2)}) collective-permute-start(bf16[2,320,128]{2,1,0:T(8,128)(2,1)S(1)} %shard_map.76.b0), channel_id=1, source_target_pairs={{0,4},{2,6},{4,0},{6,2},{1,5},{3,7},{5,1},{7,3},{8,12},{10,14},{12... | collective-permute-start | bytes 491528 | tf_op jit(solution)/shard_map/ppermute | solution.py:26
  54.4 0.7 collective-permute-start.19
  55.1 5.0 %collective-permute-done.17.b1 = bf16[2,320,128]{2,1,0:T(8,128)(2,1)S(1)} collective-permute-done((bf16[2,320,128]{2,1,0:T(8,128)(2,1)S(1)}, bf16[2,320,128]{2,1,0:T(8,128)(2,1)S(1)}, u32[]{:S(2)}, u32[]{:S(2)}) %collective-permute-start.17) | collective-permute-done | bytes 163872 | tf_op jit(solution)/shard_map/ppermute | solution.py:26
  60.1 1.8 %collective-permute-done.18.b2 = bf16[2,320,128]{2,1,0:T(8,128)(2,1)S(1)} collective-permute-done((bf16[2,320,128]{2,1,0:T(8,128)(2,1)S(1)}, bf16[2,320,128]{2,1,0:T(8,128)(2,1)S(1)}, u32[]{:S(2)}, u32[]{:S(2)}) %collective-permute-start.18) | collective-permute-done | bytes 163872 | tf_op jit(solution)/shard_map/ppermute | solution.py:26
  61.9 1.9 %collective-permute-done.19.b3 = bf16[2,320,128]{2,1,0:T(8,128)(2,1)S(1)} collective-permute-done((bf16[2,320,128]{2,1,0:T(8,128)(2,1)S(1)}, bf16[2,320,128]{2,1,0:T(8,128)(2,1)S(1)}, u32[]{:S(2)}, u32[]{:S(2)}) %collective-permute-start.19) | collective-permute-done | bytes 163872 | tf_op jit(solution)/shard_map/ppermute | solution.py:26
  63.8 0.7 shard_map.77
  64.5 1.6 %shard_map.78 = (f32[256,1280]{1,0:T(8,128)S(1)}, f32[256,1280]{1,0:T(8,128)S(1)}, bf16[320,1280]{1,0:T(8,128)(2,1)S(1)}, bf16[192,1280]{1,0:T(8,128)(2,1)S(1)}) custom-call(s32[1]{0:T(128)} %bitcast.me, bf16[2,320,512]{2,1,0:T(8,128)(2,1)S(1)} %get-tuple-element.40.full, bf16[160,1280]{1,0:T(8,128)(2,1)S(1)} %bitcast.6, bf16[160,1280]{1,0:T(8,128)(2,1)S(1)} %copy-done.1, ...), custom_call_target="tpu_custom_call" | custom-call | flops 838860800 | bytes 1048576 | tf_op jit(solution)/shard_map/pallas_call | solution.py:55
  66.1 0.1 collective-permute-start.20
  66.2 1.9 %collective-permute-done.20 = bf16[192,1280]{1,0:T(8,128)(2,1)S(1)} collective-permute-done((bf16[192,1280]{1,0:T(8,128)(2,1)S(1)}, bf16[192,1280]{1,0:T(8,128)(2,1)S(1)}, u32[]{:S(2)}, u32[]{:S(2)}) %collective-permute-start.20) | collective-permute-done | bytes 491552 | tf_op jit(solution)/shard_map/ppermute | solution.py:26
  68.0 0.1 collective-permute-start.21
  68.1 0.1 convert_element_type.58
  68.2 0.1 fusion.3
  68.3 1.7 %collective-permute-start.23 = (bf16[96,1280]{1,0:T(8,128)(2,1)S(1)}, bf16[96,1280]{1,0:T(8,128)(2,1)S(1)}, u32[]{:S(2)}, u32[]{:S(2)}) collective-permute-start(bf16[96,1280]{1,0:T(8,128)(2,1)S(1)} %fusion.3), channel_id=1, source_target_pairs={{0,8},{8,0},{16,24},{24,16},{1,9},{9,1},{17,25},{25,17},{2,10},{10... | collective-permute-start | bytes 737288 | tf_op jit(solution)/shard_map/ppermute | solution.py:30
  70.0 1.4 %collective-permute-start.26 = (bf16[320,1280]{1,0:T(8,128)(2,1)S(1)}, bf16[320,1280]{1,0:T(8,128)(2,1)S(1)}, u32[]{:S(2)}, u32[]{:S(2)}) collective-permute-start(bf16[320,1280]{1,0:T(8,128)(2,1)S(1)} %get-tuple-element.54), channel_id=1, source_target_pairs={{0,24},{24,0},{8,16},{16,8},{1,25},{25,1},{9,17},{17,9},{2,26},{26... | collective-permute-start | bytes 2457608 | tf_op jit(solution)/shard_map/ppermute | solution.py:34
  71.4 0.6 shard_map.79
  72.0 4.6 %collective-permute-done.23 = bf16[96,1280]{1,0:T(8,128)(2,1)S(1)} collective-permute-done((bf16[96,1280]{1,0:T(8,128)(2,1)S(1)}, bf16[96,1280]{1,0:T(8,128)(2,1)S(1)}, u32[]{:S(2)}, u32[]{:S(2)}) %collective-permute-start.23) | collective-permute-done | bytes 245792 | tf_op jit(solution)/shard_map/ppermute | solution.py:30
  76.6 0.1 fusion.2
  76.7 0.1 convert_element_type.57
  76.8 0.1 fusion
  76.9 1.7 %collective-permute-start.22 = (bf16[160,1280]{1,0:T(8,128)(2,1)S(1)}, bf16[160,1280]{1,0:T(8,128)(2,1)S(1)}, u32[]{:S(2)}, u32[]{:S(2)}) collective-permute-start(bf16[160,1280]{1,0:T(8,128)(2,1)S(1)} %fusion), channel_id=1, source_target_pairs={{0,8},{8,0},{16,24},{24,16},{1,9},{9,1},{17,25},{25,17},{2,10},{10... | collective-permute-start | bytes 1228808 | tf_op jit(solution)/shard_map/ppermute | solution.py:30
  78.6 3.2 %collective-permute-start.28 = (bf16[32,1280]{1,0:T(8,128)(2,1)S(1)}, bf16[32,1280]{1,0:T(8,128)(2,1)S(1)}, u32[]{:S(2)}, u32[]{:S(2)}) collective-permute-start(bf16[32,1280]{1,0:T(8,128)(2,1)S(1)} %get-tuple-element.62), channel_id=1, source_target_pairs={{0,224},{32,0},{64,32},{96,64},{128,96},{160,128},{192,160},{224,1... | collective-permute-start | bytes 245768 | tf_op jit(solution)/shard_map/ppermute | solution.py:26
  81.8 6.1 %collective-permute-done.22 = bf16[160,1280]{1,0:T(8,128)(2,1)S(1)} collective-permute-done((bf16[160,1280]{1,0:T(8,128)(2,1)S(1)}, bf16[160,1280]{1,0:T(8,128)(2,1)S(1)}, u32[]{:S(2)}, u32[]{:S(2)}) %collective-permute-start.22) | collective-permute-done | bytes 409632 | tf_op jit(solution)/shard_map/ppermute | solution.py:30
  87.9 0.1 convert_add_fusion.1
  88.0 1.0 collective-permute-done.25
  89.1 0.1 collective-permute-start.27
  89.2 1.0 %collective-permute-done.26 = bf16[320,1280]{1,0:T(8,128)(2,1)S(1)} collective-permute-done((bf16[320,1280]{1,0:T(8,128)(2,1)S(1)}, bf16[320,1280]{1,0:T(8,128)(2,1)S(1)}, u32[]{:S(2)}, u32[]{:S(2)}) %collective-permute-start.26) | collective-permute-done | bytes 819232 | tf_op jit(solution)/shard_map/ppermute | solution.py:34
  90.2 3.6 %collective-permute-start.31 = (bf16[32,1280]{1,0:T(8,128)(2,1)S(1)}, bf16[32,1280]{1,0:T(8,128)(2,1)S(1)}, u32[]{:S(2)}, u32[]{:S(2)}) collective-permute-start(bf16[32,1280]{1,0:T(8,128)(2,1)S(1)} %get-tuple-element.66), channel_id=1, source_target_pairs={{0,224},{32,0},{64,32},{96,64},{128,96},{160,128},{192,160},{224,1... | collective-permute-start | bytes 245768 | tf_op jit(solution)/shard_map/ppermute | solution.py:26
  93.9 1.6 %collective-permute-start.29 = (bf16[32,1280]{1,0:T(8,128)(2,1)S(1)}, bf16[32,1280]{1,0:T(8,128)(2,1)S(1)}, u32[]{:S(2)}, u32[]{:S(2)}) collective-permute-start(bf16[32,1280]{1,0:T(8,128)(2,1)S(1)} %get-tuple-element.60), channel_id=1, source_target_pairs={{0,192},{32,224},{64,0},{96,32},{128,64},{160,96},{192,128},{224,1... | collective-permute-start | bytes 245768 | tf_op jit(solution)/shard_map/ppermute | solution.py:26
  95.4 1.3 %convert_add_fusion = (f32[160,1280]{1,0:T(8,128)}, f32[1280,160]{0,1:T(8,128)}) fusion(f32[160,1280]{1,0:T(8,128)S(1)} %get-tuple-element.48, bf16[320,1280]{1,0:T(8,128)(2,1)S(1)} %collective-permute-done.26, f32[160,1280]{1,0:T(8,128)S(1)} %get-tuple-element.57), kind=kLoop, calls=%fused_computation.3 | loop fusion | flops 819200 | bytes 4096000 | tf_op jit(solution)/shard_map/add | solution.py:204
  96.7 2.8 %collective-permute-done.30 = bf16[32,1280]{1,0:T(8,128)(2,1)S(1)} collective-permute-done((bf16[32,1280]{1,0:T(8,128)(2,1)S(1)}, bf16[32,1280]{1,0:T(8,128)(2,1)S(1)}, u32[]{:S(2)}, u32[]{:S(2)}) %collective-permute-start.30) | collective-permute-done | bytes 81952 | tf_op jit(solution)/shard_map/ppermute | solution.py:26
  99.5 0.1 collective-permute-done.29
  99.6 0.6 fusion.8
  (32 shorter events, 0.2 us)
Async XLA Ops:
  2.2 16.1 %collective-permute-start = (bf16[32,1280]{1,0:T(8,128)(2,1)S(1)}, bf16[32,1280]{1,0:T(8,128)(2,1)S(1)}, u32[]{:S(2)}, u32[]{:S(2)}) collective-permute-start(bf16[32,1280]{1,0:T(8,128)(2,1)S(1)} %get-tuple-element.69), channel_id=1, source_target_pairs={{0,224},{32,0},{64,32},{96,64},{128,96},{160,128},{192,160},{224,1... | collective-permute-start | bytes 245768 | tf_op jit(solution)/shard_map/ppermute | solution.py:26
  8.1 10.2 %collective-permute-start.1 = (bf16[32,1280]{1,0:T(8,128)(2,1)S(1)}, bf16[32,1280]{1,0:T(8,128)(2,1)S(1)}, u32[]{:S(2)}, u32[]{:S(2)}) collective-permute-start(bf16[32,1280]{1,0:T(8,128)(2,1)S(1)} %get-tuple-element.69), channel_id=1, source_target_pairs={{0,32},{32,64},{64,96},{96,128},{128,160},{160,192},{192,224},{224... | collective-permute-start | bytes 245768 | tf_op jit(solution)/shard_map/ppermute | solution.py:26
  8.1 5.8 %collective-permute-start.2 = (bf16[32,1280]{1,0:T(8,128)(2,1)S(1)}, bf16[32,1280]{1,0:T(8,128)(2,1)S(1)}, u32[]{:S(2)}, u32[]{:S(2)}) collective-permute-start(bf16[32,1280]{1,0:T(8,128)(2,1)S(1)} %get-tuple-element.69), channel_id=1, source_target_pairs={{0,192},{32,224},{64,0},{96,32},{128,64},{160,96},{192,128},{224,1... | collective-permute-start | bytes 245768 | tf_op jit(solution)/shard_map/ppermute | solution.py:26
  10.5 7.8 %collective-permute-start.3 = (bf16[32,1280]{1,0:T(8,128)(2,1)S(1)}, bf16[32,1280]{1,0:T(8,128)(2,1)S(1)}, u32[]{:S(2)}, u32[]{:S(2)}) collective-permute-start(bf16[32,1280]{1,0:T(8,128)(2,1)S(1)} %get-tuple-element.69), channel_id=1, source_target_pairs={{0,64},{32,96},{64,128},{96,160},{128,192},{160,224},{192,0},{224,... | collective-permute-start | bytes 245768 | tf_op jit(solution)/shard_map/ppermute | solution.py:26
  11.0 24.4 %copy-start = (bf16[1280,160]{0,1:T(8,128)(2,1)S(1)}, bf16[1280,160]{0,1:T(8,128)(2,1)}, u32[]{:S(2)}) copy-start(bf16[1280,160]{0,1:T(8,128)(2,1)} %param.5) | copy-start | bytes 1228804
  11.0 24.4 %copy-start.1 = (bf16[160,1280]{1,0:T(8,128)(2,1)S(1)}, bf16[160,1280]{1,0:T(8,128)(2,1)}, u32[]{:S(2)}) copy-start(bf16[160,1280]{1,0:T(8,128)(2,1)} %wo.1) | copy-start | bytes 1228804
  12.2 19.2 %collective-permute-start.8 = (bf16[320,1280]{1,0:T(8,128)(2,1)S(1)}, bf16[320,1280]{1,0:T(8,128)(2,1)S(1)}, u32[]{:S(2)}, u32[]{:S(2)}) collective-permute-start(bf16[320,1280]{1,0:T(8,128)(2,1)S(1)} %pad_maximum_fusion), channel_id=1, source_target_pairs={{0,24},{24,0},{8,16},{16,8},{1,25},{25,1},{9,17},{17,9},{2,26},{26... | collective-permute-start | bytes 2457608 | tf_op jit(solution)/shard_map/ppermute | solution.py:34
  13.8 6.5 %collective-permute-start.4 = (bf16[32,1280]{1,0:T(8,128)(2,1)S(1)}, bf16[32,1280]{1,0:T(8,128)(2,1)S(1)}, u32[]{:S(2)}, u32[]{:S(2)}) collective-permute-start(bf16[32,1280]{1,0:T(8,128)(2,1)S(1)} %collective-permute-done.2), channel_id=1, source_target_pairs={{0,224},{32,0},{64,32},{96,64},{128,96},{160,128},{192,160},{224,1... | collective-permute-start | bytes 245768 | tf_op jit(solution)/shard_map/ppermute | solution.py:26
  18.4 11.6 %collective-permute-start.7 = (bf16[160,1280]{1,0:T(8,128)(2,1)S(1)}, bf16[160,1280]{1,0:T(8,128)(2,1)S(1)}, u32[]{:S(2)}, u32[]{:S(2)}) collective-permute-start(bf16[160,1280]{1,0:T(8,128)(2,1)S(1)} %constant_dynamic-update-slice_fusion.2.refs_0_), channel_id=1, source_target_pairs={{0,8},{8,0},{16,24},{24,16},{1,9},{9,1},{17,25},{25,17},{2,10},{10... | collective-permute-start | bytes 1228808 | tf_op jit(solution)/shard_map/ppermute | solution.py:30
  20.2 6.9 %collective-permute-start.6 = (bf16[32,1280]{1,0:T(8,128)(2,1)S(1)}, bf16[32,1280]{1,0:T(8,128)(2,1)S(1)}, u32[]{:S(2)}, u32[]{:S(2)}) collective-permute-start(bf16[32,1280]{1,0:T(8,128)(2,1)S(1)} %collective-permute-done.3), channel_id=1, source_target_pairs={{0,64},{32,96},{64,128},{96,160},{128,192},{160,224},{192,0},{224,... | collective-permute-start | bytes 245768 | tf_op jit(solution)/shard_map/ppermute | solution.py:26
  20.2 6.9 %collective-permute-start.5 = (bf16[32,1280]{1,0:T(8,128)(2,1)S(1)}, bf16[32,1280]{1,0:T(8,128)(2,1)S(1)}, u32[]{:S(2)}, u32[]{:S(2)}) collective-permute-start(bf16[32,1280]{1,0:T(8,128)(2,1)S(1)} %collective-permute-done.3), channel_id=1, source_target_pairs={{0,32},{32,64},{64,96},{96,128},{128,160},{160,192},{192,224},{224... | collective-permute-start | bytes 245768 | tf_op jit(solution)/shard_map/ppermute | solution.py:26
  27.2 6.4 %collective-permute-start.9 = (bf16[96,1280]{1,0:T(8,128)(2,1)S(1)}, bf16[96,1280]{1,0:T(8,128)(2,1)}, u32[]{:S(2)}, u32[]{:S(2)}) collective-permute-start(bf16[96,1280]{1,0:T(8,128)(2,1)S(1)} %constant_dynamic-update-slice_fusion.8.refs_1_), channel_id=1, source_target_pairs={{0,8},{8,0},{16,24},{24,16},{1,9},{9,1},{17,25},{25,17},{2,10},{10... | collective-permute-start | bytes 737288 | tf_op jit(solution)/shard_map/ppermute | solution.py:30
  28.7 4.8 %collective-permute-start.10 = (bf16[160,1280]{1,0:T(8,128)(2,1)S(1)}, bf16[160,1280]{1,0:T(8,128)(2,1)S(1)}, u32[]{:S(2)}, u32[]{:S(2)}) collective-permute-start(bf16[160,1280]{1,0:T(8,128)(2,1)S(1)} %constant_dynamic-update-slice_fusion.2.refs_0_), channel_id=1, source_target_pairs={{0,1},{1,0},{2,3},{3,2},{4,5},{5,4},{6,7},{7,6},{8,9},{9,8},{10,11... | collective-permute-start | bytes 1228808 | tf_op jit(solution)/shard_map/ppermute | solution.py:26
  31.5 3.9 %collective-permute-start.12 = (bf16[160,1280]{1,0:T(8,128)(2,1)S(1)}, bf16[160,1280]{1,0:T(8,128)(2,1)S(1)}, u32[]{:S(2)}, u32[]{:S(2)}) collective-permute-start(bf16[160,1280]{1,0:T(8,128)(2,1)S(1)} %collective-permute-done.7.refs_2_), channel_id=1, source_target_pairs={{0,1},{1,0},{2,3},{3,2},{4,5},{5,4},{6,7},{7,6},{8,9},{9,8},{10,11... | collective-permute-start | bytes 1228808 | tf_op jit(solution)/shard_map/ppermute | solution.py:26
  31.5 2.1 %collective-permute-start.11 = (bf16[96,1280]{1,0:T(8,128)(2,1)S(1)}, bf16[96,1280]{1,0:T(8,128)(2,1)}, u32[]{:S(2)}, u32[]{:S(2)}) collective-permute-start(bf16[96,1280]{1,0:T(8,128)(2,1)S(1)} %constant_dynamic-update-slice_fusion.8.refs_1_), channel_id=1, source_target_pairs={{0,1},{1,0},{2,3},{3,2},{4,5},{5,4},{6,7},{7,6},{8,9},{9,8},{10,11... | collective-permute-start | bytes 737288 | tf_op jit(solution)/shard_map/ppermute | solution.py:26
  33.6 1.9 %collective-permute-start.13 = (bf16[96,1280]{1,0:T(8,128)(2,1)}, bf16[96,1280]{1,0:T(8,128)(2,1)}, u32[]{:S(2)}, u32[]{:S(2)}) collective-permute-start(bf16[96,1280]{1,0:T(8,128)(2,1)} %collective-permute-done.9.refs_3_), channel_id=1, source_target_pairs={{0,1},{1,0},{2,3},{3,2},{4,5},{5,4},{6,7},{7,6},{8,9},{9,8},{10,11... | collective-permute-start | bytes 737288 | tf_op jit(solution)/shard_map/ppermute | solution.py:26
  38.6 7.6 %collective-permute-start.14 = (bf16[2,320,128]{2,1,0:T(8,128)(2,1)S(1)}, bf16[2,320,128]{2,1,0:T(8,128)(2,1)S(1)}, u32[]{:S(2)}, u32[]{:S(2)}) collective-permute-start(bf16[2,320,128]{2,1,0:T(8,128)(2,1)S(1)} %get-tuple-element.35), channel_id=1, source_target_pairs={{0,2},{2,4},{4,6},{6,0},{1,3},{3,5},{5,7},{7,1},{8,10},{10,12},{12... | collective-permute-start | bytes 491528 | tf_op jit(solution)/shard_map/ppermute | solution.py:26
  40.2 10.6 %collective-permute-start.15 = (bf16[2,320,128]{2,1,0:T(8,128)(2,1)S(1)}, bf16[2,320,128]{2,1,0:T(8,128)(2,1)S(1)}, u32[]{:S(2)}, u32[]{:S(2)}) collective-permute-start(bf16[2,320,128]{2,1,0:T(8,128)(2,1)S(1)} %get-tuple-element.36), channel_id=1, source_target_pairs={{0,4},{2,6},{4,0},{6,2},{1,5},{3,7},{5,1},{7,3},{8,12},{10,14},{12... | collective-permute-start | bytes 491528 | tf_op jit(solution)/shard_map/ppermute | solution.py:26
  43.1 7.7 %collective-permute-start.16 = (bf16[2,320,128]{2,1,0:T(8,128)(2,1)S(1)}, bf16[2,320,128]{2,1,0:T(8,128)(2,1)S(1)}, u32[]{:S(2)}, u32[]{:S(2)}) collective-permute-start(bf16[2,320,128]{2,1,0:T(8,128)(2,1)S(1)} %get-tuple-element.37), channel_id=1, source_target_pairs={{0,6},{2,0},{4,2},{6,4},{1,7},{3,1},{5,3},{7,5},{8,14},{10,8},{12,... | collective-permute-start | bytes 491528 | tf_op jit(solution)/shard_map/ppermute | solution.py:26
  51.0 9.1 %collective-permute-start.17 = (bf16[2,320,128]{2,1,0:T(8,128)(2,1)S(1)}, bf16[2,320,128]{2,1,0:T(8,128)(2,1)S(1)}, u32[]{:S(2)}, u32[]{:S(2)}) collective-permute-start(bf16[2,320,128]{2,1,0:T(8,128)(2,1)S(1)} %shard_map.76.b0), channel_id=1, source_target_pairs={{0,6},{2,0},{4,2},{6,4},{1,7},{3,1},{5,3},{7,5},{8,14},{10,8},{12,... | collective-permute-start | bytes 491528 | tf_op jit(solution)/shard_map/ppermute | solution.py:26
  53.2 8.7 %collective-permute-start.18 = (bf16[2,320,128]{2,1,0:T(8,128)(2,1)S(1)}, bf16[2,320,128]{2,1,0:T(8,128)(2,1)S(1)}, u32[]{:S(2)}, u32[]{:S(2)}) collective-permute-start(bf16[2,320,128]{2,1,0:T(8,128)(2,1)S(1)} %shard_map.76.b0), channel_id=1, source_target_pairs={{0,4},{2,6},{4,0},{6,2},{1,5},{3,7},{5,1},{7,3},{8,12},{10,14},{12... | collective-permute-start | bytes 491528 | tf_op jit(solution)/shard_map/ppermute | solution.py:26
  54.4 9.4 %collective-permute-start.19 = (bf16[2,320,128]{2,1,0:T(8,128)(2,1)S(1)}, bf16[2,320,128]{2,1,0:T(8,128)(2,1)S(1)}, u32[]{:S(2)}, u32[]{:S(2)}) collective-permute-start(bf16[2,320,128]{2,1,0:T(8,128)(2,1)S(1)} %shard_map.76.b0), channel_id=1, source_target_pairs={{0,2},{2,4},{4,6},{6,0},{1,3},{3,5},{5,7},{7,1},{8,10},{10,12},{12... | collective-permute-start | bytes 491528 | tf_op jit(solution)/shard_map/ppermute | solution.py:26
  66.1 2.0 %collective-permute-start.20 = (bf16[192,1280]{1,0:T(8,128)(2,1)S(1)}, bf16[192,1280]{1,0:T(8,128)(2,1)S(1)}, u32[]{:S(2)}, u32[]{:S(2)}) collective-permute-start(bf16[192,1280]{1,0:T(8,128)(2,1)S(1)} %get-tuple-element.43), channel_id=1, source_target_pairs={{0,1},{1,0},{2,3},{3,2},{4,5},{5,4},{6,7},{7,6},{8,9},{9,8},{10,11... | collective-permute-start | bytes 1474568 | tf_op jit(solution)/shard_map/ppermute | solution.py:26
  68.0 8.7 %collective-permute-start.21 = (bf16[320,1280]{1,0:T(8,128)(2,1)S(1)}, bf16[320,1280]{1,0:T(8,128)(2,1)S(1)}, u32[]{:S(2)}, u32[]{:S(2)}) collective-permute-start(bf16[320,1280]{1,0:T(8,128)(2,1)S(1)} %get-tuple-element.44), channel_id=1, source_target_pairs={{0,1},{1,0},{2,3},{3,2},{4,5},{5,4},{6,7},{7,6},{8,9},{9,8},{10,11... | collective-permute-start | bytes 2457608 | tf_op jit(solution)/shard_map/ppermute | solution.py:26
  68.3 8.3 %collective-permute-start.23 = (bf16[96,1280]{1,0:T(8,128)(2,1)S(1)}, bf16[96,1280]{1,0:T(8,128)(2,1)S(1)}, u32[]{:S(2)}, u32[]{:S(2)}) collective-permute-start(bf16[96,1280]{1,0:T(8,128)(2,1)S(1)} %fusion.3), channel_id=1, source_target_pairs={{0,8},{8,0},{16,24},{24,16},{1,9},{9,1},{17,25},{25,17},{2,10},{10... | collective-permute-start | bytes 737288 | tf_op jit(solution)/shard_map/ppermute | solution.py:30
  70.0 20.2 %collective-permute-start.26 = (bf16[320,1280]{1,0:T(8,128)(2,1)S(1)}, bf16[320,1280]{1,0:T(8,128)(2,1)S(1)}, u32[]{:S(2)}, u32[]{:S(2)}) collective-permute-start(bf16[320,1280]{1,0:T(8,128)(2,1)S(1)} %get-tuple-element.54), channel_id=1, source_target_pairs={{0,24},{24,0},{8,16},{16,8},{1,25},{25,1},{9,17},{17,9},{2,26},{26... | collective-permute-start | bytes 2457608 | tf_op jit(solution)/shard_map/ppermute | solution.py:34
  76.9 11.0 %collective-permute-start.22 = (bf16[160,1280]{1,0:T(8,128)(2,1)S(1)}, bf16[160,1280]{1,0:T(8,128)(2,1)S(1)}, u32[]{:S(2)}, u32[]{:S(2)}) collective-permute-start(bf16[160,1280]{1,0:T(8,128)(2,1)S(1)} %fusion), channel_id=1, source_target_pairs={{0,8},{8,0},{16,24},{24,16},{1,9},{9,1},{17,25},{25,17},{2,10},{10... | collective-permute-start | bytes 1228808 | tf_op jit(solution)/shard_map/ppermute | solution.py:30
  78.6 9.5 %collective-permute-start.28 = (bf16[32,1280]{1,0:T(8,128)(2,1)S(1)}, bf16[32,1280]{1,0:T(8,128)(2,1)S(1)}, u32[]{:S(2)}, u32[]{:S(2)}) collective-permute-start(bf16[32,1280]{1,0:T(8,128)(2,1)S(1)} %get-tuple-element.62), channel_id=1, source_target_pairs={{0,224},{32,0},{64,32},{96,64},{128,96},{160,128},{192,160},{224,1... | collective-permute-start | bytes 245768 | tf_op jit(solution)/shard_map/ppermute | solution.py:26
  81.8 7.2 %collective-permute-start.25 = (bf16[32,1280]{1,0:T(8,128)(2,1)S(1)}, bf16[32,1280]{1,0:T(8,128)(2,1)S(1)}, u32[]{:S(2)}, u32[]{:S(2)}) collective-permute-start(bf16[32,1280]{1,0:T(8,128)(2,1)S(1)} %get-tuple-element.63), channel_id=1, source_target_pairs={{0,64},{32,96},{64,128},{96,160},{128,192},{160,224},{192,0},{224,... | collective-permute-start | bytes 245768 | tf_op jit(solution)/shard_map/ppermute | solution.py:26
  81.8 7.2 %collective-permute-start.24 = (bf16[32,1280]{1,0:T(8,128)(2,1)S(1)}, bf16[32,1280]{1,0:T(8,128)(2,1)S(1)}, u32[]{:S(2)}, u32[]{:S(2)}) collective-permute-start(bf16[32,1280]{1,0:T(8,128)(2,1)S(1)} %get-tuple-element.64), channel_id=1, source_target_pairs={{0,32},{32,64},{64,96},{96,128},{128,160},{160,192},{192,224},{224... | collective-permute-start | bytes 245768 | tf_op jit(solution)/shard_map/ppermute | solution.py:26
  89.1 10.5 %collective-permute-start.27 = (bf16[32,1280]{1,0:T(8,128)(2,1)S(1)}, bf16[32,1280]{1,0:T(8,128)(2,1)S(1)}, u32[]{:S(2)}, u32[]{:S(2)}) collective-permute-start(bf16[32,1280]{1,0:T(8,128)(2,1)S(1)} %get-tuple-element.61), channel_id=1, source_target_pairs={{0,64},{32,96},{64,128},{96,160},{128,192},{160,224},{192,0},{224,... | collective-permute-start | bytes 245768 | tf_op jit(solution)/shard_map/ppermute | solution.py:26
  90.2 6.5 %collective-permute-start.31 = (bf16[32,1280]{1,0:T(8,128)(2,1)S(1)}, bf16[32,1280]{1,0:T(8,128)(2,1)S(1)}, u32[]{:S(2)}, u32[]{:S(2)}) collective-permute-start(bf16[32,1280]{1,0:T(8,128)(2,1)S(1)} %get-tuple-element.66), channel_id=1, source_target_pairs={{0,224},{32,0},{64,32},{96,64},{128,96},{160,128},{192,160},{224,1... | collective-permute-start | bytes 245768 | tf_op jit(solution)/shard_map/ppermute | solution.py:26
  93.9 5.7 %collective-permute-start.30 = (bf16[32,1280]{1,0:T(8,128)(2,1)S(1)}, bf16[32,1280]{1,0:T(8,128)(2,1)S(1)}, u32[]{:S(2)}, u32[]{:S(2)}) collective-permute-start(bf16[32,1280]{1,0:T(8,128)(2,1)S(1)} %get-tuple-element.65), channel_id=1, source_target_pairs={{0,32},{32,64},{64,96},{96,128},{128,160},{160,192},{192,224},{224... | collective-permute-start | bytes 245768 | tf_op jit(solution)/shard_map/ppermute | solution.py:26
  93.9 5.7 %collective-permute-start.29 = (bf16[32,1280]{1,0:T(8,128)(2,1)S(1)}, bf16[32,1280]{1,0:T(8,128)(2,1)S(1)}, u32[]{:S(2)}, u32[]{:S(2)}) collective-permute-start(bf16[32,1280]{1,0:T(8,128)(2,1)S(1)} %get-tuple-element.60), channel_id=1, source_target_pairs={{0,192},{32,224},{64,0},{96,32},{128,64},{160,96},{192,128},{224,1... | collective-permute-start | bytes 245768 | tf_op jit(solution)/shard_map/ppermute | solution.py:26

commit v7 on v6

--- a/solution.py
+++ b/solution.py
@@ -65,23 +65,32 @@
     )
 
 
+def products(value_of, wi, wo, w_pair, part):
+    h = wi.shape[0]
+    for s, w in enumerate((wi, wo)):
+        part[s, :h] = dot(w[...], value_of(s), 1, 1).astype(part.dtype)
+        part[s, h:] = dot(w_pair[s * h : s * h + h], value_of(s), 1, 1).astype(part.dtype)
+
+
+def quarter_of(tok, cot, index):
+    rows = pl.ds(pl.multiple_of(index % 4 * 128, 128), 128)
+    return lambda s: (tok, cot)[s][rows]
+
+
 def up_kernel(me, *refs):
-    quarters, wi, wo, w_pair = refs[:8], refs[8], refs[9], refs[10]
-    tok, cot, parts, whole = refs[11], refs[12], refs[13:17], refs[17]
-    h = wi.shape[0]
+    quarters, (wi, wo, w_pair, tok, cot), parts = refs[:8], refs[8:13], refs[13:]
     for q in range(4):
         for j in range(8):
             ref, i = (quarters[2 * q], j) if j < HEAD else (quarters[2 * q + 1], j - HEAD)
             row = q * 128 + j * 16
             tok[row : row + 16] = ref[i * 32 : i * 32 + 16]
             cot[row : row + 16] = ref[i * 32 + 16 : i * 32 + 32]
-    for s, (w, value) in enumerate(((wi, tok), (wo, cot))):
-        for i, left in enumerate((w[...], w_pair[s * h : s * h + h])):
-            total = dot(left, value[...], 1, 1)
-            for q in range(4):
-                whole[q, s, i * h : i * h + h] = total[:, q * 128 : q * 128 + 128]
-    for k, part in enumerate(parts):
-        part[...] = whole[(me[0] + k) % 4].astype(part.dtype)
+    for k, part in zip((2, 1, 3), parts):
+        products(quarter_of(tok, cot, me[0] + k), wi, wo, w_pair, part)
+
+
+def mine_kernel(me, tok, cot, wi, wo, w_pair, part):
+    products(quarter_of(tok, cot, me[0]), wi, wo, w_pair, part)
 
 
 def act_kernel(me, p0, p1, p2, p3, out):
@@ -114,9 +123,9 @@
                     tail[row : row + 16] = piece.astype(BF)
 
 
-def pair_kernel(me, b0, b1, b2, b3, tok, cot, full, out):
+def pair_kernel(me, b0, b2, b1, b3, tok, cot, full, out):
     h = full.shape[1] // 2
-    for k, block in enumerate((b0, b1, b2, b3)):
+    for k, block in ((0, b0), (2, b2), (1, b1), (3, b3)):
         lane = pl.multiple_of(((me[0] + k) % 4) * 128, 128)
         full[:, :, pl.ds(lane, 128)] = block[...]
     out[:h] = dot(full[0, h:], cot[...], 1, 0).astype(BF)
@@ -147,22 +156,19 @@
     far_h = token_pair(near_h)
     z[4] = send(after(z[6], near_h), "z", 2)
     near_t = cat([z[k] for k in ORDER[HEAD:]])
-    far_t = token_pair(near_t)
-    far_h = after(far_h, w_pair)
+    far_t = after(token_pair(near_t), w_pair)
     quarters = [near_h, near_t, far_h, far_t]
     quarters += [send(value, "col", 1) for value in quarters]
 
     part, rounded = shape((2, 2 * h, 128), F32), shape((2, 2 * h, 128), BF)
+    weights = [w_in_t, w_out, w_pair]
     tok, cot, *parts = call(
-        up_kernel,
-        [shape((512, d), BF)] * 2 + [part] + [rounded] * 3,
-        [me, *quarters, w_in_t, w_out, w_pair],
-        2 * flops,
-        [pltpu.VMEM((4, 2, 2 * h, 128), F32)],
-    )
-    parts[1:] = [send(parts[k], "row", k) for k in (1, 2, 3)]
+        up_kernel, [shape((512, d), BF)] * 2 + [rounded] * 3, [me, *quarters, *weights], flops
+    )
+    mine = call(mine_kernel, [part], [me, after(tok, parts[0]), cot, *weights], flops)
+    parts = mine + [send(value, "row", k) for k, value in zip((2, 1, 3), parts)]
     (block,) = call(act_kernel, [rounded], [me, *parts])
-    blocks = [block] + [send(block, "row", -k) for k in (1, 2, 3)]
+    blocks = [block] + [send(block, "row", -k) for k in (2, 1, 3)]
 
     sums = shape((256, d), F32)
     full, pair = call(
@@ -187,8 +193,9 @@
     grad_out, grad_in_t = call(
         own_kernel, [shape((h, d), F32)] * 2, [me, full, after(tok, far_t), cot], flops
     )
-    far_t = token_pair(far_t)
-    far_h = token_pair(after((far[:cut] + head[:cut]).astype(BF), grad_out))
+    far_h = after((far[:cut] + head[:cut]).astype(BF), grad_out)
+    far_t = after(token_pair(far_t), far_h)
+    far_h = token_pair(far_h)
     third = (near[cut:] + tail[rest:] + far_t.astype(F32)).astype(BF)
     near, head, far_h = after((near, head, far_h), third)
     up, down = send(third[:32], "z", 1), send(third[32:64], "z", -1)

time: 101 us -> 97.7 us (0.967)
  waiting for transfers between devices: 45.5 us -> 43 us
  starting transfers between devices: 42.4 us -> 41.2 us
    ppermute x26, waiting for transfers between devices: 29.5 us -> 26.1 us  [send(): lax.ppermute(value, axis, [(i, (i + shift) % size) for i in range(size)])]
    ppermute x26, starting transfers between devices: 32.5 us -> 31.2 us  [send(): lax.ppermute(value, axis, [(i, (i + shift) % size) for i in range(size)])]
    pallas_call x5 -> x6, Pallas kernels: 6.14 us -> 6.31 us  [call(): return list(kernel(*args))]
where the time goes in v7:
time: 97.7 us; the launch traced here: 96.8 us
  waiting for transfers between devices  43 us (44%)
  starting transfers between devices  41.2 us (42%)
  Pallas kernels  6.31 us (6%)
  other arithmetic  3.11 us (3%)
  local copies, waits for them, and re-layouts  2.31 us (2%)
    ppermute x26, starting transfers between devices, send(): lax.ppermute(value, axis, [(i, (i + shift) % size) for i in range(size)])  31.2 us
    ppermute x26, waiting for transfers between devices, send(): lax.ppermute(value, axis, [(i, (i + shift) % size) for i in range(size)])  26.1 us
    ppermute x4, waiting for transfers between devices, token_pair(): return lax.ppermute(value, 'x', [(0, 1), (1, 0), (2, 3), (3, 2)])  13.4 us
    ppermute x4, starting transfers between devices, token_pair(): return lax.ppermute(value, 'x', [(0, 1), (1, 0), (2, 3), (3, 2)])  7.01 us
    pallas_call x6, Pallas kernels, call(): return list(kernel(*args))  6.31 us
    ppermute x2, waiting for transfers between devices, weight_pair(): return lax.ppermute(value, 'x', [(0, 3), (3, 0), (1, 2), (2, 1)])  3.52 us
    ppermute x2, starting transfers between devices, weight_pair(): return lax.ppermute(value, 'x', [(0, 3), (3, 0), (1, 2), (2, 1)])  2.99 us
  transfers between devices with their start and end apart: 32, of which 17 were waited for; matrix products, arithmetic and copies ran while one was open for 3% of the time, Pallas kernels for 1%

profile of v7, /device:TPU:2, one launch (start us, length us, event | category | flops | bytes accessed | tf_op | source)
XLA Modules:
  0.0 96.8 jit_solution(13090595167042519727)
XLA Ops:
  0.6 0.8 constant_dynamic-update-slice_fusion.1
  1.4 0.8 constant_dynamic-update-slice_fusion
  2.2 5.9 %collective-permute-start = (bf16[32,1280]{1,0:T(8,128)(2,1)S(1)}, bf16[32,1280]{1,0:T(8,128)(2,1)S(1)}, u32[]{:S(2)}, u32[]{:S(2)}) collective-permute-start(bf16[32,1280]{1,0:T(8,128)(2,1)S(1)} %get-tuple-element.71), channel_id=1, source_target_pairs={{0,224},{32,0},{64,32},{96,64},{128,96},{160,128},{192,160},{224,1... | collective-permute-start | bytes 245768 | tf_op jit(solution)/shard_map/ppermute | solution.py:26
  8.1 0.0 collective-permute-start.1
  8.1 2.5 %collective-permute-start.2 = (bf16[32,1280]{1,0:T(8,128)(2,1)S(1)}, bf16[32,1280]{1,0:T(8,128)(2,1)S(1)}, u32[]{:S(2)}, u32[]{:S(2)}) collective-permute-start(bf16[32,1280]{1,0:T(8,128)(2,1)S(1)} %get-tuple-element.71), channel_id=1, source_target_pairs={{0,192},{32,224},{64,0},{96,32},{128,64},{160,96},{192,128},{224,1... | collective-permute-start | bytes 245768 | tf_op jit(solution)/shard_map/ppermute | solution.py:26
  10.5 0.5 collective-permute-start.3
  11.0 1.3 %pad_maximum_fusion = bf16[320,1280]{1,0:T(8,128)(2,1)S(1)} fusion(bf16[160,1280]{1,0:T(8,128)(2,1)} %wo.3, bf16[160,1280]{1,0:T(8,128)(2,1)} %bitcast.4), kind=kLoop, calls=%fused_computation.2 | loop fusion | flops 1638400 | bytes 1638400 | tf_op jit(solution)/shard_map/concatenate | solution.py:59
  12.2 1.6 %collective-permute-start.9 = (bf16[320,1280]{1,0:T(8,128)(2,1)S(1)}, bf16[320,1280]{1,0:T(8,128)(2,1)S(1)}, u32[]{:S(2)}, u32[]{:S(2)}) collective-permute-start(bf16[320,1280]{1,0:T(8,128)(2,1)S(1)} %pad_maximum_fusion), channel_id=1, source_target_pairs={{0,24},{24,0},{8,16},{16,8},{1,25},{25,1},{9,17},{17,9},{2,26},{26... | collective-permute-start | bytes 2457608 | tf_op jit(solution)/shard_map/ppermute | solution.py:34
  13.8 4.4 %collective-permute-start.4 = (bf16[32,1280]{1,0:T(8,128)(2,1)S(1)}, bf16[32,1280]{1,0:T(8,128)(2,1)S(1)}, u32[]{:S(2)}, u32[]{:S(2)}) collective-permute-start(bf16[32,1280]{1,0:T(8,128)(2,1)S(1)} %collective-permute-done.2), channel_id=1, source_target_pairs={{0,224},{32,0},{64,32},{96,64},{128,96},{160,128},{192,160},{224,1... | collective-permute-start | bytes 245768 | tf_op jit(solution)/shard_map/ppermute | solution.py:26
  18.3 0.0 collective-permute-done
  18.3 0.0 collective-permute-done.3
  18.4 1.9 %collective-permute-start.7 = (bf16[160,1280]{1,0:T(8,128)(2,1)S(1)}, bf16[160,1280]{1,0:T(8,128)(2,1)S(1)}, u32[]{:S(2)}, u32[]{:S(2)}) collective-permute-start(bf16[160,1280]{1,0:T(8,128)(2,1)S(1)} %constant_dynamic-update-slice_fusion.2.refs_0_), channel_id=1, source_target_pairs={{0,8},{8,0},{16,24},{24,16},{1,9},{9,1},{17,25},{25,17},{2,10},{10... | collective-permute-start | bytes 1228808 | tf_op jit(solution)/shard_map/ppermute | solution.py:30
  20.2 0.1 collective-permute-start.5
  20.3 0.0 collective-permute-done.4
  20.3 6.8 %collective-permute-done.5 = bf16[32,1280]{1,0:T(8,128)(2,1)S(1)} collective-permute-done((bf16[32,1280]{1,0:T(8,128)(2,1)S(1)}, bf16[32,1280]{1,0:T(8,128)(2,1)S(1)}, u32[]{:S(2)}, u32[]{:S(2)}) %collective-permute-start.5) | collective-permute-done | bytes 81952 | tf_op jit(solution)/shard_map/ppermute | solution.py:26
  27.2 1.6 %collective-permute-start.8 = (bf16[96,1280]{1,0:T(8,128)(2,1)S(1)}, bf16[96,1280]{1,0:T(8,128)(2,1)}, u32[]{:S(2)}, u32[]{:S(2)}) collective-permute-start(bf16[96,1280]{1,0:T(8,128)(2,1)S(1)} %constant_dynamic-update-slice_fusion.8.refs_1_), channel_id=1, source_target_pairs={{0,8},{8,0},{16,24},{24,16},{1,9},{9,1},{17,25},{25,17},{2,10},{10... | collective-permute-start | bytes 737288 | tf_op jit(solution)/shard_map/ppermute | solution.py:30
  28.8 1.2 %collective-permute-done.7.refs_2_ = bf16[160,1280]{1,0:T(8,128)(2,1)S(1)} collective-permute-done((bf16[160,1280]{1,0:T(8,128)(2,1)S(1)}, bf16[160,1280]{1,0:T(8,128)(2,1)S(1)}, u32[]{:S(2)}, u32[]{:S(2)}) %collective-permute-start.7) | collective-permute-done | bytes 409632 | tf_op jit(solution)/shard_map/ppermute | solution.py:30
  30.0 0.0 collective-permute-start.12
  30.0 0.5 collective-permute-start.11
  30.5 3.1 %collective-permute-done.8.refs_3_ = bf16[96,1280]{1,0:T(8,128)(2,1)} collective-permute-done((bf16[96,1280]{1,0:T(8,128)(2,1)S(1)}, bf16[96,1280]{1,0:T(8,128)(2,1)}, u32[]{:S(2)}, u32[]{:S(2)}) %collective-permute-start.8) | collective-permute-done | bytes 245792 | tf_op jit(solution)/shard_map/ppermute | solution.py:30
  33.6 1.8 %collective-permute-done.13.refs_7_ = bf16[96,1280]{1,0:T(8,128)(2,1)} collective-permute-done((bf16[96,1280]{1,0:T(8,128)(2,1)}, bf16[96,1280]{1,0:T(8,128)(2,1)}, u32[]{:S(2)}, u32[]{:S(2)}) %collective-permute-start.13) | collective-permute-done | bytes 245792 | tf_op jit(solution)/shard_map/ppermute | solution.py:26
  35.4 2.7 %shard_map.75 = (bf16[512,1280]{1,0:T(8,128)(2,1)S(1)}, bf16[512,1280]{1,0:T(8,128)(2,1)S(1)}, bf16[2,320,128]{2,1,0:T(8,128)(2,1)S(1)}, bf16[2,320,128]{2,1,0:T(8,128)(2,1)S(1)}, bf16[2,320,128]{2,1,0:T(8,128)(2,1)S(1)}) custom-call(s32[1]{0:T(128)} %bitcast.me, bf16[160,1280]{1,0:T(8,128)(2,1)S(1)} %constant_dynamic-update-slice_fusion.2.refs_0_, ...), custom_call_target="tpu_custom_call" | custom-call | flops 419430400 | bytes 1048576 | tf_op jit(solution)/shard_map/pallas_call | solution.py:55
  38.1 3.3 %collective-permute-start.14 = (bf16[2,320,128]{2,1,0:T(8,128)(2,1)S(1)}, bf16[2,320,128]{2,1,0:T(8,128)(2,1)S(1)}, u32[]{:S(2)}, u32[]{:S(2)}) collective-permute-start(bf16[2,320,128]{2,1,0:T(8,128)(2,1)S(1)} %get-tuple-element.36), channel_id=1, source_target_pairs={{0,4},{2,6},{4,0},{6,2},{1,5},{3,7},{5,1},{7,3},{8,12},{10,14},{12... | collective-permute-start | bytes 491528 | tf_op jit(solution)/shard_map/ppermute | solution.py:26
  41.4 0.7 collective-permute-start.15
  42.1 2.6 %collective-permute-start.16 = (bf16[2,320,128]{2,1,0:T(8,128)(2,1)S(1)}, bf16[2,320,128]{2,1,0:T(8,128)(2,1)S(1)}, u32[]{:S(2)}, u32[]{:S(2)}) collective-permute-start(bf16[2,320,128]{2,1,0:T(8,128)(2,1)S(1)} %get-tuple-element.40), channel_id=1, source_target_pairs={{0,6},{2,0},{4,2},{6,4},{1,7},{3,1},{5,3},{7,5},{8,14},{10,8},{12,... | collective-permute-start | bytes 491528 | tf_op jit(solution)/shard_map/ppermute | solution.py:26
  44.7 0.6 shard_map.76.p0
  45.3 1.5 %collective-permute-done.14.p1 = bf16[2,320,128]{2,1,0:T(8,128)(2,1)S(1)} collective-permute-done((bf16[2,320,128]{2,1,0:T(8,128)(2,1)S(1)}, bf16[2,320,128]{2,1,0:T(8,128)(2,1)S(1)}, u32[]{:S(2)}, u32[]{:S(2)}) %collective-permute-start.14) | collective-permute-done | bytes 163872 | tf_op jit(solution)/shard_map/ppermute | solution.py:26
  46.8 2.7 %collective-permute-done.15.p2 = bf16[2,320,128]{2,1,0:T(8,128)(2,1)S(1)} collective-permute-done((bf16[2,320,128]{2,1,0:T(8,128)(2,1)S(1)}, bf16[2,320,128]{2,1,0:T(8,128)(2,1)S(1)}, u32[]{:S(2)}, u32[]{:S(2)}) %collective-permute-start.15) | collective-permute-done | bytes 163872 | tf_op jit(solution)/shard_map/ppermute | solution.py:26
  49.5 0.3 collective-permute-done.16.p3
  49.8 0.2 shard_map.77.b0
  50.0 2.2 %collective-permute-start.17 = (bf16[2,320,128]{2,1,0:T(8,128)(2,1)S(1)}, bf16[2,320,128]{2,1,0:T(8,128)(2,1)S(1)}, u32[]{:S(2)}, u32[]{:S(2)}) collective-permute-start(bf16[2,320,128]{2,1,0:T(8,128)(2,1)S(1)} %shard_map.77.b0), channel_id=1, source_target_pairs={{0,4},{2,6},{4,0},{6,2},{1,5},{3,7},{5,1},{7,3},{8,12},{10,14},{12... | collective-permute-start | bytes 491528 | tf_op jit(solution)/shard_map/ppermute | solution.py:26
  52.1 2.0 %collective-permute-start.18 = (bf16[2,320,128]{2,1,0:T(8,128)(2,1)S(1)}, bf16[2,320,128]{2,1,0:T(8,128)(2,1)S(1)}, u32[]{:S(2)}, u32[]{:S(2)}) collective-permute-start(bf16[2,320,128]{2,1,0:T(8,128)(2,1)S(1)} %shard_map.77.b0), channel_id=1, source_target_pairs={{0,6},{2,0},{4,2},{6,4},{1,7},{3,1},{5,3},{7,5},{8,14},{10,8},{12,... | collective-permute-start | bytes 491528 | tf_op jit(solution)/shard_map/ppermute | solution.py:26
  54.1 0.0 collective-permute-start.19
  54.2 4.1 %collective-permute-done.17.b2 = bf16[2,320,128]{2,1,0:T(8,128)(2,1)S(1)} collective-permute-done((bf16[2,320,128]{2,1,0:T(8,128)(2,1)S(1)}, bf16[2,320,128]{2,1,0:T(8,128)(2,1)S(1)}, u32[]{:S(2)}, u32[]{:S(2)}) %collective-permute-start.17) | collective-permute-done | bytes 163872 | tf_op jit(solution)/shard_map/ppermute | solution.py:26
  58.2 2.4 %collective-permute-done.18.b1 = bf16[2,320,128]{2,1,0:T(8,128)(2,1)S(1)} collective-permute-done((bf16[2,320,128]{2,1,0:T(8,128)(2,1)S(1)}, bf16[2,320,128]{2,1,0:T(8,128)(2,1)S(1)}, u32[]{:S(2)}, u32[]{:S(2)}) %collective-permute-start.18) | collective-permute-done | bytes 163872 | tf_op jit(solution)/shard_map/ppermute | solution.py:26
  60.6 0.6 collective-permute-done.19.b3
  61.2 0.7 shard_map.78
  61.9 1.6 %shard_map.79 = (f32[256,1280]{1,0:T(8,128)S(1)}, f32[256,1280]{1,0:T(8,128)S(1)}, bf16[320,1280]{1,0:T(8,128)(2,1)S(1)}, bf16[192,1280]{1,0:T(8,128)(2,1)S(1)}) custom-call(s32[1]{0:T(128)} %bitcast.me, bf16[2,320,512]{2,1,0:T(8,128)(2,1)S(1)} %get-tuple-element.41.full, bf16[160,1280]{1,0:T(8,128)(2,1)S(1)} %bitcast.7, bf16[160,1280]{1,0:T(8,128)(2,1)S(1)} %copy-done.1, ...), custom_call_target="tpu_custom_call" | custom-call | flops 838860800 | bytes 1048576 | tf_op jit(solution)/shard_map/pallas_call | solution.py:55
  63.5 0.1 collective-permute-start.20
  63.6 1.9 %collective-permute-done.20 = bf16[192,1280]{1,0:T(8,128)(2,1)S(1)} collective-permute-done((bf16[192,1280]{1,0:T(8,128)(2,1)S(1)}, bf16[192,1280]{1,0:T(8,128)(2,1)S(1)}, u32[]{:S(2)}, u32[]{:S(2)}) %collective-permute-start.20) | collective-permute-done | bytes 491552 | tf_op jit(solution)/shard_map/ppermute | solution.py:26
  65.5 0.1 collective-permute-start.21
  65.6 0.1 convert_element_type.58
  65.7 0.1 fusion.3
  65.7 1.7 %collective-permute-start.23 = (bf16[96,1280]{1,0:T(8,128)(2,1)S(1)}, bf16[96,1280]{1,0:T(8,128)(2,1)S(1)}, u32[]{:S(2)}, u32[]{:S(2)}) collective-permute-start(bf16[96,1280]{1,0:T(8,128)(2,1)S(1)} %fusion.3), channel_id=1, source_target_pairs={{0,8},{8,0},{16,24},{24,16},{1,9},{9,1},{17,25},{25,17},{2,10},{10... | collective-permute-start | bytes 737288 | tf_op jit(solution)/shard_map/ppermute | solution.py:30
  67.5 1.4 %collective-permute-start.26 = (bf16[320,1280]{1,0:T(8,128)(2,1)S(1)}, bf16[320,1280]{1,0:T(8,128)(2,1)S(1)}, u32[]{:S(2)}, u32[]{:S(2)}) collective-permute-start(bf16[320,1280]{1,0:T(8,128)(2,1)S(1)} %get-tuple-element.56), channel_id=1, source_target_pairs={{0,24},{24,0},{8,16},{16,8},{1,25},{25,1},{9,17},{17,9},{2,26},{26... | collective-permute-start | bytes 2457608 | tf_op jit(solution)/shard_map/ppermute | solution.py:34
  68.9 0.6 shard_map.80
  69.5 0.1 convert_element_type.57
  69.6 0.1 fusion
  69.7 1.8 %collective-permute-start.22 = (bf16[160,1280]{1,0:T(8,128)(2,1)S(1)}, bf16[160,1280]{1,0:T(8,128)(2,1)S(1)}, u32[]{:S(2)}, u32[]{:S(2)}) collective-permute-start(bf16[160,1280]{1,0:T(8,128)(2,1)S(1)} %fusion), channel_id=1, source_target_pairs={{0,8},{8,0},{16,24},{24,16},{1,9},{9,1},{17,25},{25,17},{2,10},{10... | collective-permute-start | bytes 1228808 | tf_op jit(solution)/shard_map/ppermute | solution.py:30
  71.5 3.1 %collective-permute-done.23 = bf16[96,1280]{1,0:T(8,128)(2,1)S(1)} collective-permute-done((bf16[96,1280]{1,0:T(8,128)(2,1)S(1)}, bf16[96,1280]{1,0:T(8,128)(2,1)S(1)}, u32[]{:S(2)}, u32[]{:S(2)}) %collective-permute-start.23) | collective-permute-done | bytes 245792 | tf_op jit(solution)/shard_map/ppermute | solution.py:30
  74.6 0.1 fusion.2
  74.7 2.2 %collective-permute-start.28 = (bf16[32,1280]{1,0:T(8,128)(2,1)S(1)}, bf16[32,1280]{1,0:T(8,128)(2,1)S(1)}, u32[]{:S(2)}, u32[]{:S(2)}) collective-permute-start(bf16[32,1280]{1,0:T(8,128)(2,1)S(1)} %get-tuple-element.64), channel_id=1, source_target_pairs={{0,224},{32,0},{64,32},{96,64},{128,96},{160,128},{192,160},{224,1... | collective-permute-start | bytes 245768 | tf_op jit(solution)/shard_map/ppermute | solution.py:26
  76.9 6.0 %collective-permute-done.22 = bf16[160,1280]{1,0:T(8,128)(2,1)S(1)} collective-permute-done((bf16[160,1280]{1,0:T(8,128)(2,1)S(1)}, bf16[160,1280]{1,0:T(8,128)(2,1)S(1)}, u32[]{:S(2)}, u32[]{:S(2)}) %collective-permute-start.22) | collective-permute-done | bytes 409632 | tf_op jit(solution)/shard_map/ppermute | solution.py:30
  82.8 0.1 convert_add_fusion.1
  83.0 1.0 %collective-permute-done.25 = bf16[32,1280]{1,0:T(8,128)(2,1)S(1)} collective-permute-done((bf16[32,1280]{1,0:T(8,128)(2,1)S(1)}, bf16[32,1280]{1,0:T(8,128)(2,1)S(1)}, u32[]{:S(2)}, u32[]{:S(2)}) %collective-permute-start.25) | collective-permute-done | bytes 81952 | tf_op jit(solution)/shard_map/ppermute | solution.py:26
  84.0 0.0 collective-permute-done.24
  84.1 0.1 collective-permute-start.27
  84.2 3.5 %collective-permute-done.26 = bf16[320,1280]{1,0:T(8,128)(2,1)S(1)} collective-permute-done((bf16[320,1280]{1,0:T(8,128)(2,1)S(1)}, bf16[320,1280]{1,0:T(8,128)(2,1)S(1)}, u32[]{:S(2)}, u32[]{:S(2)}) %collective-permute-start.26) | collective-permute-done | bytes 819232 | tf_op jit(solution)/shard_map/ppermute | solution.py:34
  87.7 2.7 %collective-permute-start.31 = (bf16[32,1280]{1,0:T(8,128)(2,1)S(1)}, bf16[32,1280]{1,0:T(8,128)(2,1)S(1)}, u32[]{:S(2)}, u32[]{:S(2)}) collective-permute-start(bf16[32,1280]{1,0:T(8,128)(2,1)S(1)} %get-tuple-element.68), channel_id=1, source_target_pairs={{0,224},{32,0},{64,32},{96,64},{128,96},{160,128},{192,160},{224,1... | collective-permute-start | bytes 245768 | tf_op jit(solution)/shard_map/ppermute | solution.py:26
  90.4 1.5 %collective-permute-start.29 = (bf16[32,1280]{1,0:T(8,128)(2,1)S(1)}, bf16[32,1280]{1,0:T(8,128)(2,1)S(1)}, u32[]{:S(2)}, u32[]{:S(2)}) collective-permute-start(bf16[32,1280]{1,0:T(8,128)(2,1)S(1)} %get-tuple-element.62), channel_id=1, source_target_pairs={{0,192},{32,224},{64,0},{96,32},{128,64},{160,96},{192,128},{224,1... | collective-permute-start | bytes 245768 | tf_op jit(solution)/shard_map/ppermute | solution.py:26
  91.9 1.3 %convert_add_fusion = (f32[160,1280]{1,0:T(8,128)}, f32[1280,160]{0,1:T(8,128)}) fusion(f32[160,1280]{1,0:T(8,128)S(1)} %get-tuple-element.49, bf16[320,1280]{1,0:T(8,128)(2,1)S(1)} %collective-permute-done.26, f32[160,1280]{1,0:T(8,128)S(1)} %get-tuple-element.59), kind=kLoop, calls=%fused_computation.3 | loop fusion | flops 819200 | bytes 4096000 | tf_op jit(solution)/shard_map/add | solution.py:211
  93.2 2.8 %collective-permute-done.30 = bf16[32,1280]{1,0:T(8,128)(2,1)S(1)} collective-permute-done((bf16[32,1280]{1,0:T(8,128)(2,1)S(1)}, bf16[32,1280]{1,0:T(8,128)(2,1)S(1)}, u32[]{:S(2)}, u32[]{:S(2)}) %collective-permute-start.30) | collective-permute-done | bytes 81952 | tf_op jit(solution)/shard_map/ppermute | solution.py:26
  96.0 0.1 collective-permute-done.29
  96.2 0.6 fusion.8
  (33 shorter events, 0.2 us)
Async XLA Ops:
  2.2 16.1 %collective-permute-start = (bf16[32,1280]{1,0:T(8,128)(2,1)S(1)}, bf16[32,1280]{1,0:T(8,128)(2,1)S(1)}, u32[]{:S(2)}, u32[]{:S(2)}) collective-permute-start(bf16[32,1280]{1,0:T(8,128)(2,1)S(1)} %get-tuple-element.71), channel_id=1, source_target_pairs={{0,224},{32,0},{64,32},{96,64},{128,96},{160,128},{192,160},{224,1... | collective-permute-start | bytes 245768 | tf_op jit(solution)/shard_map/ppermute | solution.py:26
  8.1 10.2 %collective-permute-start.1 = (bf16[32,1280]{1,0:T(8,128)(2,1)S(1)}, bf16[32,1280]{1,0:T(8,128)(2,1)S(1)}, u32[]{:S(2)}, u32[]{:S(2)}) collective-permute-start(bf16[32,1280]{1,0:T(8,128)(2,1)S(1)} %get-tuple-element.71), channel_id=1, source_target_pairs={{0,32},{32,64},{64,96},{96,128},{128,160},{160,192},{192,224},{224... | collective-permute-start | bytes 245768 | tf_op jit(solution)/shard_map/ppermute | solution.py:26
  8.1 5.8 %collective-permute-start.2 = (bf16[32,1280]{1,0:T(8,128)(2,1)S(1)}, bf16[32,1280]{1,0:T(8,128)(2,1)S(1)}, u32[]{:S(2)}, u32[]{:S(2)}) collective-permute-start(bf16[32,1280]{1,0:T(8,128)(2,1)S(1)} %get-tuple-element.71), channel_id=1, source_target_pairs={{0,192},{32,224},{64,0},{96,32},{128,64},{160,96},{192,128},{224,1... | collective-permute-start | bytes 245768 | tf_op jit(solution)/shard_map/ppermute | solution.py:26
  10.5 7.8 %collective-permute-start.3 = (bf16[32,1280]{1,0:T(8,128)(2,1)S(1)}, bf16[32,1280]{1,0:T(8,128)(2,1)S(1)}, u32[]{:S(2)}, u32[]{:S(2)}) collective-permute-start(bf16[32,1280]{1,0:T(8,128)(2,1)S(1)} %get-tuple-element.71), channel_id=1, source_target_pairs={{0,64},{32,96},{64,128},{96,160},{128,192},{160,224},{192,0},{224,... | collective-permute-start | bytes 245768 | tf_op jit(solution)/shard_map/ppermute | solution.py:26
  11.0 24.4 %copy-start = (bf16[1280,160]{0,1:T(8,128)(2,1)S(1)}, bf16[1280,160]{0,1:T(8,128)(2,1)}, u32[]{:S(2)}) copy-start(bf16[1280,160]{0,1:T(8,128)(2,1)} %param.5) | copy-start | bytes 1228804
  11.0 24.4 %copy-start.1 = (bf16[160,1280]{1,0:T(8,128)(2,1)S(1)}, bf16[160,1280]{1,0:T(8,128)(2,1)}, u32[]{:S(2)}) copy-start(bf16[160,1280]{1,0:T(8,128)(2,1)} %wo.3) | copy-start | bytes 1228804
  12.2 21.3 %collective-permute-start.9 = (bf16[320,1280]{1,0:T(8,128)(2,1)S(1)}, bf16[320,1280]{1,0:T(8,128)(2,1)S(1)}, u32[]{:S(2)}, u32[]{:S(2)}) collective-permute-start(bf16[320,1280]{1,0:T(8,128)(2,1)S(1)} %pad_maximum_fusion), channel_id=1, source_target_pairs={{0,24},{24,0},{8,16},{16,8},{1,25},{25,1},{9,17},{17,9},{2,26},{26... | collective-permute-start | bytes 2457608 | tf_op jit(solution)/shard_map/ppermute | solution.py:34
  13.8 6.5 %collective-permute-start.4 = (bf16[32,1280]{1,0:T(8,128)(2,1)S(1)}, bf16[32,1280]{1,0:T(8,128)(2,1)S(1)}, u32[]{:S(2)}, u32[]{:S(2)}) collective-permute-start(bf16[32,1280]{1,0:T(8,128)(2,1)S(1)} %collective-permute-done.2), channel_id=1, source_target_pairs={{0,224},{32,0},{64,32},{96,64},{128,96},{160,128},{192,160},{224,1... | collective-permute-start | bytes 245768 | tf_op jit(solution)/shard_map/ppermute | solution.py:26
  18.4 11.6 %collective-permute-start.7 = (bf16[160,1280]{1,0:T(8,128)(2,1)S(1)}, bf16[160,1280]{1,0:T(8,128)(2,1)S(1)}, u32[]{:S(2)}, u32[]{:S(2)}) collective-permute-start(bf16[160,1280]{1,0:T(8,128)(2,1)S(1)} %constant_dynamic-update-slice_fusion.2.refs_0_), channel_id=1, source_target_pairs={{0,8},{8,0},{16,24},{24,16},{1,9},{9,1},{17,25},{25,17},{2,10},{10... | collective-permute-start | bytes 1228808 | tf_op jit(solution)/shard_map/ppermute | solution.py:30
  20.2 6.9 %collective-permute-start.6 = (bf16[32,1280]{1,0:T(8,128)(2,1)S(1)}, bf16[32,1280]{1,0:T(8,128)(2,1)S(1)}, u32[]{:S(2)}, u32[]{:S(2)}) collective-permute-start(bf16[32,1280]{1,0:T(8,128)(2,1)S(1)} %collective-permute-done.3), channel_id=1, source_target_pairs={{0,64},{32,96},{64,128},{96,160},{128,192},{160,224},{192,0},{224,... | collective-permute-start | bytes 245768 | tf_op jit(solution)/shard_map/ppermute | solution.py:26
  20.2 6.9 %collective-permute-start.5 = (bf16[32,1280]{1,0:T(8,128)(2,1)S(1)}, bf16[32,1280]{1,0:T(8,128)(2,1)S(1)}, u32[]{:S(2)}, u32[]{:S(2)}) collective-permute-start(bf16[32,1280]{1,0:T(8,128)(2,1)S(1)} %collective-permute-done.3), channel_id=1, source_target_pairs={{0,32},{32,64},{64,96},{96,128},{128,160},{160,192},{192,224},{224... | collective-permute-start | bytes 245768 | tf_op jit(solution)/shard_map/ppermute | solution.py:26
  27.2 6.4 %collective-permute-start.8 = (bf16[96,1280]{1,0:T(8,128)(2,1)S(1)}, bf16[96,1280]{1,0:T(8,128)(2,1)}, u32[]{:S(2)}, u32[]{:S(2)}) collective-permute-start(bf16[96,1280]{1,0:T(8,128)(2,1)S(1)} %constant_dynamic-update-slice_fusion.8.refs_1_), channel_id=1, source_target_pairs={{0,8},{8,0},{16,24},{24,16},{1,9},{9,1},{17,25},{25,17},{2,10},{10... | collective-permute-start | bytes 737288 | tf_op jit(solution)/shard_map/ppermute | solution.py:30
  28.7 4.8 %collective-permute-start.10 = (bf16[160,1280]{1,0:T(8,128)(2,1)S(1)}, bf16[160,1280]{1,0:T(8,128)(2,1)S(1)}, u32[]{:S(2)}, u32[]{:S(2)}) collective-permute-start(bf16[160,1280]{1,0:T(8,128)(2,1)S(1)} %constant_dynamic-update-slice_fusion.2.refs_0_), channel_id=1, source_target_pairs={{0,1},{1,0},{2,3},{3,2},{4,5},{5,4},{6,7},{7,6},{8,9},{9,8},{10,11... | collective-permute-start | bytes 1228808 | tf_op jit(solution)/shard_map/ppermute | solution.py:26
  30.0 3.6 %collective-permute-start.12 = (bf16[160,1280]{1,0:T(8,128)(2,1)S(1)}, bf16[160,1280]{1,0:T(8,128)(2,1)S(1)}, u32[]{:S(2)}, u32[]{:S(2)}) collective-permute-start(bf16[160,1280]{1,0:T(8,128)(2,1)S(1)} %collective-permute-done.7.refs_2_), channel_id=1, source_target_pairs={{0,1},{1,0},{2,3},{3,2},{4,5},{5,4},{6,7},{7,6},{8,9},{9,8},{10,11... | collective-permute-start | bytes 1228808 | tf_op jit(solution)/shard_map/ppermute | solution.py:26
  30.0 3.6 %collective-permute-start.11 = (bf16[96,1280]{1,0:T(8,128)(2,1)S(1)}, bf16[96,1280]{1,0:T(8,128)(2,1)}, u32[]{:S(2)}, u32[]{:S(2)}) collective-permute-start(bf16[96,1280]{1,0:T(8,128)(2,1)S(1)} %constant_dynamic-update-slice_fusion.8.refs_1_), channel_id=1, source_target_pairs={{0,1},{1,0},{2,3},{3,2},{4,5},{5,4},{6,7},{7,6},{8,9},{9,8},{10,11... | collective-permute-start | bytes 737288 | tf_op jit(solution)/shard_map/ppermute | solution.py:26
  33.6 1.9 %collective-permute-start.13 = (bf16[96,1280]{1,0:T(8,128)(2,1)}, bf16[96,1280]{1,0:T(8,128)(2,1)}, u32[]{:S(2)}, u32[]{:S(2)}) collective-permute-start(bf16[96,1280]{1,0:T(8,128)(2,1)} %collective-permute-done.8.refs_3_), channel_id=1, source_target_pairs={{0,1},{1,0},{2,3},{3,2},{4,5},{5,4},{6,7},{7,6},{8,9},{9,8},{10,11... | collective-permute-start | bytes 737288 | tf_op jit(solution)/shard_map/ppermute | solution.py:26
  38.1 8.6 %collective-permute-start.14 = (bf16[2,320,128]{2,1,0:T(8,128)(2,1)S(1)}, bf16[2,320,128]{2,1,0:T(8,128)(2,1)S(1)}, u32[]{:S(2)}, u32[]{:S(2)}) collective-permute-start(bf16[2,320,128]{2,1,0:T(8,128)(2,1)S(1)} %get-tuple-element.36), channel_id=1, source_target_pairs={{0,4},{2,6},{4,0},{6,2},{1,5},{3,7},{5,1},{7,3},{8,12},{10,14},{12... | collective-permute-start | bytes 491528 | tf_op jit(solution)/shard_map/ppermute | solution.py:26
  41.4 8.1 %collective-permute-start.15 = (bf16[2,320,128]{2,1,0:T(8,128)(2,1)S(1)}, bf16[2,320,128]{2,1,0:T(8,128)(2,1)S(1)}, u32[]{:S(2)}, u32[]{:S(2)}) collective-permute-start(bf16[2,320,128]{2,1,0:T(8,128)(2,1)S(1)} %get-tuple-element.39), channel_id=1, source_target_pairs={{0,2},{2,4},{4,6},{6,0},{1,3},{3,5},{5,7},{7,1},{8,10},{10,12},{12... | collective-permute-start | bytes 491528 | tf_op jit(solution)/shard_map/ppermute | solution.py:26
  42.1 7.7 %collective-permute-start.16 = (bf16[2,320,128]{2,1,0:T(8,128)(2,1)S(1)}, bf16[2,320,128]{2,1,0:T(8,128)(2,1)S(1)}, u32[]{:S(2)}, u32[]{:S(2)}) collective-permute-start(bf16[2,320,128]{2,1,0:T(8,128)(2,1)S(1)} %get-tuple-element.40), channel_id=1, source_target_pairs={{0,6},{2,0},{4,2},{6,4},{1,7},{3,1},{5,3},{7,5},{8,14},{10,8},{12,... | collective-permute-start | bytes 491528 | tf_op jit(solution)/shard_map/ppermute | solution.py:26
  50.0 8.2 %collective-permute-start.17 = (bf16[2,320,128]{2,1,0:T(8,128)(2,1)S(1)}, bf16[2,320,128]{2,1,0:T(8,128)(2,1)S(1)}, u32[]{:S(2)}, u32[]{:S(2)}) collective-permute-start(bf16[2,320,128]{2,1,0:T(8,128)(2,1)S(1)} %shard_map.77.b0), channel_id=1, source_target_pairs={{0,4},{2,6},{4,0},{6,2},{1,5},{3,7},{5,1},{7,3},{8,12},{10,14},{12... | collective-permute-start | bytes 491528 | tf_op jit(solution)/shard_map/ppermute | solution.py:26
  52.1 8.5 %collective-permute-start.18 = (bf16[2,320,128]{2,1,0:T(8,128)(2,1)S(1)}, bf16[2,320,128]{2,1,0:T(8,128)(2,1)S(1)}, u32[]{:S(2)}, u32[]{:S(2)}) collective-permute-start(bf16[2,320,128]{2,1,0:T(8,128)(2,1)S(1)} %shard_map.77.b0), channel_id=1, source_target_pairs={{0,6},{2,0},{4,2},{6,4},{1,7},{3,1},{5,3},{7,5},{8,14},{10,8},{12,... | collective-permute-start | bytes 491528 | tf_op jit(solution)/shard_map/ppermute | solution.py:26
  54.1 7.1 %collective-permute-start.19 = (bf16[2,320,128]{2,1,0:T(8,128)(2,1)S(1)}, bf16[2,320,128]{2,1,0:T(8,128)(2,1)S(1)}, u32[]{:S(2)}, u32[]{:S(2)}) collective-permute-start(bf16[2,320,128]{2,1,0:T(8,128)(2,1)S(1)} %shard_map.77.b0), channel_id=1, source_target_pairs={{0,2},{2,4},{4,6},{6,0},{1,3},{3,5},{5,7},{7,1},{8,10},{10,12},{12... | collective-permute-start | bytes 491528 | tf_op jit(solution)/shard_map/ppermute | solution.py:26
  63.5 2.0 %collective-permute-start.20 = (bf16[192,1280]{1,0:T(8,128)(2,1)S(1)}, bf16[192,1280]{1,0:T(8,128)(2,1)S(1)}, u32[]{:S(2)}, u32[]{:S(2)}) collective-permute-start(bf16[192,1280]{1,0:T(8,128)(2,1)S(1)} %get-tuple-element.44), channel_id=1, source_target_pairs={{0,1},{1,0},{2,3},{3,2},{4,5},{5,4},{6,7},{7,6},{8,9},{9,8},{10,11... | collective-permute-start | bytes 1474568 | tf_op jit(solution)/shard_map/ppermute | solution.py:26
  65.5 4.0 %collective-permute-start.21 = (bf16[320,1280]{1,0:T(8,128)(2,1)S(1)}, bf16[320,1280]{1,0:T(8,128)(2,1)S(1)}, u32[]{:S(2)}, u32[]{:S(2)}) collective-permute-start(bf16[320,1280]{1,0:T(8,128)(2,1)S(1)} %get-tuple-element.45), channel_id=1, source_target_pairs={{0,1},{1,0},{2,3},{3,2},{4,5},{5,4},{6,7},{7,6},{8,9},{9,8},{10,11... | collective-permute-start | bytes 2457608 | tf_op jit(solution)/shard_map/ppermute | solution.py:26
  65.7 8.9 %collective-permute-start.23 = (bf16[96,1280]{1,0:T(8,128)(2,1)S(1)}, bf16[96,1280]{1,0:T(8,128)(2,1)S(1)}, u32[]{:S(2)}, u32[]{:S(2)}) collective-permute-start(bf16[96,1280]{1,0:T(8,128)(2,1)S(1)} %fusion.3), channel_id=1, source_target_pairs={{0,8},{8,0},{16,24},{24,16},{1,9},{9,1},{17,25},{25,17},{2,10},{10... | collective-permute-start | bytes 737288 | tf_op jit(solution)/shard_map/ppermute | solution.py:30
  67.5 20.2 %collective-permute-start.26 = (bf16[320,1280]{1,0:T(8,128)(2,1)S(1)}, bf16[320,1280]{1,0:T(8,128)(2,1)S(1)}, u32[]{:S(2)}, u32[]{:S(2)}) collective-permute-start(bf16[320,1280]{1,0:T(8,128)(2,1)S(1)} %get-tuple-element.56), channel_id=1, source_target_pairs={{0,24},{24,0},{8,16},{16,8},{1,25},{25,1},{9,17},{17,9},{2,26},{26... | collective-permute-start | bytes 2457608 | tf_op jit(solution)/shard_map/ppermute | solution.py:34
  69.7 13.1 %collective-permute-start.22 = (bf16[160,1280]{1,0:T(8,128)(2,1)S(1)}, bf16[160,1280]{1,0:T(8,128)(2,1)S(1)}, u32[]{:S(2)}, u32[]{:S(2)}) collective-permute-start(bf16[160,1280]{1,0:T(8,128)(2,1)S(1)} %fusion), channel_id=1, source_target_pairs={{0,8},{8,0},{16,24},{24,16},{1,9},{9,1},{17,25},{25,17},{2,10},{10... | collective-permute-start | bytes 1228808 | tf_op jit(solution)/shard_map/ppermute | solution.py:30
  74.7 8.3 %collective-permute-start.28 = (bf16[32,1280]{1,0:T(8,128)(2,1)S(1)}, bf16[32,1280]{1,0:T(8,128)(2,1)S(1)}, u32[]{:S(2)}, u32[]{:S(2)}) collective-permute-start(bf16[32,1280]{1,0:T(8,128)(2,1)S(1)} %get-tuple-element.64), channel_id=1, source_target_pairs={{0,224},{32,0},{64,32},{96,64},{128,96},{160,128},{192,160},{224,1... | collective-permute-start | bytes 245768 | tf_op jit(solution)/shard_map/ppermute | solution.py:26
  76.9 7.1 %collective-permute-start.25 = (bf16[32,1280]{1,0:T(8,128)(2,1)S(1)}, bf16[32,1280]{1,0:T(8,128)(2,1)S(1)}, u32[]{:S(2)}, u32[]{:S(2)}) collective-permute-start(bf16[32,1280]{1,0:T(8,128)(2,1)S(1)} %get-tuple-element.65), channel_id=1, source_target_pairs={{0,64},{32,96},{64,128},{96,160},{128,192},{160,224},{192,0},{224,... | collective-permute-start | bytes 245768 | tf_op jit(solution)/shard_map/ppermute | solution.py:26
  76.9 7.2 %collective-permute-start.24 = (bf16[32,1280]{1,0:T(8,128)(2,1)S(1)}, bf16[32,1280]{1,0:T(8,128)(2,1)S(1)}, u32[]{:S(2)}, u32[]{:S(2)}) collective-permute-start(bf16[32,1280]{1,0:T(8,128)(2,1)S(1)} %get-tuple-element.66), channel_id=1, source_target_pairs={{0,32},{32,64},{64,96},{96,128},{128,160},{160,192},{192,224},{224... | collective-permute-start | bytes 245768 | tf_op jit(solution)/shard_map/ppermute | solution.py:26
  84.1 12.0 %collective-permute-start.27 = (bf16[32,1280]{1,0:T(8,128)(2,1)S(1)}, bf16[32,1280]{1,0:T(8,128)(2,1)S(1)}, u32[]{:S(2)}, u32[]{:S(2)}) collective-permute-start(bf16[32,1280]{1,0:T(8,128)(2,1)S(1)} %get-tuple-element.63), channel_id=1, source_target_pairs={{0,64},{32,96},{64,128},{96,160},{128,192},{160,224},{192,0},{224,... | collective-permute-start | bytes 245768 | tf_op jit(solution)/shard_map/ppermute | solution.py:26
  87.7 5.5 %collective-permute-start.31 = (bf16[32,1280]{1,0:T(8,128)(2,1)S(1)}, bf16[32,1280]{1,0:T(8,128)(2,1)S(1)}, u32[]{:S(2)}, u32[]{:S(2)}) collective-permute-start(bf16[32,1280]{1,0:T(8,128)(2,1)S(1)} %get-tuple-element.68), channel_id=1, source_target_pairs={{0,224},{32,0},{64,32},{96,64},{128,96},{160,128},{192,160},{224,1... | collective-permute-start | bytes 245768 | tf_op jit(solution)/shard_map/ppermute | solution.py:26
  90.4 5.7 %collective-permute-start.30 = (bf16[32,1280]{1,0:T(8,128)(2,1)S(1)}, bf16[32,1280]{1,0:T(8,128)(2,1)S(1)}, u32[]{:S(2)}, u32[]{:S(2)}) collective-permute-start(bf16[32,1280]{1,0:T(8,128)(2,1)S(1)} %get-tuple-element.67), channel_id=1, source_target_pairs={{0,32},{32,64},{64,96},{96,128},{128,160},{160,192},{192,224},{224... | collective-permute-start | bytes 245768 | tf_op jit(solution)/shard_map/ppermute | solution.py:26
  90.4 5.7 %collective-permute-start.29 = (bf16[32,1280]{1,0:T(8,128)(2,1)S(1)}, bf16[32,1280]{1,0:T(8,128)(2,1)S(1)}, u32[]{:S(2)}, u32[]{:S(2)}) collective-permute-start(bf16[32,1280]{1,0:T(8,128)(2,1)S(1)} %get-tuple-element.62), channel_id=1, source_target_pairs={{0,192},{32,224},{64,0},{96,32},{128,64},{160,96},{192,128},{224,1... | collective-permute-start | bytes 245768 | tf_op jit(solution)/shard_map/ppermute | solution.py:26

commit v8 on v7

--- a/solution.py
+++ b/solution.py
@@ -78,13 +78,19 @@
 
 
 def up_kernel(me, *refs):
-    quarters, (wi, wo, w_pair, tok, cot), parts = refs[:8], refs[8:13], refs[13:]
+    held, (wi, wo, w_pair, tok, cot), parts = refs[:8], refs[8:13], refs[13:]
     for q in range(4):
+        half, chip = q // 2 * 4, q % 2
         for j in range(8):
-            ref, i = (quarters[2 * q], j) if j < HEAD else (quarters[2 * q + 1], j - HEAD)
+            if j < 3:
+                ref, i = held[half], j * 64 + chip * 32
+            elif j < HEAD:
+                ref, i = held[half + 1], chip * 64 + (j - 3) * 32
+            else:
+                ref, i = held[half + 2 + chip], (j - HEAD) * 32
             row = q * 128 + j * 16
-            tok[row : row + 16] = ref[i * 32 : i * 32 + 16]
-            cot[row : row + 16] = ref[i * 32 + 16 : i * 32 + 32]
+            tok[row : row + 16] = ref[i : i + 16]
+            cot[row : row + 16] = ref[i + 16 : i + 32]
     for k, part in zip((2, 1, 3), parts):
         products(quarter_of(tok, cot, me[0] + k), wi, wo, w_pair, part)
 
@@ -146,24 +152,25 @@
     flops = 2 * 1024 * d * h
 
     base = cat([tokens, cotangent])
-    z = {0: base}
-    z[2], z[6] = send(base, "z", -2), send(base, "z", 2)
-    z[1], z[7] = send(base, "z", -1), send(base, "z", 1)
+    z = {2: send(base, "z", -2), 6: send(base, "z", 2)}
+    both = cat([base, token_pair(base)])
     w_in_t = w_in.T
     w_pair = weight_pair(after(cat([w_in_t, w_out]), base))
     z[3], z[5] = send(z[2], "z", -1), send(z[6], "z", 1)
-    near_h = cat([z[k] for k in ORDER[:HEAD]])
-    far_h = token_pair(near_h)
-    z[4] = send(after(z[6], near_h), "z", 2)
+    second = cat([z[2], z[6]])
+    z[4] = send(after(z[6], second), "z", 2)
+    second = cat([second, token_pair(second)])
     near_t = cat([z[k] for k in ORDER[HEAD:]])
+    both = after(both, z[3])
+    first = cat([both, send(both, "z", -1), send(both, "z", 1)])
     far_t = after(token_pair(near_t), w_pair)
-    quarters = [near_h, near_t, far_h, far_t]
-    quarters += [send(value, "col", 1) for value in quarters]
+    held = [first, second, near_t, far_t]
+    held += [send(value, "col", 1) for value in held]
 
     part, rounded = shape((2, 2 * h, 128), F32), shape((2, 2 * h, 128), BF)
     weights = [w_in_t, w_out, w_pair]
     tok, cot, *parts = call(
-        up_kernel, [shape((512, d), BF)] * 2 + [rounded] * 3, [me, *quarters, *weights], flops
+        up_kernel, [shape((512, d), BF)] * 2 + [rounded] * 3, [me, *held, *weights], flops
     )
     mine = call(mine_kernel, [part], [me, after(tok, parts[0]), cot, *weights], flops)
     parts = mine + [send(value, "row", k) for k, value in zip((2, 1, 3), parts)]
@@ -193,20 +200,25 @@
     grad_out, grad_in_t = call(
         own_kernel, [shape((h, d), F32)] * 2, [me, full, after(tok, far_t), cot], flops
     )
-    far_h = after((far[:cut] + head[:cut]).astype(BF), grad_out)
-    far_t = after(token_pair(far_t), far_h)
-    far_h = token_pair(far_h)
+    far_t = token_pair(far_t)
+    head = after(head, grad_out)
+    far_h = far[:cut] + head[:cut]
+    near_h = near[:cut] + head[cut:]
+    up_1 = cat([near_h[32:64], far_h[32:64]]).astype(BF)
+    down_1 = cat([near_h[64:96], far_h[64:96]]).astype(BF)
+    near = after(near, (up_1, down_1))
+    up_1, down_1 = send(up_1, "z", 1).astype(F32), send(down_1, "z", -1).astype(F32)
+    far_2 = token_pair(far_h[96:].astype(BF)).astype(F32)
     third = (near[cut:] + tail[rest:] + far_t.astype(F32)).astype(BF)
-    near, head, far_h = after((near, head, far_h), third)
     up, down = send(third[:32], "z", 1), send(third[32:64], "z", -1)
     up_2 = send(third[64:], "z", 2)
-    near_h = near[:cut] + head[cut:] + far_h.astype(F32)
-    up = up.astype(F32) + up_2.astype(F32) + near_h[96:128]
-    down = down.astype(F32) + near_h[128:]
-    up, down = up.astype(BF), down.astype(BF)
-    near_h, near_1 = after((near_h, near_h[32:96].astype(BF)), (up, pair))
-    total = near_h[:32] + send(up, "z", 2).astype(F32) + send(down, "z", -2).astype(F32)
-    total += send(near_1[:32], "z", 1).astype(F32) + send(near_1[32:], "z", -1).astype(F32)
+    far_0 = after(far_h[:32], third) + up_1[32:] + down_1[32:]
+    far_0 = token_pair(far_0.astype(BF)).astype(F32)
+    near_2 = after(near_h[96:], far_0)
+    up = (up.astype(F32) + up_2.astype(F32) + near_2[:32] + far_2[:32]).astype(BF)
+    down = (down.astype(F32) + near_2[32:] + far_2[32:]).astype(BF)
+    total = after(near_h[:32], up) + up_1[:32] + down_1[:32] + far_0
+    total += send(up, "z", 2).astype(F32) + send(down, "z", -2).astype(F32)
     output, input_grad = total[:16].astype(BF), total[16:].astype(BF)
     grad_out = grad_out + pair[:h].astype(F32)
     grad_in_t = grad_in_t + pair[h:].astype(F32)

time: 97.7 us -> 94.4 us (0.966)
  waiting for transfers between devices: 43 us -> 34 us
  starting transfers between devices: 41.2 us -> 47.2 us
    ppermute x4 -> x6, waiting for transfers between devices: 13.4 us -> 4.42 us  [token_pair(): return lax.ppermute(value, 'x', [(0, 1), (1, 0), (2, 3), (3, 2)])]
    ppermute x26, starting transfers between devices: 31.2 us -> 35.6 us  [send(): lax.ppermute(value, axis, [(i, (i + shift) % size) for i in range(size)])]
    ppermute x2, waiting for transfers between devices: 3.52 us -> 0.01 us  [weight_pair(): return lax.ppermute(value, 'x', [(0, 3), (3, 0), (1, 2), (2, 1)])]
    ppermute x26, waiting for transfers between devices: 26.1 us -> 29.6 us  [send(): lax.ppermute(value, axis, [(i, (i + shift) % size) for i in range(size)])]
    ppermute x4 -> x6, starting transfers between devices: 7.01 us -> 7.86 us  [token_pair(): return lax.ppermute(value, 'x', [(0, 1), (1, 0), (2, 3), (3, 2)])]
  transfers between devices with their start and end apart: 32 -> 34, of which waited for: 17 -> 17; matrix products, arithmetic and copies ran while one was open for 3% -> 4% of each run, Pallas kernels for 1% -> 1%
where the time goes in v8:
time: 94.4 us; the launch traced here: 94.2 us
  starting transfers between devices  47.2 us (50%)
  waiting for transfers between devices  34 us (36%)
  Pallas kernels  6.3 us (7%)
  other arithmetic  3.23 us (3%)
  local copies, waits for them, and re-layouts  2.47 us (3%)
  between operations  1.01 us (1%)
    ppermute x26, starting transfers between devices, send(): lax.ppermute(value, axis, [(i, (i + shift) % size) for i in range(size)])  35.6 us
    ppermute x26, waiting for transfers between devices, send(): lax.ppermute(value, axis, [(i, (i + shift) % size) for i in range(size)])  29.6 us
    ppermute x6, starting transfers between devices, token_pair(): return lax.ppermute(value, 'x', [(0, 1), (1, 0), (2, 3), (3, 2)])  7.86 us
    pallas_call x6, Pallas kernels, call(): return list(kernel(*args))  6.3 us
    ppermute x6, waiting for transfers between devices, token_pair(): return lax.ppermute(value, 'x', [(0, 1), (1, 0), (2, 3), (3, 2)])  4.42 us
    ppermute x2, starting transfers between devices, weight_pair(): return lax.ppermute(value, 'x', [(0, 3), (3, 0), (1, 2), (2, 1)])  3.66 us
  transfers between devices with their start and end apart: 34, of which 17 were waited for; matrix products, arithmetic and copies ran while one was open for 4% of the time, Pallas kernels for 1%

profile of v8, /device:TPU:2, one launch (start us, length us, event | category | flops | bytes accessed | tf_op | source)
XLA Modules:
  0.0 94.2 jit_solution(4105973265859389015)
XLA Ops:
  0.7 0.8 constant_dynamic-update-slice_fusion.1
  1.5 0.8 constant_dynamic-update-slice_fusion
  2.3 6.3 %collective-permute-start.1 = (bf16[32,1280]{1,0:T(8,128)(2,1)S(1)}, bf16[32,1280]{1,0:T(8,128)(2,1)S(1)}, u32[]{:S(2)}, u32[]{:S(2)}) collective-permute-start(bf16[32,1280]{1,0:T(8,128)(2,1)S(1)} %constant_dynamic-update-slice_fusion), channel_id=1, source_target_pairs={{0,192},{32,224},{64,0},{96,32},{128,64},{160,96},{192,128},{224,1... | collective-permute-start | bytes 245768 | tf_op jit(solution)/shard_map/ppermute | solution.py:26
  8.6 0.5 collective-permute-start
  9.1 1.2 %pad_maximum_fusion = bf16[320,1280]{1,0:T(8,128)(2,1)S(1)} fusion(bf16[160,1280]{1,0:T(8,128)(2,1)} %wo.3, bf16[160,1280]{1,0:T(8,128)(2,1)} %bitcast.4), kind=kLoop, calls=%fused_computation | loop fusion | flops 1638400 | bytes 1638400 | tf_op jit(solution)/shard_map/concatenate | solution.py:59
  10.3 2.2 %collective-permute-start.10 = (bf16[320,1280]{1,0:T(8,128)(2,1)S(1)}, bf16[320,1280]{1,0:T(8,128)(2,1)S(1)}, u32[]{:S(2)}, u32[]{:S(2)}) collective-permute-start(bf16[320,1280]{1,0:T(8,128)(2,1)S(1)} %pad_maximum_fusion), channel_id=1, source_target_pairs={{0,24},{24,0},{8,16},{16,8},{1,25},{25,1},{9,17},{17,9},{2,26},{26... | collective-permute-start | bytes 2457608 | tf_op jit(solution)/shard_map/ppermute | solution.py:34
  12.6 3.3 %collective-permute-done.5 = bf16[32,1280]{1,0:T(8,128)(2,1)S(1)} collective-permute-done((bf16[32,1280]{1,0:T(8,128)(2,1)S(1)}, bf16[32,1280]{1,0:T(8,128)(2,1)S(1)}, u32[]{:S(2)}, u32[]{:S(2)}) %collective-permute-start.5) | collective-permute-done | bytes 81952 | tf_op jit(solution)/shard_map/ppermute | solution.py:26
  15.9 0.6 collective-permute-start.6
  16.5 4.2 %collective-permute-start.2 = (bf16[32,1280]{1,0:T(8,128)(2,1)S(1)}, bf16[32,1280]{1,0:T(8,128)(2,1)S(1)}, u32[]{:S(2)}, u32[]{:S(2)}) collective-permute-start(bf16[32,1280]{1,0:T(8,128)(2,1)S(1)} %collective-permute-done.1), channel_id=1, source_target_pairs={{0,224},{32,0},{64,32},{96,64},{128,96},{160,128},{192,160},{224,1... | collective-permute-start | bytes 245768 | tf_op jit(solution)/shard_map/ppermute | solution.py:26
  20.7 2.0 %collective-permute-done.2 = bf16[32,1280]{1,0:T(8,128)(2,1)S(1)} collective-permute-done((bf16[32,1280]{1,0:T(8,128)(2,1)S(1)}, bf16[32,1280]{1,0:T(8,128)(2,1)S(1)}, u32[]{:S(2)}, u32[]{:S(2)}) %collective-permute-start.2) | collective-permute-done | bytes 81952 | tf_op jit(solution)/shard_map/ppermute | solution.py:26
  22.7 3.7 %collective-permute-start.3 = (bf16[64,1280]{1,0:T(8,128)(2,1)S(1)}, bf16[64,1280]{1,0:T(8,128)(2,1)S(1)}, u32[]{:S(2)}, u32[]{:S(2)}) collective-permute-start(bf16[64,1280]{1,0:T(8,128)(2,1)S(1)} %pad_maximum_fusion.1), channel_id=1, source_target_pairs={{0,224},{32,0},{64,32},{96,64},{128,96},{160,128},{192,160},{224,1... | collective-permute-start | bytes 491528 | tf_op jit(solution)/shard_map/ppermute | solution.py:26
  26.4 0.1 collective-permute-start.4
  26.6 1.7 %collective-permute-start.9 = (bf16[96,1280]{1,0:T(8,128)(2,1)S(1)}, bf16[96,1280]{1,0:T(8,128)(2,1)}, u32[]{:S(2)}, u32[]{:S(2)}) collective-permute-start(bf16[96,1280]{1,0:T(8,128)(2,1)S(1)} %constant_dynamic-update-slice_fusion.10.refs_2_), channel_id=1, source_target_pairs={{0,8},{8,0},{16,24},{24,16},{1,9},{9,1},{17,25},{25,17},{2,10},{10... | collective-permute-start | bytes 737288 | tf_op jit(solution)/shard_map/ppermute | solution.py:30
  28.2 1.0 %collective-permute-done.3 = bf16[64,1280]{1,0:T(8,128)(2,1)S(1)} collective-permute-done((bf16[64,1280]{1,0:T(8,128)(2,1)S(1)}, bf16[64,1280]{1,0:T(8,128)(2,1)S(1)}, u32[]{:S(2)}, u32[]{:S(2)}) %collective-permute-start.3) | collective-permute-done | bytes 163872 | tf_op jit(solution)/shard_map/ppermute | solution.py:26
  29.3 3.8 %collective-permute-done.4 = bf16[64,1280]{1,0:T(8,128)(2,1)S(1)} collective-permute-done((bf16[64,1280]{1,0:T(8,128)(2,1)S(1)}, bf16[64,1280]{1,0:T(8,128)(2,1)S(1)}, u32[]{:S(2)}, u32[]{:S(2)}) %collective-permute-start.4) | collective-permute-done | bytes 163872 | tf_op jit(solution)/shard_map/ppermute | solution.py:26
  33.0 0.1 collective-permute-start.11
  33.2 0.6 collective-permute-start.12
  33.8 0.1 collective-permute-start.13
  33.9 0.4 collective-permute-start.14
  34.3 1.7 %collective-permute-done.13.refs_6_ = bf16[96,1280]{1,0:T(8,128)(2,1)} collective-permute-done((bf16[96,1280]{1,0:T(8,128)(2,1)S(1)}, bf16[96,1280]{1,0:T(8,128)(2,1)}, u32[]{:S(2)}, u32[]{:S(2)}) %collective-permute-start.13) | collective-permute-done | bytes 245792 | tf_op jit(solution)/shard_map/ppermute | solution.py:26
  35.9 0.6 collective-permute-done.14.refs_7_
  36.5 2.7 %shard_map.75 = (bf16[512,1280]{1,0:T(8,128)(2,1)S(1)}, bf16[512,1280]{1,0:T(8,128)(2,1)S(1)}, bf16[2,320,128]{2,1,0:T(8,128)(2,1)S(1)}, bf16[2,320,128]{2,1,0:T(8,128)(2,1)S(1)}, bf16[2,320,128]{2,1,0:T(8,128)(2,1)S(1)}) custom-call(s32[1]{0:T(128)} %bitcast.me, bf16[192,1280]{1,0:T(8,128)(2,1)S(1)} %constant_dynamic-update-slice_fusion.2.refs_0_, ...), custom_call_target="tpu_custom_call" | custom-call | flops 419430400 | bytes 1048576 | tf_op jit(solution)/shard_map/pallas_call | solution.py:55
  39.2 3.3 %collective-permute-start.15 = (bf16[2,320,128]{2,1,0:T(8,128)(2,1)S(1)}, bf16[2,320,128]{2,1,0:T(8,128)(2,1)S(1)}, u32[]{:S(2)}, u32[]{:S(2)}) collective-permute-start(bf16[2,320,128]{2,1,0:T(8,128)(2,1)S(1)} %get-tuple-element.36), channel_id=1, source_target_pairs={{0,4},{2,6},{4,0},{6,2},{1,5},{3,7},{5,1},{7,3},{8,12},{10,14},{12... | collective-permute-start | bytes 491528 | tf_op jit(solution)/shard_map/ppermute | solution.py:26
  42.5 0.7 collective-permute-start.16
  43.2 2.6 %collective-permute-start.17 = (bf16[2,320,128]{2,1,0:T(8,128)(2,1)S(1)}, bf16[2,320,128]{2,1,0:T(8,128)(2,1)S(1)}, u32[]{:S(2)}, u32[]{:S(2)}) collective-permute-start(bf16[2,320,128]{2,1,0:T(8,128)(2,1)S(1)} %get-tuple-element.40), channel_id=1, source_target_pairs={{0,6},{2,0},{4,2},{6,4},{1,7},{3,1},{5,3},{7,5},{8,14},{10,8},{12,... | collective-permute-start | bytes 491528 | tf_op jit(solution)/shard_map/ppermute | solution.py:26
  45.8 0.6 shard_map.76.p0
  46.3 1.5 %collective-permute-done.15.p1 = bf16[2,320,128]{2,1,0:T(8,128)(2,1)S(1)} collective-permute-done((bf16[2,320,128]{2,1,0:T(8,128)(2,1)S(1)}, bf16[2,320,128]{2,1,0:T(8,128)(2,1)S(1)}, u32[]{:S(2)}, u32[]{:S(2)}) %collective-permute-start.15) | collective-permute-done | bytes 163872 | tf_op jit(solution)/shard_map/ppermute | solution.py:26
  47.9 2.7 %collective-permute-done.16.p2 = bf16[2,320,128]{2,1,0:T(8,128)(2,1)S(1)} collective-permute-done((bf16[2,320,128]{2,1,0:T(8,128)(2,1)S(1)}, bf16[2,320,128]{2,1,0:T(8,128)(2,1)S(1)}, u32[]{:S(2)}, u32[]{:S(2)}) %collective-permute-start.16) | collective-permute-done | bytes 163872 | tf_op jit(solution)/shard_map/ppermute | solution.py:26
  50.6 0.3 collective-permute-done.17.p3
  50.9 0.2 shard_map.77.b0
  51.1 2.2 %collective-permute-start.18 = (bf16[2,320,128]{2,1,0:T(8,128)(2,1)S(1)}, bf16[2,320,128]{2,1,0:T(8,128)(2,1)S(1)}, u32[]{:S(2)}, u32[]{:S(2)}) collective-permute-start(bf16[2,320,128]{2,1,0:T(8,128)(2,1)S(1)} %shard_map.77.b0), channel_id=1, source_target_pairs={{0,4},{2,6},{4,0},{6,2},{1,5},{3,7},{5,1},{7,3},{8,12},{10,14},{12... | collective-permute-start | bytes 491528 | tf_op jit(solution)/shard_map/ppermute | solution.py:26
  53.2 2.0 %collective-permute-start.19 = (bf16[2,320,128]{2,1,0:T(8,128)(2,1)S(1)}, bf16[2,320,128]{2,1,0:T(8,128)(2,1)S(1)}, u32[]{:S(2)}, u32[]{:S(2)}) collective-permute-start(bf16[2,320,128]{2,1,0:T(8,128)(2,1)S(1)} %shard_map.77.b0), channel_id=1, source_target_pairs={{0,6},{2,0},{4,2},{6,4},{1,7},{3,1},{5,3},{7,5},{8,14},{10,8},{12,... | collective-permute-start | bytes 491528 | tf_op jit(solution)/shard_map/ppermute | solution.py:26
  55.3 4.1 %collective-permute-done.18.b2 = bf16[2,320,128]{2,1,0:T(8,128)(2,1)S(1)} collective-permute-done((bf16[2,320,128]{2,1,0:T(8,128)(2,1)S(1)}, bf16[2,320,128]{2,1,0:T(8,128)(2,1)S(1)}, u32[]{:S(2)}, u32[]{:S(2)}) %collective-permute-start.18) | collective-permute-done | bytes 163872 | tf_op jit(solution)/shard_map/ppermute | solution.py:26
  59.3 2.4 %collective-permute-done.19.b1 = bf16[2,320,128]{2,1,0:T(8,128)(2,1)S(1)} collective-permute-done((bf16[2,320,128]{2,1,0:T(8,128)(2,1)S(1)}, bf16[2,320,128]{2,1,0:T(8,128)(2,1)S(1)}, u32[]{:S(2)}, u32[]{:S(2)}) %collective-permute-start.19) | collective-permute-done | bytes 163872 | tf_op jit(solution)/shard_map/ppermute | solution.py:26
  61.7 0.6 collective-permute-done.20.b3
  62.3 0.7 shard_map.78
  63.0 1.6 %shard_map.79 = (f32[256,1280]{1,0:T(8,128)S(1)}, f32[256,1280]{1,0:T(8,128)S(1)}, bf16[320,1280]{1,0:T(8,128)(2,1)S(1)}, bf16[192,1280]{1,0:T(8,128)(2,1)S(1)}) custom-call(s32[1]{0:T(128)} %bitcast.me, bf16[2,320,512]{2,1,0:T(8,128)(2,1)S(1)} %get-tuple-element.41.full, bf16[160,1280]{1,0:T(8,128)(2,1)S(1)} %bitcast.7, bf16[160,1280]{1,0:T(8,128)(2,1)S(1)} %copy-done.1, ...), custom_call_target="tpu_custom_call" | custom-call | flops 838860800 | bytes 1048576 | tf_op jit(solution)/shard_map/pallas_call | solution.py:55
  64.6 0.1 collective-permute-start.21
  64.7 1.9 %collective-permute-done.21 = bf16[192,1280]{1,0:T(8,128)(2,1)S(1)} collective-permute-done((bf16[192,1280]{1,0:T(8,128)(2,1)S(1)}, bf16[192,1280]{1,0:T(8,128)(2,1)S(1)}, u32[]{:S(2)}, u32[]{:S(2)}) %collective-permute-start.21) | collective-permute-done | bytes 491552 | tf_op jit(solution)/shard_map/ppermute | solution.py:26
  66.6 0.1 collective-permute-start.22
  66.7 0.1 convert_element_type.63
  66.8 1.7 %collective-permute-start.23 = (bf16[96,1280]{1,0:T(8,128)(2,1)S(1)}, bf16[96,1280]{1,0:T(8,128)(2,1)S(1)}, u32[]{:S(2)}, u32[]{:S(2)}) collective-permute-start(bf16[96,1280]{1,0:T(8,128)(2,1)S(1)} %fusion.2), channel_id=1, source_target_pairs={{0,8},{8,0},{16,24},{24,16},{1,9},{9,1},{17,25},{25,17},{2,10},{10... | collective-permute-start | bytes 737288 | tf_op jit(solution)/shard_map/ppermute | solution.py:30
  68.5 1.4 %collective-permute-start.33 = (bf16[320,1280]{1,0:T(8,128)(2,1)S(1)}, bf16[320,1280]{1,0:T(8,128)(2,1)S(1)}, u32[]{:S(2)}, u32[]{:S(2)}) collective-permute-start(bf16[320,1280]{1,0:T(8,128)(2,1)S(1)} %get-tuple-element.57), channel_id=1, source_target_pairs={{0,24},{24,0},{8,16},{16,8},{1,25},{25,1},{9,17},{17,9},{2,26},{26... | collective-permute-start | bytes 2457608 | tf_op jit(solution)/shard_map/ppermute | solution.py:34
  70.0 0.6 shard_map.80
  70.6 0.1 convert_element_type.62
  70.7 0.2 fusion.9
  71.0 0.1 collective-permute-start.26
  71.1 3.3 %collective-permute-start.27 = (bf16[64,1280]{1,0:T(8,128)(2,1)S(1)}, bf16[64,1280]{1,0:T(8,128)(2,1)S(1)}, u32[]{:S(2)}, u32[]{:S(2)}) collective-permute-start(bf16[64,1280]{1,0:T(8,128)(2,1)S(1)} %pad_maximum_fusion.3), channel_id=1, source_target_pairs={{0,224},{32,0},{64,32},{96,64},{128,96},{160,128},{192,160},{224,1... | collective-permute-start | bytes 491528 | tf_op jit(solution)/shard_map/ppermute | solution.py:26
  74.4 0.8 collective-permute-done.23
  75.2 0.1 fusion.1
  75.3 0.1 collective-permute-start.24
  75.4 0.8 collective-permute-start.25
  76.2 1.9 %collective-permute-done.26 = bf16[64,1280]{1,0:T(8,128)(2,1)S(1)} collective-permute-done((bf16[64,1280]{1,0:T(8,128)(2,1)S(1)}, bf16[64,1280]{1,0:T(8,128)(2,1)S(1)}, u32[]{:S(2)}, u32[]{:S(2)}) %collective-permute-start.26) | collective-permute-done | bytes 163872 | tf_op jit(solution)/shard_map/ppermute | solution.py:26
  78.2 0.8 collective-permute-start.31
  79.0 1.7 %collective-permute-start.29 = (bf16[64,1280]{1,0:T(8,128)(2,1)S(1)}, bf16[64,1280]{1,0:T(8,128)(2,1)S(1)}, u32[]{:S(2)}, u32[]{:S(2)}) collective-permute-start(bf16[64,1280]{1,0:T(8,128)(2,1)S(1)} %slice.144), channel_id=1, source_target_pairs={{0,8},{8,0},{16,24},{24,16},{1,9},{9,1},{17,25},{25,17},{2,10},{10... | collective-permute-start | bytes 491528 | tf_op jit(solution)/shard_map/ppermute | solution.py:30
  80.7 3.6 %collective-permute-done.29 = bf16[64,1280]{1,0:T(8,128)(2,1)S(1)} collective-permute-done((bf16[64,1280]{1,0:T(8,128)(2,1)S(1)}, bf16[64,1280]{1,0:T(8,128)(2,1)S(1)}, u32[]{:S(2)}, u32[]{:S(2)}) %collective-permute-start.29) | collective-permute-done | bytes 163872 | tf_op jit(solution)/shard_map/ppermute | solution.py:30
  84.4 1.6 %collective-permute-start.28 = (bf16[32,1280]{1,0:T(8,128)(2,1)S(1)}, bf16[32,1280]{1,0:T(8,128)(2,1)S(1)}, u32[]{:S(2)}, u32[]{:S(2)}) collective-permute-start(bf16[32,1280]{1,0:T(8,128)(2,1)S(1)} %fusion.8), channel_id=1, source_target_pairs={{0,8},{8,0},{16,24},{24,16},{1,9},{9,1},{17,25},{25,17},{2,10},{10... | collective-permute-start | bytes 245768 | tf_op jit(solution)/shard_map/ppermute | solution.py:30
  86.1 0.1 fusion.3
  86.1 0.8 collective-permute-start.30
  86.9 3.4 %collective-permute-start.32 = (bf16[32,1280]{1,0:T(8,128)(2,1)S(1)}, bf16[32,1280]{1,0:T(8,128)(2,1)S(1)}, u32[]{:S(2)}, u32[]{:S(2)}) collective-permute-start(bf16[32,1280]{1,0:T(8,128)(2,1)S(1)} %get-tuple-element.66), channel_id=1, source_target_pairs={{0,192},{32,224},{64,0},{96,32},{128,64},{160,96},{192,128},{224,1... | collective-permute-start | bytes 245768 | tf_op jit(solution)/shard_map/ppermute | solution.py:26
  90.3 1.3 %convert_add_fusion = (f32[160,1280]{1,0:T(8,128)}, f32[1280,160]{0,1:T(8,128)}) fusion(f32[160,1280]{1,0:T(8,128)S(1)} %get-tuple-element.48, bf16[320,1280]{1,0:T(8,128)(2,1)S(1)} %collective-permute-done.33, f32[160,1280]{1,0:T(8,128)S(1)} %get-tuple-element.55), kind=kLoop, calls=%fused_computation.1 | loop fusion | flops 819200 | bytes 4096000 | tf_op jit(solution)/shard_map/add | solution.py:223
  91.7 1.8 %collective-permute-done.30 = bf16[32,1280]{1,0:T(8,128)(2,1)S(1)} collective-permute-done((bf16[32,1280]{1,0:T(8,128)(2,1)S(1)}, bf16[32,1280]{1,0:T(8,128)(2,1)S(1)}, u32[]{:S(2)}, u32[]{:S(2)}) %collective-permute-start.30) | collective-permute-done | bytes 81952 | tf_op jit(solution)/shard_map/ppermute | solution.py:26
  93.5 0.1 fusion.6
  93.5 0.6 fusion.14
  (52 shorter events, 0.5 us)
Async XLA Ops:
  0.6 20.0 %copy-start.2 = (bf16[16,1280]{1,0:T(8,128)(2,1)S(1)}, bf16[16,1280]{1,0:T(8,128)(2,1)}, u32[]{:S(2)}) copy-start(bf16[16,1280]{1,0:T(8,128)(2,1)} %param.4) | copy-start | bytes 122884
  0.6 20.0 %copy-start.3 = (bf16[16,1280]{1,0:T(8,128)(2,1)S(1)}, bf16[16,1280]{1,0:T(8,128)(2,1)}, u32[]{:S(2)}) copy-start(bf16[16,1280]{1,0:T(8,128)(2,1)} %param.7) | copy-start | bytes 122884
  2.3 10.3 %collective-permute-start.1 = (bf16[32,1280]{1,0:T(8,128)(2,1)S(1)}, bf16[32,1280]{1,0:T(8,128)(2,1)S(1)}, u32[]{:S(2)}, u32[]{:S(2)}) collective-permute-start(bf16[32,1280]{1,0:T(8,128)(2,1)S(1)} %constant_dynamic-update-slice_fusion), channel_id=1, source_target_pairs={{0,192},{32,224},{64,0},{96,32},{128,64},{160,96},{192,128},{224,1... | collective-permute-start | bytes 245768 | tf_op jit(solution)/shard_map/ppermute | solution.py:26
  8.6 7.3 %collective-permute-start.5 = (bf16[32,1280]{1,0:T(8,128)(2,1)S(1)}, bf16[32,1280]{1,0:T(8,128)(2,1)S(1)}, u32[]{:S(2)}, u32[]{:S(2)}) collective-permute-start(bf16[32,1280]{1,0:T(8,128)(2,1)S(1)} %constant_dynamic-update-slice_fusion), channel_id=1, source_target_pairs={{0,64},{32,96},{64,128},{96,160},{128,192},{160,224},{192,0},{224,... | collective-permute-start | bytes 245768 | tf_op jit(solution)/shard_map/ppermute | solution.py:26
  8.6 12.1 %collective-permute-start = (bf16[32,1280]{1,0:T(8,128)(2,1)S(1)}, bf16[32,1280]{1,0:T(8,128)(2,1)S(1)}, u32[]{:S(2)}, u32[]{:S(2)}) collective-permute-start(bf16[32,1280]{1,0:T(8,128)(2,1)S(1)} %constant_dynamic-update-slice_fusion), channel_id=1, source_target_pairs={{0,8},{8,0},{16,24},{24,16},{1,9},{9,1},{17,25},{25,17},{2,10},{10... | collective-permute-start | bytes 245768 | tf_op jit(solution)/shard_map/ppermute | solution.py:30
  10.3 26.2 %copy-start = (bf16[1280,160]{0,1:T(8,128)(2,1)S(1)}, bf16[1280,160]{0,1:T(8,128)(2,1)}, u32[]{:S(2)}) copy-start(bf16[1280,160]{0,1:T(8,128)(2,1)} %param.5) | copy-start | bytes 1228804
  10.3 26.2 %copy-start.1 = (bf16[160,1280]{1,0:T(8,128)(2,1)S(1)}, bf16[160,1280]{1,0:T(8,128)(2,1)}, u32[]{:S(2)}) copy-start(bf16[160,1280]{1,0:T(8,128)(2,1)} %wo.3) | copy-start | bytes 1228804
  10.3 23.5 %collective-permute-start.10 = (bf16[320,1280]{1,0:T(8,128)(2,1)S(1)}, bf16[320,1280]{1,0:T(8,128)(2,1)S(1)}, u32[]{:S(2)}, u32[]{:S(2)}) collective-permute-start(bf16[320,1280]{1,0:T(8,128)(2,1)S(1)} %pad_maximum_fusion), channel_id=1, source_target_pairs={{0,24},{24,0},{8,16},{16,8},{1,25},{25,1},{9,17},{17,9},{2,26},{26... | collective-permute-start | bytes 2457608 | tf_op jit(solution)/shard_map/ppermute | solution.py:34
  15.9 17.3 %collective-permute-start.6 = (bf16[64,1280]{1,0:T(8,128)(2,1)S(1)}, bf16[64,1280]{1,0:T(8,128)(2,1)S(1)}, u32[]{:S(2)}, u32[]{:S(2)}) collective-permute-start(bf16[64,1280]{1,0:T(8,128)(2,1)S(1)} %get-tuple-element.77), channel_id=1, source_target_pairs={{0,8},{8,0},{16,24},{24,16},{1,9},{9,1},{17,25},{25,17},{2,10},{10... | collective-permute-start | bytes 491528 | tf_op jit(solution)/shard_map/ppermute | solution.py:30
  16.5 10.0 %collective-permute-start.8 = (bf16[32,1280]{1,0:T(8,128)(2,1)S(1)}, bf16[32,1280]{1,0:T(8,128)(2,1)S(1)}, u32[]{:S(2)}, u32[]{:S(2)}) collective-permute-start(bf16[32,1280]{1,0:T(8,128)(2,1)S(1)} %collective-permute-done.5), channel_id=1, source_target_pairs={{0,64},{32,96},{64,128},{96,160},{128,192},{160,224},{192,0},{224,... | collective-permute-start | bytes 245768 | tf_op jit(solution)/shard_map/ppermute | solution.py:26
  16.5 6.2 %collective-permute-start.2 = (bf16[32,1280]{1,0:T(8,128)(2,1)S(1)}, bf16[32,1280]{1,0:T(8,128)(2,1)S(1)}, u32[]{:S(2)}, u32[]{:S(2)}) collective-permute-start(bf16[32,1280]{1,0:T(8,128)(2,1)S(1)} %collective-permute-done.1), channel_id=1, source_target_pairs={{0,224},{32,0},{64,32},{96,64},{128,96},{160,128},{192,160},{224,1... | collective-permute-start | bytes 245768 | tf_op jit(solution)/shard_map/ppermute | solution.py:26
  20.7 5.8 %collective-permute-start.7 = (bf16[32,1280]{1,0:T(8,128)(2,1)S(1)}, bf16[32,1280]{1,0:T(8,128)(2,1)S(1)}, u32[]{:S(2)}, u32[]{:S(2)}) collective-permute-start(bf16[32,1280]{1,0:T(8,128)(2,1)S(1)} %collective-permute-done.5), channel_id=1, source_target_pairs={{0,32},{32,64},{64,96},{96,128},{128,160},{160,192},{192,224},{224... | collective-permute-start | bytes 245768 | tf_op jit(solution)/shard_map/ppermute | solution.py:26
  22.7 6.5 %collective-permute-start.3 = (bf16[64,1280]{1,0:T(8,128)(2,1)S(1)}, bf16[64,1280]{1,0:T(8,128)(2,1)S(1)}, u32[]{:S(2)}, u32[]{:S(2)}) collective-permute-start(bf16[64,1280]{1,0:T(8,128)(2,1)S(1)} %pad_maximum_fusion.1), channel_id=1, source_target_pairs={{0,224},{32,0},{64,32},{96,64},{128,96},{160,128},{192,160},{224,1... | collective-permute-start | bytes 491528 | tf_op jit(solution)/shard_map/ppermute | solution.py:26
  26.4 6.6 %collective-permute-start.4 = (bf16[64,1280]{1,0:T(8,128)(2,1)S(1)}, bf16[64,1280]{1,0:T(8,128)(2,1)S(1)}, u32[]{:S(2)}, u32[]{:S(2)}) collective-permute-start(bf16[64,1280]{1,0:T(8,128)(2,1)S(1)} %pad_maximum_fusion.1), channel_id=1, source_target_pairs={{0,32},{32,64},{64,96},{96,128},{128,160},{160,192},{192,224},{224... | collective-permute-start | bytes 491528 | tf_op jit(solution)/shard_map/ppermute | solution.py:26
  26.6 7.3 %collective-permute-start.9 = (bf16[96,1280]{1,0:T(8,128)(2,1)S(1)}, bf16[96,1280]{1,0:T(8,128)(2,1)}, u32[]{:S(2)}, u32[]{:S(2)}) collective-permute-start(bf16[96,1280]{1,0:T(8,128)(2,1)S(1)} %constant_dynamic-update-slice_fusion.10.refs_2_), channel_id=1, source_target_pairs={{0,8},{8,0},{16,24},{24,16},{1,9},{9,1},{17,25},{25,17},{2,10},{10... | collective-permute-start | bytes 737288 | tf_op jit(solution)/shard_map/ppermute | solution.py:30
  33.0 2.9 %collective-permute-start.11 = (bf16[192,1280]{1,0:T(8,128)(2,1)S(1)}, bf16[192,1280]{1,0:T(8,128)(2,1)S(1)}, u32[]{:S(2)}, u32[]{:S(2)}) collective-permute-start(bf16[192,1280]{1,0:T(8,128)(2,1)S(1)} %constant_dynamic-update-slice_fusion.2.refs_0_), channel_id=1, source_target_pairs={{0,1},{1,0},{2,3},{3,2},{4,5},{5,4},{6,7},{7,6},{8,9},{9,8},{10,11... | collective-permute-start | bytes 1474568 | tf_op jit(solution)/shard_map/ppermute | solution.py:26
  33.2 2.8 %collective-permute-start.12 = (bf16[128,1280]{1,0:T(8,128)(2,1)S(1)}, bf16[128,1280]{1,0:T(8,128)(2,1)S(1)}, u32[]{:S(2)}, u32[]{:S(2)}) collective-permute-start(bf16[128,1280]{1,0:T(8,128)(2,1)S(1)} %constant_dynamic-update-slice_fusion.7.refs_1_), channel_id=1, source_target_pairs={{0,1},{1,0},{2,3},{3,2},{4,5},{5,4},{6,7},{7,6},{8,9},{9,8},{10,11... | collective-permute-start | bytes 983048 | tf_op jit(solution)/shard_map/ppermute | solution.py:26
  33.8 2.2 %collective-permute-start.13 = (bf16[96,1280]{1,0:T(8,128)(2,1)S(1)}, bf16[96,1280]{1,0:T(8,128)(2,1)}, u32[]{:S(2)}, u32[]{:S(2)}) collective-permute-start(bf16[96,1280]{1,0:T(8,128)(2,1)S(1)} %constant_dynamic-update-slice_fusion.10.refs_2_), channel_id=1, source_target_pairs={{0,1},{1,0},{2,3},{3,2},{4,5},{5,4},{6,7},{7,6},{8,9},{9,8},{10,11... | collective-permute-start | bytes 737288 | tf_op jit(solution)/shard_map/ppermute | solution.py:26
  33.9 2.7 %collective-permute-start.14 = (bf16[96,1280]{1,0:T(8,128)(2,1)}, bf16[96,1280]{1,0:T(8,128)(2,1)}, u32[]{:S(2)}, u32[]{:S(2)}) collective-permute-start(bf16[96,1280]{1,0:T(8,128)(2,1)} %collective-permute-done.9.refs_3_), channel_id=1, source_target_pairs={{0,1},{1,0},{2,3},{3,2},{4,5},{5,4},{6,7},{7,6},{8,9},{9,8},{10,11... | collective-permute-start | bytes 737288 | tf_op jit(solution)/shard_map/ppermute | solution.py:26
  39.2 8.6 %collective-permute-start.15 = (bf16[2,320,128]{2,1,0:T(8,128)(2,1)S(1)}, bf16[2,320,128]{2,1,0:T(8,128)(2,1)S(1)}, u32[]{:S(2)}, u32[]{:S(2)}) collective-permute-start(bf16[2,320,128]{2,1,0:T(8,128)(2,1)S(1)} %get-tuple-element.36), channel_id=1, source_target_pairs={{0,4},{2,6},{4,0},{6,2},{1,5},{3,7},{5,1},{7,3},{8,12},{10,14},{12... | collective-permute-start | bytes 491528 | tf_op jit(solution)/shard_map/ppermute | solution.py:26
  42.5 8.1 %collective-permute-start.16 = (bf16[2,320,128]{2,1,0:T(8,128)(2,1)S(1)}, bf16[2,320,128]{2,1,0:T(8,128)(2,1)S(1)}, u32[]{:S(2)}, u32[]{:S(2)}) collective-permute-start(bf16[2,320,128]{2,1,0:T(8,128)(2,1)S(1)} %get-tuple-element.39), channel_id=1, source_target_pairs={{0,2},{2,4},{4,6},{6,0},{1,3},{3,5},{5,7},{7,1},{8,10},{10,12},{12... | collective-permute-start | bytes 491528 | tf_op jit(solution)/shard_map/ppermute | solution.py:26
  43.2 7.7 %collective-permute-start.17 = (bf16[2,320,128]{2,1,0:T(8,128)(2,1)S(1)}, bf16[2,320,128]{2,1,0:T(8,128)(2,1)S(1)}, u32[]{:S(2)}, u32[]{:S(2)}) collective-permute-start(bf16[2,320,128]{2,1,0:T(8,128)(2,1)S(1)} %get-tuple-element.40), channel_id=1, source_target_pairs={{0,6},{2,0},{4,2},{6,4},{1,7},{3,1},{5,3},{7,5},{8,14},{10,8},{12,... | collective-permute-start | bytes 491528 | tf_op jit(solution)/shard_map/ppermute | solution.py:26
  51.1 8.2 %collective-permute-start.18 = (bf16[2,320,128]{2,1,0:T(8,128)(2,1)S(1)}, bf16[2,320,128]{2,1,0:T(8,128)(2,1)S(1)}, u32[]{:S(2)}, u32[]{:S(2)}) collective-permute-start(bf16[2,320,128]{2,1,0:T(8,128)(2,1)S(1)} %shard_map.77.b0), channel_id=1, source_target_pairs={{0,4},{2,6},{4,0},{6,2},{1,5},{3,7},{5,1},{7,3},{8,12},{10,14},{12... | collective-permute-start | bytes 491528 | tf_op jit(solution)/shard_map/ppermute | solution.py:26
  53.2 8.5 %collective-permute-start.19 = (bf16[2,320,128]{2,1,0:T(8,128)(2,1)S(1)}, bf16[2,320,128]{2,1,0:T(8,128)(2,1)S(1)}, u32[]{:S(2)}, u32[]{:S(2)}) collective-permute-start(bf16[2,320,128]{2,1,0:T(8,128)(2,1)S(1)} %shard_map.77.b0), channel_id=1, source_target_pairs={{0,6},{2,0},{4,2},{6,4},{1,7},{3,1},{5,3},{7,5},{8,14},{10,8},{12,... | collective-permute-start | bytes 491528 | tf_op jit(solution)/shard_map/ppermute | solution.py:26
  55.2 7.1 %collective-permute-start.20 = (bf16[2,320,128]{2,1,0:T(8,128)(2,1)S(1)}, bf16[2,320,128]{2,1,0:T(8,128)(2,1)S(1)}, u32[]{:S(2)}, u32[]{:S(2)}) collective-permute-start(bf16[2,320,128]{2,1,0:T(8,128)(2,1)S(1)} %shard_map.77.b0), channel_id=1, source_target_pairs={{0,2},{2,4},{4,6},{6,0},{1,3},{3,5},{5,7},{7,1},{8,10},{10,12},{12... | collective-permute-start | bytes 491528 | tf_op jit(solution)/shard_map/ppermute | solution.py:26
  64.6 2.0 %collective-permute-start.21 = (bf16[192,1280]{1,0:T(8,128)(2,1)S(1)}, bf16[192,1280]{1,0:T(8,128)(2,1)S(1)}, u32[]{:S(2)}, u32[]{:S(2)}) collective-permute-start(bf16[192,1280]{1,0:T(8,128)(2,1)S(1)} %get-tuple-element.44), channel_id=1, source_target_pairs={{0,1},{1,0},{2,3},{3,2},{4,5},{5,4},{6,7},{7,6},{8,9},{9,8},{10,11... | collective-permute-start | bytes 1474568 | tf_op jit(solution)/shard_map/ppermute | solution.py:26
  66.6 4.0 %collective-permute-start.22 = (bf16[320,1280]{1,0:T(8,128)(2,1)S(1)}, bf16[320,1280]{1,0:T(8,128)(2,1)S(1)}, u32[]{:S(2)}, u32[]{:S(2)}) collective-permute-start(bf16[320,1280]{1,0:T(8,128)(2,1)S(1)} %get-tuple-element.45), channel_id=1, source_target_pairs={{0,1},{1,0},{2,3},{3,2},{4,5},{5,4},{6,7},{7,6},{8,9},{9,8},{10,11... | collective-permute-start | bytes 2457608 | tf_op jit(solution)/shard_map/ppermute | solution.py:26
  66.8 8.3 %collective-permute-start.23 = (bf16[96,1280]{1,0:T(8,128)(2,1)S(1)}, bf16[96,1280]{1,0:T(8,128)(2,1)S(1)}, u32[]{:S(2)}, u32[]{:S(2)}) collective-permute-start(bf16[96,1280]{1,0:T(8,128)(2,1)S(1)} %fusion.2), channel_id=1, source_target_pairs={{0,8},{8,0},{16,24},{24,16},{1,9},{9,1},{17,25},{25,17},{2,10},{10... | collective-permute-start | bytes 737288 | tf_op jit(solution)/shard_map/ppermute | solution.py:30
  68.5 21.8 %collective-permute-start.33 = (bf16[320,1280]{1,0:T(8,128)(2,1)S(1)}, bf16[320,1280]{1,0:T(8,128)(2,1)S(1)}, u32[]{:S(2)}, u32[]{:S(2)}) collective-permute-start(bf16[320,1280]{1,0:T(8,128)(2,1)S(1)} %get-tuple-element.57), channel_id=1, source_target_pairs={{0,24},{24,0},{8,16},{16,8},{1,25},{25,1},{9,17},{17,9},{2,26},{26... | collective-permute-start | bytes 2457608 | tf_op jit(solution)/shard_map/ppermute | solution.py:34
  71.0 7.2 %collective-permute-start.26 = (bf16[64,1280]{1,0:T(8,128)(2,1)S(1)}, bf16[64,1280]{1,0:T(8,128)(2,1)S(1)}, u32[]{:S(2)}, u32[]{:S(2)}) collective-permute-start(bf16[64,1280]{1,0:T(8,128)(2,1)S(1)} %pad_maximum_fusion.2), channel_id=1, source_target_pairs={{0,32},{32,64},{64,96},{96,128},{128,160},{160,192},{192,224},{224... | collective-permute-start | bytes 491528 | tf_op jit(solution)/shard_map/ppermute | solution.py:26
  71.1 7.9 %collective-permute-start.27 = (bf16[64,1280]{1,0:T(8,128)(2,1)S(1)}, bf16[64,1280]{1,0:T(8,128)(2,1)S(1)}, u32[]{:S(2)}, u32[]{:S(2)}) collective-permute-start(bf16[64,1280]{1,0:T(8,128)(2,1)S(1)} %pad_maximum_fusion.3), channel_id=1, source_target_pairs={{0,224},{32,0},{64,32},{96,64},{128,96},{160,128},{192,160},{224,1... | collective-permute-start | bytes 491528 | tf_op jit(solution)/shard_map/ppermute | solution.py:26
  75.3 10.7 %collective-permute-start.24 = (bf16[32,1280]{1,0:T(8,128)(2,1)S(1)}, bf16[32,1280]{1,0:T(8,128)(2,1)S(1)}, u32[]{:S(2)}, u32[]{:S(2)}) collective-permute-start(bf16[32,1280]{1,0:T(8,128)(2,1)S(1)} %get-tuple-element.74), channel_id=1, source_target_pairs={{0,32},{32,64},{64,96},{96,128},{128,160},{160,192},{192,224},{224... | collective-permute-start | bytes 245768 | tf_op jit(solution)/shard_map/ppermute | solution.py:26
  75.4 10.7 %collective-permute-start.25 = (bf16[32,1280]{1,0:T(8,128)(2,1)S(1)}, bf16[32,1280]{1,0:T(8,128)(2,1)S(1)}, u32[]{:S(2)}, u32[]{:S(2)}) collective-permute-start(bf16[32,1280]{1,0:T(8,128)(2,1)S(1)} %get-tuple-element.73), channel_id=1, source_target_pairs={{0,64},{32,96},{64,128},{96,160},{128,192},{160,224},{192,0},{224,... | collective-permute-start | bytes 245768 | tf_op jit(solution)/shard_map/ppermute | solution.py:26
  78.2 7.9 %collective-permute-start.31 = (bf16[32,1280]{1,0:T(8,128)(2,1)S(1)}, bf16[32,1280]{1,0:T(8,128)(2,1)S(1)}, u32[]{:S(2)}, u32[]{:S(2)}) collective-permute-start(bf16[32,1280]{1,0:T(8,128)(2,1)S(1)} %get-tuple-element.72), channel_id=1, source_target_pairs={{0,224},{32,0},{64,32},{96,64},{128,96},{160,128},{192,160},{224,1... | collective-permute-start | bytes 245768 | tf_op jit(solution)/shard_map/ppermute | solution.py:26
  79.0 5.4 %collective-permute-start.29 = (bf16[64,1280]{1,0:T(8,128)(2,1)S(1)}, bf16[64,1280]{1,0:T(8,128)(2,1)S(1)}, u32[]{:S(2)}, u32[]{:S(2)}) collective-permute-start(bf16[64,1280]{1,0:T(8,128)(2,1)S(1)} %slice.144), channel_id=1, source_target_pairs={{0,8},{8,0},{16,24},{24,16},{1,9},{9,1},{17,25},{25,17},{2,10},{10... | collective-permute-start | bytes 491528 | tf_op jit(solution)/shard_map/ppermute | solution.py:30
  84.4 7.3 %collective-permute-start.28 = (bf16[32,1280]{1,0:T(8,128)(2,1)S(1)}, bf16[32,1280]{1,0:T(8,128)(2,1)S(1)}, u32[]{:S(2)}, u32[]{:S(2)}) collective-permute-start(bf16[32,1280]{1,0:T(8,128)(2,1)S(1)} %fusion.8), channel_id=1, source_target_pairs={{0,8},{8,0},{16,24},{24,16},{1,9},{9,1},{17,25},{25,17},{2,10},{10... | collective-permute-start | bytes 245768 | tf_op jit(solution)/shard_map/ppermute | solution.py:30
  86.1 7.4 %collective-permute-start.30 = (bf16[32,1280]{1,0:T(8,128)(2,1)S(1)}, bf16[32,1280]{1,0:T(8,128)(2,1)S(1)}, u32[]{:S(2)}, u32[]{:S(2)}) collective-permute-start(bf16[32,1280]{1,0:T(8,128)(2,1)S(1)} %get-tuple-element.67), channel_id=1, source_target_pairs={{0,64},{32,96},{64,128},{96,160},{128,192},{160,224},{192,0},{224,... | collective-permute-start | bytes 245768 | tf_op jit(solution)/shard_map/ppermute | solution.py:26
  86.9 6.6 %collective-permute-start.32 = (bf16[32,1280]{1,0:T(8,128)(2,1)S(1)}, bf16[32,1280]{1,0:T(8,128)(2,1)S(1)}, u32[]{:S(2)}, u32[]{:S(2)}) collective-permute-start(bf16[32,1280]{1,0:T(8,128)(2,1)S(1)} %get-tuple-element.66), channel_id=1, source_target_pairs={{0,192},{32,224},{64,0},{96,32},{128,64},{160,96},{192,128},{224,1... | collective-permute-start | bytes 245768 | tf_op jit(solution)/shard_map/ppermute | solution.py:26

commit v9 on v8

--- a/solution.py
+++ b/solution.py
@@ -38,7 +38,7 @@
     return lax.optimization_barrier((value, other))[0]
 
 
-def call(body, outs, args, flops=1 << 20, scratch=()):
+def call(body, outs, args, flops=1 << 20, scratch=(), aliases=None):
     specs = [pl.BlockSpec(memory_space=pltpu.SMEM)]
     specs += [pl.BlockSpec(memory_space=pltpu.VMEM)] * (len(args) - 1)
     kernel = pl.pallas_call(
@@ -47,6 +47,7 @@
         in_specs=specs,
         out_specs=[pl.BlockSpec(memory_space=pltpu.VMEM)] * len(outs),
         scratch_shapes=list(scratch),
+        input_output_aliases=aliases or {},
         compiler_params=pltpu.CompilerParams(vmem_limit_bytes=40 << 20),
         cost_estimate=pl.CostEstimate(
             flops=flops, bytes_accessed=1 << 20, transcendentals=0
@@ -72,31 +73,39 @@
         part[s, h:] = dot(w_pair[s * h : s * h + h], value_of(s), 1, 1).astype(part.dtype)
 
 
-def quarter_of(tok, cot, index):
-    rows = pl.ds(pl.multiple_of(index % 4 * 128, 128), 128)
-    return lambda s: (tok, cot)[s][rows]
-
-
-def up_kernel(me, *refs):
-    held, (wi, wo, w_pair, tok, cot), parts = refs[:8], refs[8:13], refs[13:]
-    for q in range(4):
-        half, chip = q // 2 * 4, q % 2
-        for j in range(8):
-            if j < 3:
-                ref, i = held[half], j * 64 + chip * 32
-            elif j < HEAD:
-                ref, i = held[half + 1], chip * 64 + (j - 3) * 32
-            else:
-                ref, i = held[half + 2 + chip], (j - HEAD) * 32
-            row = q * 128 + j * 16
-            tok[row : row + 16] = ref[i : i + 16]
-            cot[row : row + 16] = ref[i + 16 : i + 32]
-    for k, part in zip((2, 1, 3), parts):
-        products(quarter_of(tok, cot, me[0] + k), wi, wo, w_pair, part)
-
-
-def mine_kernel(me, tok, cot, wi, wo, w_pair, part):
-    products(quarter_of(tok, cot, me[0]), wi, wo, w_pair, part)
+def order_tokens(q, held, slots, tok, cot):
+    first, second, third = held
+    chip = q % 2
+    for j in slots:
+        if j < 3:
+            ref, i = first, j * 64 + chip * 32
+        elif j < HEAD:
+            ref, i = second, chip * 64 + (j - 3) * 32
+        else:
+            ref, i = third, (j - HEAD) * 32
+        row = q * 128 + j * 16
+        tok[row : row + 16] = ref[i : i + 16]
+        cot[row : row + 16] = ref[i + 16 : i + 32]
+
+
+def up_kernel(me, a0, a1, a2, a3, b0, b1, b2, wi, wo, w_pair, tok, cot, whole):
+    del me
+    order_tokens(0, (a0, a1, a2), range(8), tok, cot)
+    order_tokens(1, (a0, a1, a3), range(8), tok, cot)
+    order_tokens(2, (b0, b1, b2), range(8), tok, cot)
+    order_tokens(3, (b0, b1, None), range(HEAD), tok, cot)
+    for q in range(3):
+        rows = slice(q * 128, q * 128 + 128)
+        products(lambda s: (tok, cot)[s][rows], wi, wo, w_pair, whole.at[q])
+
+
+def last_kernel(me, tok_in, cot_in, b3, wi, wo, w_pair, three, tok, cot, p0, p2, p1, p3, whole):
+    del tok_in, cot_in
+    order_tokens(3, (None, None, b3), range(HEAD, 8), tok, cot)
+    whole[:3] = three[...]
+    products(lambda s: (tok, cot)[s][384:], wi, wo, w_pair, whole.at[3])
+    for k, part in ((2, p2), (1, p1), (3, p3), (0, p0)):
+        part[...] = whole[(me[0] + k) % 4].astype(part.dtype)
 
 
 def act_kernel(me, p0, p1, p2, p3, out):
@@ -109,8 +118,10 @@
     out[1] = (grad_act * smooth_slope(pre)).astype(BF)
 
 
-def down_kernel(me, full, wi, wo, w_pair, near, far, head, tail):
-    del me
+def down_kernel(me, c0, c2, c1, c3, wi, wo, w_pair, near, far, head, tail, full):
+    for k, block in ((0, c0), (2, c2), (1, c1), (3, c3)):
+        lane = pl.multiple_of(((me[0] + k) % 4) * 128, 128)
+        full[:, :, pl.ds(lane, 128)] = block[...]
     h = wi.shape[0]
     for s, w in enumerate((wo, wi)):
         value = dot(full[s, :h], w[...], 0, 0)
@@ -129,11 +140,9 @@
                     tail[row : row + 16] = piece.astype(BF)
 
 
-def pair_kernel(me, b0, b2, b1, b3, tok, cot, full, out):
+def pair_kernel(me, full, tok, cot, out):
+    del me
     h = full.shape[1] // 2
-    for k, block in ((0, b0), (2, b2), (1, b1), (3, b3)):
-        lane = pl.multiple_of(((me[0] + k) % 4) * 128, 128)
-        full[:, :, pl.ds(lane, 128)] = block[...]
     out[:h] = dot(full[0, h:], cot[...], 1, 0).astype(BF)
     out[h:] = dot(full[1, h:], tok[...], 1, 0).astype(BF)
 
@@ -169,25 +178,27 @@
 
     part, rounded = shape((2, 2 * h, 128), F32), shape((2, 2 * h, 128), BF)
     weights = [w_in_t, w_out, w_pair]
+    tokens_all = [shape((512, d), BF)] * 2
+    tok, cot, three = call(
+        up_kernel, tokens_all + [shape((3, *part.shape), F32)], [me, *held[:7], *weights], flops
+    )
     tok, cot, *parts = call(
-        up_kernel, [shape((512, d), BF)] * 2 + [rounded] * 3, [me, *held, *weights], flops
-    )
-    mine = call(mine_kernel, [part], [me, after(tok, parts[0]), cot, *weights], flops)
-    parts = mine + [send(value, "row", k) for k, value in zip((2, 1, 3), parts)]
+        last_kernel,
+        tokens_all + [part] + [rounded] * 3,
+        [me, tok, cot, held[7], *weights, three],
+        flops,
+        [pltpu.VMEM((4, *part.shape), F32)],
+        {1: 0, 2: 1},
+    )
+    parts[1:] = [send(value, "row", k) for k, value in zip((2, 1, 3), parts[1:])]
     (block,) = call(act_kernel, [rounded], [me, *parts])
     blocks = [block] + [send(block, "row", -k) for k in (2, 1, 3)]
 
     sums = shape((256, d), F32)
-    full, pair = call(
-        pair_kernel,
-        [shape((2, 2 * h, 512), BF), shape((2 * h, d), BF)],
-        [me, *blocks, tok, cot],
-        flops,
-    )
-    near, far, head, tail = call(
+    near, far, head, tail, full = call(
         down_kernel,
-        [sums, sums, shape((HEAD * 64, d), BF), shape(((8 - HEAD) * 64, d), BF)],
-        [me, full, w_in_t, w_out, w_pair],
+        [sums, sums, shape((HEAD * 64, d), BF), shape(((8 - HEAD) * 64, d), BF), shape((2, 2 * h, 512), BF)],
+        [me, *blocks, w_in_t, w_out, w_pair],
         2 * flops,
     )
     cut, rest = HEAD * 32, (8 - HEAD) * 32
@@ -196,11 +207,13 @@
     tail = tail.astype(F32)
     far_t = (far[cut:] + tail[:rest]).astype(BF)
     far = after(far, far_t)
-    pair = weight_pair(after(pair, far_t))
+    (pair,) = call(
+        pair_kernel, [shape((2 * h, d), BF)], [me, after(full, far_t), tok, cot], flops
+    )
+    pair = weight_pair(pair)
     grad_out, grad_in_t = call(
         own_kernel, [shape((h, d), F32)] * 2, [me, full, after(tok, far_t), cot], flops
     )
-    far_t = token_pair(far_t)
     head = after(head, grad_out)
     far_h = far[:cut] + head[:cut]
     near_h = near[:cut] + head[cut:]
@@ -208,7 +221,9 @@
     down_1 = cat([near_h[64:96], far_h[64:96]]).astype(BF)
     near = after(near, (up_1, down_1))
     up_1, down_1 = send(up_1, "z", 1).astype(F32), send(down_1, "z", -1).astype(F32)
-    far_2 = token_pair(far_h[96:].astype(BF)).astype(F32)
+    far_2 = far_h[96:].astype(BF)
+    far_t = after(token_pair(far_t), far_2)
+    far_2 = token_pair(far_2).astype(F32)
     third = (near[cut:] + tail[rest:] + far_t.astype(F32)).astype(BF)
     up, down = send(third[:32], "z", 1), send(third[32:64], "z", -1)
     up_2 = send(third[64:], "z", 2)

time: 94.4 us -> 95.6 us (1.013)
  starting transfers between devices: 47.2 us -> 49 us
  waiting for transfers between devices: 34 us -> 32.4 us
    ppermute x6, waiting for transfers between devices: 4.42 us -> 0.02 us  [token_pair(): return lax.ppermute(value, 'x', [(0, 1), (1, 0), (2, 3), (3, 2)])]
    ppermute x26, waiting for transfers between devices: 29.6 us -> 32.4 us  [send(): lax.ppermute(value, axis, [(i, (i + shift) % size) for i in range(size)])]
    ppermute x26, starting transfers between devices: 35.6 us -> 37 us  [send(): lax.ppermute(value, axis, [(i, (i + shift) % size) for i in range(size)])]
  transfers between devices with their start and end apart: 34 -> 34, of which waited for: 17 -> 15; matrix products, arithmetic and copies ran while one was open for 4% -> 4% of each run, Pallas kernels for 1% -> 4%
where the time goes in v9:
time: 95.6 us; the launch traced here: 95.3 us
  starting transfers between devices  49 us (51%)
  waiting for transfers between devices  32.4 us (34%)
  Pallas kernels  7.23 us (8%)
  other arithmetic  3.21 us (3%)
  local copies, waits for them, and re-layouts  2.47 us (3%)
  between operations  1.03 us (1%)
    ppermute x26, starting transfers between devices, send(): lax.ppermute(value, axis, [(i, (i + shift) % size) for i in range(size)])  37 us
    ppermute x26, waiting for transfers between devices, send(): lax.ppermute(value, axis, [(i, (i + shift) % size) for i in range(size)])  32.4 us
    ppermute x6, starting transfers between devices, token_pair(): return lax.ppermute(value, 'x', [(0, 1), (1, 0), (2, 3), (3, 2)])  8.2 us
    pallas_call x6, Pallas kernels, call(): return list(kernel(*args))  7.23 us
    ppermute x2, starting transfers between devices, weight_pair(): return lax.ppermute(value, 'x', [(0, 3), (3, 0), (1, 2), (2, 1)])  3.73 us
  transfers between devices with their start and end apart: 34, of which 15 were waited for; matrix products, arithmetic and copies ran while one was open for 4% of the time, Pallas kernels for 4%

profile of v9, /device:TPU:2, one launch (start us, length us, event | category | flops | bytes accessed | tf_op | source)
XLA Modules:
  0.0 95.3 jit_solution(17792646400023671526)
XLA Ops:
  0.6 0.0 copy-start.3
  0.7 0.8 constant_dynamic-update-slice_fusion.1
  1.5 0.8 constant_dynamic-update-slice_fusion
  2.3 6.3 %collective-permute-start.1 = (bf16[32,1280]{1,0:T(8,128)(2,1)S(1)}, bf16[32,1280]{1,0:T(8,128)(2,1)S(1)}, u32[]{:S(2)}, u32[]{:S(2)}) collective-permute-start(bf16[32,1280]{1,0:T(8,128)(2,1)S(1)} %constant_dynamic-update-slice_fusion), channel_id=1, source_target_pairs={{0,192},{32,224},{64,0},{96,32},{128,64},{160,96},{192,128},{224,1... | collective-permute-start | bytes 245768 | tf_op jit(solution)/shard_map/ppermute | solution.py:26
  8.6 0.5 collective-permute-start
  9.1 1.2 %pad_maximum_fusion = bf16[320,1280]{1,0:T(8,128)(2,1)S(1)} fusion(bf16[160,1280]{1,0:T(8,128)(2,1)} %wo.5, bf16[160,1280]{1,0:T(8,128)(2,1)} %bitcast.4), kind=kLoop, calls=%fused_computation | loop fusion | flops 1638400 | bytes 1638400 | tf_op jit(solution)/shard_map/concatenate | solution.py:60
  10.3 2.2 %collective-permute-start.10 = (bf16[320,1280]{1,0:T(8,128)(2,1)S(1)}, bf16[320,1280]{1,0:T(8,128)(2,1)S(1)}, u32[]{:S(2)}, u32[]{:S(2)}) collective-permute-start(bf16[320,1280]{1,0:T(8,128)(2,1)S(1)} %pad_maximum_fusion), channel_id=1, source_target_pairs={{0,24},{24,0},{8,16},{16,8},{1,25},{25,1},{9,17},{17,9},{2,26},{26... | collective-permute-start | bytes 2457608 | tf_op jit(solution)/shard_map/ppermute | solution.py:34
  12.6 3.3 %collective-permute-done.5 = bf16[32,1280]{1,0:T(8,128)(2,1)S(1)} collective-permute-done((bf16[32,1280]{1,0:T(8,128)(2,1)S(1)}, bf16[32,1280]{1,0:T(8,128)(2,1)S(1)}, u32[]{:S(2)}, u32[]{:S(2)}) %collective-permute-start.5) | collective-permute-done | bytes 81952 | tf_op jit(solution)/shard_map/ppermute | solution.py:26
  15.9 0.6 collective-permute-start.6
  16.5 4.2 %collective-permute-start.2 = (bf16[32,1280]{1,0:T(8,128)(2,1)S(1)}, bf16[32,1280]{1,0:T(8,128)(2,1)S(1)}, u32[]{:S(2)}, u32[]{:S(2)}) collective-permute-start(bf16[32,1280]{1,0:T(8,128)(2,1)S(1)} %collective-permute-done.1), channel_id=1, source_target_pairs={{0,224},{32,0},{64,32},{96,64},{128,96},{160,128},{192,160},{224,1... | collective-permute-start | bytes 245768 | tf_op jit(solution)/shard_map/ppermute | solution.py:26
  20.7 2.0 %collective-permute-done.2 = bf16[32,1280]{1,0:T(8,128)(2,1)S(1)} collective-permute-done((bf16[32,1280]{1,0:T(8,128)(2,1)S(1)}, bf16[32,1280]{1,0:T(8,128)(2,1)S(1)}, u32[]{:S(2)}, u32[]{:S(2)}) %collective-permute-start.2) | collective-permute-done | bytes 81952 | tf_op jit(solution)/shard_map/ppermute | solution.py:26
  22.7 3.7 %collective-permute-start.3 = (bf16[64,1280]{1,0:T(8,128)(2,1)S(1)}, bf16[64,1280]{1,0:T(8,128)(2,1)S(1)}, u32[]{:S(2)}, u32[]{:S(2)}) collective-permute-start(bf16[64,1280]{1,0:T(8,128)(2,1)S(1)} %pad_maximum_fusion.1), channel_id=1, source_target_pairs={{0,224},{32,0},{64,32},{96,64},{128,96},{160,128},{192,160},{224,1... | collective-permute-start | bytes 491528 | tf_op jit(solution)/shard_map/ppermute | solution.py:26
  26.4 0.1 collective-permute-start.4
  26.6 1.7 %collective-permute-start.9 = (bf16[96,1280]{1,0:T(8,128)(2,1)S(1)}, bf16[96,1280]{1,0:T(8,128)(2,1)}, u32[]{:S(2)}, u32[]{:S(2)}) collective-permute-start(bf16[96,1280]{1,0:T(8,128)(2,1)S(1)} %constant_dynamic-update-slice_fusion.10.a2), channel_id=1, source_target_pairs={{0,8},{8,0},{16,24},{24,16},{1,9},{9,1},{17,25},{25,17},{2,10},{10... | collective-permute-start | bytes 737288 | tf_op jit(solution)/shard_map/ppermute | solution.py:30
  28.2 1.0 %collective-permute-done.3 = bf16[64,1280]{1,0:T(8,128)(2,1)S(1)} collective-permute-done((bf16[64,1280]{1,0:T(8,128)(2,1)S(1)}, bf16[64,1280]{1,0:T(8,128)(2,1)S(1)}, u32[]{:S(2)}, u32[]{:S(2)}) %collective-permute-start.3) | collective-permute-done | bytes 163872 | tf_op jit(solution)/shard_map/ppermute | solution.py:26
  29.3 3.8 %collective-permute-done.4 = bf16[64,1280]{1,0:T(8,128)(2,1)S(1)} collective-permute-done((bf16[64,1280]{1,0:T(8,128)(2,1)S(1)}, bf16[64,1280]{1,0:T(8,128)(2,1)S(1)}, u32[]{:S(2)}, u32[]{:S(2)}) %collective-permute-start.4) | collective-permute-done | bytes 163872 | tf_op jit(solution)/shard_map/ppermute | solution.py:26
  33.0 0.1 collective-permute-start.11
  33.2 0.6 collective-permute-start.12
  33.8 0.1 collective-permute-start.13
  33.9 0.4 collective-permute-start.14
  34.3 1.7 %collective-permute-done.13.b2 = bf16[96,1280]{1,0:T(8,128)(2,1)} collective-permute-done((bf16[96,1280]{1,0:T(8,128)(2,1)S(1)}, bf16[96,1280]{1,0:T(8,128)(2,1)}, u32[]{:S(2)}, u32[]{:S(2)}) %collective-permute-start.13) | collective-permute-done | bytes 245792 | tf_op jit(solution)/shard_map/ppermute | solution.py:26
  36.0 2.5 %shard_map.75 = (bf16[512,1280]{1,0:T(8,128)(2,1)S(1)}, bf16[512,1280]{1,0:T(8,128)(2,1)S(1)}, f32[3,2,320,128]{3,2,1,0:T(8,128)S(1)}) custom-call(s32[1]{0:T(128)} %bitcast.me, bf16[192,1280]{1,0:T(8,128)(2,1)S(1)} %constant_dynamic-update-slice_fusion.2.a0, bf16[128,1280]{1,0:T(8,128)(2,1)S(1)} %constant_dynamic-update-slice_fusion.7.a1, ...), custom_call_target="tpu_custom_call" | custom-call | flops 419430400 | bytes 1048576 | tf_op jit(solution)/shard_map/pallas_call | solution.py:56
  38.5 1.7 %shard_map.76 = (bf16[512,1280]{1,0:T(8,128)(2,1)S(1)}, bf16[512,1280]{1,0:T(8,128)(2,1)S(1)}, f32[2,320,128]{2,1,0:T(8,128)S(1)}, bf16[2,320,128]{2,1,0:T(8,128...) custom-call(s32[1]{0:T(128)} %bitcast.me, ...), custom_call_target="tpu_custom_call", output_to_operand_aliasing={{0}: (1, {}), {1}: (2, {})} | custom-call | flops 419430400 | bytes 1048576 | tf_op jit(solution)/shard_map/pallas_call | solution.py:56
  40.2 3.3 %collective-permute-start.15 = (bf16[2,320,128]{2,1,0:T(8,128)(2,1)S(1)}, bf16[2,320,128]{2,1,0:T(8,128)(2,1)S(1)}, u32[]{:S(2)}, u32[]{:S(2)}) collective-permute-start(bf16[2,320,128]{2,1,0:T(8,128)(2,1)S(1)} %get-tuple-element.42), channel_id=1, source_target_pairs={{0,4},{2,6},{4,0},{6,2},{1,5},{3,7},{5,1},{7,3},{8,12},{10,14},{12... | collective-permute-start | bytes 491528 | tf_op jit(solution)/shard_map/ppermute | solution.py:26
  43.5 0.7 collective-permute-start.16
  44.1 2.6 %collective-permute-start.17 = (bf16[2,320,128]{2,1,0:T(8,128)(2,1)S(1)}, bf16[2,320,128]{2,1,0:T(8,128)(2,1)S(1)}, u32[]{:S(2)}, u32[]{:S(2)}) collective-permute-start(bf16[2,320,128]{2,1,0:T(8,128)(2,1)S(1)} %get-tuple-element.44), channel_id=1, source_target_pairs={{0,6},{2,0},{4,2},{6,4},{1,7},{3,1},{5,3},{7,5},{8,14},{10,8},{12,... | collective-permute-start | bytes 491528 | tf_op jit(solution)/shard_map/ppermute | solution.py:26
  46.7 2.1 %collective-permute-done.15.p1 = bf16[2,320,128]{2,1,0:T(8,128)(2,1)S(1)} collective-permute-done((bf16[2,320,128]{2,1,0:T(8,128)(2,1)S(1)}, bf16[2,320,128]{2,1,0:T(8,128)(2,1)S(1)}, u32[]{:S(2)}, u32[]{:S(2)}) %collective-permute-start.15) | collective-permute-done | bytes 163872 | tf_op jit(solution)/shard_map/ppermute | solution.py:26
  48.8 3.0 %collective-permute-done.16.p2 = bf16[2,320,128]{2,1,0:T(8,128)(2,1)S(1)} collective-permute-done((bf16[2,320,128]{2,1,0:T(8,128)(2,1)S(1)}, bf16[2,320,128]{2,1,0:T(8,128)(2,1)S(1)}, u32[]{:S(2)}, u32[]{:S(2)}) %collective-permute-start.16) | collective-permute-done | bytes 163872 | tf_op jit(solution)/shard_map/ppermute | solution.py:26
  51.7 0.3 collective-permute-done.17.p3
  52.1 0.2 shard_map.77.c0
  52.2 2.2 %collective-permute-start.18 = (bf16[2,320,128]{2,1,0:T(8,128)(2,1)S(1)}, bf16[2,320,128]{2,1,0:T(8,128)(2,1)S(1)}, u32[]{:S(2)}, u32[]{:S(2)}) collective-permute-start(bf16[2,320,128]{2,1,0:T(8,128)(2,1)S(1)} %shard_map.77.c0), channel_id=1, source_target_pairs={{0,4},{2,6},{4,0},{6,2},{1,5},{3,7},{5,1},{7,3},{8,12},{10,14},{12... | collective-permute-start | bytes 491528 | tf_op jit(solution)/shard_map/ppermute | solution.py:26
  54.4 2.0 %collective-permute-start.19 = (bf16[2,320,128]{2,1,0:T(8,128)(2,1)S(1)}, bf16[2,320,128]{2,1,0:T(8,128)(2,1)S(1)}, u32[]{:S(2)}, u32[]{:S(2)}) collective-permute-start(bf16[2,320,128]{2,1,0:T(8,128)(2,1)S(1)} %shard_map.77.c0), channel_id=1, source_target_pairs={{0,6},{2,0},{4,2},{6,4},{1,7},{3,1},{5,3},{7,5},{8,14},{10,8},{12,... | collective-permute-start | bytes 491528 | tf_op jit(solution)/shard_map/ppermute | solution.py:26
  56.4 0.0 collective-permute-start.20
  56.4 4.5 %collective-permute-done.18.c2 = bf16[2,320,128]{2,1,0:T(8,128)(2,1)S(1)} collective-permute-done((bf16[2,320,128]{2,1,0:T(8,128)(2,1)S(1)}, bf16[2,320,128]{2,1,0:T(8,128)(2,1)S(1)}, u32[]{:S(2)}, u32[]{:S(2)}) %collective-permute-start.18) | collective-permute-done | bytes 163872 | tf_op jit(solution)/shard_map/ppermute | solution.py:26
  61.0 2.2 %collective-permute-done.19.c1 = bf16[2,320,128]{2,1,0:T(8,128)(2,1)S(1)} collective-permute-done((bf16[2,320,128]{2,1,0:T(8,128)(2,1)S(1)}, bf16[2,320,128]{2,1,0:T(8,128)(2,1)S(1)}, u32[]{:S(2)}, u32[]{:S(2)}) %collective-permute-start.19) | collective-permute-done | bytes 163872 | tf_op jit(solution)/shard_map/ppermute | solution.py:26
  63.2 0.6 collective-permute-done.20.c3
  63.7 1.7 %shard_map.78 = (f32[256,1280]{1,0:T(8,128)S(1)}, f32[256,1280]{1,0:T(8,128)S(1)}, bf16[320,1280]{1,0:T(8,128)(2,1)S(1)}, bf16[192,1280]{1,0:T(8,128)(2,1)S(1)}, bf16[2,320,512]{2,1,0:T(8,128)(2,1)S(1)}) custom-call(s32[1]{0:T(128)} %bitcast.me, bf16[2,320,128]{2,1,0:T(8,128)(2,1)S(1)} %shard_map.77.c0, bf16[2,320,128]{2,1,0:T(8,128)(2,1)S(1)} %collective-permute-done.18.c2, ...), custom_call_target="tpu_custom_call" | custom-call | flops 838860800 | bytes 1048576 | tf_op jit(solution)/shard_map/pallas_call | solution.py:56
  65.5 0.1 collective-permute-start.21
  65.6 1.9 %collective-permute-done.21 = bf16[192,1280]{1,0:T(8,128)(2,1)S(1)} collective-permute-done((bf16[192,1280]{1,0:T(8,128)(2,1)S(1)}, bf16[192,1280]{1,0:T(8,128)(2,1)S(1)}, u32[]{:S(2)}, u32[]{:S(2)}) %collective-permute-start.21) | collective-permute-done | bytes 491552 | tf_op jit(solution)/shard_map/ppermute | solution.py:26
  67.4 0.1 collective-permute-start.22
  67.6 0.1 convert_element_type.63
  67.6 0.1 fusion.2
  67.7 1.7 %collective-permute-start.23 = (bf16[96,1280]{1,0:T(8,128)(2,1)S(1)}, bf16[96,1280]{1,0:T(8,128)(2,1)S(1)}, u32[]{:S(2)}, u32[]{:S(2)}) collective-permute-start(bf16[96,1280]{1,0:T(8,128)(2,1)S(1)} %fusion.2), channel_id=1, source_target_pairs={{0,8},{8,0},{16,24},{24,16},{1,9},{9,1},{17,25},{25,17},{2,10},{10... | collective-permute-start | bytes 737288 | tf_op jit(solution)/shard_map/ppermute | solution.py:30
  69.4 0.6 shard_map.80
  70.0 1.5 %collective-permute-start.33 = (bf16[320,1280]{1,0:T(8,128)(2,1)S(1)}, bf16[320,1280]{1,0:T(8,128)(2,1)S(1)}, u32[]{:S(2)}, u32[]{:S(2)}) collective-permute-start(bf16[320,1280]{1,0:T(8,128)(2,1)S(1)} %shard_map.80), channel_id=1, source_target_pairs={{0,24},{24,0},{8,16},{16,8},{1,25},{25,1},{9,17},{17,9},{2,26},{26... | collective-permute-start | bytes 2457608 | tf_op jit(solution)/shard_map/ppermute | solution.py:34
  71.5 0.6 shard_map.79
  72.1 0.1 convert_element_type.62
  72.2 0.2 fusion.9
  72.5 0.1 collective-permute-start.26
  72.6 3.3 %collective-permute-start.27 = (bf16[64,1280]{1,0:T(8,128)(2,1)S(1)}, bf16[64,1280]{1,0:T(8,128)(2,1)S(1)}, u32[]{:S(2)}, u32[]{:S(2)}) collective-permute-start(bf16[64,1280]{1,0:T(8,128)(2,1)S(1)} %pad_maximum_fusion.3), channel_id=1, source_target_pairs={{0,224},{32,0},{64,32},{96,64},{128,96},{160,128},{192,160},{224,1... | collective-permute-start | bytes 491528 | tf_op jit(solution)/shard_map/ppermute | solution.py:26
  75.9 1.8 %collective-permute-start.29 = (bf16[64,1280]{1,0:T(8,128)(2,1)S(1)}, bf16[64,1280]{1,0:T(8,128)(2,1)S(1)}, u32[]{:S(2)}, u32[]{:S(2)}) collective-permute-start(bf16[64,1280]{1,0:T(8,128)(2,1)S(1)} %slice.138), channel_id=1, source_target_pairs={{0,8},{8,0},{16,24},{24,16},{1,9},{9,1},{17,25},{25,17},{2,10},{10... | collective-permute-start | bytes 491528 | tf_op jit(solution)/shard_map/ppermute | solution.py:30
  77.7 0.1 fusion.1
  77.8 0.1 collective-permute-start.24
  77.9 1.8 %collective-permute-done.26 = bf16[64,1280]{1,0:T(8,128)(2,1)S(1)} collective-permute-done((bf16[64,1280]{1,0:T(8,128)(2,1)S(1)}, bf16[64,1280]{1,0:T(8,128)(2,1)S(1)}, u32[]{:S(2)}, u32[]{:S(2)}) %collective-permute-start.26) | collective-permute-done | bytes 163872 | tf_op jit(solution)/shard_map/ppermute | solution.py:26
  79.7 3.0 %collective-permute-start.31 = (bf16[32,1280]{1,0:T(8,128)(2,1)S(1)}, bf16[32,1280]{1,0:T(8,128)(2,1)S(1)}, u32[]{:S(2)}, u32[]{:S(2)}) collective-permute-start(bf16[32,1280]{1,0:T(8,128)(2,1)S(1)} %get-tuple-element.78), channel_id=1, source_target_pairs={{0,224},{32,0},{64,32},{96,64},{128,96},{160,128},{192,160},{224,1... | collective-permute-start | bytes 245768 | tf_op jit(solution)/shard_map/ppermute | solution.py:26
  82.8 1.9 %collective-permute-start.28 = (bf16[32,1280]{1,0:T(8,128)(2,1)S(1)}, bf16[32,1280]{1,0:T(8,128)(2,1)S(1)}, u32[]{:S(2)}, u32[]{:S(2)}) collective-permute-start(bf16[32,1280]{1,0:T(8,128)(2,1)S(1)} %fusion.8), channel_id=1, source_target_pairs={{0,8},{8,0},{16,24},{24,16},{1,9},{9,1},{17,25},{25,17},{2,10},{10... | collective-permute-start | bytes 245768 | tf_op jit(solution)/shard_map/ppermute | solution.py:30
  84.7 2.4 %collective-permute-done.25 = bf16[32,1280]{1,0:T(8,128)(2,1)S(1)} collective-permute-done((bf16[32,1280]{1,0:T(8,128)(2,1)S(1)}, bf16[32,1280]{1,0:T(8,128)(2,1)S(1)}, u32[]{:S(2)}, u32[]{:S(2)}) %collective-permute-start.25) | collective-permute-done | bytes 81952 | tf_op jit(solution)/shard_map/ppermute | solution.py:26
  87.1 0.1 fusion.3
  87.2 0.1 collective-permute-start.30
  87.2 4.1 %collective-permute-start.32 = (bf16[32,1280]{1,0:T(8,128)(2,1)S(1)}, bf16[32,1280]{1,0:T(8,128)(2,1)S(1)}, u32[]{:S(2)}, u32[]{:S(2)}) collective-permute-start(bf16[32,1280]{1,0:T(8,128)(2,1)S(1)} %get-tuple-element.72), channel_id=1, source_target_pairs={{0,192},{32,224},{64,0},{96,32},{128,64},{160,96},{192,128},{224,1... | collective-permute-start | bytes 245768 | tf_op jit(solution)/shard_map/ppermute | solution.py:26
  91.4 1.3 %convert_add_fusion = (f32[160,1280]{1,0:T(8,128)}, f32[1280,160]{0,1:T(8,128)}) fusion(f32[160,1280]{1,0:T(8,128)S(1)} %get-tuple-element.54, bf16[320,1280]{1,0:T(8,128)(2,1)S(1)} %collective-permute-done.33, f32[160,1280]{1,0:T(8,128)S(1)} %get-tuple-element.62), kind=kLoop, calls=%fused_computation.1 | loop fusion | flops 819200 | bytes 4096000 | tf_op jit(solution)/shard_map/add | solution.py:238
  92.7 1.9 %collective-permute-done.30 = bf16[32,1280]{1,0:T(8,128)(2,1)S(1)} collective-permute-done((bf16[32,1280]{1,0:T(8,128)(2,1)S(1)}, bf16[32,1280]{1,0:T(8,128)(2,1)S(1)}, u32[]{:S(2)}, u32[]{:S(2)}) %collective-permute-start.30) | collective-permute-done | bytes 81952 | tf_op jit(solution)/shard_map/ppermute | solution.py:26
  94.6 0.1 fusion.6
  94.7 0.6 fusion.14
  (52 shorter events, 0.4 us)
Async XLA Ops:
  0.6 20.0 %copy-start.2 = (bf16[16,1280]{1,0:T(8,128)(2,1)S(1)}, bf16[16,1280]{1,0:T(8,128)(2,1)}, u32[]{:S(2)}) copy-start(bf16[16,1280]{1,0:T(8,128)(2,1)} %param.4) | copy-start | bytes 122884
  0.6 20.0 %copy-start.3 = (bf16[16,1280]{1,0:T(8,128)(2,1)S(1)}, bf16[16,1280]{1,0:T(8,128)(2,1)}, u32[]{:S(2)}) copy-start(bf16[16,1280]{1,0:T(8,128)(2,1)} %param.7) | copy-start | bytes 122884
  2.3 10.3 %collective-permute-start.1 = (bf16[32,1280]{1,0:T(8,128)(2,1)S(1)}, bf16[32,1280]{1,0:T(8,128)(2,1)S(1)}, u32[]{:S(2)}, u32[]{:S(2)}) collective-permute-start(bf16[32,1280]{1,0:T(8,128)(2,1)S(1)} %constant_dynamic-update-slice_fusion), channel_id=1, source_target_pairs={{0,192},{32,224},{64,0},{96,32},{128,64},{160,96},{192,128},{224,1... | collective-permute-start | bytes 245768 | tf_op jit(solution)/shard_map/ppermute | solution.py:26
  8.6 7.3 %collective-permute-start.5 = (bf16[32,1280]{1,0:T(8,128)(2,1)S(1)}, bf16[32,1280]{1,0:T(8,128)(2,1)S(1)}, u32[]{:S(2)}, u32[]{:S(2)}) collective-permute-start(bf16[32,1280]{1,0:T(8,128)(2,1)S(1)} %constant_dynamic-update-slice_fusion), channel_id=1, source_target_pairs={{0,64},{32,96},{64,128},{96,160},{128,192},{160,224},{192,0},{224,... | collective-permute-start | bytes 245768 | tf_op jit(solution)/shard_map/ppermute | solution.py:26
  8.6 12.1 %collective-permute-start = (bf16[32,1280]{1,0:T(8,128)(2,1)S(1)}, bf16[32,1280]{1,0:T(8,128)(2,1)S(1)}, u32[]{:S(2)}, u32[]{:S(2)}) collective-permute-start(bf16[32,1280]{1,0:T(8,128)(2,1)S(1)} %constant_dynamic-update-slice_fusion), channel_id=1, source_target_pairs={{0,8},{8,0},{16,24},{24,16},{1,9},{9,1},{17,25},{25,17},{2,10},{10... | collective-permute-start | bytes 245768 | tf_op jit(solution)/shard_map/ppermute | solution.py:30
  10.3 25.7 %copy-start = (bf16[1280,160]{0,1:T(8,128)(2,1)S(1)}, bf16[1280,160]{0,1:T(8,128)(2,1)}, u32[]{:S(2)}) copy-start(bf16[1280,160]{0,1:T(8,128)(2,1)} %param.5) | copy-start | bytes 1228804
  10.3 25.6 %copy-start.1 = (bf16[160,1280]{1,0:T(8,128)(2,1)S(1)}, bf16[160,1280]{1,0:T(8,128)(2,1)}, u32[]{:S(2)}) copy-start(bf16[160,1280]{1,0:T(8,128)(2,1)} %wo.5) | copy-start | bytes 1228804
  10.3 23.5 %collective-permute-start.10 = (bf16[320,1280]{1,0:T(8,128)(2,1)S(1)}, bf16[320,1280]{1,0:T(8,128)(2,1)S(1)}, u32[]{:S(2)}, u32[]{:S(2)}) collective-permute-start(bf16[320,1280]{1,0:T(8,128)(2,1)S(1)} %pad_maximum_fusion), channel_id=1, source_target_pairs={{0,24},{24,0},{8,16},{16,8},{1,25},{25,1},{9,17},{17,9},{2,26},{26... | collective-permute-start | bytes 2457608 | tf_op jit(solution)/shard_map/ppermute | solution.py:34
  15.9 17.3 %collective-permute-start.6 = (bf16[64,1280]{1,0:T(8,128)(2,1)S(1)}, bf16[64,1280]{1,0:T(8,128)(2,1)S(1)}, u32[]{:S(2)}, u32[]{:S(2)}) collective-permute-start(bf16[64,1280]{1,0:T(8,128)(2,1)S(1)} %get-tuple-element.83), channel_id=1, source_target_pairs={{0,8},{8,0},{16,24},{24,16},{1,9},{9,1},{17,25},{25,17},{2,10},{10... | collective-permute-start | bytes 491528 | tf_op jit(solution)/shard_map/ppermute | solution.py:30
  16.5 10.0 %collective-permute-start.8 = (bf16[32,1280]{1,0:T(8,128)(2,1)S(1)}, bf16[32,1280]{1,0:T(8,128)(2,1)S(1)}, u32[]{:S(2)}, u32[]{:S(2)}) collective-permute-start(bf16[32,1280]{1,0:T(8,128)(2,1)S(1)} %collective-permute-done.5), channel_id=1, source_target_pairs={{0,64},{32,96},{64,128},{96,160},{128,192},{160,224},{192,0},{224,... | collective-permute-start | bytes 245768 | tf_op jit(solution)/shard_map/ppermute | solution.py:26
  16.5 6.2 %collective-permute-start.2 = (bf16[32,1280]{1,0:T(8,128)(2,1)S(1)}, bf16[32,1280]{1,0:T(8,128)(2,1)S(1)}, u32[]{:S(2)}, u32[]{:S(2)}) collective-permute-start(bf16[32,1280]{1,0:T(8,128)(2,1)S(1)} %collective-permute-done.1), channel_id=1, source_target_pairs={{0,224},{32,0},{64,32},{96,64},{128,96},{160,128},{192,160},{224,1... | collective-permute-start | bytes 245768 | tf_op jit(solution)/shard_map/ppermute | solution.py:26
  20.7 5.8 %collective-permute-start.7 = (bf16[32,1280]{1,0:T(8,128)(2,1)S(1)}, bf16[32,1280]{1,0:T(8,128)(2,1)S(1)}, u32[]{:S(2)}, u32[]{:S(2)}) collective-permute-start(bf16[32,1280]{1,0:T(8,128)(2,1)S(1)} %collective-permute-done.5), channel_id=1, source_target_pairs={{0,32},{32,64},{64,96},{96,128},{128,160},{160,192},{192,224},{224... | collective-permute-start | bytes 245768 | tf_op jit(solution)/shard_map/ppermute | solution.py:26
  22.7 6.5 %collective-permute-start.3 = (bf16[64,1280]{1,0:T(8,128)(2,1)S(1)}, bf16[64,1280]{1,0:T(8,128)(2,1)S(1)}, u32[]{:S(2)}, u32[]{:S(2)}) collective-permute-start(bf16[64,1280]{1,0:T(8,128)(2,1)S(1)} %pad_maximum_fusion.1), channel_id=1, source_target_pairs={{0,224},{32,0},{64,32},{96,64},{128,96},{160,128},{192,160},{224,1... | collective-permute-start | bytes 491528 | tf_op jit(solution)/shard_map/ppermute | solution.py:26
  26.4 6.6 %collective-permute-start.4 = (bf16[64,1280]{1,0:T(8,128)(2,1)S(1)}, bf16[64,1280]{1,0:T(8,128)(2,1)S(1)}, u32[]{:S(2)}, u32[]{:S(2)}) collective-permute-start(bf16[64,1280]{1,0:T(8,128)(2,1)S(1)} %pad_maximum_fusion.1), channel_id=1, source_target_pairs={{0,32},{32,64},{64,96},{96,128},{128,160},{160,192},{192,224},{224... | collective-permute-start | bytes 491528 | tf_op jit(solution)/shard_map/ppermute | solution.py:26
  26.6 7.3 %collective-permute-start.9 = (bf16[96,1280]{1,0:T(8,128)(2,1)S(1)}, bf16[96,1280]{1,0:T(8,128)(2,1)}, u32[]{:S(2)}, u32[]{:S(2)}) collective-permute-start(bf16[96,1280]{1,0:T(8,128)(2,1)S(1)} %constant_dynamic-update-slice_fusion.10.a2), channel_id=1, source_target_pairs={{0,8},{8,0},{16,24},{24,16},{1,9},{9,1},{17,25},{25,17},{2,10},{10... | collective-permute-start | bytes 737288 | tf_op jit(solution)/shard_map/ppermute | solution.py:30
  33.0 2.9 %collective-permute-start.11 = (bf16[192,1280]{1,0:T(8,128)(2,1)S(1)}, bf16[192,1280]{1,0:T(8,128)(2,1)S(1)}, u32[]{:S(2)}, u32[]{:S(2)}) collective-permute-start(bf16[192,1280]{1,0:T(8,128)(2,1)S(1)} %constant_dynamic-update-slice_fusion.2.a0), channel_id=1, source_target_pairs={{0,1},{1,0},{2,3},{3,2},{4,5},{5,4},{6,7},{7,6},{8,9},{9,8},{10,11... | collective-permute-start | bytes 1474568 | tf_op jit(solution)/shard_map/ppermute | solution.py:26
  33.2 2.8 %collective-permute-start.12 = (bf16[128,1280]{1,0:T(8,128)(2,1)S(1)}, bf16[128,1280]{1,0:T(8,128)(2,1)S(1)}, u32[]{:S(2)}, u32[]{:S(2)}) collective-permute-start(bf16[128,1280]{1,0:T(8,128)(2,1)S(1)} %constant_dynamic-update-slice_fusion.7.a1), channel_id=1, source_target_pairs={{0,1},{1,0},{2,3},{3,2},{4,5},{5,4},{6,7},{7,6},{8,9},{9,8},{10,11... | collective-permute-start | bytes 983048 | tf_op jit(solution)/shard_map/ppermute | solution.py:26
  33.8 2.2 %collective-permute-start.13 = (bf16[96,1280]{1,0:T(8,128)(2,1)S(1)}, bf16[96,1280]{1,0:T(8,128)(2,1)}, u32[]{:S(2)}, u32[]{:S(2)}) collective-permute-start(bf16[96,1280]{1,0:T(8,128)(2,1)S(1)} %constant_dynamic-update-slice_fusion.10.a2), channel_id=1, source_target_pairs={{0,1},{1,0},{2,3},{3,2},{4,5},{5,4},{6,7},{7,6},{8,9},{9,8},{10,11... | collective-permute-start | bytes 737288 | tf_op jit(solution)/shard_map/ppermute | solution.py:26
  33.9 4.6 %collective-permute-start.14 = (bf16[96,1280]{1,0:T(8,128)(2,1)}, bf16[96,1280]{1,0:T(8,128)(2,1)}, u32[]{:S(2)}, u32[]{:S(2)}) collective-permute-start(bf16[96,1280]{1,0:T(8,128)(2,1)} %collective-permute-done.9.a3), channel_id=1, source_target_pairs={{0,1},{1,0},{2,3},{3,2},{4,5},{5,4},{6,7},{7,6},{8,9},{9,8},{10,11... | collective-permute-start | bytes 737288 | tf_op jit(solution)/shard_map/ppermute | solution.py:26
  40.2 8.6 %collective-permute-start.15 = (bf16[2,320,128]{2,1,0:T(8,128)(2,1)S(1)}, bf16[2,320,128]{2,1,0:T(8,128)(2,1)S(1)}, u32[]{:S(2)}, u32[]{:S(2)}) collective-permute-start(bf16[2,320,128]{2,1,0:T(8,128)(2,1)S(1)} %get-tuple-element.42), channel_id=1, source_target_pairs={{0,4},{2,6},{4,0},{6,2},{1,5},{3,7},{5,1},{7,3},{8,12},{10,14},{12... | collective-permute-start | bytes 491528 | tf_op jit(solution)/shard_map/ppermute | solution.py:26
  43.5 8.3 %collective-permute-start.16 = (bf16[2,320,128]{2,1,0:T(8,128)(2,1)S(1)}, bf16[2,320,128]{2,1,0:T(8,128)(2,1)S(1)}, u32[]{:S(2)}, u32[]{:S(2)}) collective-permute-start(bf16[2,320,128]{2,1,0:T(8,128)(2,1)S(1)} %get-tuple-element.43), channel_id=1, source_target_pairs={{0,2},{2,4},{4,6},{6,0},{1,3},{3,5},{5,7},{7,1},{8,10},{10,12},{12... | collective-permute-start | bytes 491528 | tf_op jit(solution)/shard_map/ppermute | solution.py:26
  44.1 7.9 %collective-permute-start.17 = (bf16[2,320,128]{2,1,0:T(8,128)(2,1)S(1)}, bf16[2,320,128]{2,1,0:T(8,128)(2,1)S(1)}, u32[]{:S(2)}, u32[]{:S(2)}) collective-permute-start(bf16[2,320,128]{2,1,0:T(8,128)(2,1)S(1)} %get-tuple-element.44), channel_id=1, source_target_pairs={{0,6},{2,0},{4,2},{6,4},{1,7},{3,1},{5,3},{7,5},{8,14},{10,8},{12,... | collective-permute-start | bytes 491528 | tf_op jit(solution)/shard_map/ppermute | solution.py:26
  52.2 8.7 %collective-permute-start.18 = (bf16[2,320,128]{2,1,0:T(8,128)(2,1)S(1)}, bf16[2,320,128]{2,1,0:T(8,128)(2,1)S(1)}, u32[]{:S(2)}, u32[]{:S(2)}) collective-permute-start(bf16[2,320,128]{2,1,0:T(8,128)(2,1)S(1)} %shard_map.77.c0), channel_id=1, source_target_pairs={{0,4},{2,6},{4,0},{6,2},{1,5},{3,7},{5,1},{7,3},{8,12},{10,14},{12... | collective-permute-start | bytes 491528 | tf_op jit(solution)/shard_map/ppermute | solution.py:26
  54.4 8.7 %collective-permute-start.19 = (bf16[2,320,128]{2,1,0:T(8,128)(2,1)S(1)}, bf16[2,320,128]{2,1,0:T(8,128)(2,1)S(1)}, u32[]{:S(2)}, u32[]{:S(2)}) collective-permute-start(bf16[2,320,128]{2,1,0:T(8,128)(2,1)S(1)} %shard_map.77.c0), channel_id=1, source_target_pairs={{0,6},{2,0},{4,2},{6,4},{1,7},{3,1},{5,3},{7,5},{8,14},{10,8},{12,... | collective-permute-start | bytes 491528 | tf_op jit(solution)/shard_map/ppermute | solution.py:26
  56.4 7.3 %collective-permute-start.20 = (bf16[2,320,128]{2,1,0:T(8,128)(2,1)S(1)}, bf16[2,320,128]{2,1,0:T(8,128)(2,1)S(1)}, u32[]{:S(2)}, u32[]{:S(2)}) collective-permute-start(bf16[2,320,128]{2,1,0:T(8,128)(2,1)S(1)} %shard_map.77.c0), channel_id=1, source_target_pairs={{0,2},{2,4},{4,6},{6,0},{1,3},{3,5},{5,7},{7,1},{8,10},{10,12},{12... | collective-permute-start | bytes 491528 | tf_op jit(solution)/shard_map/ppermute | solution.py:26
  65.5 2.0 %collective-permute-start.21 = (bf16[192,1280]{1,0:T(8,128)(2,1)S(1)}, bf16[192,1280]{1,0:T(8,128)(2,1)S(1)}, u32[]{:S(2)}, u32[]{:S(2)}) collective-permute-start(bf16[192,1280]{1,0:T(8,128)(2,1)S(1)} %get-tuple-element.47), channel_id=1, source_target_pairs={{0,1},{1,0},{2,3},{3,2},{4,5},{5,4},{6,7},{7,6},{8,9},{9,8},{10,11... | collective-permute-start | bytes 1474568 | tf_op jit(solution)/shard_map/ppermute | solution.py:26
  67.4 4.6 %collective-permute-start.22 = (bf16[320,1280]{1,0:T(8,128)(2,1)S(1)}, bf16[320,1280]{1,0:T(8,128)(2,1)S(1)}, u32[]{:S(2)}, u32[]{:S(2)}) collective-permute-start(bf16[320,1280]{1,0:T(8,128)(2,1)S(1)} %get-tuple-element.48), channel_id=1, source_target_pairs={{0,1},{1,0},{2,3},{3,2},{4,5},{5,4},{6,7},{7,6},{8,9},{9,8},{10,11... | collective-permute-start | bytes 2457608 | tf_op jit(solution)/shard_map/ppermute | solution.py:26
  67.7 10.0 %collective-permute-start.23 = (bf16[96,1280]{1,0:T(8,128)(2,1)S(1)}, bf16[96,1280]{1,0:T(8,128)(2,1)S(1)}, u32[]{:S(2)}, u32[]{:S(2)}) collective-permute-start(bf16[96,1280]{1,0:T(8,128)(2,1)S(1)} %fusion.2), channel_id=1, source_target_pairs={{0,8},{8,0},{16,24},{24,16},{1,9},{9,1},{17,25},{25,17},{2,10},{10... | collective-permute-start | bytes 737288 | tf_op jit(solution)/shard_map/ppermute | solution.py:30
  70.0 21.4 %collective-permute-start.33 = (bf16[320,1280]{1,0:T(8,128)(2,1)S(1)}, bf16[320,1280]{1,0:T(8,128)(2,1)S(1)}, u32[]{:S(2)}, u32[]{:S(2)}) collective-permute-start(bf16[320,1280]{1,0:T(8,128)(2,1)S(1)} %shard_map.80), channel_id=1, source_target_pairs={{0,24},{24,0},{8,16},{16,8},{1,25},{25,1},{9,17},{17,9},{2,26},{26... | collective-permute-start | bytes 2457608 | tf_op jit(solution)/shard_map/ppermute | solution.py:34
  72.5 7.2 %collective-permute-start.26 = (bf16[64,1280]{1,0:T(8,128)(2,1)S(1)}, bf16[64,1280]{1,0:T(8,128)(2,1)S(1)}, u32[]{:S(2)}, u32[]{:S(2)}) collective-permute-start(bf16[64,1280]{1,0:T(8,128)(2,1)S(1)} %pad_maximum_fusion.2), channel_id=1, source_target_pairs={{0,32},{32,64},{64,96},{96,128},{128,160},{160,192},{192,224},{224... | collective-permute-start | bytes 491528 | tf_op jit(solution)/shard_map/ppermute | solution.py:26
  72.6 7.1 %collective-permute-start.27 = (bf16[64,1280]{1,0:T(8,128)(2,1)S(1)}, bf16[64,1280]{1,0:T(8,128)(2,1)S(1)}, u32[]{:S(2)}, u32[]{:S(2)}) collective-permute-start(bf16[64,1280]{1,0:T(8,128)(2,1)S(1)} %pad_maximum_fusion.3), channel_id=1, source_target_pairs={{0,224},{32,0},{64,32},{96,64},{128,96},{160,128},{192,160},{224,1... | collective-permute-start | bytes 491528 | tf_op jit(solution)/shard_map/ppermute | solution.py:26
  75.9 6.9 %collective-permute-start.29 = (bf16[64,1280]{1,0:T(8,128)(2,1)S(1)}, bf16[64,1280]{1,0:T(8,128)(2,1)S(1)}, u32[]{:S(2)}, u32[]{:S(2)}) collective-permute-start(bf16[64,1280]{1,0:T(8,128)(2,1)S(1)} %slice.138), channel_id=1, source_target_pairs={{0,8},{8,0},{16,24},{24,16},{1,9},{9,1},{17,25},{25,17},{2,10},{10... | collective-permute-start | bytes 491528 | tf_op jit(solution)/shard_map/ppermute | solution.py:30
  77.8 6.9 %collective-permute-start.24 = (bf16[32,1280]{1,0:T(8,128)(2,1)S(1)}, bf16[32,1280]{1,0:T(8,128)(2,1)S(1)}, u32[]{:S(2)}, u32[]{:S(2)}) collective-permute-start(bf16[32,1280]{1,0:T(8,128)(2,1)S(1)} %get-tuple-element.80), channel_id=1, source_target_pairs={{0,32},{32,64},{64,96},{96,128},{128,160},{160,192},{192,224},{224... | collective-permute-start | bytes 245768 | tf_op jit(solution)/shard_map/ppermute | solution.py:26
  79.7 7.4 %collective-permute-start.25 = (bf16[32,1280]{1,0:T(8,128)(2,1)S(1)}, bf16[32,1280]{1,0:T(8,128)(2,1)S(1)}, u32[]{:S(2)}, u32[]{:S(2)}) collective-permute-start(bf16[32,1280]{1,0:T(8,128)(2,1)S(1)} %get-tuple-element.79), channel_id=1, source_target_pairs={{0,64},{32,96},{64,128},{96,160},{128,192},{160,224},{192,0},{224,... | collective-permute-start | bytes 245768 | tf_op jit(solution)/shard_map/ppermute | solution.py:26
  79.7 7.4 %collective-permute-start.31 = (bf16[32,1280]{1,0:T(8,128)(2,1)S(1)}, bf16[32,1280]{1,0:T(8,128)(2,1)S(1)}, u32[]{:S(2)}, u32[]{:S(2)}) collective-permute-start(bf16[32,1280]{1,0:T(8,128)(2,1)S(1)} %get-tuple-element.78), channel_id=1, source_target_pairs={{0,224},{32,0},{64,32},{96,64},{128,96},{160,128},{192,160},{224,1... | collective-permute-start | bytes 245768 | tf_op jit(solution)/shard_map/ppermute | solution.py:26
  82.8 9.9 %collective-permute-start.28 = (bf16[32,1280]{1,0:T(8,128)(2,1)S(1)}, bf16[32,1280]{1,0:T(8,128)(2,1)S(1)}, u32[]{:S(2)}, u32[]{:S(2)}) collective-permute-start(bf16[32,1280]{1,0:T(8,128)(2,1)S(1)} %fusion.8), channel_id=1, source_target_pairs={{0,8},{8,0},{16,24},{24,16},{1,9},{9,1},{17,25},{25,17},{2,10},{10... | collective-permute-start | bytes 245768 | tf_op jit(solution)/shard_map/ppermute | solution.py:30
  87.2 7.5 %collective-permute-start.30 = (bf16[32,1280]{1,0:T(8,128)(2,1)S(1)}, bf16[32,1280]{1,0:T(8,128)(2,1)S(1)}, u32[]{:S(2)}, u32[]{:S(2)}) collective-permute-start(bf16[32,1280]{1,0:T(8,128)(2,1)S(1)} %get-tuple-element.73), channel_id=1, source_target_pairs={{0,64},{32,96},{64,128},{96,160},{128,192},{160,224},{192,0},{224,... | collective-permute-start | bytes 245768 | tf_op jit(solution)/shard_map/ppermute | solution.py:26
  87.2 7.4 %collective-permute-start.32 = (bf16[32,1280]{1,0:T(8,128)(2,1)S(1)}, bf16[32,1280]{1,0:T(8,128)(2,1)S(1)}, u32[]{:S(2)}, u32[]{:S(2)}) collective-permute-start(bf16[32,1280]{1,0:T(8,128)(2,1)S(1)} %get-tuple-element.72), channel_id=1, source_target_pairs={{0,192},{32,224},{64,0},{96,32},{128,64},{160,96},{192,128},{224,1... | collective-permute-start | bytes 245768 | tf_op jit(solution)/shard_map/ppermute | solution.py:26

commit v10 on v8

--- a/solution.py
+++ b/solution.py
@@ -80,14 +80,17 @@
 def up_kernel(me, *refs):
     held, (wi, wo, w_pair, tok, cot), parts = refs[:8], refs[8:13], refs[13:]
     for q in range(4):
-        half, chip = q // 2 * 4, q % 2
+        first, second, third, fourth = held[q // 2 * 4 : q // 2 * 4 + 4]
+        chip = q % 2
         for j in range(8):
             if j < 3:
-                ref, i = held[half], j * 64 + chip * 32
-            elif j < HEAD:
-                ref, i = held[half + 1], chip * 64 + (j - 3) * 32
+                ref, i = first, j * 64 + chip * 32
+            elif j < 5:
+                ref, i = second, chip * 64 + (j - 3) * 32
+            elif j < 7:
+                ref, i = third, chip * 64 + (j - 5) * 32
             else:
-                ref, i = held[half + 2 + chip], (j - HEAD) * 32
+                ref, i = fourth, chip * 32
             row = q * 128 + j * 16
             tok[row : row + 16] = ref[i : i + 16]
             cot[row : row + 16] = ref[i + 16 : i + 32]
@@ -109,8 +112,10 @@
     out[1] = (grad_act * smooth_slope(pre)).astype(BF)
 
 
-def down_kernel(me, full, wi, wo, w_pair, near, far, head, tail):
-    del me
+def down_kernel(me, c0, c2, c1, c3, wi, wo, w_pair, near, far, head, tail, full):
+    for k, block in ((0, c0), (2, c2), (1, c1), (3, c3)):
+        lane = pl.multiple_of(((me[0] + k) % 4) * 128, 128)
+        full[:, :, pl.ds(lane, 128)] = block[...]
     h = wi.shape[0]
     for s, w in enumerate((wo, wi)):
         value = dot(full[s, :h], w[...], 0, 0)
@@ -129,11 +134,9 @@
                     tail[row : row + 16] = piece.astype(BF)
 
 
-def pair_kernel(me, b0, b2, b1, b3, tok, cot, full, out):
+def pair_kernel(me, full, tok, cot, out):
+    del me
     h = full.shape[1] // 2
-    for k, block in ((0, b0), (2, b2), (1, b1), (3, b3)):
-        lane = pl.multiple_of(((me[0] + k) % 4) * 128, 128)
-        full[:, :, pl.ds(lane, 128)] = block[...]
     out[:h] = dot(full[0, h:], cot[...], 1, 0).astype(BF)
     out[h:] = dot(full[1, h:], tok[...], 1, 0).astype(BF)
 
@@ -158,13 +161,14 @@
     w_pair = weight_pair(after(cat([w_in_t, w_out]), base))
     z[3], z[5] = send(z[2], "z", -1), send(z[6], "z", 1)
     second = cat([z[2], z[6]])
-    z[4] = send(after(z[6], second), "z", 2)
     second = cat([second, token_pair(second)])
-    near_t = cat([z[k] for k in ORDER[HEAD:]])
-    both = after(both, z[3])
+    fourth = cat([second[32:64], second[96:]])
+    both = after(both, (fourth, z[3]))
+    fourth = send(fourth, "z", 2)
+    third = cat([z[3], z[5]])
     first = cat([both, send(both, "z", -1), send(both, "z", 1)])
-    far_t = after(token_pair(near_t), w_pair)
-    held = [first, second, near_t, far_t]
+    third = cat([third, after(token_pair(third), w_pair)])
+    held = [first, second, third, fourth]
     held += [send(value, "col", 1) for value in held]
 
     part, rounded = shape((2, 2 * h, 128), F32), shape((2, 2 * h, 128), BF)
@@ -178,44 +182,45 @@
     blocks = [block] + [send(block, "row", -k) for k in (2, 1, 3)]
 
     sums = shape((256, d), F32)
-    full, pair = call(
-        pair_kernel,
-        [shape((2, 2 * h, 512), BF), shape((2 * h, d), BF)],
-        [me, *blocks, tok, cot],
-        flops,
-    )
-    near, far, head, tail = call(
+    near, far, head, tail, full = call(
         down_kernel,
-        [sums, sums, shape((HEAD * 64, d), BF), shape(((8 - HEAD) * 64, d), BF)],
-        [me, full, w_in_t, w_out, w_pair],
+        [sums, sums, shape((HEAD * 64, d), BF), shape(((8 - HEAD) * 64, d), BF), shape((2, 2 * h, 512), BF)],
+        [me, *blocks, w_in_t, w_out, w_pair],
         2 * flops,
     )
     cut, rest = HEAD * 32, (8 - HEAD) * 32
     tail = send(tail, "col", 1)
     head = send(after(head, tail), "col", 1).astype(F32)
     tail = tail.astype(F32)
-    far_t = (far[cut:] + tail[:rest]).astype(BF)
-    far = after(far, far_t)
-    pair = weight_pair(after(pair, far_t))
+    far_t = far[cut:] + tail[:rest]
+    near_t = near[cut:] + tail[rest:]
+    fourth = cat([near_t[64:], far_t[64:]]).astype(BF)
+    far_t = far_t[:64].astype(BF)
+    near, far = after((near, far), far_t)
+    (pair,) = call(
+        pair_kernel, [shape((2 * h, d), BF)], [me, after(full, far_t), tok, cot], flops
+    )
+    pair = weight_pair(pair)
     grad_out, grad_in_t = call(
         own_kernel, [shape((h, d), F32)] * 2, [me, full, after(tok, far_t), cot], flops
     )
-    far_t = token_pair(far_t)
+    fourth = send(fourth, "z", 2).astype(F32)
     head = after(head, grad_out)
     far_h = far[:cut] + head[:cut]
     near_h = near[:cut] + head[cut:]
     up_1 = cat([near_h[32:64], far_h[32:64]]).astype(BF)
     down_1 = cat([near_h[64:96], far_h[64:96]]).astype(BF)
-    near = after(near, (up_1, down_1))
+    near_t = after(near_t, (up_1, down_1))
     up_1, down_1 = send(up_1, "z", 1).astype(F32), send(down_1, "z", -1).astype(F32)
-    far_2 = token_pair(far_h[96:].astype(BF)).astype(F32)
-    third = (near[cut:] + tail[rest:] + far_t.astype(F32)).astype(BF)
-    up, down = send(third[:32], "z", 1), send(third[32:64], "z", -1)
-    up_2 = send(third[64:], "z", 2)
+    third = (near_t[:64] + token_pair(far_t).astype(F32)).astype(BF)
+    up, down = send(third[:32], "z", 1), send(third[32:], "z", -1)
+    far_2, near_2 = after((far_h[96:], near_h[96:]), third)
+    far_2 = cat([far_2[:32] + fourth[32:], far_2[32:]]).astype(BF)
+    far_2 = token_pair(far_2).astype(F32)
     far_0 = after(far_h[:32], third) + up_1[32:] + down_1[32:]
     far_0 = token_pair(far_0.astype(BF)).astype(F32)
-    near_2 = after(near_h[96:], far_0)
-    up = (up.astype(F32) + up_2.astype(F32) + near_2[:32] + far_2[:32]).astype(BF)
+    near_2 = after(near_2, far_0)
+    up = (up.astype(F32) + fourth[:32] + near_2[:32] + far_2[:32]).astype(BF)
     down = (down.astype(F32) + near_2[32:] + far_2[32:]).astype(BF)
     total = after(near_h[:32], up) + up_1[:32] + down_1[:32] + far_0
     total += send(up, "z", 2).astype(F32) + send(down, "z", -2).astype(F32)

time: 94.4 us -> 101 us (1.070)
  waiting for transfers between devices: 34 us -> 44.7 us
  starting transfers between devices: 47.2 us -> 42 us
    ppermute x26, waiting for transfers between devices: 29.6 us -> 44.5 us  [send(): lax.ppermute(value, axis, [(i, (i + shift) % size) for i in range(size)])]
    ppermute x6, waiting for transfers between devices: 4.42 us -> 0.18 us  [token_pair(): return lax.ppermute(value, 'x', [(0, 1), (1, 0), (2, 3), (3, 2)])]
    ppermute x6, starting transfers between devices: 7.86 us -> 4.21 us  [token_pair(): return lax.ppermute(value, 'x', [(0, 1), (1, 0), (2, 3), (3, 2)])]
    ppermute x26, starting transfers between devices: 35.6 us -> 33.4 us  [send(): lax.ppermute(value, axis, [(i, (i + shift) % size) for i in range(size)])]
  transfers between devices with their start and end apart: 34 -> 34, of which waited for: 17 -> 21; matrix products, arithmetic and copies ran while one was open for 4% -> 4% of each run, Pallas kernels for 1% -> 2%
where the time goes in v10:
time: 101 us; the launch traced here: 99.9 us
  waiting for transfers between devices  44.7 us (44%)
  starting transfers between devices  42 us (42%)
  Pallas kernels  6.3 us (6%)
  other arithmetic  3.34 us (3%)
  local copies, waits for them, and re-layouts  2.52 us (2%)
  between operations  1.08 us (1%)
    ppermute x26, waiting for transfers between devices, send(): lax.ppermute(value, axis, [(i, (i + shift) % size) for i in range(size)])  44.5 us
    ppermute x26, starting transfers between devices, send(): lax.ppermute(value, axis, [(i, (i + shift) % size) for i in range(size)])  33.4 us
    pallas_call x6, Pallas kernels, call(): return list(kernel(*args))  6.3 us
    ppermute x2, starting transfers between devices, weight_pair(): return lax.ppermute(value, 'x', [(0, 3), (3, 0), (1, 2), (2, 1)])  4.43 us
    ppermute x6, starting transfers between devices, token_pair(): return lax.ppermute(value, 'x', [(0, 1), (1, 0), (2, 3), (3, 2)])  4.21 us
  transfers between devices with their start and end apart: 34, of which 21 were waited for; matrix products, arithmetic and copies ran while one was open for 4% of the time, Pallas kernels for 2%

profile of v10, /device:TPU:2, one launch (start us, length us, event | category | flops | bytes accessed | tf_op | source)
XLA Modules:
  0.0 99.9 jit_solution(6752965476063563422)
XLA Ops:
  0.7 0.8 constant_dynamic-update-slice_fusion.1
  1.5 0.8 constant_dynamic-update-slice_fusion
  2.3 3.3 %collective-permute-start.1 = (bf16[32,1280]{1,0:T(8,128)(2,1)S(1)}, bf16[32,1280]{1,0:T(8,128)(2,1)S(1)}, u32[]{:S(2)}, u32[]{:S(2)}) collective-permute-start(bf16[32,1280]{1,0:T(8,128)(2,1)S(1)} %constant_dynamic-update-slice_fusion), channel_id=1, source_target_pairs={{0,64},{32,96},{64,128},{96,160},{128,192},{160,224},{192,0},{224,... | collective-permute-start | bytes 245768 | tf_op jit(solution)/shard_map/ppermute | solution.py:26
  5.5 3.0 %collective-permute-start.2 = (bf16[32,1280]{1,0:T(8,128)(2,1)S(1)}, bf16[32,1280]{1,0:T(8,128)(2,1)S(1)}, u32[]{:S(2)}, u32[]{:S(2)}) collective-permute-start(bf16[32,1280]{1,0:T(8,128)(2,1)S(1)} %constant_dynamic-update-slice_fusion), channel_id=1, source_target_pairs={{0,192},{32,224},{64,0},{96,32},{128,64},{160,96},{192,128},{224,1... | collective-permute-start | bytes 245768 | tf_op jit(solution)/shard_map/ppermute | solution.py:26
  8.6 0.5 collective-permute-start
  9.1 1.2 %pad_maximum_fusion = bf16[320,1280]{1,0:T(8,128)(2,1)S(1)} fusion(bf16[160,1280]{1,0:T(8,128)(2,1)} %wo.3, bf16[160,1280]{1,0:T(8,128)(2,1)} %bitcast.4), kind=kLoop, calls=%fused_computation | loop fusion | flops 1638400 | bytes 1638400 | tf_op jit(solution)/shard_map/concatenate | solution.py:59
  10.3 2.2 %collective-permute-start.9 = (bf16[320,1280]{1,0:T(8,128)(2,1)S(1)}, bf16[320,1280]{1,0:T(8,128)(2,1)S(1)}, u32[]{:S(2)}, u32[]{:S(2)}) collective-permute-start(bf16[320,1280]{1,0:T(8,128)(2,1)S(1)} %pad_maximum_fusion), channel_id=1, source_target_pairs={{0,24},{24,0},{8,16},{16,8},{1,25},{25,1},{9,17},{17,9},{2,26},{26... | collective-permute-start | bytes 2457608 | tf_op jit(solution)/shard_map/ppermute | solution.py:34
  12.5 1.4 %collective-permute-done.2 = bf16[32,1280]{1,0:T(8,128)(2,1)S(1)} collective-permute-done((bf16[32,1280]{1,0:T(8,128)(2,1)S(1)}, bf16[32,1280]{1,0:T(8,128)(2,1)S(1)}, u32[]{:S(2)}, u32[]{:S(2)}) %collective-permute-start.2) | collective-permute-done | bytes 81952 | tf_op jit(solution)/shard_map/ppermute | solution.py:26
  14.0 0.6 collective-permute-start.3
  14.6 2.0 %collective-permute-start.4 = (bf16[32,1280]{1,0:T(8,128)(2,1)S(1)}, bf16[32,1280]{1,0:T(8,128)(2,1)S(1)}, u32[]{:S(2)}, u32[]{:S(2)}) collective-permute-start(bf16[32,1280]{1,0:T(8,128)(2,1)S(1)} %collective-permute-done.2), channel_id=1, source_target_pairs={{0,224},{32,0},{64,32},{96,64},{128,96},{160,128},{192,160},{224,1... | collective-permute-start | bytes 245768 | tf_op jit(solution)/shard_map/ppermute | solution.py:26
  16.7 2.3 %collective-permute-done.4 = bf16[32,1280]{1,0:T(8,128)(2,1)S(1)} collective-permute-done((bf16[32,1280]{1,0:T(8,128)(2,1)S(1)}, bf16[32,1280]{1,0:T(8,128)(2,1)S(1)}, u32[]{:S(2)}, u32[]{:S(2)}) %collective-permute-start.4) | collective-permute-done | bytes 81952 | tf_op jit(solution)/shard_map/ppermute | solution.py:26
  19.0 3.2 %collective-permute-done.7 = bf16[32,1280]{1,0:T(8,128)(2,1)S(1)} collective-permute-done((bf16[32,1280]{1,0:T(8,128)(2,1)S(1)}, bf16[32,1280]{1,0:T(8,128)(2,1)S(1)}, u32[]{:S(2)}, u32[]{:S(2)}) %collective-permute-start.7) | collective-permute-done | bytes 81952 | tf_op jit(solution)/shard_map/ppermute | solution.py:26
  22.2 0.8 collective-permute-start.8
  23.1 0.9 collective-permute-start.5
  24.0 1.2 %collective-permute-start.6 = (bf16[64,1280]{1,0:T(8,128)(2,1)S(1)}, bf16[64,1280]{1,0:T(8,128)(2,1)S(1)}, u32[]{:S(2)}, u32[]{:S(2)}) collective-permute-start(bf16[64,1280]{1,0:T(8,128)(2,1)S(1)} %pad_maximum_fusion.1), channel_id=1, source_target_pairs={{0,32},{32,64},{64,96},{96,128},{128,160},{160,192},{192,224},{224... | collective-permute-start | bytes 491528 | tf_op jit(solution)/shard_map/ppermute | solution.py:26
  25.2 1.6 %collective-permute-start.10 = (bf16[64,1280]{1,0:T(8,128)(2,1)S(1)}, bf16[64,1280]{1,0:T(8,128)(2,1)S(1)}, u32[]{:S(2)}, u32[]{:S(2)}) collective-permute-start(bf16[64,1280]{1,0:T(8,128)(2,1)S(1)} %pad_maximum_fusion.3), channel_id=1, source_target_pairs={{0,64},{32,96},{64,128},{96,160},{128,192},{160,224},{192,0},{224,... | collective-permute-start | bytes 491528 | tf_op jit(solution)/shard_map/ppermute | solution.py:26
  26.8 1.7 %collective-permute-done.5 = bf16[64,1280]{1,0:T(8,128)(2,1)S(1)} collective-permute-done((bf16[64,1280]{1,0:T(8,128)(2,1)S(1)}, bf16[64,1280]{1,0:T(8,128)(2,1)S(1)}, u32[]{:S(2)}, u32[]{:S(2)}) %collective-permute-start.5) | collective-permute-done | bytes 163872 | tf_op jit(solution)/shard_map/ppermute | solution.py:26
  28.5 3.5 %collective-permute-done.6 = bf16[64,1280]{1,0:T(8,128)(2,1)S(1)} collective-permute-done((bf16[64,1280]{1,0:T(8,128)(2,1)S(1)}, bf16[64,1280]{1,0:T(8,128)(2,1)S(1)}, u32[]{:S(2)}, u32[]{:S(2)}) %collective-permute-start.6) | collective-permute-done | bytes 163872 | tf_op jit(solution)/shard_map/ppermute | solution.py:26
  32.0 0.1 collective-permute-start.11
  32.2 0.6 collective-permute-start.13
  32.8 2.7 %collective-permute-done.10.refs_3_ = bf16[64,1280]{1,0:T(8,128)(2,1)S(1)} collective-permute-done((bf16[64,1280]{1,0:T(8,128)(2,1)S(1)}, bf16[64,1280]{1,0:T(8,128)(2,1)S(1)}, u32[]{:S(2)}, u32[]{:S(2)}) %collective-permute-start.10) | collective-permute-done | bytes 163872 | tf_op jit(solution)/shard_map/ppermute | solution.py:26
  35.5 1.5 %collective-permute-done.14.refs_7_ = bf16[64,1280]{1,0:T(8,128)(2,1)} collective-permute-done((bf16[64,1280]{1,0:T(8,128)(2,1)S(1)}, bf16[64,1280]{1,0:T(8,128)(2,1)}, u32[]{:S(2)}, u32[]{:S(2)}) %collective-permute-start.14) | collective-permute-done | bytes 163872 | tf_op jit(solution)/shard_map/ppermute | solution.py:26
  37.0 2.7 %shard_map.75 = (bf16[512,1280]{1,0:T(8,128)(2,1)S(1)}, bf16[512,1280]{1,0:T(8,128)(2,1)S(1)}, bf16[2,320,128]{2,1,0:T(8,128)(2,1)S(1)}, bf16[2,320,128]{2,1,0:T(8,128)(2,1)S(1)}, bf16[2,320,128]{2,1,0:T(8,128)(2,1)S(1)}) custom-call(s32[1]{0:T(128)} %bitcast.me, bf16[192,1280]{1,0:T(8,128)(2,1)S(1)} %constant_dynamic-update-slice_fusion.2.refs_0_, ...), custom_call_target="tpu_custom_call" | custom-call | flops 419430400 | bytes 1048576 | tf_op jit(solution)/shard_map/pallas_call | solution.py:55
  39.7 3.3 %collective-permute-start.15 = (bf16[2,320,128]{2,1,0:T(8,128)(2,1)S(1)}, bf16[2,320,128]{2,1,0:T(8,128)(2,1)S(1)}, u32[]{:S(2)}, u32[]{:S(2)}) collective-permute-start(bf16[2,320,128]{2,1,0:T(8,128)(2,1)S(1)} %get-tuple-element.36), channel_id=1, source_target_pairs={{0,4},{2,6},{4,0},{6,2},{1,5},{3,7},{5,1},{7,3},{8,12},{10,14},{12... | collective-permute-start | bytes 491528 | tf_op jit(solution)/shard_map/ppermute | solution.py:26
  43.0 0.7 collective-permute-start.16
  43.6 2.6 %collective-permute-start.17 = (bf16[2,320,128]{2,1,0:T(8,128)(2,1)S(1)}, bf16[2,320,128]{2,1,0:T(8,128)(2,1)S(1)}, u32[]{:S(2)}, u32[]{:S(2)}) collective-permute-start(bf16[2,320,128]{2,1,0:T(8,128)(2,1)S(1)} %get-tuple-element.40), channel_id=1, source_target_pairs={{0,6},{2,0},{4,2},{6,4},{1,7},{3,1},{5,3},{7,5},{8,14},{10,8},{12,... | collective-permute-start | bytes 491528 | tf_op jit(solution)/shard_map/ppermute | solution.py:26
  46.2 0.6 shard_map.76.p0
  46.8 1.5 %collective-permute-done.15.p1 = bf16[2,320,128]{2,1,0:T(8,128)(2,1)S(1)} collective-permute-done((bf16[2,320,128]{2,1,0:T(8,128)(2,1)S(1)}, bf16[2,320,128]{2,1,0:T(8,128)(2,1)S(1)}, u32[]{:S(2)}, u32[]{:S(2)}) %collective-permute-start.15) | collective-permute-done | bytes 163872 | tf_op jit(solution)/shard_map/ppermute | solution.py:26
  48.3 2.7 %collective-permute-done.16.p2 = bf16[2,320,128]{2,1,0:T(8,128)(2,1)S(1)} collective-permute-done((bf16[2,320,128]{2,1,0:T(8,128)(2,1)S(1)}, bf16[2,320,128]{2,1,0:T(8,128)(2,1)S(1)}, u32[]{:S(2)}, u32[]{:S(2)}) %collective-permute-start.16) | collective-permute-done | bytes 163872 | tf_op jit(solution)/shard_map/ppermute | solution.py:26
  51.0 0.4 collective-permute-done.17.p3
  51.4 0.2 shard_map.77.c0
  51.5 2.2 %collective-permute-start.18 = (bf16[2,320,128]{2,1,0:T(8,128)(2,1)S(1)}, bf16[2,320,128]{2,1,0:T(8,128)(2,1)S(1)}, u32[]{:S(2)}, u32[]{:S(2)}) collective-permute-start(bf16[2,320,128]{2,1,0:T(8,128)(2,1)S(1)} %shard_map.77.c0), channel_id=1, source_target_pairs={{0,4},{2,6},{4,0},{6,2},{1,5},{3,7},{5,1},{7,3},{8,12},{10,14},{12... | collective-permute-start | bytes 491528 | tf_op jit(solution)/shard_map/ppermute | solution.py:26
  53.7 2.0 %collective-permute-start.19 = (bf16[2,320,128]{2,1,0:T(8,128)(2,1)S(1)}, bf16[2,320,128]{2,1,0:T(8,128)(2,1)S(1)}, u32[]{:S(2)}, u32[]{:S(2)}) collective-permute-start(bf16[2,320,128]{2,1,0:T(8,128)(2,1)S(1)} %shard_map.77.c0), channel_id=1, source_target_pairs={{0,6},{2,0},{4,2},{6,4},{1,7},{3,1},{5,3},{7,5},{8,14},{10,8},{12,... | collective-permute-start | bytes 491528 | tf_op jit(solution)/shard_map/ppermute | solution.py:26
  55.7 4.1 %collective-permute-done.18.c2 = bf16[2,320,128]{2,1,0:T(8,128)(2,1)S(1)} collective-permute-done((bf16[2,320,128]{2,1,0:T(8,128)(2,1)S(1)}, bf16[2,320,128]{2,1,0:T(8,128)(2,1)S(1)}, u32[]{:S(2)}, u32[]{:S(2)}) %collective-permute-start.18) | collective-permute-done | bytes 163872 | tf_op jit(solution)/shard_map/ppermute | solution.py:26
  59.9 2.3 %collective-permute-done.19.c1 = bf16[2,320,128]{2,1,0:T(8,128)(2,1)S(1)} collective-permute-done((bf16[2,320,128]{2,1,0:T(8,128)(2,1)S(1)}, bf16[2,320,128]{2,1,0:T(8,128)(2,1)S(1)}, u32[]{:S(2)}, u32[]{:S(2)}) %collective-permute-start.19) | collective-permute-done | bytes 163872 | tf_op jit(solution)/shard_map/ppermute | solution.py:26
  62.2 0.6 collective-permute-done.20.c3
  62.8 1.7 %shard_map.78 = (f32[256,1280]{1,0:T(8,128)S(1)}, f32[256,1280]{1,0:T(8,128)S(1)}, bf16[320,1280]{1,0:T(8,128)(2,1)S(1)}, bf16[192,1280]{1,0:T(8,128)(2,1)S(1)}, bf16[2,320,512]{2,1,0:T(8,128)(2,1)S(1)}) custom-call(s32[1]{0:T(128)} %bitcast.me, bf16[2,320,128]{2,1,0:T(8,128)(2,1)S(1)} %shard_map.77.c0, bf16[2,320,128]{2,1,0:T(8,128)(2,1)S(1)} %collective-permute-done.18.c2, ...), custom_call_target="tpu_custom_call" | custom-call | flops 838860800 | bytes 1048576 | tf_op jit(solution)/shard_map/pallas_call | solution.py:55
  64.7 1.9 %collective-permute-done.21 = bf16[192,1280]{1,0:T(8,128)(2,1)S(1)} collective-permute-done((bf16[192,1280]{1,0:T(8,128)(2,1)S(1)}, bf16[192,1280]{1,0:T(8,128)(2,1)S(1)}, u32[]{:S(2)}, u32[]{:S(2)}) %collective-permute-start.21) | collective-permute-done | bytes 491552 | tf_op jit(solution)/shard_map/ppermute | solution.py:26
  66.5 0.1 collective-permute-start.22
  66.7 0.1 slice_add_fusion.2
  66.9 1.2 %collective-permute-start.25 = (bf16[64,1280]{1,0:T(8,128)(2,1)S(1)}, bf16[64,1280]{1,0:T(8,128)(2,1)S(1)}, u32[]{:S(2)}, u32[]{:S(2)}) collective-permute-start(bf16[64,1280]{1,0:T(8,128)(2,1)S(1)} %pad_maximum_fusion.7), channel_id=1, source_target_pairs={{0,64},{32,96},{64,128},{96,160},{128,192},{160,224},{192,0},{224,... | collective-permute-start | bytes 491528 | tf_op jit(solution)/shard_map/ppermute | solution.py:26
  68.1 0.4 collective-permute-start.23
  68.5 0.6 shard_map.80
  69.1 2.2 %collective-permute-start.33 = (bf16[320,1280]{1,0:T(8,128)(2,1)S(1)}, bf16[320,1280]{1,0:T(8,128)(2,1)S(1)}, u32[]{:S(2)}, u32[]{:S(2)}) collective-permute-start(bf16[320,1280]{1,0:T(8,128)(2,1)S(1)} %shard_map.80), channel_id=1, source_target_pairs={{0,24},{24,0},{8,16},{16,8},{1,25},{25,1},{9,17},{17,9},{2,26},{26... | collective-permute-start | bytes 2457608 | tf_op jit(solution)/shard_map/ppermute | solution.py:34
  71.3 0.6 shard_map.79
  71.9 7.2 %collective-permute-done.25 = bf16[64,1280]{1,0:T(8,128)(2,1)S(1)} collective-permute-done((bf16[64,1280]{1,0:T(8,128)(2,1)S(1)}, bf16[64,1280]{1,0:T(8,128)(2,1)S(1)}, u32[]{:S(2)}, u32[]{:S(2)}) %collective-permute-start.25) | collective-permute-done | bytes 163872 | tf_op jit(solution)/shard_map/ppermute | solution.py:26
  79.1 0.1 convert_element_type.62
  79.3 0.2 fusion.9
  79.5 0.9 collective-permute-start.26
  80.4 2.5 %collective-permute-start.27 = (bf16[64,1280]{1,0:T(8,128)(2,1)S(1)}, bf16[64,1280]{1,0:T(8,128)(2,1)S(1)}, u32[]{:S(2)}, u32[]{:S(2)}) collective-permute-start(bf16[64,1280]{1,0:T(8,128)(2,1)S(1)} %pad_maximum_fusion.6), channel_id=1, source_target_pairs={{0,224},{32,0},{64,32},{96,64},{128,96},{160,128},{192,160},{224,1... | collective-permute-start | bytes 491528 | tf_op jit(solution)/shard_map/ppermute | solution.py:26
  83.2 0.4 collective-permute-start.29
  83.5 0.5 collective-permute-start.24
  84.0 2.6 %collective-permute-done.26 = bf16[64,1280]{1,0:T(8,128)(2,1)S(1)} collective-permute-done((bf16[64,1280]{1,0:T(8,128)(2,1)S(1)}, bf16[64,1280]{1,0:T(8,128)(2,1)S(1)}, u32[]{:S(2)}, u32[]{:S(2)}) %collective-permute-start.26) | collective-permute-done | bytes 163872 | tf_op jit(solution)/shard_map/ppermute | solution.py:26
  86.6 0.5 collective-permute-start.31
  87.2 1.5 %collective-permute-start.28 = (bf16[32,1280]{1,0:T(8,128)(2,1)S(1)}, bf16[32,1280]{1,0:T(8,128)(2,1)S(1)}, u32[]{:S(2)}, u32[]{:S(2)}) collective-permute-start(bf16[32,1280]{1,0:T(8,128)(2,1)S(1)} %fusion.7), channel_id=1, source_target_pairs={{0,8},{8,0},{16,24},{24,16},{1,9},{9,1},{17,25},{25,17},{2,10},{10... | collective-permute-start | bytes 245768 | tf_op jit(solution)/shard_map/ppermute | solution.py:30
  88.7 0.2 collective-permute-done.29
  88.9 0.3 collective-permute-done.24
  89.2 1.9 %collective-permute-done.31 = bf16[32,1280]{1,0:T(8,128)(2,1)S(1)} collective-permute-done((bf16[32,1280]{1,0:T(8,128)(2,1)S(1)}, bf16[32,1280]{1,0:T(8,128)(2,1)S(1)}, u32[]{:S(2)}, u32[]{:S(2)}) %collective-permute-start.31) | collective-permute-done | bytes 81952 | tf_op jit(solution)/shard_map/ppermute | solution.py:26
  91.1 1.1 %collective-permute-start.30 = (bf16[32,1280]{1,0:T(8,128)(2,1)S(1)}, bf16[32,1280]{1,0:T(8,128)(2,1)S(1)}, u32[]{:S(2)}, u32[]{:S(2)}) collective-permute-start(bf16[32,1280]{1,0:T(8,128)(2,1)S(1)} %get-tuple-element.71), channel_id=1, source_target_pairs={{0,64},{32,96},{64,128},{96,160},{128,192},{160,224},{192,0},{224,... | collective-permute-start | bytes 245768 | tf_op jit(solution)/shard_map/ppermute | solution.py:26
  92.2 3.1 %collective-permute-start.32 = (bf16[32,1280]{1,0:T(8,128)(2,1)S(1)}, bf16[32,1280]{1,0:T(8,128)(2,1)S(1)}, u32[]{:S(2)}, u32[]{:S(2)}) collective-permute-start(bf16[32,1280]{1,0:T(8,128)(2,1)S(1)} %get-tuple-element.70), channel_id=1, source_target_pairs={{0,192},{32,224},{64,0},{96,32},{128,64},{160,96},{192,128},{224,1... | collective-permute-start | bytes 245768 | tf_op jit(solution)/shard_map/ppermute | solution.py:26
  95.3 1.3 %convert_add_fusion = (f32[160,1280]{1,0:T(8,128)}, f32[1280,160]{0,1:T(8,128)}) fusion(f32[160,1280]{1,0:T(8,128)S(1)} %get-tuple-element.49, bf16[320,1280]{1,0:T(8,128)(2,1)S(1)} %collective-permute-done.33, f32[160,1280]{1,0:T(8,128)S(1)} %get-tuple-element.58), kind=kLoop, calls=%fused_computation.1 | loop fusion | flops 819200 | bytes 4096000 | tf_op jit(solution)/shard_map/add | solution.py:228
  96.7 1.9 %collective-permute-done.30 = bf16[32,1280]{1,0:T(8,128)(2,1)S(1)} collective-permute-done((bf16[32,1280]{1,0:T(8,128)(2,1)S(1)}, bf16[32,1280]{1,0:T(8,128)(2,1)S(1)}, u32[]{:S(2)}, u32[]{:S(2)}) %collective-permute-start.30) | collective-permute-done | bytes 81952 | tf_op jit(solution)/shard_map/ppermute | solution.py:26
  98.6 0.6 collective-permute-done.32
  99.2 0.6 fusion.14
  (64 shorter events, 0.9 us)
Async XLA Ops:
  0.6 16.0 %copy-start.2 = (bf16[16,1280]{1,0:T(8,128)(2,1)S(1)}, bf16[16,1280]{1,0:T(8,128)(2,1)}, u32[]{:S(2)}) copy-start(bf16[16,1280]{1,0:T(8,128)(2,1)} %param.4) | copy-start | bytes 122884
  0.6 16.0 %copy-start.3 = (bf16[16,1280]{1,0:T(8,128)(2,1)S(1)}, bf16[16,1280]{1,0:T(8,128)(2,1)}, u32[]{:S(2)}) copy-start(bf16[16,1280]{1,0:T(8,128)(2,1)} %param.7) | copy-start | bytes 122884
  2.3 10.3 %collective-permute-start.1 = (bf16[32,1280]{1,0:T(8,128)(2,1)S(1)}, bf16[32,1280]{1,0:T(8,128)(2,1)S(1)}, u32[]{:S(2)}, u32[]{:S(2)}) collective-permute-start(bf16[32,1280]{1,0:T(8,128)(2,1)S(1)} %constant_dynamic-update-slice_fusion), channel_id=1, source_target_pairs={{0,64},{32,96},{64,128},{96,160},{128,192},{160,224},{192,0},{224,... | collective-permute-start | bytes 245768 | tf_op jit(solution)/shard_map/ppermute | solution.py:26
  5.5 8.4 %collective-permute-start.2 = (bf16[32,1280]{1,0:T(8,128)(2,1)S(1)}, bf16[32,1280]{1,0:T(8,128)(2,1)S(1)}, u32[]{:S(2)}, u32[]{:S(2)}) collective-permute-start(bf16[32,1280]{1,0:T(8,128)(2,1)S(1)} %constant_dynamic-update-slice_fusion), channel_id=1, source_target_pairs={{0,192},{32,224},{64,0},{96,32},{128,64},{160,96},{192,128},{224,1... | collective-permute-start | bytes 245768 | tf_op jit(solution)/shard_map/ppermute | solution.py:26
  8.6 8.0 %collective-permute-start = (bf16[32,1280]{1,0:T(8,128)(2,1)S(1)}, bf16[32,1280]{1,0:T(8,128)(2,1)S(1)}, u32[]{:S(2)}, u32[]{:S(2)}) collective-permute-start(bf16[32,1280]{1,0:T(8,128)(2,1)S(1)} %constant_dynamic-update-slice_fusion), channel_id=1, source_target_pairs={{0,8},{8,0},{16,24},{24,16},{1,9},{9,1},{17,25},{25,17},{2,10},{10... | collective-permute-start | bytes 245768 | tf_op jit(solution)/shard_map/ppermute | solution.py:30
  10.3 21.9 %collective-permute-start.9 = (bf16[320,1280]{1,0:T(8,128)(2,1)S(1)}, bf16[320,1280]{1,0:T(8,128)(2,1)S(1)}, u32[]{:S(2)}, u32[]{:S(2)}) collective-permute-start(bf16[320,1280]{1,0:T(8,128)(2,1)S(1)} %pad_maximum_fusion), channel_id=1, source_target_pairs={{0,24},{24,0},{8,16},{16,8},{1,25},{25,1},{9,17},{17,9},{2,26},{26... | collective-permute-start | bytes 2457608 | tf_op jit(solution)/shard_map/ppermute | solution.py:34
  14.0 9.1 %collective-permute-start.3 = (bf16[64,1280]{1,0:T(8,128)(2,1)S(1)}, bf16[64,1280]{1,0:T(8,128)(2,1)S(1)}, u32[]{:S(2)}, u32[]{:S(2)}) collective-permute-start(bf16[64,1280]{1,0:T(8,128)(2,1)S(1)} %pad_maximum_fusion.2), channel_id=1, source_target_pairs={{0,8},{8,0},{16,24},{24,16},{1,9},{9,1},{17,25},{25,17},{2,10},{10... | collective-permute-start | bytes 491528 | tf_op jit(solution)/shard_map/ppermute | solution.py:30
  14.6 4.4 %collective-permute-start.4 = (bf16[32,1280]{1,0:T(8,128)(2,1)S(1)}, bf16[32,1280]{1,0:T(8,128)(2,1)S(1)}, u32[]{:S(2)}, u32[]{:S(2)}) collective-permute-start(bf16[32,1280]{1,0:T(8,128)(2,1)S(1)} %collective-permute-done.2), channel_id=1, source_target_pairs={{0,224},{32,0},{64,32},{96,64},{128,96},{160,128},{192,160},{224,1... | collective-permute-start | bytes 245768 | tf_op jit(solution)/shard_map/ppermute | solution.py:26
  16.6 5.7 %collective-permute-start.7 = (bf16[32,1280]{1,0:T(8,128)(2,1)S(1)}, bf16[32,1280]{1,0:T(8,128)(2,1)S(1)}, u32[]{:S(2)}, u32[]{:S(2)}) collective-permute-start(bf16[32,1280]{1,0:T(8,128)(2,1)S(1)} %collective-permute-done.1), channel_id=1, source_target_pairs={{0,32},{32,64},{64,96},{96,128},{128,160},{160,192},{192,224},{224... | collective-permute-start | bytes 245768 | tf_op jit(solution)/shard_map/ppermute | solution.py:26
  22.2 14.8 %copy-start = (bf16[1280,160]{0,1:T(8,128)(2,1)S(1)}, bf16[1280,160]{0,1:T(8,128)(2,1)}, u32[]{:S(2)}) copy-start(bf16[1280,160]{0,1:T(8,128)(2,1)} %param.5) | copy-start | bytes 1228804
  22.2 14.8 %copy-start.1 = (bf16[160,1280]{1,0:T(8,128)(2,1)S(1)}, bf16[160,1280]{1,0:T(8,128)(2,1)}, u32[]{:S(2)}) copy-start(bf16[160,1280]{1,0:T(8,128)(2,1)} %wo.3) | copy-start | bytes 1228804
  22.2 9.9 %collective-permute-start.8 = (bf16[64,1280]{1,0:T(8,128)(2,1)S(1)}, bf16[64,1280]{1,0:T(8,128)(2,1)S(1)}, u32[]{:S(2)}, u32[]{:S(2)}) collective-permute-start(bf16[64,1280]{1,0:T(8,128)(2,1)S(1)} %pad_maximum_fusion.4), channel_id=1, source_target_pairs={{0,8},{8,0},{16,24},{24,16},{1,9},{9,1},{17,25},{25,17},{2,10},{10... | collective-permute-start | bytes 491528 | tf_op jit(solution)/shard_map/ppermute | solution.py:30
  23.1 5.4 %collective-permute-start.5 = (bf16[64,1280]{1,0:T(8,128)(2,1)S(1)}, bf16[64,1280]{1,0:T(8,128)(2,1)S(1)}, u32[]{:S(2)}, u32[]{:S(2)}) collective-permute-start(bf16[64,1280]{1,0:T(8,128)(2,1)S(1)} %pad_maximum_fusion.1), channel_id=1, source_target_pairs={{0,224},{32,0},{64,32},{96,64},{128,96},{160,128},{192,160},{224,1... | collective-permute-start | bytes 491528 | tf_op jit(solution)/shard_map/ppermute | solution.py:26
  24.0 8.0 %collective-permute-start.6 = (bf16[64,1280]{1,0:T(8,128)(2,1)S(1)}, bf16[64,1280]{1,0:T(8,128)(2,1)S(1)}, u32[]{:S(2)}, u32[]{:S(2)}) collective-permute-start(bf16[64,1280]{1,0:T(8,128)(2,1)S(1)} %pad_maximum_fusion.1), channel_id=1, source_target_pairs={{0,32},{32,64},{64,96},{96,128},{128,160},{160,192},{192,224},{224... | collective-permute-start | bytes 491528 | tf_op jit(solution)/shard_map/ppermute | solution.py:26
  25.2 10.3 %collective-permute-start.10 = (bf16[64,1280]{1,0:T(8,128)(2,1)S(1)}, bf16[64,1280]{1,0:T(8,128)(2,1)S(1)}, u32[]{:S(2)}, u32[]{:S(2)}) collective-permute-start(bf16[64,1280]{1,0:T(8,128)(2,1)S(1)} %pad_maximum_fusion.3), channel_id=1, source_target_pairs={{0,64},{32,96},{64,128},{96,160},{128,192},{160,224},{192,0},{224,... | collective-permute-start | bytes 491528 | tf_op jit(solution)/shard_map/ppermute | solution.py:26
  28.5 8.5 %collective-permute-start.12 = (bf16[128,1280]{1,0:T(8,128)(2,1)S(1)}, bf16[128,1280]{1,0:T(8,128)(2,1)}, u32[]{:S(2)}, u32[]{:S(2)}) collective-permute-start(bf16[128,1280]{1,0:T(8,128)(2,1)S(1)} %constant_dynamic-update-slice_fusion.5.refs_1_), channel_id=1, source_target_pairs={{0,1},{1,0},{2,3},{3,2},{4,5},{5,4},{6,7},{7,6},{8,9},{9,8},{10,11... | collective-permute-start | bytes 983048 | tf_op jit(solution)/shard_map/ppermute | solution.py:26
  32.0 5.0 %collective-permute-start.11 = (bf16[192,1280]{1,0:T(8,128)(2,1)S(1)}, bf16[192,1280]{1,0:T(8,128)(2,1)S(1)}, u32[]{:S(2)}, u32[]{:S(2)}) collective-permute-start(bf16[192,1280]{1,0:T(8,128)(2,1)S(1)} %constant_dynamic-update-slice_fusion.2.refs_0_), channel_id=1, source_target_pairs={{0,1},{1,0},{2,3},{3,2},{4,5},{5,4},{6,7},{7,6},{8,9},{9,8},{10,11... | collective-permute-start | bytes 1474568 | tf_op jit(solution)/shard_map/ppermute | solution.py:26
  32.2 4.8 %collective-permute-start.13 = (bf16[128,1280]{1,0:T(8,128)(2,1)S(1)}, bf16[128,1280]{1,0:T(8,128)(2,1)}, u32[]{:S(2)}, u32[]{:S(2)}) collective-permute-start(bf16[128,1280]{1,0:T(8,128)(2,1)S(1)} %constant_dynamic-update-slice_fusion.8.refs_2_), channel_id=1, source_target_pairs={{0,1},{1,0},{2,3},{3,2},{4,5},{5,4},{6,7},{7,6},{8,9},{9,8},{10,11... | collective-permute-start | bytes 983048 | tf_op jit(solution)/shard_map/ppermute | solution.py:26
  35.5 1.5 %collective-permute-start.14 = (bf16[64,1280]{1,0:T(8,128)(2,1)S(1)}, bf16[64,1280]{1,0:T(8,128)(2,1)}, u32[]{:S(2)}, u32[]{:S(2)}) collective-permute-start(bf16[64,1280]{1,0:T(8,128)(2,1)S(1)} %collective-permute-done.10.refs_3_), channel_id=1, source_target_pairs={{0,1},{1,0},{2,3},{3,2},{4,5},{5,4},{6,7},{7,6},{8,9},{9,8},{10,11... | collective-permute-start | bytes 491528 | tf_op jit(solution)/shard_map/ppermute | solution.py:26
  39.7 8.6 %collective-permute-start.15 = (bf16[2,320,128]{2,1,0:T(8,128)(2,1)S(1)}, bf16[2,320,128]{2,1,0:T(8,128)(2,1)S(1)}, u32[]{:S(2)}, u32[]{:S(2)}) collective-permute-start(bf16[2,320,128]{2,1,0:T(8,128)(2,1)S(1)} %get-tuple-element.36), channel_id=1, source_target_pairs={{0,4},{2,6},{4,0},{6,2},{1,5},{3,7},{5,1},{7,3},{8,12},{10,14},{12... | collective-permute-start | bytes 491528 | tf_op jit(solution)/shard_map/ppermute | solution.py:26
  43.0 8.1 %collective-permute-start.16 = (bf16[2,320,128]{2,1,0:T(8,128)(2,1)S(1)}, bf16[2,320,128]{2,1,0:T(8,128)(2,1)S(1)}, u32[]{:S(2)}, u32[]{:S(2)}) collective-permute-start(bf16[2,320,128]{2,1,0:T(8,128)(2,1)S(1)} %get-tuple-element.39), channel_id=1, source_target_pairs={{0,2},{2,4},{4,6},{6,0},{1,3},{3,5},{5,7},{7,1},{8,10},{10,12},{12... | collective-permute-start | bytes 491528 | tf_op jit(solution)/shard_map/ppermute | solution.py:26
  43.6 7.7 %collective-permute-start.17 = (bf16[2,320,128]{2,1,0:T(8,128)(2,1)S(1)}, bf16[2,320,128]{2,1,0:T(8,128)(2,1)S(1)}, u32[]{:S(2)}, u32[]{:S(2)}) collective-permute-start(bf16[2,320,128]{2,1,0:T(8,128)(2,1)S(1)} %get-tuple-element.40), channel_id=1, source_target_pairs={{0,6},{2,0},{4,2},{6,4},{1,7},{3,1},{5,3},{7,5},{8,14},{10,8},{12,... | collective-permute-start | bytes 491528 | tf_op jit(solution)/shard_map/ppermute | solution.py:26
  51.5 8.3 %collective-permute-start.18 = (bf16[2,320,128]{2,1,0:T(8,128)(2,1)S(1)}, bf16[2,320,128]{2,1,0:T(8,128)(2,1)S(1)}, u32[]{:S(2)}, u32[]{:S(2)}) collective-permute-start(bf16[2,320,128]{2,1,0:T(8,128)(2,1)S(1)} %shard_map.77.c0), channel_id=1, source_target_pairs={{0,4},{2,6},{4,0},{6,2},{1,5},{3,7},{5,1},{7,3},{8,12},{10,14},{12... | collective-permute-start | bytes 491528 | tf_op jit(solution)/shard_map/ppermute | solution.py:26
  53.7 8.5 %collective-permute-start.19 = (bf16[2,320,128]{2,1,0:T(8,128)(2,1)S(1)}, bf16[2,320,128]{2,1,0:T(8,128)(2,1)S(1)}, u32[]{:S(2)}, u32[]{:S(2)}) collective-permute-start(bf16[2,320,128]{2,1,0:T(8,128)(2,1)S(1)} %shard_map.77.c0), channel_id=1, source_target_pairs={{0,6},{2,0},{4,2},{6,4},{1,7},{3,1},{5,3},{7,5},{8,14},{10,8},{12,... | collective-permute-start | bytes 491528 | tf_op jit(solution)/shard_map/ppermute | solution.py:26
  55.7 7.1 %collective-permute-start.20 = (bf16[2,320,128]{2,1,0:T(8,128)(2,1)S(1)}, bf16[2,320,128]{2,1,0:T(8,128)(2,1)S(1)}, u32[]{:S(2)}, u32[]{:S(2)}) collective-permute-start(bf16[2,320,128]{2,1,0:T(8,128)(2,1)S(1)} %shard_map.77.c0), channel_id=1, source_target_pairs={{0,2},{2,4},{4,6},{6,0},{1,3},{3,5},{5,7},{7,1},{8,10},{10,12},{12... | collective-permute-start | bytes 491528 | tf_op jit(solution)/shard_map/ppermute | solution.py:26
  64.6 2.0 %collective-permute-start.21 = (bf16[192,1280]{1,0:T(8,128)(2,1)S(1)}, bf16[192,1280]{1,0:T(8,128)(2,1)S(1)}, u32[]{:S(2)}, u32[]{:S(2)}) collective-permute-start(bf16[192,1280]{1,0:T(8,128)(2,1)S(1)} %get-tuple-element.43), channel_id=1, source_target_pairs={{0,1},{1,0},{2,3},{3,2},{4,5},{5,4},{6,7},{7,6},{8,9},{9,8},{10,11... | collective-permute-start | bytes 1474568 | tf_op jit(solution)/shard_map/ppermute | solution.py:26
  66.5 12.6 %collective-permute-start.22 = (bf16[320,1280]{1,0:T(8,128)(2,1)S(1)}, bf16[320,1280]{1,0:T(8,128)(2,1)S(1)}, u32[]{:S(2)}, u32[]{:S(2)}) collective-permute-start(bf16[320,1280]{1,0:T(8,128)(2,1)S(1)} %get-tuple-element.46), channel_id=1, source_target_pairs={{0,1},{1,0},{2,3},{3,2},{4,5},{5,4},{6,7},{7,6},{8,9},{9,8},{10,11... | collective-permute-start | bytes 2457608 | tf_op jit(solution)/shard_map/ppermute | solution.py:26
  66.9 12.2 %collective-permute-start.25 = (bf16[64,1280]{1,0:T(8,128)(2,1)S(1)}, bf16[64,1280]{1,0:T(8,128)(2,1)S(1)}, u32[]{:S(2)}, u32[]{:S(2)}) collective-permute-start(bf16[64,1280]{1,0:T(8,128)(2,1)S(1)} %pad_maximum_fusion.7), channel_id=1, source_target_pairs={{0,64},{32,96},{64,128},{96,160},{128,192},{160,224},{192,0},{224,... | collective-permute-start | bytes 491528 | tf_op jit(solution)/shard_map/ppermute | solution.py:26
  68.1 14.9 %collective-permute-start.23 = (bf16[64,1280]{1,0:T(8,128)(2,1)S(1)}, bf16[64,1280]{1,0:T(8,128)(2,1)S(1)}, u32[]{:S(2)}, u32[]{:S(2)}) collective-permute-start(bf16[64,1280]{1,0:T(8,128)(2,1)S(1)} %slice.168), channel_id=1, source_target_pairs={{0,8},{8,0},{16,24},{24,16},{1,9},{9,1},{17,25},{25,17},{2,10},{10... | collective-permute-start | bytes 491528 | tf_op jit(solution)/shard_map/ppermute | solution.py:30
  69.1 26.3 %collective-permute-start.33 = (bf16[320,1280]{1,0:T(8,128)(2,1)S(1)}, bf16[320,1280]{1,0:T(8,128)(2,1)S(1)}, u32[]{:S(2)}, u32[]{:S(2)}) collective-permute-start(bf16[320,1280]{1,0:T(8,128)(2,1)S(1)} %shard_map.80), channel_id=1, source_target_pairs={{0,24},{24,0},{8,16},{16,8},{1,25},{25,1},{9,17},{17,9},{2,26},{26... | collective-permute-start | bytes 2457608 | tf_op jit(solution)/shard_map/ppermute | solution.py:34
  79.5 7.1 %collective-permute-start.26 = (bf16[64,1280]{1,0:T(8,128)(2,1)S(1)}, bf16[64,1280]{1,0:T(8,128)(2,1)S(1)}, u32[]{:S(2)}, u32[]{:S(2)}) collective-permute-start(bf16[64,1280]{1,0:T(8,128)(2,1)S(1)} %pad_maximum_fusion.5), channel_id=1, source_target_pairs={{0,32},{32,64},{64,96},{96,128},{128,160},{160,192},{192,224},{224... | collective-permute-start | bytes 491528 | tf_op jit(solution)/shard_map/ppermute | solution.py:26
  80.4 6.7 %collective-permute-start.27 = (bf16[64,1280]{1,0:T(8,128)(2,1)S(1)}, bf16[64,1280]{1,0:T(8,128)(2,1)S(1)}, u32[]{:S(2)}, u32[]{:S(2)}) collective-permute-start(bf16[64,1280]{1,0:T(8,128)(2,1)S(1)} %pad_maximum_fusion.6), channel_id=1, source_target_pairs={{0,224},{32,0},{64,32},{96,64},{128,96},{160,128},{192,160},{224,1... | collective-permute-start | bytes 491528 | tf_op jit(solution)/shard_map/ppermute | solution.py:26
  83.2 5.7 %collective-permute-start.29 = (bf16[64,1280]{1,0:T(8,128)(2,1)S(1)}, bf16[64,1280]{1,0:T(8,128)(2,1)S(1)}, u32[]{:S(2)}, u32[]{:S(2)}) collective-permute-start(bf16[64,1280]{1,0:T(8,128)(2,1)S(1)} %pad_maximum_fusion.8), channel_id=1, source_target_pairs={{0,8},{8,0},{16,24},{24,16},{1,9},{9,1},{17,25},{25,17},{2,10},{10... | collective-permute-start | bytes 491528 | tf_op jit(solution)/shard_map/ppermute | solution.py:30
  83.5 5.7 %collective-permute-start.24 = (bf16[32,1280]{1,0:T(8,128)(2,1)S(1)}, bf16[32,1280]{1,0:T(8,128)(2,1)S(1)}, u32[]{:S(2)}, u32[]{:S(2)}) collective-permute-start(bf16[32,1280]{1,0:T(8,128)(2,1)S(1)} %get-tuple-element.77), channel_id=1, source_target_pairs={{0,32},{32,64},{64,96},{96,128},{128,160},{160,192},{192,224},{224... | collective-permute-start | bytes 245768 | tf_op jit(solution)/shard_map/ppermute | solution.py:26
  86.6 4.4 %collective-permute-start.31 = (bf16[32,1280]{1,0:T(8,128)(2,1)S(1)}, bf16[32,1280]{1,0:T(8,128)(2,1)S(1)}, u32[]{:S(2)}, u32[]{:S(2)}) collective-permute-start(bf16[32,1280]{1,0:T(8,128)(2,1)S(1)} %get-tuple-element.76), channel_id=1, source_target_pairs={{0,224},{32,0},{64,32},{96,64},{128,96},{160,128},{192,160},{224,1... | collective-permute-start | bytes 245768 | tf_op jit(solution)/shard_map/ppermute | solution.py:26
  87.2 9.4 %collective-permute-start.28 = (bf16[32,1280]{1,0:T(8,128)(2,1)S(1)}, bf16[32,1280]{1,0:T(8,128)(2,1)S(1)}, u32[]{:S(2)}, u32[]{:S(2)}) collective-permute-start(bf16[32,1280]{1,0:T(8,128)(2,1)S(1)} %fusion.7), channel_id=1, source_target_pairs={{0,8},{8,0},{16,24},{24,16},{1,9},{9,1},{17,25},{25,17},{2,10},{10... | collective-permute-start | bytes 245768 | tf_op jit(solution)/shard_map/ppermute | solution.py:30
  91.1 7.4 %collective-permute-start.30 = (bf16[32,1280]{1,0:T(8,128)(2,1)S(1)}, bf16[32,1280]{1,0:T(8,128)(2,1)S(1)}, u32[]{:S(2)}, u32[]{:S(2)}) collective-permute-start(bf16[32,1280]{1,0:T(8,128)(2,1)S(1)} %get-tuple-element.71), channel_id=1, source_target_pairs={{0,64},{32,96},{64,128},{96,160},{128,192},{160,224},{192,0},{224,... | collective-permute-start | bytes 245768 | tf_op jit(solution)/shard_map/ppermute | solution.py:26
  92.2 6.9 %collective-permute-start.32 = (bf16[32,1280]{1,0:T(8,128)(2,1)S(1)}, bf16[32,1280]{1,0:T(8,128)(2,1)S(1)}, u32[]{:S(2)}, u32[]{:S(2)}) collective-permute-start(bf16[32,1280]{1,0:T(8,128)(2,1)S(1)} %get-tuple-element.70), channel_id=1, source_target_pairs={{0,192},{32,224},{64,0},{96,32},{128,64},{160,96},{192,128},{224,1... | collective-permute-start | bytes 245768 | tf_op jit(solution)/shard_map/ppermute | solution.py:26

commit v11 on v8

--- a/solution.py
+++ b/solution.py
@@ -109,8 +109,10 @@
     out[1] = (grad_act * smooth_slope(pre)).astype(BF)
 
 
-def down_kernel(me, full, wi, wo, w_pair, near, far, head, tail):
-    del me
+def down_kernel(me, c0, c2, c1, c3, wi, wo, w_pair, near, far, head, tail, full):
+    for k, block in ((0, c0), (2, c2), (1, c1), (3, c3)):
+        lane = pl.multiple_of(((me[0] + k) % 4) * 128, 128)
+        full[:, :, pl.ds(lane, 128)] = block[...]
     h = wi.shape[0]
     for s, w in enumerate((wo, wi)):
         value = dot(full[s, :h], w[...], 0, 0)
@@ -122,18 +124,16 @@
                 if q < 2:
                     (near, far)[q][row : row + 16] = piece
                 elif j < HEAD:
-                    row += (3 - q) * HEAD * 32
+                    row += (4 - q) * HEAD * 32 - (2 * HEAD - 8) * 32
                     head[row : row + 16] = piece.astype(BF)
                 else:
-                    row += (3 - q) * (8 - HEAD) * 32 - HEAD * 32
-                    tail[row : row + 16] = piece.astype(BF)
-
-
-def pair_kernel(me, b0, b2, b1, b3, tok, cot, full, out):
+                    row -= HEAD * 32
+                    (head, tail)[q - 2][row : row + 16] = piece.astype(BF)
+
+
+def pair_kernel(me, full, tok, cot, out):
+    del me
     h = full.shape[1] // 2
-    for k, block in ((0, b0), (2, b2), (1, b1), (3, b3)):
-        lane = pl.multiple_of(((me[0] + k) % 4) * 128, 128)
-        full[:, :, pl.ds(lane, 128)] = block[...]
     out[:h] = dot(full[0, h:], cot[...], 1, 0).astype(BF)
     out[h:] = dot(full[1, h:], tok[...], 1, 0).astype(BF)
 
@@ -173,49 +173,47 @@
         up_kernel, [shape((512, d), BF)] * 2 + [rounded] * 3, [me, *held, *weights], flops
     )
     mine = call(mine_kernel, [part], [me, after(tok, parts[0]), cot, *weights], flops)
+    parts[1:] = after(tuple(parts[1:]), mine[0])
     parts = mine + [send(value, "row", k) for k, value in zip((2, 1, 3), parts)]
     (block,) = call(act_kernel, [rounded], [me, *parts])
     blocks = [block] + [send(block, "row", -k) for k in (2, 1, 3)]
 
     sums = shape((256, d), F32)
-    full, pair = call(
-        pair_kernel,
-        [shape((2, 2 * h, 512), BF), shape((2 * h, d), BF)],
-        [me, *blocks, tok, cot],
-        flops,
-    )
-    near, far, head, tail = call(
+    near, far, head, tail, full = call(
         down_kernel,
-        [sums, sums, shape((HEAD * 64, d), BF), shape(((8 - HEAD) * 64, d), BF)],
-        [me, full, w_in_t, w_out, w_pair],
+        [sums, sums, shape((256 + HEAD * 32, d), BF), shape((256 - HEAD * 32, d), BF), shape((2, 2 * h, 512), BF)],
+        [me, *blocks, w_in_t, w_out, w_pair],
         2 * flops,
     )
     cut, rest = HEAD * 32, (8 - HEAD) * 32
     tail = send(tail, "col", 1)
     head = send(after(head, tail), "col", 1).astype(F32)
-    tail = tail.astype(F32)
-    far_t = (far[cut:] + tail[:rest]).astype(BF)
+    far_t = (far[cut:] + tail.astype(F32)).astype(BF)
     far = after(far, far_t)
-    pair = weight_pair(after(pair, far_t))
+    (pair,) = call(
+        pair_kernel, [shape((2 * h, d), BF)], [me, after(full, far_t), tok, cot], flops
+    )
+    pair = weight_pair(pair)
     grad_out, grad_in_t = call(
         own_kernel, [shape((h, d), F32)] * 2, [me, full, after(tok, far_t), cot], flops
     )
-    far_t = token_pair(far_t)
     head = after(head, grad_out)
-    far_h = far[:cut] + head[:cut]
-    near_h = near[:cut] + head[cut:]
+    far_h = far[:cut] + head[rest:256]
+    near_h = near[:cut] + head[256:]
     up_1 = cat([near_h[32:64], far_h[32:64]]).astype(BF)
     down_1 = cat([near_h[64:96], far_h[64:96]]).astype(BF)
-    near = after(near, (up_1, down_1))
+    near, head = after((near, head), (up_1, down_1))
     up_1, down_1 = send(up_1, "z", 1).astype(F32), send(down_1, "z", -1).astype(F32)
-    far_2 = token_pair(far_h[96:].astype(BF)).astype(F32)
-    third = (near[cut:] + tail[rest:] + far_t.astype(F32)).astype(BF)
+    far_2 = far_h[96:].astype(BF)
+    far_t = after(token_pair(far_t), far_2)
+    far_2 = token_pair(far_2).astype(F32)
+    third = (near[cut:] + head[:rest] + far_t.astype(F32)).astype(BF)
+    up_2 = send(third[64:], "z", 2)
     up, down = send(third[:32], "z", 1), send(third[32:64], "z", -1)
-    up_2 = send(third[64:], "z", 2)
     far_0 = after(far_h[:32], third) + up_1[32:] + down_1[32:]
     far_0 = token_pair(far_0.astype(BF)).astype(F32)
     near_2 = after(near_h[96:], far_0)
-    up = (up.astype(F32) + up_2.astype(F32) + near_2[:32] + far_2[:32]).astype(BF)
+    up = (up_2.astype(F32) + up.astype(F32) + near_2[:32] + far_2[:32]).astype(BF)
     down = (down.astype(F32) + near_2[32:] + far_2[32:]).astype(BF)
     total = after(near_h[:32], up) + up_1[:32] + down_1[:32] + far_0
     total += send(up, "z", 2).astype(F32) + send(down, "z", -2).astype(F32)

time: 94.4 us -> 96.5 us (1.022); the launches traced: 94.2 us -> 94.8 us
  starting transfers between devices: 47.2 us -> 50.2 us
  waiting for transfers between devices: 34 us -> 31.6 us
    ppermute x26, starting transfers between devices: 35.6 us -> 38.3 us  [send(): lax.ppermute(value, axis, [(i, (i + shift) % size) for i in range(size)])]
    ppermute x6, waiting for transfers between devices: 4.42 us -> 2.44 us  [token_pair(): return lax.ppermute(value, 'x', [(0, 1), (1, 0), (2, 3), (3, 2)])]
  transfers between devices with their start and end apart: 34 -> 34, of which waited for: 17 -> 17; matrix products, arithmetic and copies ran while one was open for 4% -> 4% of each run, Pallas kernels for 1% -> 2%
where the time goes in v11:
time: 96.5 us; the launch traced here: 94.8 us
  starting transfers between devices  50.2 us (52%)
  waiting for transfers between devices  31.6 us (33%)
  Pallas kernels  6.35 us (7%)
  other arithmetic  3.19 us (3%)
  local copies, waits for them, and re-layouts  2.47 us (3%)
  between operations  0.98 us (1%)
    ppermute x26, starting transfers between devices, send(): lax.ppermute(value, axis, [(i, (i + shift) % size) for i in range(size)])  38.3 us
    ppermute x26, waiting for transfers between devices, send(): lax.ppermute(value, axis, [(i, (i + shift) % size) for i in range(size)])  29.2 us
    ppermute x6, starting transfers between devices, token_pair(): return lax.ppermute(value, 'x', [(0, 1), (1, 0), (2, 3), (3, 2)])  8.08 us
    pallas_call x6, Pallas kernels, call(): return list(kernel(*args))  6.35 us
    ppermute x2, starting transfers between devices, weight_pair(): return lax.ppermute(value, 'x', [(0, 3), (3, 0), (1, 2), (2, 1)])  3.82 us
    ppermute x6, waiting for transfers between devices, token_pair(): return lax.ppermute(value, 'x', [(0, 1), (1, 0), (2, 3), (3, 2)])  2.44 us
  transfers between devices with their start and end apart: 34, of which 17 were waited for; matrix products, arithmetic and copies ran while one was open for 4% of the time, Pallas kernels for 2%

profile of v11, /device:TPU:2, one launch (start us, length us, event | category | flops | bytes accessed | tf_op | source)
XLA Modules:
  0.0 94.8 jit_solution(11945142558438203326)
XLA Ops:
  0.7 0.8 constant_dynamic-update-slice_fusion.1
  1.5 0.8 constant_dynamic-update-slice_fusion
  2.3 3.3 %collective-permute-start.5 = (bf16[32,1280]{1,0:T(8,128)(2,1)S(1)}, bf16[32,1280]{1,0:T(8,128)(2,1)S(1)}, u32[]{:S(2)}, u32[]{:S(2)}) collective-permute-start(bf16[32,1280]{1,0:T(8,128)(2,1)S(1)} %constant_dynamic-update-slice_fusion), channel_id=1, source_target_pairs={{0,64},{32,96},{64,128},{96,160},{128,192},{160,224},{192,0},{224,... | collective-permute-start | bytes 245768 | tf_op jit(solution)/shard_map/ppermute | solution.py:26
  5.5 3.0 %collective-permute-start.1 = (bf16[32,1280]{1,0:T(8,128)(2,1)S(1)}, bf16[32,1280]{1,0:T(8,128)(2,1)S(1)}, u32[]{:S(2)}, u32[]{:S(2)}) collective-permute-start(bf16[32,1280]{1,0:T(8,128)(2,1)S(1)} %constant_dynamic-update-slice_fusion), channel_id=1, source_target_pairs={{0,192},{32,224},{64,0},{96,32},{128,64},{160,96},{192,128},{224,1... | collective-permute-start | bytes 245768 | tf_op jit(solution)/shard_map/ppermute | solution.py:26
  8.6 0.5 collective-permute-start
  9.1 1.2 %pad_maximum_fusion = bf16[320,1280]{1,0:T(8,128)(2,1)S(1)} fusion(bf16[160,1280]{1,0:T(8,128)(2,1)} %wo.3, bf16[160,1280]{1,0:T(8,128)(2,1)} %bitcast.4), kind=kLoop, calls=%fused_computation | loop fusion | flops 1638400 | bytes 1638400 | tf_op jit(solution)/shard_map/concatenate | solution.py:59
  10.3 2.2 %collective-permute-start.10 = (bf16[320,1280]{1,0:T(8,128)(2,1)S(1)}, bf16[320,1280]{1,0:T(8,128)(2,1)S(1)}, u32[]{:S(2)}, u32[]{:S(2)}) collective-permute-start(bf16[320,1280]{1,0:T(8,128)(2,1)S(1)} %pad_maximum_fusion), channel_id=1, source_target_pairs={{0,24},{24,0},{8,16},{16,8},{1,25},{25,1},{9,17},{17,9},{2,26},{26... | collective-permute-start | bytes 2457608 | tf_op jit(solution)/shard_map/ppermute | solution.py:34
  12.6 1.4 %collective-permute-done.1 = bf16[32,1280]{1,0:T(8,128)(2,1)S(1)} collective-permute-done((bf16[32,1280]{1,0:T(8,128)(2,1)S(1)}, bf16[32,1280]{1,0:T(8,128)(2,1)S(1)}, u32[]{:S(2)}, u32[]{:S(2)}) %collective-permute-start.1) | collective-permute-done | bytes 81952 | tf_op jit(solution)/shard_map/ppermute | solution.py:26
  14.0 0.6 collective-permute-start.6
  14.6 3.9 %collective-permute-start.8 = (bf16[32,1280]{1,0:T(8,128)(2,1)S(1)}, bf16[32,1280]{1,0:T(8,128)(2,1)S(1)}, u32[]{:S(2)}, u32[]{:S(2)}) collective-permute-start(bf16[32,1280]{1,0:T(8,128)(2,1)S(1)} %collective-permute-done.5), channel_id=1, source_target_pairs={{0,64},{32,96},{64,128},{96,160},{128,192},{160,224},{192,0},{224,... | collective-permute-start | bytes 245768 | tf_op jit(solution)/shard_map/ppermute | solution.py:26
  18.5 0.4 collective-permute-start.7
  18.9 2.8 %collective-permute-start.2 = (bf16[32,1280]{1,0:T(8,128)(2,1)S(1)}, bf16[32,1280]{1,0:T(8,128)(2,1)S(1)}, u32[]{:S(2)}, u32[]{:S(2)}) collective-permute-start(bf16[32,1280]{1,0:T(8,128)(2,1)S(1)} %collective-permute-done.1), channel_id=1, source_target_pairs={{0,224},{32,0},{64,32},{96,64},{128,96},{160,128},{192,160},{224,1... | collective-permute-start | bytes 245768 | tf_op jit(solution)/shard_map/ppermute | solution.py:26
  21.8 2.0 %collective-permute-done.2 = bf16[32,1280]{1,0:T(8,128)(2,1)S(1)} collective-permute-done((bf16[32,1280]{1,0:T(8,128)(2,1)S(1)}, bf16[32,1280]{1,0:T(8,128)(2,1)S(1)}, u32[]{:S(2)}, u32[]{:S(2)}) %collective-permute-start.2) | collective-permute-done | bytes 81952 | tf_op jit(solution)/shard_map/ppermute | solution.py:26
  23.8 0.9 collective-permute-start.4
  24.8 2.8 %collective-permute-start.3 = (bf16[64,1280]{1,0:T(8,128)(2,1)S(1)}, bf16[64,1280]{1,0:T(8,128)(2,1)S(1)}, u32[]{:S(2)}, u32[]{:S(2)}) collective-permute-start(bf16[64,1280]{1,0:T(8,128)(2,1)S(1)} %pad_maximum_fusion.1), channel_id=1, source_target_pairs={{0,224},{32,0},{64,32},{96,64},{128,96},{160,128},{192,160},{224,1... | collective-permute-start | bytes 491528 | tf_op jit(solution)/shard_map/ppermute | solution.py:26
  27.6 1.6 %collective-permute-start.9 = (bf16[96,1280]{1,0:T(8,128)(2,1)S(1)}, bf16[96,1280]{1,0:T(8,128)(2,1)}, u32[]{:S(2)}, u32[]{:S(2)}) collective-permute-start(bf16[96,1280]{1,0:T(8,128)(2,1)S(1)} %constant_dynamic-update-slice_fusion.10.refs_2_), channel_id=1, source_target_pairs={{0,8},{8,0},{16,24},{24,16},{1,9},{9,1},{17,25},{25,17},{2,10},{10... | collective-permute-start | bytes 737288 | tf_op jit(solution)/shard_map/ppermute | solution.py:30
  29.1 1.2 %collective-permute-done.3 = bf16[64,1280]{1,0:T(8,128)(2,1)S(1)} collective-permute-done((bf16[64,1280]{1,0:T(8,128)(2,1)S(1)}, bf16[64,1280]{1,0:T(8,128)(2,1)S(1)}, u32[]{:S(2)}, u32[]{:S(2)}) %collective-permute-start.3) | collective-permute-done | bytes 163872 | tf_op jit(solution)/shard_map/ppermute | solution.py:26
  30.4 0.3 collective-permute-done.4
  30.7 0.1 collective-permute-start.11
  30.9 0.6 collective-permute-start.12
  31.4 0.1 collective-permute-start.13
  31.5 2.4 %collective-permute-done.9.refs_3_ = bf16[96,1280]{1,0:T(8,128)(2,1)} collective-permute-done((bf16[96,1280]{1,0:T(8,128)(2,1)S(1)}, bf16[96,1280]{1,0:T(8,128)(2,1)}, u32[]{:S(2)}, u32[]{:S(2)}) %collective-permute-start.9) | collective-permute-done | bytes 245792 | tf_op jit(solution)/shard_map/ppermute | solution.py:30
  34.0 1.8 %collective-permute-done.14.refs_7_ = bf16[96,1280]{1,0:T(8,128)(2,1)} collective-permute-done((bf16[96,1280]{1,0:T(8,128)(2,1)}, bf16[96,1280]{1,0:T(8,128)(2,1)}, u32[]{:S(2)}, u32[]{:S(2)}) %collective-permute-start.14) | collective-permute-done | bytes 245792 | tf_op jit(solution)/shard_map/ppermute | solution.py:26
  35.8 2.7 %shard_map.75 = (bf16[512,1280]{1,0:T(8,128)(2,1)S(1)}, bf16[512,1280]{1,0:T(8,128)(2,1)S(1)}, bf16[2,320,128]{2,1,0:T(8,128)(2,1)S(1)}, bf16[2,320,128]{2,1,0:T(8,128)(2,1)S(1)}, bf16[2,320,128]{2,1,0:T(8,128)(2,1)S(1)}) custom-call(s32[1]{0:T(128)} %bitcast.me, bf16[192,1280]{1,0:T(8,128)(2,1)S(1)} %constant_dynamic-update-slice_fusion.2.refs_0_, ...), custom_call_target="tpu_custom_call" | custom-call | flops 419430400 | bytes 1048576 | tf_op jit(solution)/shard_map/pallas_call | solution.py:55
  38.5 3.3 %collective-permute-start.15 = (bf16[2,320,128]{2,1,0:T(8,128)(2,1)S(1)}, bf16[2,320,128]{2,1,0:T(8,128)(2,1)S(1)}, u32[]{:S(2)}, u32[]{:S(2)}) collective-permute-start(bf16[2,320,128]{2,1,0:T(8,128)(2,1)S(1)} %get-tuple-element.39), channel_id=1, source_target_pairs={{0,4},{2,6},{4,0},{6,2},{1,5},{3,7},{5,1},{7,3},{8,12},{10,14},{12... | collective-permute-start | bytes 491528 | tf_op jit(solution)/shard_map/ppermute | solution.py:26
  41.8 0.6 shard_map.76.p0
  42.4 0.9 collective-permute-start.16
  43.3 2.6 %collective-permute-start.17 = (bf16[2,320,128]{2,1,0:T(8,128)(2,1)S(1)}, bf16[2,320,128]{2,1,0:T(8,128)(2,1)S(1)}, u32[]{:S(2)}, u32[]{:S(2)}) collective-permute-start(bf16[2,320,128]{2,1,0:T(8,128)(2,1)S(1)} %get-tuple-element.45), channel_id=1, source_target_pairs={{0,6},{2,0},{4,2},{6,4},{1,7},{3,1},{5,3},{7,5},{8,14},{10,8},{12,... | collective-permute-start | bytes 491528 | tf_op jit(solution)/shard_map/ppermute | solution.py:26
  45.9 1.1 %collective-permute-done.15.p1 = bf16[2,320,128]{2,1,0:T(8,128)(2,1)S(1)} collective-permute-done((bf16[2,320,128]{2,1,0:T(8,128)(2,1)S(1)}, bf16[2,320,128]{2,1,0:T(8,128)(2,1)S(1)}, u32[]{:S(2)}, u32[]{:S(2)}) %collective-permute-start.15) | collective-permute-done | bytes 163872 | tf_op jit(solution)/shard_map/ppermute | solution.py:26
  47.0 3.1 %collective-permute-done.16.p2 = bf16[2,320,128]{2,1,0:T(8,128)(2,1)S(1)} collective-permute-done((bf16[2,320,128]{2,1,0:T(8,128)(2,1)S(1)}, bf16[2,320,128]{2,1,0:T(8,128)(2,1)S(1)}, u32[]{:S(2)}, u32[]{:S(2)}) %collective-permute-start.16) | collective-permute-done | bytes 163872 | tf_op jit(solution)/shard_map/ppermute | solution.py:26
  50.2 0.2 shard_map.77.c0
  50.4 1.5 %collective-permute-start.20 = (bf16[2,320,128]{2,1,0:T(8,128)(2,1)S(1)}, bf16[2,320,128]{2,1,0:T(8,128)(2,1)S(1)}, u32[]{:S(2)}, u32[]{:S(2)}) collective-permute-start(bf16[2,320,128]{2,1,0:T(8,128)(2,1)S(1)} %shard_map.77.c0), channel_id=1, source_target_pairs={{0,2},{2,4},{4,6},{6,0},{1,3},{3,5},{5,7},{7,1},{8,10},{10,12},{12... | collective-permute-start | bytes 491528 | tf_op jit(solution)/shard_map/ppermute | solution.py:26
  51.8 1.8 %collective-permute-start.19 = (bf16[2,320,128]{2,1,0:T(8,128)(2,1)S(1)}, bf16[2,320,128]{2,1,0:T(8,128)(2,1)S(1)}, u32[]{:S(2)}, u32[]{:S(2)}) collective-permute-start(bf16[2,320,128]{2,1,0:T(8,128)(2,1)S(1)} %shard_map.77.c0), channel_id=1, source_target_pairs={{0,6},{2,0},{4,2},{6,4},{1,7},{3,1},{5,3},{7,5},{8,14},{10,8},{12,... | collective-permute-start | bytes 491528 | tf_op jit(solution)/shard_map/ppermute | solution.py:26
  53.7 1.6 %collective-permute-start.18 = (bf16[2,320,128]{2,1,0:T(8,128)(2,1)S(1)}, bf16[2,320,128]{2,1,0:T(8,128)(2,1)S(1)}, u32[]{:S(2)}, u32[]{:S(2)}) collective-permute-start(bf16[2,320,128]{2,1,0:T(8,128)(2,1)S(1)} %shard_map.77.c0), channel_id=1, source_target_pairs={{0,4},{2,6},{4,0},{6,2},{1,5},{3,7},{5,1},{7,3},{8,12},{10,14},{12... | collective-permute-start | bytes 491528 | tf_op jit(solution)/shard_map/ppermute | solution.py:26
  55.3 2.3 %collective-permute-done.20.c3 = bf16[2,320,128]{2,1,0:T(8,128)(2,1)S(1)} collective-permute-done((bf16[2,320,128]{2,1,0:T(8,128)(2,1)S(1)}, bf16[2,320,128]{2,1,0:T(8,128)(2,1)S(1)}, u32[]{:S(2)}, u32[]{:S(2)}) %collective-permute-start.20) | collective-permute-done | bytes 163872 | tf_op jit(solution)/shard_map/ppermute | solution.py:26
  57.6 1.4 %collective-permute-done.19.c1 = bf16[2,320,128]{2,1,0:T(8,128)(2,1)S(1)} collective-permute-done((bf16[2,320,128]{2,1,0:T(8,128)(2,1)S(1)}, bf16[2,320,128]{2,1,0:T(8,128)(2,1)S(1)}, u32[]{:S(2)}, u32[]{:S(2)}) %collective-permute-start.19) | collective-permute-done | bytes 163872 | tf_op jit(solution)/shard_map/ppermute | solution.py:26
  59.0 2.8 %collective-permute-done.18.c2 = bf16[2,320,128]{2,1,0:T(8,128)(2,1)S(1)} collective-permute-done((bf16[2,320,128]{2,1,0:T(8,128)(2,1)S(1)}, bf16[2,320,128]{2,1,0:T(8,128)(2,1)S(1)}, u32[]{:S(2)}, u32[]{:S(2)}) %collective-permute-start.18) | collective-permute-done | bytes 163872 | tf_op jit(solution)/shard_map/ppermute | solution.py:26
  61.8 1.7 %shard_map.78 = (f32[256,1280]{1,0:T(8,128)S(1)}, f32[256,1280]{1,0:T(8,128)S(1)}, bf16[416,1280]{1,0:T(8,128)(2,1)S(1)}, bf16[96,1280]{1,0:T(8,128)(2,1)S(1)}, bf16[2,320,512]{2,1,0:T(8,128)(2,1)S(1)}) custom-call(s32[1]{0:T(128)} %bitcast.me, bf16[2,320,128]{2,1,0:T(8,128)(2,1)S(1)} %shard_map.77.c0, bf16[2,320,128]{2,1,0:T(8,128)(2,1)S(1)} %collective-permute-done.18.c2, ...), custom_call_target="tpu_custom_call" | custom-call | flops 838860800 | bytes 1048576 | tf_op jit(solution)/shard_map/pallas_call | solution.py:55
  63.5 0.1 collective-permute-start.21
  63.6 1.5 %collective-permute-done.21 = bf16[96,1280]{1,0:T(8,128)(2,1)S(1)} collective-permute-done((bf16[96,1280]{1,0:T(8,128)(2,1)S(1)}, bf16[96,1280]{1,0:T(8,128)(2,1)S(1)}, u32[]{:S(2)}, u32[]{:S(2)}) %collective-permute-start.21) | collective-permute-done | bytes 245792 | tf_op jit(solution)/shard_map/ppermute | solution.py:26
  65.1 0.1 collective-permute-start.22
  65.3 1.6 %collective-permute-start.23 = (bf16[96,1280]{1,0:T(8,128)(2,1)S(1)}, bf16[96,1280]{1,0:T(8,128)(2,1)S(1)}, u32[]{:S(2)}, u32[]{:S(2)}) collective-permute-start(bf16[96,1280]{1,0:T(8,128)(2,1)S(1)} %add_convert_fusion.1), channel_id=1, source_target_pairs={{0,8},{8,0},{16,24},{24,16},{1,9},{9,1},{17,25},{25,17},{2,10},{10... | collective-permute-start | bytes 737288 | tf_op jit(solution)/shard_map/ppermute | solution.py:30
  66.8 0.6 shard_map.80
  67.4 1.6 %collective-permute-start.33 = (bf16[320,1280]{1,0:T(8,128)(2,1)S(1)}, bf16[320,1280]{1,0:T(8,128)(2,1)S(1)}, u32[]{:S(2)}, u32[]{:S(2)}) collective-permute-start(bf16[320,1280]{1,0:T(8,128)(2,1)S(1)} %shard_map.80), channel_id=1, source_target_pairs={{0,24},{24,0},{8,16},{16,8},{1,25},{25,1},{9,17},{17,9},{2,26},{26... | collective-permute-start | bytes 2457608 | tf_op jit(solution)/shard_map/ppermute | solution.py:34
  69.0 0.6 shard_map.79
  69.6 0.1 convert_element_type.62
  69.8 0.2 fusion.6
  70.1 2.1 %collective-permute-start.27 = (bf16[64,1280]{1,0:T(8,128)(2,1)S(1)}, bf16[64,1280]{1,0:T(8,128)(2,1)S(1)}, u32[]{:S(2)}, u32[]{:S(2)}) collective-permute-start(bf16[64,1280]{1,0:T(8,128)(2,1)S(1)} %pad_maximum_fusion.3), channel_id=1, source_target_pairs={{0,224},{32,0},{64,32},{96,64},{128,96},{160,128},{192,160},{224,1... | collective-permute-start | bytes 491528 | tf_op jit(solution)/shard_map/ppermute | solution.py:26
  72.2 0.1 collective-permute-start.26
  72.3 1.9 %collective-permute-start.29 = (bf16[64,1280]{1,0:T(8,128)(2,1)S(1)}, bf16[64,1280]{1,0:T(8,128)(2,1)S(1)}, u32[]{:S(2)}, u32[]{:S(2)}) collective-permute-start(bf16[64,1280]{1,0:T(8,128)(2,1)S(1)} %slice.132), channel_id=1, source_target_pairs={{0,8},{8,0},{16,24},{24,16},{1,9},{9,1},{17,25},{25,17},{2,10},{10... | collective-permute-start | bytes 491528 | tf_op jit(solution)/shard_map/ppermute | solution.py:30
  74.2 0.1 add_convert_fusion
  74.3 3.2 %collective-permute-start.31 = (bf16[32,1280]{1,0:T(8,128)(2,1)S(1)}, bf16[32,1280]{1,0:T(8,128)(2,1)S(1)}, u32[]{:S(2)}, u32[]{:S(2)}) collective-permute-start(bf16[32,1280]{1,0:T(8,128)(2,1)S(1)} %get-tuple-element.78), channel_id=1, source_target_pairs={{0,224},{32,0},{64,32},{96,64},{128,96},{160,128},{192,160},{224,1... | collective-permute-start | bytes 245768 | tf_op jit(solution)/shard_map/ppermute | solution.py:26
  77.6 1.5 %collective-permute-done.26 = bf16[64,1280]{1,0:T(8,128)(2,1)S(1)} collective-permute-done((bf16[64,1280]{1,0:T(8,128)(2,1)S(1)}, bf16[64,1280]{1,0:T(8,128)(2,1)S(1)}, u32[]{:S(2)}, u32[]{:S(2)}) %collective-permute-start.26) | collective-permute-done | bytes 163872 | tf_op jit(solution)/shard_map/ppermute | solution.py:26
  79.2 1.9 %collective-permute-start.28 = (bf16[32,1280]{1,0:T(8,128)(2,1)S(1)}, bf16[32,1280]{1,0:T(8,128)(2,1)S(1)}, u32[]{:S(2)}, u32[]{:S(2)}) collective-permute-start(bf16[32,1280]{1,0:T(8,128)(2,1)S(1)} %fusion.5), channel_id=1, source_target_pairs={{0,8},{8,0},{16,24},{24,16},{1,9},{9,1},{17,25},{25,17},{2,10},{10... | collective-permute-start | bytes 245768 | tf_op jit(solution)/shard_map/ppermute | solution.py:30
  81.1 2.2 %collective-permute-done.25 = bf16[32,1280]{1,0:T(8,128)(2,1)S(1)} collective-permute-done((bf16[32,1280]{1,0:T(8,128)(2,1)S(1)}, bf16[32,1280]{1,0:T(8,128)(2,1)S(1)}, u32[]{:S(2)}, u32[]{:S(2)}) %collective-permute-start.25) | collective-permute-done | bytes 81952 | tf_op jit(solution)/shard_map/ppermute | solution.py:26
  83.3 3.4 %collective-permute-done.24 = bf16[32,1280]{1,0:T(8,128)(2,1)S(1)} collective-permute-done((bf16[32,1280]{1,0:T(8,128)(2,1)S(1)}, bf16[32,1280]{1,0:T(8,128)(2,1)S(1)}, u32[]{:S(2)}, u32[]{:S(2)}) %collective-permute-start.24) | collective-permute-done | bytes 81952 | tf_op jit(solution)/shard_map/ppermute | solution.py:26
  86.7 0.1 fusion
  86.7 0.7 collective-permute-start.32
  87.4 2.3 %collective-permute-start.30 = (bf16[32,1280]{1,0:T(8,128)(2,1)S(1)}, bf16[32,1280]{1,0:T(8,128)(2,1)S(1)}, u32[]{:S(2)}, u32[]{:S(2)}) collective-permute-start(bf16[32,1280]{1,0:T(8,128)(2,1)S(1)} %get-tuple-element.73), channel_id=1, source_target_pairs={{0,64},{32,96},{64,128},{96,160},{128,192},{160,224},{192,0},{224,... | collective-permute-start | bytes 245768 | tf_op jit(solution)/shard_map/ppermute | solution.py:26
  89.7 1.3 %convert_add_fusion = (f32[160,1280]{1,0:T(8,128)}, f32[1280,160]{0,1:T(8,128)}) fusion(f32[160,1280]{1,0:T(8,128)S(1)} %get-tuple-element.53, bf16[320,1280]{1,0:T(8,128)(2,1)S(1)} %collective-permute-done.33, f32[160,1280]{1,0:T(8,128)S(1)} %get-tuple-element.62), kind=kLoop, calls=%fused_computation.1 | loop fusion | flops 819200 | bytes 4096000 | tf_op jit(solution)/shard_map/add | solution.py:221
  91.1 1.4 %collective-permute-done.32 = bf16[32,1280]{1,0:T(8,128)(2,1)S(1)} collective-permute-done((bf16[32,1280]{1,0:T(8,128)(2,1)S(1)}, bf16[32,1280]{1,0:T(8,128)(2,1)S(1)}, u32[]{:S(2)}, u32[]{:S(2)}) %collective-permute-start.32) | collective-permute-done | bytes 81952 | tf_op jit(solution)/shard_map/ppermute | solution.py:26
  92.5 1.6 %collective-permute-done.30 = bf16[32,1280]{1,0:T(8,128)(2,1)S(1)} collective-permute-done((bf16[32,1280]{1,0:T(8,128)(2,1)S(1)}, bf16[32,1280]{1,0:T(8,128)(2,1)S(1)}, u32[]{:S(2)}, u32[]{:S(2)}) %collective-permute-start.30) | collective-permute-done | bytes 81952 | tf_op jit(solution)/shard_map/ppermute | solution.py:26
  94.1 0.1 fusion.3
  94.2 0.6 fusion.11
  (51 shorter events, 0.5 us)
Async XLA Ops:
  0.6 21.1 %copy-start.2 = (bf16[16,1280]{1,0:T(8,128)(2,1)S(1)}, bf16[16,1280]{1,0:T(8,128)(2,1)}, u32[]{:S(2)}) copy-start(bf16[16,1280]{1,0:T(8,128)(2,1)} %param.4) | copy-start | bytes 122884
  0.6 21.1 %copy-start.3 = (bf16[16,1280]{1,0:T(8,128)(2,1)S(1)}, bf16[16,1280]{1,0:T(8,128)(2,1)}, u32[]{:S(2)}) copy-start(bf16[16,1280]{1,0:T(8,128)(2,1)} %param.7) | copy-start | bytes 122884
  2.3 11.7 %collective-permute-start.5 = (bf16[32,1280]{1,0:T(8,128)(2,1)S(1)}, bf16[32,1280]{1,0:T(8,128)(2,1)S(1)}, u32[]{:S(2)}, u32[]{:S(2)}) collective-permute-start(bf16[32,1280]{1,0:T(8,128)(2,1)S(1)} %constant_dynamic-update-slice_fusion), channel_id=1, source_target_pairs={{0,64},{32,96},{64,128},{96,160},{128,192},{160,224},{192,0},{224,... | collective-permute-start | bytes 245768 | tf_op jit(solution)/shard_map/ppermute | solution.py:26
  5.5 8.4 %collective-permute-start.1 = (bf16[32,1280]{1,0:T(8,128)(2,1)S(1)}, bf16[32,1280]{1,0:T(8,128)(2,1)S(1)}, u32[]{:S(2)}, u32[]{:S(2)}) collective-permute-start(bf16[32,1280]{1,0:T(8,128)(2,1)S(1)} %constant_dynamic-update-slice_fusion), channel_id=1, source_target_pairs={{0,192},{32,224},{64,0},{96,32},{128,64},{160,96},{192,128},{224,1... | collective-permute-start | bytes 245768 | tf_op jit(solution)/shard_map/ppermute | solution.py:26
  8.6 10.4 %collective-permute-start = (bf16[32,1280]{1,0:T(8,128)(2,1)S(1)}, bf16[32,1280]{1,0:T(8,128)(2,1)S(1)}, u32[]{:S(2)}, u32[]{:S(2)}) collective-permute-start(bf16[32,1280]{1,0:T(8,128)(2,1)S(1)} %constant_dynamic-update-slice_fusion), channel_id=1, source_target_pairs={{0,8},{8,0},{16,24},{24,16},{1,9},{9,1},{17,25},{25,17},{2,10},{10... | collective-permute-start | bytes 245768 | tf_op jit(solution)/shard_map/ppermute | solution.py:30
  10.3 25.5 %copy-start = (bf16[1280,160]{0,1:T(8,128)(2,1)S(1)}, bf16[1280,160]{0,1:T(8,128)(2,1)}, u32[]{:S(2)}) copy-start(bf16[1280,160]{0,1:T(8,128)(2,1)} %param.5) | copy-start | bytes 1228804
  10.3 25.5 %copy-start.1 = (bf16[160,1280]{1,0:T(8,128)(2,1)S(1)}, bf16[160,1280]{1,0:T(8,128)(2,1)}, u32[]{:S(2)}) copy-start(bf16[160,1280]{1,0:T(8,128)(2,1)} %wo.3) | copy-start | bytes 1228804
  10.3 23.6 %collective-permute-start.10 = (bf16[320,1280]{1,0:T(8,128)(2,1)S(1)}, bf16[320,1280]{1,0:T(8,128)(2,1)S(1)}, u32[]{:S(2)}, u32[]{:S(2)}) collective-permute-start(bf16[320,1280]{1,0:T(8,128)(2,1)S(1)} %pad_maximum_fusion), channel_id=1, source_target_pairs={{0,24},{24,0},{8,16},{16,8},{1,25},{25,1},{9,17},{17,9},{2,26},{26... | collective-permute-start | bytes 2457608 | tf_op jit(solution)/shard_map/ppermute | solution.py:34
  14.0 16.8 %collective-permute-start.6 = (bf16[64,1280]{1,0:T(8,128)(2,1)S(1)}, bf16[64,1280]{1,0:T(8,128)(2,1)S(1)}, u32[]{:S(2)}, u32[]{:S(2)}) collective-permute-start(bf16[64,1280]{1,0:T(8,128)(2,1)S(1)} %get-tuple-element.83), channel_id=1, source_target_pairs={{0,8},{8,0},{16,24},{24,16},{1,9},{9,1},{17,25},{25,17},{2,10},{10... | collective-permute-start | bytes 491528 | tf_op jit(solution)/shard_map/ppermute | solution.py:30
  14.6 12.9 %collective-permute-start.8 = (bf16[32,1280]{1,0:T(8,128)(2,1)S(1)}, bf16[32,1280]{1,0:T(8,128)(2,1)S(1)}, u32[]{:S(2)}, u32[]{:S(2)}) collective-permute-start(bf16[32,1280]{1,0:T(8,128)(2,1)S(1)} %collective-permute-done.5), channel_id=1, source_target_pairs={{0,64},{32,96},{64,128},{96,160},{128,192},{160,224},{192,0},{224,... | collective-permute-start | bytes 245768 | tf_op jit(solution)/shard_map/ppermute | solution.py:26
  18.5 6.2 %collective-permute-start.7 = (bf16[32,1280]{1,0:T(8,128)(2,1)S(1)}, bf16[32,1280]{1,0:T(8,128)(2,1)S(1)}, u32[]{:S(2)}, u32[]{:S(2)}) collective-permute-start(bf16[32,1280]{1,0:T(8,128)(2,1)S(1)} %collective-permute-done.5), channel_id=1, source_target_pairs={{0,32},{32,64},{64,96},{96,128},{128,160},{160,192},{192,224},{224... | collective-permute-start | bytes 245768 | tf_op jit(solution)/shard_map/ppermute | solution.py:26
  18.9 4.9 %collective-permute-start.2 = (bf16[32,1280]{1,0:T(8,128)(2,1)S(1)}, bf16[32,1280]{1,0:T(8,128)(2,1)S(1)}, u32[]{:S(2)}, u32[]{:S(2)}) collective-permute-start(bf16[32,1280]{1,0:T(8,128)(2,1)S(1)} %collective-permute-done.1), channel_id=1, source_target_pairs={{0,224},{32,0},{64,32},{96,64},{128,96},{160,128},{192,160},{224,1... | collective-permute-start | bytes 245768 | tf_op jit(solution)/shard_map/ppermute | solution.py:26
  23.8 6.9 %collective-permute-start.4 = (bf16[64,1280]{1,0:T(8,128)(2,1)S(1)}, bf16[64,1280]{1,0:T(8,128)(2,1)S(1)}, u32[]{:S(2)}, u32[]{:S(2)}) collective-permute-start(bf16[64,1280]{1,0:T(8,128)(2,1)S(1)} %pad_maximum_fusion.1), channel_id=1, source_target_pairs={{0,32},{32,64},{64,96},{96,128},{128,160},{160,192},{192,224},{224... | collective-permute-start | bytes 491528 | tf_op jit(solution)/shard_map/ppermute | solution.py:26
  24.8 5.6 %collective-permute-start.3 = (bf16[64,1280]{1,0:T(8,128)(2,1)S(1)}, bf16[64,1280]{1,0:T(8,128)(2,1)S(1)}, u32[]{:S(2)}, u32[]{:S(2)}) collective-permute-start(bf16[64,1280]{1,0:T(8,128)(2,1)S(1)} %pad_maximum_fusion.1), channel_id=1, source_target_pairs={{0,224},{32,0},{64,32},{96,64},{128,96},{160,128},{192,160},{224,1... | collective-permute-start | bytes 491528 | tf_op jit(solution)/shard_map/ppermute | solution.py:26
  27.6 6.4 %collective-permute-start.9 = (bf16[96,1280]{1,0:T(8,128)(2,1)S(1)}, bf16[96,1280]{1,0:T(8,128)(2,1)}, u32[]{:S(2)}, u32[]{:S(2)}) collective-permute-start(bf16[96,1280]{1,0:T(8,128)(2,1)S(1)} %constant_dynamic-update-slice_fusion.10.refs_2_), channel_id=1, source_target_pairs={{0,8},{8,0},{16,24},{24,16},{1,9},{9,1},{17,25},{25,17},{2,10},{10... | collective-permute-start | bytes 737288 | tf_op jit(solution)/shard_map/ppermute | solution.py:30
  30.7 3.3 %collective-permute-start.11 = (bf16[192,1280]{1,0:T(8,128)(2,1)S(1)}, bf16[192,1280]{1,0:T(8,128)(2,1)S(1)}, u32[]{:S(2)}, u32[]{:S(2)}) collective-permute-start(bf16[192,1280]{1,0:T(8,128)(2,1)S(1)} %constant_dynamic-update-slice_fusion.2.refs_0_), channel_id=1, source_target_pairs={{0,1},{1,0},{2,3},{3,2},{4,5},{5,4},{6,7},{7,6},{8,9},{9,8},{10,11... | collective-permute-start | bytes 1474568 | tf_op jit(solution)/shard_map/ppermute | solution.py:26
  30.9 3.1 %collective-permute-start.12 = (bf16[128,1280]{1,0:T(8,128)(2,1)S(1)}, bf16[128,1280]{1,0:T(8,128)(2,1)S(1)}, u32[]{:S(2)}, u32[]{:S(2)}) collective-permute-start(bf16[128,1280]{1,0:T(8,128)(2,1)S(1)} %constant_dynamic-update-slice_fusion.7.refs_1_), channel_id=1, source_target_pairs={{0,1},{1,0},{2,3},{3,2},{4,5},{5,4},{6,7},{7,6},{8,9},{9,8},{10,11... | collective-permute-start | bytes 983048 | tf_op jit(solution)/shard_map/ppermute | solution.py:26
  31.4 2.5 %collective-permute-start.13 = (bf16[96,1280]{1,0:T(8,128)(2,1)S(1)}, bf16[96,1280]{1,0:T(8,128)(2,1)}, u32[]{:S(2)}, u32[]{:S(2)}) collective-permute-start(bf16[96,1280]{1,0:T(8,128)(2,1)S(1)} %constant_dynamic-update-slice_fusion.10.refs_2_), channel_id=1, source_target_pairs={{0,1},{1,0},{2,3},{3,2},{4,5},{5,4},{6,7},{7,6},{8,9},{9,8},{10,11... | collective-permute-start | bytes 737288 | tf_op jit(solution)/shard_map/ppermute | solution.py:26
  34.0 1.9 %collective-permute-start.14 = (bf16[96,1280]{1,0:T(8,128)(2,1)}, bf16[96,1280]{1,0:T(8,128)(2,1)}, u32[]{:S(2)}, u32[]{:S(2)}) collective-permute-start(bf16[96,1280]{1,0:T(8,128)(2,1)} %collective-permute-done.9.refs_3_), channel_id=1, source_target_pairs={{0,1},{1,0},{2,3},{3,2},{4,5},{5,4},{6,7},{7,6},{8,9},{9,8},{10,11... | collective-permute-start | bytes 737288 | tf_op jit(solution)/shard_map/ppermute | solution.py:26
  38.5 8.5 %collective-permute-start.15 = (bf16[2,320,128]{2,1,0:T(8,128)(2,1)S(1)}, bf16[2,320,128]{2,1,0:T(8,128)(2,1)S(1)}, u32[]{:S(2)}, u32[]{:S(2)}) collective-permute-start(bf16[2,320,128]{2,1,0:T(8,128)(2,1)S(1)} %get-tuple-element.39), channel_id=1, source_target_pairs={{0,4},{2,6},{4,0},{6,2},{1,5},{3,7},{5,1},{7,3},{8,12},{10,14},{12... | collective-permute-start | bytes 491528 | tf_op jit(solution)/shard_map/ppermute | solution.py:26
  42.4 7.8 %collective-permute-start.16 = (bf16[2,320,128]{2,1,0:T(8,128)(2,1)S(1)}, bf16[2,320,128]{2,1,0:T(8,128)(2,1)S(1)}, u32[]{:S(2)}, u32[]{:S(2)}) collective-permute-start(bf16[2,320,128]{2,1,0:T(8,128)(2,1)S(1)} %get-tuple-element.44), channel_id=1, source_target_pairs={{0,2},{2,4},{4,6},{6,0},{1,3},{3,5},{5,7},{7,1},{8,10},{10,12},{12... | collective-permute-start | bytes 491528 | tf_op jit(solution)/shard_map/ppermute | solution.py:26
  43.3 6.9 %collective-permute-start.17 = (bf16[2,320,128]{2,1,0:T(8,128)(2,1)S(1)}, bf16[2,320,128]{2,1,0:T(8,128)(2,1)S(1)}, u32[]{:S(2)}, u32[]{:S(2)}) collective-permute-start(bf16[2,320,128]{2,1,0:T(8,128)(2,1)S(1)} %get-tuple-element.45), channel_id=1, source_target_pairs={{0,6},{2,0},{4,2},{6,4},{1,7},{3,1},{5,3},{7,5},{8,14},{10,8},{12,... | collective-permute-start | bytes 491528 | tf_op jit(solution)/shard_map/ppermute | solution.py:26
  50.4 7.2 %collective-permute-start.20 = (bf16[2,320,128]{2,1,0:T(8,128)(2,1)S(1)}, bf16[2,320,128]{2,1,0:T(8,128)(2,1)S(1)}, u32[]{:S(2)}, u32[]{:S(2)}) collective-permute-start(bf16[2,320,128]{2,1,0:T(8,128)(2,1)S(1)} %shard_map.77.c0), channel_id=1, source_target_pairs={{0,2},{2,4},{4,6},{6,0},{1,3},{3,5},{5,7},{7,1},{8,10},{10,12},{12... | collective-permute-start | bytes 491528 | tf_op jit(solution)/shard_map/ppermute | solution.py:26
  51.8 7.1 %collective-permute-start.19 = (bf16[2,320,128]{2,1,0:T(8,128)(2,1)S(1)}, bf16[2,320,128]{2,1,0:T(8,128)(2,1)S(1)}, u32[]{:S(2)}, u32[]{:S(2)}) collective-permute-start(bf16[2,320,128]{2,1,0:T(8,128)(2,1)S(1)} %shard_map.77.c0), channel_id=1, source_target_pairs={{0,6},{2,0},{4,2},{6,4},{1,7},{3,1},{5,3},{7,5},{8,14},{10,8},{12,... | collective-permute-start | bytes 491528 | tf_op jit(solution)/shard_map/ppermute | solution.py:26
  53.7 8.1 %collective-permute-start.18 = (bf16[2,320,128]{2,1,0:T(8,128)(2,1)S(1)}, bf16[2,320,128]{2,1,0:T(8,128)(2,1)S(1)}, u32[]{:S(2)}, u32[]{:S(2)}) collective-permute-start(bf16[2,320,128]{2,1,0:T(8,128)(2,1)S(1)} %shard_map.77.c0), channel_id=1, source_target_pairs={{0,4},{2,6},{4,0},{6,2},{1,5},{3,7},{5,1},{7,3},{8,12},{10,14},{12... | collective-permute-start | bytes 491528 | tf_op jit(solution)/shard_map/ppermute | solution.py:26
  63.5 1.6 %collective-permute-start.21 = (bf16[96,1280]{1,0:T(8,128)(2,1)S(1)}, bf16[96,1280]{1,0:T(8,128)(2,1)S(1)}, u32[]{:S(2)}, u32[]{:S(2)}) collective-permute-start(bf16[96,1280]{1,0:T(8,128)(2,1)S(1)} %get-tuple-element.48), channel_id=1, source_target_pairs={{0,1},{1,0},{2,3},{3,2},{4,5},{5,4},{6,7},{7,6},{8,9},{9,8},{10,11... | collective-permute-start | bytes 737288 | tf_op jit(solution)/shard_map/ppermute | solution.py:26
  65.1 4.6 %collective-permute-start.22 = (bf16[416,1280]{1,0:T(8,128)(2,1)S(1)}, bf16[416,1280]{1,0:T(8,128)(2,1)S(1)}, u32[]{:S(2)}, u32[]{:S(2)}) collective-permute-start(bf16[416,1280]{1,0:T(8,128)(2,1)S(1)} %get-tuple-element.49), channel_id=1, source_target_pairs={{0,1},{1,0},{2,3},{3,2},{4,5},{5,4},{6,7},{7,6},{8,9},{9,8},{10,11... | collective-permute-start | bytes 3194888 | tf_op jit(solution)/shard_map/ppermute | solution.py:26
  65.3 8.9 %collective-permute-start.23 = (bf16[96,1280]{1,0:T(8,128)(2,1)S(1)}, bf16[96,1280]{1,0:T(8,128)(2,1)S(1)}, u32[]{:S(2)}, u32[]{:S(2)}) collective-permute-start(bf16[96,1280]{1,0:T(8,128)(2,1)S(1)} %add_convert_fusion.1), channel_id=1, source_target_pairs={{0,8},{8,0},{16,24},{24,16},{1,9},{9,1},{17,25},{25,17},{2,10},{10... | collective-permute-start | bytes 737288 | tf_op jit(solution)/shard_map/ppermute | solution.py:30
  67.4 22.3 %collective-permute-start.33 = (bf16[320,1280]{1,0:T(8,128)(2,1)S(1)}, bf16[320,1280]{1,0:T(8,128)(2,1)S(1)}, u32[]{:S(2)}, u32[]{:S(2)}) collective-permute-start(bf16[320,1280]{1,0:T(8,128)(2,1)S(1)} %shard_map.80), channel_id=1, source_target_pairs={{0,24},{24,0},{8,16},{16,8},{1,25},{25,1},{9,17},{17,9},{2,26},{26... | collective-permute-start | bytes 2457608 | tf_op jit(solution)/shard_map/ppermute | solution.py:34
  70.1 7.4 %collective-permute-start.27 = (bf16[64,1280]{1,0:T(8,128)(2,1)S(1)}, bf16[64,1280]{1,0:T(8,128)(2,1)S(1)}, u32[]{:S(2)}, u32[]{:S(2)}) collective-permute-start(bf16[64,1280]{1,0:T(8,128)(2,1)S(1)} %pad_maximum_fusion.3), channel_id=1, source_target_pairs={{0,224},{32,0},{64,32},{96,64},{128,96},{160,128},{192,160},{224,1... | collective-permute-start | bytes 491528 | tf_op jit(solution)/shard_map/ppermute | solution.py:26
  72.2 6.9 %collective-permute-start.26 = (bf16[64,1280]{1,0:T(8,128)(2,1)S(1)}, bf16[64,1280]{1,0:T(8,128)(2,1)S(1)}, u32[]{:S(2)}, u32[]{:S(2)}) collective-permute-start(bf16[64,1280]{1,0:T(8,128)(2,1)S(1)} %pad_maximum_fusion.2), channel_id=1, source_target_pairs={{0,32},{32,64},{64,96},{96,128},{128,160},{160,192},{192,224},{224... | collective-permute-start | bytes 491528 | tf_op jit(solution)/shard_map/ppermute | solution.py:26
  72.3 6.9 %collective-permute-start.29 = (bf16[64,1280]{1,0:T(8,128)(2,1)S(1)}, bf16[64,1280]{1,0:T(8,128)(2,1)S(1)}, u32[]{:S(2)}, u32[]{:S(2)}) collective-permute-start(bf16[64,1280]{1,0:T(8,128)(2,1)S(1)} %slice.132), channel_id=1, source_target_pairs={{0,8},{8,0},{16,24},{24,16},{1,9},{9,1},{17,25},{25,17},{2,10},{10... | collective-permute-start | bytes 491528 | tf_op jit(solution)/shard_map/ppermute | solution.py:30
  74.3 6.8 %collective-permute-start.31 = (bf16[32,1280]{1,0:T(8,128)(2,1)S(1)}, bf16[32,1280]{1,0:T(8,128)(2,1)S(1)}, u32[]{:S(2)}, u32[]{:S(2)}) collective-permute-start(bf16[32,1280]{1,0:T(8,128)(2,1)S(1)} %get-tuple-element.78), channel_id=1, source_target_pairs={{0,224},{32,0},{64,32},{96,64},{128,96},{160,128},{192,160},{224,1... | collective-permute-start | bytes 245768 | tf_op jit(solution)/shard_map/ppermute | solution.py:26
  77.5 5.8 %collective-permute-start.25 = (bf16[32,1280]{1,0:T(8,128)(2,1)S(1)}, bf16[32,1280]{1,0:T(8,128)(2,1)S(1)}, u32[]{:S(2)}, u32[]{:S(2)}) collective-permute-start(bf16[32,1280]{1,0:T(8,128)(2,1)S(1)} %get-tuple-element.79), channel_id=1, source_target_pairs={{0,32},{32,64},{64,96},{96,128},{128,160},{160,192},{192,224},{224... | collective-permute-start | bytes 245768 | tf_op jit(solution)/shard_map/ppermute | solution.py:26
  79.1 7.6 %collective-permute-start.24 = (bf16[32,1280]{1,0:T(8,128)(2,1)S(1)}, bf16[32,1280]{1,0:T(8,128)(2,1)S(1)}, u32[]{:S(2)}, u32[]{:S(2)}) collective-permute-start(bf16[32,1280]{1,0:T(8,128)(2,1)S(1)} %get-tuple-element.80), channel_id=1, source_target_pairs={{0,64},{32,96},{64,128},{96,160},{128,192},{160,224},{192,0},{224,... | collective-permute-start | bytes 245768 | tf_op jit(solution)/shard_map/ppermute | solution.py:26
  79.2 11.9 %collective-permute-start.28 = (bf16[32,1280]{1,0:T(8,128)(2,1)S(1)}, bf16[32,1280]{1,0:T(8,128)(2,1)S(1)}, u32[]{:S(2)}, u32[]{:S(2)}) collective-permute-start(bf16[32,1280]{1,0:T(8,128)(2,1)S(1)} %fusion.5), channel_id=1, source_target_pairs={{0,8},{8,0},{16,24},{24,16},{1,9},{9,1},{17,25},{25,17},{2,10},{10... | collective-permute-start | bytes 245768 | tf_op jit(solution)/shard_map/ppermute | solution.py:30
  86.7 5.7 %collective-permute-start.32 = (bf16[32,1280]{1,0:T(8,128)(2,1)S(1)}, bf16[32,1280]{1,0:T(8,128)(2,1)S(1)}, u32[]{:S(2)}, u32[]{:S(2)}) collective-permute-start(bf16[32,1280]{1,0:T(8,128)(2,1)S(1)} %get-tuple-element.72), channel_id=1, source_target_pairs={{0,192},{32,224},{64,0},{96,32},{128,64},{160,96},{192,128},{224,1... | collective-permute-start | bytes 245768 | tf_op jit(solution)/shard_map/ppermute | solution.py:26
  87.4 6.7 %collective-permute-start.30 = (bf16[32,1280]{1,0:T(8,128)(2,1)S(1)}, bf16[32,1280]{1,0:T(8,128)(2,1)S(1)}, u32[]{:S(2)}, u32[]{:S(2)}) collective-permute-start(bf16[32,1280]{1,0:T(8,128)(2,1)S(1)} %get-tuple-element.73), channel_id=1, source_target_pairs={{0,64},{32,96},{64,128},{96,160},{128,192},{160,224},{192,0},{224,... | collective-permute-start | bytes 245768 | tf_op jit(solution)/shard_map/ppermute | solution.py:26

commit v12 on v11

--- a/solution.py
+++ b/solution.py
@@ -65,11 +65,9 @@
     )
 
 
-def products(value_of, wi, wo, w_pair, part):
-    h = wi.shape[0]
-    for s, w in enumerate((wi, wo)):
-        part[s, :h] = dot(w[...], value_of(s), 1, 1).astype(part.dtype)
-        part[s, h:] = dot(w_pair[s * h : s * h + h], value_of(s), 1, 1).astype(part.dtype)
+def products(value_of, weights, part):
+    for s in range(2):
+        part[s] = dot(weights[s], value_of(s), 1, 1).astype(part.dtype)
 
 
 def quarter_of(tok, cot, index):
@@ -78,7 +76,11 @@
 
 
 def up_kernel(me, *refs):
-    held, (wi, wo, w_pair, tok, cot), parts = refs[:8], refs[8:13], refs[13:]
+    held, (wi, wo, w_pair, tok, cot, weights), parts = refs[:8], refs[8:14], refs[14:]
+    h = wi.shape[0]
+    for s, w in enumerate((wi, wo)):
+        weights[s, :h] = w[...]
+        weights[s, h:] = w_pair[s * h : s * h + h]
     for q in range(4):
         half, chip = q // 2 * 4, q % 2
         for j in range(8):
@@ -92,11 +94,11 @@
             tok[row : row + 16] = ref[i : i + 16]
             cot[row : row + 16] = ref[i + 16 : i + 32]
     for k, part in zip((2, 1, 3), parts):
-        products(quarter_of(tok, cot, me[0] + k), wi, wo, w_pair, part)
-
-
-def mine_kernel(me, tok, cot, wi, wo, w_pair, part):
-    products(quarter_of(tok, cot, me[0]), wi, wo, w_pair, part)
+        products(quarter_of(tok, cot, me[0] + k), weights, part)
+
+
+def mine_kernel(me, tok, cot, weights, part):
+    products(quarter_of(tok, cot, me[0]), weights, part)
 
 
 def act_kernel(me, p0, p1, p2, p3, out):
@@ -109,14 +111,12 @@
     out[1] = (grad_act * smooth_slope(pre)).astype(BF)
 
 
-def down_kernel(me, c0, c2, c1, c3, wi, wo, w_pair, near, far, head, tail, full):
+def down_kernel(me, c0, c2, c1, c3, weights, near, far, head, tail, full):
     for k, block in ((0, c0), (2, c2), (1, c1), (3, c3)):
         lane = pl.multiple_of(((me[0] + k) % 4) * 128, 128)
         full[:, :, pl.ds(lane, 128)] = block[...]
-    h = wi.shape[0]
-    for s, w in enumerate((wo, wi)):
-        value = dot(full[s, :h], w[...], 0, 0)
-        value += dot(full[s, h:], w_pair[(1 - s) * h : (2 - s) * h], 0, 0)
+    for s in range(2):
+        value = dot(full[s], weights[1 - s], 0, 0)
         for q in range(4):
             for j in range(8):
                 piece = value[q * 128 + j * 16 : q * 128 + j * 16 + 16]
@@ -168,11 +168,13 @@
     held += [send(value, "col", 1) for value in held]
 
     part, rounded = shape((2, 2 * h, 128), F32), shape((2, 2 * h, 128), BF)
-    weights = [w_in_t, w_out, w_pair]
-    tok, cot, *parts = call(
-        up_kernel, [shape((512, d), BF)] * 2 + [rounded] * 3, [me, *held, *weights], flops
-    )
-    mine = call(mine_kernel, [part], [me, after(tok, parts[0]), cot, *weights], flops)
+    tok, cot, weights, *parts = call(
+        up_kernel,
+        [shape((512, d), BF)] * 2 + [shape((2, 2 * h, d), BF)] + [rounded] * 3,
+        [me, *held, w_in_t, w_out, w_pair],
+        flops,
+    )
+    mine = call(mine_kernel, [part], [me, after(tok, parts[0]), cot, weights], flops)
     parts[1:] = after(tuple(parts[1:]), mine[0])
     parts = mine + [send(value, "row", k) for k, value in zip((2, 1, 3), parts)]
     (block,) = call(act_kernel, [rounded], [me, *parts])
@@ -182,7 +184,7 @@
     near, far, head, tail, full = call(
         down_kernel,
         [sums, sums, shape((256 + HEAD * 32, d), BF), shape((256 - HEAD * 32, d), BF), shape((2, 2 * h, 512), BF)],
-        [me, *blocks, w_in_t, w_out, w_pair],
+        [me, *blocks, weights],
         2 * flops,
     )
     cut, rest = HEAD * 32, (8 - HEAD) * 32

time: 96.5 us -> 96.4 us (level)
  no operation moved by 1% of the time
where the time goes in v12:
time: 96.4 us; the launch traced here: 94.6 us
  starting transfers between devices  50.2 us (52%)
  waiting for transfers between devices  31.4 us (33%)
  Pallas kernels  6.4 us (7%)
  other arithmetic  3.17 us (3%)
  local copies, waits for them, and re-layouts  2.47 us (3%)
  between operations  0.99 us (1%)
    ppermute x26, starting transfers between devices, send(): lax.ppermute(value, axis, [(i, (i + shift) % size) for i in range(size)])  38.3 us
    ppermute x26, waiting for transfers between devices, send(): lax.ppermute(value, axis, [(i, (i + shift) % size) for i in range(size)])  29 us
    ppermute x6, starting transfers between devices, token_pair(): return lax.ppermute(value, 'x', [(0, 1), (1, 0), (2, 3), (3, 2)])  8.1 us
    pallas_call x6, Pallas kernels, call(): return list(kernel(*args))  6.4 us
    ppermute x2, starting transfers between devices, weight_pair(): return lax.ppermute(value, 'x', [(0, 3), (3, 0), (1, 2), (2, 1)])  3.82 us
    ppermute x6, waiting for transfers between devices, token_pair(): return lax.ppermute(value, 'x', [(0, 1), (1, 0), (2, 3), (3, 2)])  2.44 us
  transfers between devices with their start and end apart: 34, of which 17 were waited for; matrix products, arithmetic and copies ran while one was open for 4% of the time, Pallas kernels for 2%

profile of v12, /device:TPU:2, one launch (start us, length us, event | category | flops | bytes accessed | tf_op | source)
XLA Modules:
  0.0 94.6 jit_solution(7747864830243021766)
XLA Ops:
  0.7 0.8 constant_dynamic-update-slice_fusion.1
  1.5 0.8 constant_dynamic-update-slice_fusion
  2.3 3.3 %collective-permute-start.5 = (bf16[32,1280]{1,0:T(8,128)(2,1)S(1)}, bf16[32,1280]{1,0:T(8,128)(2,1)S(1)}, u32[]{:S(2)}, u32[]{:S(2)}) collective-permute-start(bf16[32,1280]{1,0:T(8,128)(2,1)S(1)} %constant_dynamic-update-slice_fusion), channel_id=1, source_target_pairs={{0,64},{32,96},{64,128},{96,160},{128,192},{160,224},{192,0},{224,... | collective-permute-start | bytes 245768 | tf_op jit(solution)/shard_map/ppermute | solution.py:26
  5.5 3.0 %collective-permute-start.1 = (bf16[32,1280]{1,0:T(8,128)(2,1)S(1)}, bf16[32,1280]{1,0:T(8,128)(2,1)S(1)}, u32[]{:S(2)}, u32[]{:S(2)}) collective-permute-start(bf16[32,1280]{1,0:T(8,128)(2,1)S(1)} %constant_dynamic-update-slice_fusion), channel_id=1, source_target_pairs={{0,192},{32,224},{64,0},{96,32},{128,64},{160,96},{192,128},{224,1... | collective-permute-start | bytes 245768 | tf_op jit(solution)/shard_map/ppermute | solution.py:26
  8.6 0.5 collective-permute-start
  9.1 1.2 %pad_maximum_fusion = bf16[320,1280]{1,0:T(8,128)(2,1)S(1)} fusion(bf16[160,1280]{1,0:T(8,128)(2,1)} %refs_9_.1, bf16[160,1280]{1,0:T(8,128)(2,1)} %bitcast.4), kind=kLoop, calls=%fused_computation | loop fusion | flops 1638400 | bytes 1638400 | tf_op jit(solution)/shard_map/concatenate | solution.py:59
  10.3 2.2 %collective-permute-start.10 = (bf16[320,1280]{1,0:T(8,128)(2,1)S(1)}, bf16[320,1280]{1,0:T(8,128)(2,1)S(1)}, u32[]{:S(2)}, u32[]{:S(2)}) collective-permute-start(bf16[320,1280]{1,0:T(8,128)(2,1)S(1)} %pad_maximum_fusion), channel_id=1, source_target_pairs={{0,24},{24,0},{8,16},{16,8},{1,25},{25,1},{9,17},{17,9},{2,26},{26... | collective-permute-start | bytes 2457608 | tf_op jit(solution)/shard_map/ppermute | solution.py:34
  12.6 1.4 %collective-permute-done.1 = bf16[32,1280]{1,0:T(8,128)(2,1)S(1)} collective-permute-done((bf16[32,1280]{1,0:T(8,128)(2,1)S(1)}, bf16[32,1280]{1,0:T(8,128)(2,1)S(1)}, u32[]{:S(2)}, u32[]{:S(2)}) %collective-permute-start.1) | collective-permute-done | bytes 81952 | tf_op jit(solution)/shard_map/ppermute | solution.py:26
  14.0 0.6 collective-permute-start.6
  14.6 3.9 %collective-permute-start.8 = (bf16[32,1280]{1,0:T(8,128)(2,1)S(1)}, bf16[32,1280]{1,0:T(8,128)(2,1)S(1)}, u32[]{:S(2)}, u32[]{:S(2)}) collective-permute-start(bf16[32,1280]{1,0:T(8,128)(2,1)S(1)} %collective-permute-done.5), channel_id=1, source_target_pairs={{0,64},{32,96},{64,128},{96,160},{128,192},{160,224},{192,0},{224,... | collective-permute-start | bytes 245768 | tf_op jit(solution)/shard_map/ppermute | solution.py:26
  18.5 0.4 collective-permute-start.7
  18.9 2.8 %collective-permute-start.2 = (bf16[32,1280]{1,0:T(8,128)(2,1)S(1)}, bf16[32,1280]{1,0:T(8,128)(2,1)S(1)}, u32[]{:S(2)}, u32[]{:S(2)}) collective-permute-start(bf16[32,1280]{1,0:T(8,128)(2,1)S(1)} %collective-permute-done.1), channel_id=1, source_target_pairs={{0,224},{32,0},{64,32},{96,64},{128,96},{160,128},{192,160},{224,1... | collective-permute-start | bytes 245768 | tf_op jit(solution)/shard_map/ppermute | solution.py:26
  21.8 2.0 %collective-permute-done.2 = bf16[32,1280]{1,0:T(8,128)(2,1)S(1)} collective-permute-done((bf16[32,1280]{1,0:T(8,128)(2,1)S(1)}, bf16[32,1280]{1,0:T(8,128)(2,1)S(1)}, u32[]{:S(2)}, u32[]{:S(2)}) %collective-permute-start.2) | collective-permute-done | bytes 81952 | tf_op jit(solution)/shard_map/ppermute | solution.py:26
  23.8 0.9 collective-permute-start.4
  24.8 2.8 %collective-permute-start.3 = (bf16[64,1280]{1,0:T(8,128)(2,1)S(1)}, bf16[64,1280]{1,0:T(8,128)(2,1)S(1)}, u32[]{:S(2)}, u32[]{:S(2)}) collective-permute-start(bf16[64,1280]{1,0:T(8,128)(2,1)S(1)} %pad_maximum_fusion.1), channel_id=1, source_target_pairs={{0,224},{32,0},{64,32},{96,64},{128,96},{160,128},{192,160},{224,1... | collective-permute-start | bytes 491528 | tf_op jit(solution)/shard_map/ppermute | solution.py:26
  27.6 1.6 %collective-permute-start.9 = (bf16[96,1280]{1,0:T(8,128)(2,1)S(1)}, bf16[96,1280]{1,0:T(8,128)(2,1)}, u32[]{:S(2)}, u32[]{:S(2)}) collective-permute-start(bf16[96,1280]{1,0:T(8,128)(2,1)S(1)} %constant_dynamic-update-slice_fusion.10.refs_2_), channel_id=1, source_target_pairs={{0,8},{8,0},{16,24},{24,16},{1,9},{9,1},{17,25},{25,17},{2,10},{10... | collective-permute-start | bytes 737288 | tf_op jit(solution)/shard_map/ppermute | solution.py:30
  29.1 1.2 %collective-permute-done.3 = bf16[64,1280]{1,0:T(8,128)(2,1)S(1)} collective-permute-done((bf16[64,1280]{1,0:T(8,128)(2,1)S(1)}, bf16[64,1280]{1,0:T(8,128)(2,1)S(1)}, u32[]{:S(2)}, u32[]{:S(2)}) %collective-permute-start.3) | collective-permute-done | bytes 163872 | tf_op jit(solution)/shard_map/ppermute | solution.py:26
  30.4 0.3 collective-permute-done.4
  30.7 0.1 collective-permute-start.11
  30.9 0.6 collective-permute-start.12
  31.4 0.1 collective-permute-start.13
  31.5 2.4 %collective-permute-done.9.refs_3_ = bf16[96,1280]{1,0:T(8,128)(2,1)} collective-permute-done((bf16[96,1280]{1,0:T(8,128)(2,1)S(1)}, bf16[96,1280]{1,0:T(8,128)(2,1)}, u32[]{:S(2)}, u32[]{:S(2)}) %collective-permute-start.9) | collective-permute-done | bytes 245792 | tf_op jit(solution)/shard_map/ppermute | solution.py:30
  34.0 1.8 %collective-permute-done.14.refs_7_ = bf16[96,1280]{1,0:T(8,128)(2,1)} collective-permute-done((bf16[96,1280]{1,0:T(8,128)(2,1)}, bf16[96,1280]{1,0:T(8,128)(2,1)}, u32[]{:S(2)}, u32[]{:S(2)}) %collective-permute-start.14) | collective-permute-done | bytes 245792 | tf_op jit(solution)/shard_map/ppermute | solution.py:26
  35.8 2.8 %shard_map.75 = (bf16[512,1280]{1,0:T(8,128)(2,1)S(1)}, bf16[512,1280]{1,0:T(8,128)(2,1)S(1)}, bf16[2,320,1280]{2,1,0:T(8,128)(2,1)S(1)}, bf16[2,320,128]{2,1,0:...) custom-call(s32[1]{0:T(128)} %bitcast.me, ...), custom_call_target="tpu_custom_call" | custom-call | flops 419430400 | bytes 1048576 | tf_op jit(solution)/shard_map/pallas_call | solution.py:55
  38.6 3.3 %collective-permute-start.15 = (bf16[2,320,128]{2,1,0:T(8,128)(2,1)S(1)}, bf16[2,320,128]{2,1,0:T(8,128)(2,1)S(1)}, u32[]{:S(2)}, u32[]{:S(2)}) collective-permute-start(bf16[2,320,128]{2,1,0:T(8,128)(2,1)S(1)} %get-tuple-element.40), channel_id=1, source_target_pairs={{0,4},{2,6},{4,0},{6,2},{1,5},{3,7},{5,1},{7,3},{8,12},{10,14},{12... | collective-permute-start | bytes 491528 | tf_op jit(solution)/shard_map/ppermute | solution.py:26
  41.9 0.6 shard_map.76.p0
  42.5 0.9 collective-permute-start.16
  43.4 2.6 %collective-permute-start.17 = (bf16[2,320,128]{2,1,0:T(8,128)(2,1)S(1)}, bf16[2,320,128]{2,1,0:T(8,128)(2,1)S(1)}, u32[]{:S(2)}, u32[]{:S(2)}) collective-permute-start(bf16[2,320,128]{2,1,0:T(8,128)(2,1)S(1)} %get-tuple-element.47), channel_id=1, source_target_pairs={{0,6},{2,0},{4,2},{6,4},{1,7},{3,1},{5,3},{7,5},{8,14},{10,8},{12,... | collective-permute-start | bytes 491528 | tf_op jit(solution)/shard_map/ppermute | solution.py:26
  46.0 1.2 %collective-permute-done.15.p1 = bf16[2,320,128]{2,1,0:T(8,128)(2,1)S(1)} collective-permute-done((bf16[2,320,128]{2,1,0:T(8,128)(2,1)S(1)}, bf16[2,320,128]{2,1,0:T(8,128)(2,1)S(1)}, u32[]{:S(2)}, u32[]{:S(2)}) %collective-permute-start.15) | collective-permute-done | bytes 163872 | tf_op jit(solution)/shard_map/ppermute | solution.py:26
  47.1 3.1 %collective-permute-done.16.p2 = bf16[2,320,128]{2,1,0:T(8,128)(2,1)S(1)} collective-permute-done((bf16[2,320,128]{2,1,0:T(8,128)(2,1)S(1)}, bf16[2,320,128]{2,1,0:T(8,128)(2,1)S(1)}, u32[]{:S(2)}, u32[]{:S(2)}) %collective-permute-start.16) | collective-permute-done | bytes 163872 | tf_op jit(solution)/shard_map/ppermute | solution.py:26
  50.3 0.2 shard_map.77.c0
  50.5 1.5 %collective-permute-start.20 = (bf16[2,320,128]{2,1,0:T(8,128)(2,1)S(1)}, bf16[2,320,128]{2,1,0:T(8,128)(2,1)S(1)}, u32[]{:S(2)}, u32[]{:S(2)}) collective-permute-start(bf16[2,320,128]{2,1,0:T(8,128)(2,1)S(1)} %shard_map.77.c0), channel_id=1, source_target_pairs={{0,2},{2,4},{4,6},{6,0},{1,3},{3,5},{5,7},{7,1},{8,10},{10,12},{12... | collective-permute-start | bytes 491528 | tf_op jit(solution)/shard_map/ppermute | solution.py:26
  51.9 1.8 %collective-permute-start.19 = (bf16[2,320,128]{2,1,0:T(8,128)(2,1)S(1)}, bf16[2,320,128]{2,1,0:T(8,128)(2,1)S(1)}, u32[]{:S(2)}, u32[]{:S(2)}) collective-permute-start(bf16[2,320,128]{2,1,0:T(8,128)(2,1)S(1)} %shard_map.77.c0), channel_id=1, source_target_pairs={{0,6},{2,0},{4,2},{6,4},{1,7},{3,1},{5,3},{7,5},{8,14},{10,8},{12,... | collective-permute-start | bytes 491528 | tf_op jit(solution)/shard_map/ppermute | solution.py:26
  53.8 1.6 %collective-permute-start.18 = (bf16[2,320,128]{2,1,0:T(8,128)(2,1)S(1)}, bf16[2,320,128]{2,1,0:T(8,128)(2,1)S(1)}, u32[]{:S(2)}, u32[]{:S(2)}) collective-permute-start(bf16[2,320,128]{2,1,0:T(8,128)(2,1)S(1)} %shard_map.77.c0), channel_id=1, source_target_pairs={{0,4},{2,6},{4,0},{6,2},{1,5},{3,7},{5,1},{7,3},{8,12},{10,14},{12... | collective-permute-start | bytes 491528 | tf_op jit(solution)/shard_map/ppermute | solution.py:26
  55.4 2.3 %collective-permute-done.20.c3 = bf16[2,320,128]{2,1,0:T(8,128)(2,1)S(1)} collective-permute-done((bf16[2,320,128]{2,1,0:T(8,128)(2,1)S(1)}, bf16[2,320,128]{2,1,0:T(8,128)(2,1)S(1)}, u32[]{:S(2)}, u32[]{:S(2)}) %collective-permute-start.20) | collective-permute-done | bytes 163872 | tf_op jit(solution)/shard_map/ppermute | solution.py:26
  57.7 1.3 %collective-permute-done.19.c1 = bf16[2,320,128]{2,1,0:T(8,128)(2,1)S(1)} collective-permute-done((bf16[2,320,128]{2,1,0:T(8,128)(2,1)S(1)}, bf16[2,320,128]{2,1,0:T(8,128)(2,1)S(1)}, u32[]{:S(2)}, u32[]{:S(2)}) %collective-permute-start.19) | collective-permute-done | bytes 163872 | tf_op jit(solution)/shard_map/ppermute | solution.py:26
  59.1 2.8 %collective-permute-done.18.c2 = bf16[2,320,128]{2,1,0:T(8,128)(2,1)S(1)} collective-permute-done((bf16[2,320,128]{2,1,0:T(8,128)(2,1)S(1)}, bf16[2,320,128]{2,1,0:T(8,128)(2,1)S(1)}, u32[]{:S(2)}, u32[]{:S(2)}) %collective-permute-start.18) | collective-permute-done | bytes 163872 | tf_op jit(solution)/shard_map/ppermute | solution.py:26
  61.8 1.7 %shard_map.78 = (f32[256,1280]{1,0:T(8,128)S(1)}, f32[256,1280]{1,0:T(8,128)S(1)}, bf16[416,1280]{1,0:T(8,128)(2,1)S(1)}, bf16[96,1280]{1,0:T(8,128)(2,1)S(1)}, bf16[2,320,512]{2,1,0:T(8,128)(2,1)S(1)}) custom-call(s32[1]{0:T(128)} %bitcast.me, bf16[2,320,128]{2,1,0:T(8,128)(2,1)S(1)} %shard_map.77.c0, bf16[2,320,128]{2,1,0:T(8,128)(2,1)S(1)} %collective-permute-done.18.c2, ...), custom_call_target="tpu_custom_call" | custom-call | flops 838860800 | bytes 1048576 | tf_op jit(solution)/shard_map/pallas_call | solution.py:55
  63.5 0.1 collective-permute-start.21
  63.6 1.5 %collective-permute-done.21 = bf16[96,1280]{1,0:T(8,128)(2,1)S(1)} collective-permute-done((bf16[96,1280]{1,0:T(8,128)(2,1)S(1)}, bf16[96,1280]{1,0:T(8,128)(2,1)S(1)}, u32[]{:S(2)}, u32[]{:S(2)}) %collective-permute-start.21) | collective-permute-done | bytes 245792 | tf_op jit(solution)/shard_map/ppermute | solution.py:26
  65.1 0.1 collective-permute-start.22
  65.3 1.6 %collective-permute-start.23 = (bf16[96,1280]{1,0:T(8,128)(2,1)S(1)}, bf16[96,1280]{1,0:T(8,128)(2,1)S(1)}, u32[]{:S(2)}, u32[]{:S(2)}) collective-permute-start(bf16[96,1280]{1,0:T(8,128)(2,1)S(1)} %add_convert_fusion.1), channel_id=1, source_target_pairs={{0,8},{8,0},{16,24},{24,16},{1,9},{9,1},{17,25},{25,17},{2,10},{10... | collective-permute-start | bytes 737288 | tf_op jit(solution)/shard_map/ppermute | solution.py:30
  66.9 0.6 shard_map.80
  67.5 1.6 %collective-permute-start.33 = (bf16[320,1280]{1,0:T(8,128)(2,1)S(1)}, bf16[320,1280]{1,0:T(8,128)(2,1)S(1)}, u32[]{:S(2)}, u32[]{:S(2)}) collective-permute-start(bf16[320,1280]{1,0:T(8,128)(2,1)S(1)} %shard_map.80), channel_id=1, source_target_pairs={{0,24},{24,0},{8,16},{16,8},{1,25},{25,1},{9,17},{17,9},{2,26},{26... | collective-permute-start | bytes 2457608 | tf_op jit(solution)/shard_map/ppermute | solution.py:34
  69.1 0.6 shard_map.79
  69.7 0.1 convert_element_type.62
  69.8 0.2 fusion.6
  70.1 2.1 %collective-permute-start.27 = (bf16[64,1280]{1,0:T(8,128)(2,1)S(1)}, bf16[64,1280]{1,0:T(8,128)(2,1)S(1)}, u32[]{:S(2)}, u32[]{:S(2)}) collective-permute-start(bf16[64,1280]{1,0:T(8,128)(2,1)S(1)} %pad_maximum_fusion.3), channel_id=1, source_target_pairs={{0,224},{32,0},{64,32},{96,64},{128,96},{160,128},{192,160},{224,1... | collective-permute-start | bytes 491528 | tf_op jit(solution)/shard_map/ppermute | solution.py:26
  72.2 0.1 collective-permute-start.26
  72.3 1.9 %collective-permute-start.29 = (bf16[64,1280]{1,0:T(8,128)(2,1)S(1)}, bf16[64,1280]{1,0:T(8,128)(2,1)S(1)}, u32[]{:S(2)}, u32[]{:S(2)}) collective-permute-start(bf16[64,1280]{1,0:T(8,128)(2,1)S(1)} %slice.132), channel_id=1, source_target_pairs={{0,8},{8,0},{16,24},{24,16},{1,9},{9,1},{17,25},{25,17},{2,10},{10... | collective-permute-start | bytes 491528 | tf_op jit(solution)/shard_map/ppermute | solution.py:30
  74.2 0.1 add_convert_fusion
  74.4 3.2 %collective-permute-start.31 = (bf16[32,1280]{1,0:T(8,128)(2,1)S(1)}, bf16[32,1280]{1,0:T(8,128)(2,1)S(1)}, u32[]{:S(2)}, u32[]{:S(2)}) collective-permute-start(bf16[32,1280]{1,0:T(8,128)(2,1)S(1)} %get-tuple-element.80), channel_id=1, source_target_pairs={{0,224},{32,0},{64,32},{96,64},{128,96},{160,128},{192,160},{224,1... | collective-permute-start | bytes 245768 | tf_op jit(solution)/shard_map/ppermute | solution.py:26
  77.6 1.5 %collective-permute-done.26 = bf16[64,1280]{1,0:T(8,128)(2,1)S(1)} collective-permute-done((bf16[64,1280]{1,0:T(8,128)(2,1)S(1)}, bf16[64,1280]{1,0:T(8,128)(2,1)S(1)}, u32[]{:S(2)}, u32[]{:S(2)}) %collective-permute-start.26) | collective-permute-done | bytes 163872 | tf_op jit(solution)/shard_map/ppermute | solution.py:26
  79.2 1.9 %collective-permute-start.28 = (bf16[32,1280]{1,0:T(8,128)(2,1)S(1)}, bf16[32,1280]{1,0:T(8,128)(2,1)S(1)}, u32[]{:S(2)}, u32[]{:S(2)}) collective-permute-start(bf16[32,1280]{1,0:T(8,128)(2,1)S(1)} %fusion.5), channel_id=1, source_target_pairs={{0,8},{8,0},{16,24},{24,16},{1,9},{9,1},{17,25},{25,17},{2,10},{10... | collective-permute-start | bytes 245768 | tf_op jit(solution)/shard_map/ppermute | solution.py:30
  81.2 2.2 %collective-permute-done.25 = bf16[32,1280]{1,0:T(8,128)(2,1)S(1)} collective-permute-done((bf16[32,1280]{1,0:T(8,128)(2,1)S(1)}, bf16[32,1280]{1,0:T(8,128)(2,1)S(1)}, u32[]{:S(2)}, u32[]{:S(2)}) %collective-permute-start.25) | collective-permute-done | bytes 81952 | tf_op jit(solution)/shard_map/ppermute | solution.py:26
  83.4 3.3 %collective-permute-done.24 = bf16[32,1280]{1,0:T(8,128)(2,1)S(1)} collective-permute-done((bf16[32,1280]{1,0:T(8,128)(2,1)S(1)}, bf16[32,1280]{1,0:T(8,128)(2,1)S(1)}, u32[]{:S(2)}, u32[]{:S(2)}) %collective-permute-start.24) | collective-permute-done | bytes 81952 | tf_op jit(solution)/shard_map/ppermute | solution.py:26
  86.7 0.1 fusion
  86.7 0.6 collective-permute-start.32
  87.3 2.4 %collective-permute-start.30 = (bf16[32,1280]{1,0:T(8,128)(2,1)S(1)}, bf16[32,1280]{1,0:T(8,128)(2,1)S(1)}, u32[]{:S(2)}, u32[]{:S(2)}) collective-permute-start(bf16[32,1280]{1,0:T(8,128)(2,1)S(1)} %get-tuple-element.75), channel_id=1, source_target_pairs={{0,64},{32,96},{64,128},{96,160},{128,192},{160,224},{192,0},{224,... | collective-permute-start | bytes 245768 | tf_op jit(solution)/shard_map/ppermute | solution.py:26
  89.7 1.3 %convert_add_fusion = (f32[160,1280]{1,0:T(8,128)}, f32[1280,160]{0,1:T(8,128)}) fusion(f32[160,1280]{1,0:T(8,128)S(1)} %get-tuple-element.55, bf16[320,1280]{1,0:T(8,128)(2,1)S(1)} %collective-permute-done.33, f32[160,1280]{1,0:T(8,128)S(1)} %get-tuple-element.64), kind=kLoop, calls=%fused_computation.1 | loop fusion | flops 819200 | bytes 4096000 | tf_op jit(solution)/shard_map/add | solution.py:223
  91.0 1.4 %collective-permute-done.32 = bf16[32,1280]{1,0:T(8,128)(2,1)S(1)} collective-permute-done((bf16[32,1280]{1,0:T(8,128)(2,1)S(1)}, bf16[32,1280]{1,0:T(8,128)(2,1)S(1)}, u32[]{:S(2)}, u32[]{:S(2)}) %collective-permute-start.32) | collective-permute-done | bytes 81952 | tf_op jit(solution)/shard_map/ppermute | solution.py:26
  92.4 1.5 %collective-permute-done.30 = bf16[32,1280]{1,0:T(8,128)(2,1)S(1)} collective-permute-done((bf16[32,1280]{1,0:T(8,128)(2,1)S(1)}, bf16[32,1280]{1,0:T(8,128)(2,1)S(1)}, u32[]{:S(2)}, u32[]{:S(2)}) %collective-permute-start.30) | collective-permute-done | bytes 81952 | tf_op jit(solution)/shard_map/ppermute | solution.py:26
  93.9 0.1 fusion.3
  94.0 0.6 fusion.11
  (51 shorter events, 0.5 us)
Async XLA Ops:
  0.6 21.1 %copy-start.2 = (bf16[16,1280]{1,0:T(8,128)(2,1)S(1)}, bf16[16,1280]{1,0:T(8,128)(2,1)}, u32[]{:S(2)}) copy-start(bf16[16,1280]{1,0:T(8,128)(2,1)} %param.4) | copy-start | bytes 122884
  0.6 21.1 %copy-start.3 = (bf16[16,1280]{1,0:T(8,128)(2,1)S(1)}, bf16[16,1280]{1,0:T(8,128)(2,1)}, u32[]{:S(2)}) copy-start(bf16[16,1280]{1,0:T(8,128)(2,1)} %param.7) | copy-start | bytes 122884
  2.3 11.7 %collective-permute-start.5 = (bf16[32,1280]{1,0:T(8,128)(2,1)S(1)}, bf16[32,1280]{1,0:T(8,128)(2,1)S(1)}, u32[]{:S(2)}, u32[]{:S(2)}) collective-permute-start(bf16[32,1280]{1,0:T(8,128)(2,1)S(1)} %constant_dynamic-update-slice_fusion), channel_id=1, source_target_pairs={{0,64},{32,96},{64,128},{96,160},{128,192},{160,224},{192,0},{224,... | collective-permute-start | bytes 245768 | tf_op jit(solution)/shard_map/ppermute | solution.py:26
  5.5 8.4 %collective-permute-start.1 = (bf16[32,1280]{1,0:T(8,128)(2,1)S(1)}, bf16[32,1280]{1,0:T(8,128)(2,1)S(1)}, u32[]{:S(2)}, u32[]{:S(2)}) collective-permute-start(bf16[32,1280]{1,0:T(8,128)(2,1)S(1)} %constant_dynamic-update-slice_fusion), channel_id=1, source_target_pairs={{0,192},{32,224},{64,0},{96,32},{128,64},{160,96},{192,128},{224,1... | collective-permute-start | bytes 245768 | tf_op jit(solution)/shard_map/ppermute | solution.py:26
  8.6 10.4 %collective-permute-start = (bf16[32,1280]{1,0:T(8,128)(2,1)S(1)}, bf16[32,1280]{1,0:T(8,128)(2,1)S(1)}, u32[]{:S(2)}, u32[]{:S(2)}) collective-permute-start(bf16[32,1280]{1,0:T(8,128)(2,1)S(1)} %constant_dynamic-update-slice_fusion), channel_id=1, source_target_pairs={{0,8},{8,0},{16,24},{24,16},{1,9},{9,1},{17,25},{25,17},{2,10},{10... | collective-permute-start | bytes 245768 | tf_op jit(solution)/shard_map/ppermute | solution.py:30
  10.3 25.5 %copy-start = (bf16[1280,160]{0,1:T(8,128)(2,1)S(1)}, bf16[1280,160]{0,1:T(8,128)(2,1)}, u32[]{:S(2)}) copy-start(bf16[1280,160]{0,1:T(8,128)(2,1)} %param.5) | copy-start | bytes 1228804
  10.3 25.5 %copy-start.1 = (bf16[160,1280]{1,0:T(8,128)(2,1)S(1)}, bf16[160,1280]{1,0:T(8,128)(2,1)}, u32[]{:S(2)}) copy-start(bf16[160,1280]{1,0:T(8,128)(2,1)} %refs_9_.1) | copy-start | bytes 1228804
  10.3 23.6 %collective-permute-start.10 = (bf16[320,1280]{1,0:T(8,128)(2,1)S(1)}, bf16[320,1280]{1,0:T(8,128)(2,1)S(1)}, u32[]{:S(2)}, u32[]{:S(2)}) collective-permute-start(bf16[320,1280]{1,0:T(8,128)(2,1)S(1)} %pad_maximum_fusion), channel_id=1, source_target_pairs={{0,24},{24,0},{8,16},{16,8},{1,25},{25,1},{9,17},{17,9},{2,26},{26... | collective-permute-start | bytes 2457608 | tf_op jit(solution)/shard_map/ppermute | solution.py:34
  14.0 16.8 %collective-permute-start.6 = (bf16[64,1280]{1,0:T(8,128)(2,1)S(1)}, bf16[64,1280]{1,0:T(8,128)(2,1)S(1)}, u32[]{:S(2)}, u32[]{:S(2)}) collective-permute-start(bf16[64,1280]{1,0:T(8,128)(2,1)S(1)} %get-tuple-element.85), channel_id=1, source_target_pairs={{0,8},{8,0},{16,24},{24,16},{1,9},{9,1},{17,25},{25,17},{2,10},{10... | collective-permute-start | bytes 491528 | tf_op jit(solution)/shard_map/ppermute | solution.py:30
  14.6 12.9 %collective-permute-start.8 = (bf16[32,1280]{1,0:T(8,128)(2,1)S(1)}, bf16[32,1280]{1,0:T(8,128)(2,1)S(1)}, u32[]{:S(2)}, u32[]{:S(2)}) collective-permute-start(bf16[32,1280]{1,0:T(8,128)(2,1)S(1)} %collective-permute-done.5), channel_id=1, source_target_pairs={{0,64},{32,96},{64,128},{96,160},{128,192},{160,224},{192,0},{224,... | collective-permute-start | bytes 245768 | tf_op jit(solution)/shard_map/ppermute | solution.py:26
  18.5 6.2 %collective-permute-start.7 = (bf16[32,1280]{1,0:T(8,128)(2,1)S(1)}, bf16[32,1280]{1,0:T(8,128)(2,1)S(1)}, u32[]{:S(2)}, u32[]{:S(2)}) collective-permute-start(bf16[32,1280]{1,0:T(8,128)(2,1)S(1)} %collective-permute-done.5), channel_id=1, source_target_pairs={{0,32},{32,64},{64,96},{96,128},{128,160},{160,192},{192,224},{224... | collective-permute-start | bytes 245768 | tf_op jit(solution)/shard_map/ppermute | solution.py:26
  18.9 4.9 %collective-permute-start.2 = (bf16[32,1280]{1,0:T(8,128)(2,1)S(1)}, bf16[32,1280]{1,0:T(8,128)(2,1)S(1)}, u32[]{:S(2)}, u32[]{:S(2)}) collective-permute-start(bf16[32,1280]{1,0:T(8,128)(2,1)S(1)} %collective-permute-done.1), channel_id=1, source_target_pairs={{0,224},{32,0},{64,32},{96,64},{128,96},{160,128},{192,160},{224,1... | collective-permute-start | bytes 245768 | tf_op jit(solution)/shard_map/ppermute | solution.py:26
  23.8 6.9 %collective-permute-start.4 = (bf16[64,1280]{1,0:T(8,128)(2,1)S(1)}, bf16[64,1280]{1,0:T(8,128)(2,1)S(1)}, u32[]{:S(2)}, u32[]{:S(2)}) collective-permute-start(bf16[64,1280]{1,0:T(8,128)(2,1)S(1)} %pad_maximum_fusion.1), channel_id=1, source_target_pairs={{0,32},{32,64},{64,96},{96,128},{128,160},{160,192},{192,224},{224... | collective-permute-start | bytes 491528 | tf_op jit(solution)/shard_map/ppermute | solution.py:26
  24.8 5.6 %collective-permute-start.3 = (bf16[64,1280]{1,0:T(8,128)(2,1)S(1)}, bf16[64,1280]{1,0:T(8,128)(2,1)S(1)}, u32[]{:S(2)}, u32[]{:S(2)}) collective-permute-start(bf16[64,1280]{1,0:T(8,128)(2,1)S(1)} %pad_maximum_fusion.1), channel_id=1, source_target_pairs={{0,224},{32,0},{64,32},{96,64},{128,96},{160,128},{192,160},{224,1... | collective-permute-start | bytes 491528 | tf_op jit(solution)/shard_map/ppermute | solution.py:26
  27.6 6.4 %collective-permute-start.9 = (bf16[96,1280]{1,0:T(8,128)(2,1)S(1)}, bf16[96,1280]{1,0:T(8,128)(2,1)}, u32[]{:S(2)}, u32[]{:S(2)}) collective-permute-start(bf16[96,1280]{1,0:T(8,128)(2,1)S(1)} %constant_dynamic-update-slice_fusion.10.refs_2_), channel_id=1, source_target_pairs={{0,8},{8,0},{16,24},{24,16},{1,9},{9,1},{17,25},{25,17},{2,10},{10... | collective-permute-start | bytes 737288 | tf_op jit(solution)/shard_map/ppermute | solution.py:30
  30.7 3.3 %collective-permute-start.11 = (bf16[192,1280]{1,0:T(8,128)(2,1)S(1)}, bf16[192,1280]{1,0:T(8,128)(2,1)S(1)}, u32[]{:S(2)}, u32[]{:S(2)}) collective-permute-start(bf16[192,1280]{1,0:T(8,128)(2,1)S(1)} %constant_dynamic-update-slice_fusion.2.refs_0_), channel_id=1, source_target_pairs={{0,1},{1,0},{2,3},{3,2},{4,5},{5,4},{6,7},{7,6},{8,9},{9,8},{10,11... | collective-permute-start | bytes 1474568 | tf_op jit(solution)/shard_map/ppermute | solution.py:26
  30.9 3.1 %collective-permute-start.12 = (bf16[128,1280]{1,0:T(8,128)(2,1)S(1)}, bf16[128,1280]{1,0:T(8,128)(2,1)S(1)}, u32[]{:S(2)}, u32[]{:S(2)}) collective-permute-start(bf16[128,1280]{1,0:T(8,128)(2,1)S(1)} %constant_dynamic-update-slice_fusion.7.refs_1_), channel_id=1, source_target_pairs={{0,1},{1,0},{2,3},{3,2},{4,5},{5,4},{6,7},{7,6},{8,9},{9,8},{10,11... | collective-permute-start | bytes 983048 | tf_op jit(solution)/shard_map/ppermute | solution.py:26
  31.4 2.5 %collective-permute-start.13 = (bf16[96,1280]{1,0:T(8,128)(2,1)S(1)}, bf16[96,1280]{1,0:T(8,128)(2,1)}, u32[]{:S(2)}, u32[]{:S(2)}) collective-permute-start(bf16[96,1280]{1,0:T(8,128)(2,1)S(1)} %constant_dynamic-update-slice_fusion.10.refs_2_), channel_id=1, source_target_pairs={{0,1},{1,0},{2,3},{3,2},{4,5},{5,4},{6,7},{7,6},{8,9},{9,8},{10,11... | collective-permute-start | bytes 737288 | tf_op jit(solution)/shard_map/ppermute | solution.py:26
  34.0 1.9 %collective-permute-start.14 = (bf16[96,1280]{1,0:T(8,128)(2,1)}, bf16[96,1280]{1,0:T(8,128)(2,1)}, u32[]{:S(2)}, u32[]{:S(2)}) collective-permute-start(bf16[96,1280]{1,0:T(8,128)(2,1)} %collective-permute-done.9.refs_3_), channel_id=1, source_target_pairs={{0,1},{1,0},{2,3},{3,2},{4,5},{5,4},{6,7},{7,6},{8,9},{9,8},{10,11... | collective-permute-start | bytes 737288 | tf_op jit(solution)/shard_map/ppermute | solution.py:26
  38.6 8.5 %collective-permute-start.15 = (bf16[2,320,128]{2,1,0:T(8,128)(2,1)S(1)}, bf16[2,320,128]{2,1,0:T(8,128)(2,1)S(1)}, u32[]{:S(2)}, u32[]{:S(2)}) collective-permute-start(bf16[2,320,128]{2,1,0:T(8,128)(2,1)S(1)} %get-tuple-element.40), channel_id=1, source_target_pairs={{0,4},{2,6},{4,0},{6,2},{1,5},{3,7},{5,1},{7,3},{8,12},{10,14},{12... | collective-permute-start | bytes 491528 | tf_op jit(solution)/shard_map/ppermute | solution.py:26
  42.5 7.8 %collective-permute-start.16 = (bf16[2,320,128]{2,1,0:T(8,128)(2,1)S(1)}, bf16[2,320,128]{2,1,0:T(8,128)(2,1)S(1)}, u32[]{:S(2)}, u32[]{:S(2)}) collective-permute-start(bf16[2,320,128]{2,1,0:T(8,128)(2,1)S(1)} %get-tuple-element.46), channel_id=1, source_target_pairs={{0,2},{2,4},{4,6},{6,0},{1,3},{3,5},{5,7},{7,1},{8,10},{10,12},{12... | collective-permute-start | bytes 491528 | tf_op jit(solution)/shard_map/ppermute | solution.py:26
  43.4 6.9 %collective-permute-start.17 = (bf16[2,320,128]{2,1,0:T(8,128)(2,1)S(1)}, bf16[2,320,128]{2,1,0:T(8,128)(2,1)S(1)}, u32[]{:S(2)}, u32[]{:S(2)}) collective-permute-start(bf16[2,320,128]{2,1,0:T(8,128)(2,1)S(1)} %get-tuple-element.47), channel_id=1, source_target_pairs={{0,6},{2,0},{4,2},{6,4},{1,7},{3,1},{5,3},{7,5},{8,14},{10,8},{12,... | collective-permute-start | bytes 491528 | tf_op jit(solution)/shard_map/ppermute | solution.py:26
  50.5 7.3 %collective-permute-start.20 = (bf16[2,320,128]{2,1,0:T(8,128)(2,1)S(1)}, bf16[2,320,128]{2,1,0:T(8,128)(2,1)S(1)}, u32[]{:S(2)}, u32[]{:S(2)}) collective-permute-start(bf16[2,320,128]{2,1,0:T(8,128)(2,1)S(1)} %shard_map.77.c0), channel_id=1, source_target_pairs={{0,2},{2,4},{4,6},{6,0},{1,3},{3,5},{5,7},{7,1},{8,10},{10,12},{12... | collective-permute-start | bytes 491528 | tf_op jit(solution)/shard_map/ppermute | solution.py:26
  51.9 7.1 %collective-permute-start.19 = (bf16[2,320,128]{2,1,0:T(8,128)(2,1)S(1)}, bf16[2,320,128]{2,1,0:T(8,128)(2,1)S(1)}, u32[]{:S(2)}, u32[]{:S(2)}) collective-permute-start(bf16[2,320,128]{2,1,0:T(8,128)(2,1)S(1)} %shard_map.77.c0), channel_id=1, source_target_pairs={{0,6},{2,0},{4,2},{6,4},{1,7},{3,1},{5,3},{7,5},{8,14},{10,8},{12,... | collective-permute-start | bytes 491528 | tf_op jit(solution)/shard_map/ppermute | solution.py:26
  53.8 8.1 %collective-permute-start.18 = (bf16[2,320,128]{2,1,0:T(8,128)(2,1)S(1)}, bf16[2,320,128]{2,1,0:T(8,128)(2,1)S(1)}, u32[]{:S(2)}, u32[]{:S(2)}) collective-permute-start(bf16[2,320,128]{2,1,0:T(8,128)(2,1)S(1)} %shard_map.77.c0), channel_id=1, source_target_pairs={{0,4},{2,6},{4,0},{6,2},{1,5},{3,7},{5,1},{7,3},{8,12},{10,14},{12... | collective-permute-start | bytes 491528 | tf_op jit(solution)/shard_map/ppermute | solution.py:26
  63.5 1.6 %collective-permute-start.21 = (bf16[96,1280]{1,0:T(8,128)(2,1)S(1)}, bf16[96,1280]{1,0:T(8,128)(2,1)S(1)}, u32[]{:S(2)}, u32[]{:S(2)}) collective-permute-start(bf16[96,1280]{1,0:T(8,128)(2,1)S(1)} %get-tuple-element.50), channel_id=1, source_target_pairs={{0,1},{1,0},{2,3},{3,2},{4,5},{5,4},{6,7},{7,6},{8,9},{9,8},{10,11... | collective-permute-start | bytes 737288 | tf_op jit(solution)/shard_map/ppermute | solution.py:26
  65.1 4.6 %collective-permute-start.22 = (bf16[416,1280]{1,0:T(8,128)(2,1)S(1)}, bf16[416,1280]{1,0:T(8,128)(2,1)S(1)}, u32[]{:S(2)}, u32[]{:S(2)}) collective-permute-start(bf16[416,1280]{1,0:T(8,128)(2,1)S(1)} %get-tuple-element.51), channel_id=1, source_target_pairs={{0,1},{1,0},{2,3},{3,2},{4,5},{5,4},{6,7},{7,6},{8,9},{9,8},{10,11... | collective-permute-start | bytes 3194888 | tf_op jit(solution)/shard_map/ppermute | solution.py:26
  65.3 8.9 %collective-permute-start.23 = (bf16[96,1280]{1,0:T(8,128)(2,1)S(1)}, bf16[96,1280]{1,0:T(8,128)(2,1)S(1)}, u32[]{:S(2)}, u32[]{:S(2)}) collective-permute-start(bf16[96,1280]{1,0:T(8,128)(2,1)S(1)} %add_convert_fusion.1), channel_id=1, source_target_pairs={{0,8},{8,0},{16,24},{24,16},{1,9},{9,1},{17,25},{25,17},{2,10},{10... | collective-permute-start | bytes 737288 | tf_op jit(solution)/shard_map/ppermute | solution.py:30
  67.5 22.2 %collective-permute-start.33 = (bf16[320,1280]{1,0:T(8,128)(2,1)S(1)}, bf16[320,1280]{1,0:T(8,128)(2,1)S(1)}, u32[]{:S(2)}, u32[]{:S(2)}) collective-permute-start(bf16[320,1280]{1,0:T(8,128)(2,1)S(1)} %shard_map.80), channel_id=1, source_target_pairs={{0,24},{24,0},{8,16},{16,8},{1,25},{25,1},{9,17},{17,9},{2,26},{26... | collective-permute-start | bytes 2457608 | tf_op jit(solution)/shard_map/ppermute | solution.py:34
  70.1 7.5 %collective-permute-start.27 = (bf16[64,1280]{1,0:T(8,128)(2,1)S(1)}, bf16[64,1280]{1,0:T(8,128)(2,1)S(1)}, u32[]{:S(2)}, u32[]{:S(2)}) collective-permute-start(bf16[64,1280]{1,0:T(8,128)(2,1)S(1)} %pad_maximum_fusion.3), channel_id=1, source_target_pairs={{0,224},{32,0},{64,32},{96,64},{128,96},{160,128},{192,160},{224,1... | collective-permute-start | bytes 491528 | tf_op jit(solution)/shard_map/ppermute | solution.py:26
  72.2 6.9 %collective-permute-start.26 = (bf16[64,1280]{1,0:T(8,128)(2,1)S(1)}, bf16[64,1280]{1,0:T(8,128)(2,1)S(1)}, u32[]{:S(2)}, u32[]{:S(2)}) collective-permute-start(bf16[64,1280]{1,0:T(8,128)(2,1)S(1)} %pad_maximum_fusion.2), channel_id=1, source_target_pairs={{0,32},{32,64},{64,96},{96,128},{128,160},{160,192},{192,224},{224... | collective-permute-start | bytes 491528 | tf_op jit(solution)/shard_map/ppermute | solution.py:26
  72.3 6.9 %collective-permute-start.29 = (bf16[64,1280]{1,0:T(8,128)(2,1)S(1)}, bf16[64,1280]{1,0:T(8,128)(2,1)S(1)}, u32[]{:S(2)}, u32[]{:S(2)}) collective-permute-start(bf16[64,1280]{1,0:T(8,128)(2,1)S(1)} %slice.132), channel_id=1, source_target_pairs={{0,8},{8,0},{16,24},{24,16},{1,9},{9,1},{17,25},{25,17},{2,10},{10... | collective-permute-start | bytes 491528 | tf_op jit(solution)/shard_map/ppermute | solution.py:30
  74.4 6.8 %collective-permute-start.31 = (bf16[32,1280]{1,0:T(8,128)(2,1)S(1)}, bf16[32,1280]{1,0:T(8,128)(2,1)S(1)}, u32[]{:S(2)}, u32[]{:S(2)}) collective-permute-start(bf16[32,1280]{1,0:T(8,128)(2,1)S(1)} %get-tuple-element.80), channel_id=1, source_target_pairs={{0,224},{32,0},{64,32},{96,64},{128,96},{160,128},{192,160},{224,1... | collective-permute-start | bytes 245768 | tf_op jit(solution)/shard_map/ppermute | solution.py:26
  77.6 5.8 %collective-permute-start.25 = (bf16[32,1280]{1,0:T(8,128)(2,1)S(1)}, bf16[32,1280]{1,0:T(8,128)(2,1)S(1)}, u32[]{:S(2)}, u32[]{:S(2)}) collective-permute-start(bf16[32,1280]{1,0:T(8,128)(2,1)S(1)} %get-tuple-element.81), channel_id=1, source_target_pairs={{0,32},{32,64},{64,96},{96,128},{128,160},{160,192},{192,224},{224... | collective-permute-start | bytes 245768 | tf_op jit(solution)/shard_map/ppermute | solution.py:26
  79.2 7.5 %collective-permute-start.24 = (bf16[32,1280]{1,0:T(8,128)(2,1)S(1)}, bf16[32,1280]{1,0:T(8,128)(2,1)S(1)}, u32[]{:S(2)}, u32[]{:S(2)}) collective-permute-start(bf16[32,1280]{1,0:T(8,128)(2,1)S(1)} %get-tuple-element.82), channel_id=1, source_target_pairs={{0,64},{32,96},{64,128},{96,160},{128,192},{160,224},{192,0},{224,... | collective-permute-start | bytes 245768 | tf_op jit(solution)/shard_map/ppermute | solution.py:26
  79.2 11.8 %collective-permute-start.28 = (bf16[32,1280]{1,0:T(8,128)(2,1)S(1)}, bf16[32,1280]{1,0:T(8,128)(2,1)S(1)}, u32[]{:S(2)}, u32[]{:S(2)}) collective-permute-start(bf16[32,1280]{1,0:T(8,128)(2,1)S(1)} %fusion.5), channel_id=1, source_target_pairs={{0,8},{8,0},{16,24},{24,16},{1,9},{9,1},{17,25},{25,17},{2,10},{10... | collective-permute-start | bytes 245768 | tf_op jit(solution)/shard_map/ppermute | solution.py:30
  86.7 5.7 %collective-permute-start.32 = (bf16[32,1280]{1,0:T(8,128)(2,1)S(1)}, bf16[32,1280]{1,0:T(8,128)(2,1)S(1)}, u32[]{:S(2)}, u32[]{:S(2)}) collective-permute-start(bf16[32,1280]{1,0:T(8,128)(2,1)S(1)} %get-tuple-element.74), channel_id=1, source_target_pairs={{0,192},{32,224},{64,0},{96,32},{128,64},{160,96},{192,128},{224,1... | collective-permute-start | bytes 245768 | tf_op jit(solution)/shard_map/ppermute | solution.py:26
  87.3 6.7 %collective-permute-start.30 = (bf16[32,1280]{1,0:T(8,128)(2,1)S(1)}, bf16[32,1280]{1,0:T(8,128)(2,1)S(1)}, u32[]{:S(2)}, u32[]{:S(2)}) collective-permute-start(bf16[32,1280]{1,0:T(8,128)(2,1)S(1)} %get-tuple-element.75), channel_id=1, source_target_pairs={{0,64},{32,96},{64,128},{96,160},{128,192},{160,224},{192,0},{224,... | collective-permute-start | bytes 245768 | tf_op jit(solution)/shard_map/ppermute | solution.py:26

commit v13 on v12

--- a/solution.py
+++ b/solution.py
@@ -151,7 +151,10 @@
     shape = jax.ShapeDtypeStruct
     flops = 2 * 1024 * d * h
 
-    base = cat([tokens, cotangent])
+    top = lax.broadcasted_iota(jnp.int32, (32, d), 0) < 16
+    base = jnp.where(
+        top, jnp.pad(tokens, ((0, 16), (0, 0))), jnp.pad(cotangent, ((16, 0), (0, 0)))
+    )
     z = {2: send(base, "z", -2), 6: send(base, "z", 2)}
     both = cat([base, token_pair(base)])
     w_in_t = w_in.T

time: 96.4 us -> 95.3 us (0.989)
  local copies, waits for them, and re-layouts: 2.47 us -> 0.85 us
where the time goes in v13:
time: 95.3 us; the launch traced here: 94.1 us
  starting transfers between devices  50.3 us (53%)
  waiting for transfers between devices  31.5 us (33%)
  Pallas kernels  6.4 us (7%)
  other arithmetic  4.06 us (4%)
  between operations  0.98 us (1%)
    ppermute x26, starting transfers between devices, send(): lax.ppermute(value, axis, [(i, (i + shift) % size) for i in range(size)])  38.4 us
    ppermute x26, waiting for transfers between devices, send(): lax.ppermute(value, axis, [(i, (i + shift) % size) for i in range(size)])  29.1 us
    ppermute x6, starting transfers between devices, token_pair(): return lax.ppermute(value, 'x', [(0, 1), (1, 0), (2, 3), (3, 2)])  8.16 us
    pallas_call x6, Pallas kernels, call(): return list(kernel(*args))  6.4 us
    ppermute x2, starting transfers between devices, weight_pair(): return lax.ppermute(value, 'x', [(0, 3), (3, 0), (1, 2), (2, 1)])  3.82 us
    ppermute x6, waiting for transfers between devices, token_pair(): return lax.ppermute(value, 'x', [(0, 1), (1, 0), (2, 3), (3, 2)])  2.44 us
  transfers between devices with their start and end apart: 34, of which 17 were waited for; matrix products, arithmetic and copies ran while one was open for 4% of the time, Pallas kernels for 2%

profile of v13, /device:TPU:2, one launch (start us, length us, event | category | flops | bytes accessed | tf_op | source)
XLA Modules:
  0.0 94.1 jit_solution(1661219236475734663)
XLA Ops:
  0.6 0.9 pad_select_fusion
  1.5 3.3 %collective-permute-start.5 = (bf16[32,1280]{1,0:T(8,128)(2,1)S(1)}, bf16[32,1280]{1,0:T(8,128)(2,1)S(1)}, u32[]{:S(2)}, u32[]{:S(2)}) collective-permute-start(bf16[32,1280]{1,0:T(8,128)(2,1)S(1)} %pad_select_fusion), channel_id=1, source_target_pairs={{0,64},{32,96},{64,128},{96,160},{128,192},{160,224},{192,0},{224,... | collective-permute-start | bytes 245768 | tf_op jit(solution)/shard_map/ppermute | solution.py:26
  4.9 3.1 %collective-permute-start.1 = (bf16[32,1280]{1,0:T(8,128)(2,1)S(1)}, bf16[32,1280]{1,0:T(8,128)(2,1)S(1)}, u32[]{:S(2)}, u32[]{:S(2)}) collective-permute-start(bf16[32,1280]{1,0:T(8,128)(2,1)S(1)} %pad_select_fusion), channel_id=1, source_target_pairs={{0,192},{32,224},{64,0},{96,32},{128,64},{160,96},{192,128},{224,1... | collective-permute-start | bytes 245768 | tf_op jit(solution)/shard_map/ppermute | solution.py:26
  8.0 0.5 collective-permute-start
  8.5 1.2 %pad_maximum_fusion = bf16[320,1280]{1,0:T(8,128)(2,1)S(1)} fusion(bf16[160,1280]{1,0:T(8,128)(2,1)} %refs_9_.1, bf16[160,1280]{1,0:T(8,128)(2,1)} %bitcast.4), kind=kLoop, calls=%fused_computation | loop fusion | flops 1638400 | bytes 1638400 | tf_op jit(solution)/shard_map/concatenate | solution.py:59
  9.7 2.2 %collective-permute-start.10 = (bf16[320,1280]{1,0:T(8,128)(2,1)S(1)}, bf16[320,1280]{1,0:T(8,128)(2,1)S(1)}, u32[]{:S(2)}, u32[]{:S(2)}) collective-permute-start(bf16[320,1280]{1,0:T(8,128)(2,1)S(1)} %pad_maximum_fusion), channel_id=1, source_target_pairs={{0,24},{24,0},{8,16},{16,8},{1,25},{25,1},{9,17},{17,9},{2,26},{26... | collective-permute-start | bytes 2457608 | tf_op jit(solution)/shard_map/ppermute | solution.py:34
  12.0 1.3 %collective-permute-done.1 = bf16[32,1280]{1,0:T(8,128)(2,1)S(1)} collective-permute-done((bf16[32,1280]{1,0:T(8,128)(2,1)S(1)}, bf16[32,1280]{1,0:T(8,128)(2,1)S(1)}, u32[]{:S(2)}, u32[]{:S(2)}) %collective-permute-start.1) | collective-permute-done | bytes 81952 | tf_op jit(solution)/shard_map/ppermute | solution.py:26
  13.3 0.6 collective-permute-start.6
  13.9 3.9 %collective-permute-start.8 = (bf16[32,1280]{1,0:T(8,128)(2,1)S(1)}, bf16[32,1280]{1,0:T(8,128)(2,1)S(1)}, u32[]{:S(2)}, u32[]{:S(2)}) collective-permute-start(bf16[32,1280]{1,0:T(8,128)(2,1)S(1)} %collective-permute-done.5), channel_id=1, source_target_pairs={{0,64},{32,96},{64,128},{96,160},{128,192},{160,224},{192,0},{224,... | collective-permute-start | bytes 245768 | tf_op jit(solution)/shard_map/ppermute | solution.py:26
  17.8 0.5 collective-permute-start.7
  18.3 2.8 %collective-permute-start.2 = (bf16[32,1280]{1,0:T(8,128)(2,1)S(1)}, bf16[32,1280]{1,0:T(8,128)(2,1)S(1)}, u32[]{:S(2)}, u32[]{:S(2)}) collective-permute-start(bf16[32,1280]{1,0:T(8,128)(2,1)S(1)} %collective-permute-done.1), channel_id=1, source_target_pairs={{0,224},{32,0},{64,32},{96,64},{128,96},{160,128},{192,160},{224,1... | collective-permute-start | bytes 245768 | tf_op jit(solution)/shard_map/ppermute | solution.py:26
  21.1 2.0 %collective-permute-done.2 = bf16[32,1280]{1,0:T(8,128)(2,1)S(1)} collective-permute-done((bf16[32,1280]{1,0:T(8,128)(2,1)S(1)}, bf16[32,1280]{1,0:T(8,128)(2,1)S(1)}, u32[]{:S(2)}, u32[]{:S(2)}) %collective-permute-start.2) | collective-permute-done | bytes 81952 | tf_op jit(solution)/shard_map/ppermute | solution.py:26
  23.1 1.0 %collective-permute-start.4 = (bf16[64,1280]{1,0:T(8,128)(2,1)S(1)}, bf16[64,1280]{1,0:T(8,128)(2,1)S(1)}, u32[]{:S(2)}, u32[]{:S(2)}) collective-permute-start(bf16[64,1280]{1,0:T(8,128)(2,1)S(1)} %pad_maximum_fusion.1), channel_id=1, source_target_pairs={{0,32},{32,64},{64,96},{96,128},{128,160},{160,192},{192,224},{224... | collective-permute-start | bytes 491528 | tf_op jit(solution)/shard_map/ppermute | solution.py:26
  24.1 2.7 %collective-permute-start.3 = (bf16[64,1280]{1,0:T(8,128)(2,1)S(1)}, bf16[64,1280]{1,0:T(8,128)(2,1)S(1)}, u32[]{:S(2)}, u32[]{:S(2)}) collective-permute-start(bf16[64,1280]{1,0:T(8,128)(2,1)S(1)} %pad_maximum_fusion.1), channel_id=1, source_target_pairs={{0,224},{32,0},{64,32},{96,64},{128,96},{160,128},{192,160},{224,1... | collective-permute-start | bytes 491528 | tf_op jit(solution)/shard_map/ppermute | solution.py:26
  26.8 1.6 %collective-permute-start.9 = (bf16[96,1280]{1,0:T(8,128)(2,1)S(1)}, bf16[96,1280]{1,0:T(8,128)(2,1)}, u32[]{:S(2)}, u32[]{:S(2)}) collective-permute-start(bf16[96,1280]{1,0:T(8,128)(2,1)S(1)} %constant_dynamic-update-slice_fusion.8.refs_2_), channel_id=1, source_target_pairs={{0,8},{8,0},{16,24},{24,16},{1,9},{9,1},{17,25},{25,17},{2,10},{10... | collective-permute-start | bytes 737288 | tf_op jit(solution)/shard_map/ppermute | solution.py:30
  28.4 1.2 %collective-permute-done.3 = bf16[64,1280]{1,0:T(8,128)(2,1)S(1)} collective-permute-done((bf16[64,1280]{1,0:T(8,128)(2,1)S(1)}, bf16[64,1280]{1,0:T(8,128)(2,1)S(1)}, u32[]{:S(2)}, u32[]{:S(2)}) %collective-permute-start.3) | collective-permute-done | bytes 163872 | tf_op jit(solution)/shard_map/ppermute | solution.py:26
  29.7 0.3 collective-permute-done.4
  30.0 0.1 collective-permute-start.11
  30.1 0.6 collective-permute-start.12
  30.7 0.1 collective-permute-start.13
  30.8 2.4 %collective-permute-done.9.refs_3_ = bf16[96,1280]{1,0:T(8,128)(2,1)} collective-permute-done((bf16[96,1280]{1,0:T(8,128)(2,1)S(1)}, bf16[96,1280]{1,0:T(8,128)(2,1)}, u32[]{:S(2)}, u32[]{:S(2)}) %collective-permute-start.9) | collective-permute-done | bytes 245792 | tf_op jit(solution)/shard_map/ppermute | solution.py:30
  33.3 1.8 %collective-permute-done.14.refs_7_ = bf16[96,1280]{1,0:T(8,128)(2,1)} collective-permute-done((bf16[96,1280]{1,0:T(8,128)(2,1)}, bf16[96,1280]{1,0:T(8,128)(2,1)}, u32[]{:S(2)}, u32[]{:S(2)}) %collective-permute-start.14) | collective-permute-done | bytes 245792 | tf_op jit(solution)/shard_map/ppermute | solution.py:26
  35.1 2.8 %shard_map.75 = (bf16[512,1280]{1,0:T(8,128)(2,1)S(1)}, bf16[512,1280]{1,0:T(8,128)(2,1)S(1)}, bf16[2,320,1280]{2,1,0:T(8,128)(2,1)S(1)}, bf16[2,320,128]{2,1,0:...) custom-call(s32[1]{0:T(128)} %bitcast.me, ...), custom_call_target="tpu_custom_call" | custom-call | flops 419430400 | bytes 1048576 | tf_op jit(solution)/shard_map/pallas_call | solution.py:55
  37.9 3.3 %collective-permute-start.15 = (bf16[2,320,128]{2,1,0:T(8,128)(2,1)S(1)}, bf16[2,320,128]{2,1,0:T(8,128)(2,1)S(1)}, u32[]{:S(2)}, u32[]{:S(2)}) collective-permute-start(bf16[2,320,128]{2,1,0:T(8,128)(2,1)S(1)} %get-tuple-element.40), channel_id=1, source_target_pairs={{0,4},{2,6},{4,0},{6,2},{1,5},{3,7},{5,1},{7,3},{8,12},{10,14},{12... | collective-permute-start | bytes 491528 | tf_op jit(solution)/shard_map/ppermute | solution.py:26
  41.2 0.6 shard_map.76.p0
  41.7 0.9 collective-permute-start.16
  42.7 2.6 %collective-permute-start.17 = (bf16[2,320,128]{2,1,0:T(8,128)(2,1)S(1)}, bf16[2,320,128]{2,1,0:T(8,128)(2,1)S(1)}, u32[]{:S(2)}, u32[]{:S(2)}) collective-permute-start(bf16[2,320,128]{2,1,0:T(8,128)(2,1)S(1)} %get-tuple-element.47), channel_id=1, source_target_pairs={{0,6},{2,0},{4,2},{6,4},{1,7},{3,1},{5,3},{7,5},{8,14},{10,8},{12,... | collective-permute-start | bytes 491528 | tf_op jit(solution)/shard_map/ppermute | solution.py:26
  45.2 1.2 %collective-permute-done.15.p1 = bf16[2,320,128]{2,1,0:T(8,128)(2,1)S(1)} collective-permute-done((bf16[2,320,128]{2,1,0:T(8,128)(2,1)S(1)}, bf16[2,320,128]{2,1,0:T(8,128)(2,1)S(1)}, u32[]{:S(2)}, u32[]{:S(2)}) %collective-permute-start.15) | collective-permute-done | bytes 163872 | tf_op jit(solution)/shard_map/ppermute | solution.py:26
  46.4 3.1 %collective-permute-done.16.p2 = bf16[2,320,128]{2,1,0:T(8,128)(2,1)S(1)} collective-permute-done((bf16[2,320,128]{2,1,0:T(8,128)(2,1)S(1)}, bf16[2,320,128]{2,1,0:T(8,128)(2,1)S(1)}, u32[]{:S(2)}, u32[]{:S(2)}) %collective-permute-start.16) | collective-permute-done | bytes 163872 | tf_op jit(solution)/shard_map/ppermute | solution.py:26
  49.6 0.0 collective-permute-done.17.p3
  49.6 0.2 shard_map.77.c0
  49.7 1.5 %collective-permute-start.20 = (bf16[2,320,128]{2,1,0:T(8,128)(2,1)S(1)}, bf16[2,320,128]{2,1,0:T(8,128)(2,1)S(1)}, u32[]{:S(2)}, u32[]{:S(2)}) collective-permute-start(bf16[2,320,128]{2,1,0:T(8,128)(2,1)S(1)} %shard_map.77.c0), channel_id=1, source_target_pairs={{0,2},{2,4},{4,6},{6,0},{1,3},{3,5},{5,7},{7,1},{8,10},{10,12},{12... | collective-permute-start | bytes 491528 | tf_op jit(solution)/shard_map/ppermute | solution.py:26
  51.2 1.8 %collective-permute-start.19 = (bf16[2,320,128]{2,1,0:T(8,128)(2,1)S(1)}, bf16[2,320,128]{2,1,0:T(8,128)(2,1)S(1)}, u32[]{:S(2)}, u32[]{:S(2)}) collective-permute-start(bf16[2,320,128]{2,1,0:T(8,128)(2,1)S(1)} %shard_map.77.c0), channel_id=1, source_target_pairs={{0,6},{2,0},{4,2},{6,4},{1,7},{3,1},{5,3},{7,5},{8,14},{10,8},{12,... | collective-permute-start | bytes 491528 | tf_op jit(solution)/shard_map/ppermute | solution.py:26
  53.0 1.6 %collective-permute-start.18 = (bf16[2,320,128]{2,1,0:T(8,128)(2,1)S(1)}, bf16[2,320,128]{2,1,0:T(8,128)(2,1)S(1)}, u32[]{:S(2)}, u32[]{:S(2)}) collective-permute-start(bf16[2,320,128]{2,1,0:T(8,128)(2,1)S(1)} %shard_map.77.c0), channel_id=1, source_target_pairs={{0,4},{2,6},{4,0},{6,2},{1,5},{3,7},{5,1},{7,3},{8,12},{10,14},{12... | collective-permute-start | bytes 491528 | tf_op jit(solution)/shard_map/ppermute | solution.py:26
  54.7 2.3 %collective-permute-done.20.c3 = bf16[2,320,128]{2,1,0:T(8,128)(2,1)S(1)} collective-permute-done((bf16[2,320,128]{2,1,0:T(8,128)(2,1)S(1)}, bf16[2,320,128]{2,1,0:T(8,128)(2,1)S(1)}, u32[]{:S(2)}, u32[]{:S(2)}) %collective-permute-start.20) | collective-permute-done | bytes 163872 | tf_op jit(solution)/shard_map/ppermute | solution.py:26
  57.0 1.3 %collective-permute-done.19.c1 = bf16[2,320,128]{2,1,0:T(8,128)(2,1)S(1)} collective-permute-done((bf16[2,320,128]{2,1,0:T(8,128)(2,1)S(1)}, bf16[2,320,128]{2,1,0:T(8,128)(2,1)S(1)}, u32[]{:S(2)}, u32[]{:S(2)}) %collective-permute-start.19) | collective-permute-done | bytes 163872 | tf_op jit(solution)/shard_map/ppermute | solution.py:26
  58.3 2.8 %collective-permute-done.18.c2 = bf16[2,320,128]{2,1,0:T(8,128)(2,1)S(1)} collective-permute-done((bf16[2,320,128]{2,1,0:T(8,128)(2,1)S(1)}, bf16[2,320,128]{2,1,0:T(8,128)(2,1)S(1)}, u32[]{:S(2)}, u32[]{:S(2)}) %collective-permute-start.18) | collective-permute-done | bytes 163872 | tf_op jit(solution)/shard_map/ppermute | solution.py:26
  61.1 1.7 %shard_map.78 = (f32[256,1280]{1,0:T(8,128)S(1)}, f32[256,1280]{1,0:T(8,128)S(1)}, bf16[416,1280]{1,0:T(8,128)(2,1)S(1)}, bf16[96,1280]{1,0:T(8,128)(2,1)S(1)}, bf16[2,320,512]{2,1,0:T(8,128)(2,1)S(1)}) custom-call(s32[1]{0:T(128)} %bitcast.me, bf16[2,320,128]{2,1,0:T(8,128)(2,1)S(1)} %shard_map.77.c0, bf16[2,320,128]{2,1,0:T(8,128)(2,1)S(1)} %collective-permute-done.18.c2, ...), custom_call_target="tpu_custom_call" | custom-call | flops 838860800 | bytes 1048576 | tf_op jit(solution)/shard_map/pallas_call | solution.py:55
  62.8 0.1 collective-permute-start.21
  62.9 1.5 %collective-permute-done.21 = bf16[96,1280]{1,0:T(8,128)(2,1)S(1)} collective-permute-done((bf16[96,1280]{1,0:T(8,128)(2,1)S(1)}, bf16[96,1280]{1,0:T(8,128)(2,1)S(1)}, u32[]{:S(2)}, u32[]{:S(2)}) %collective-permute-start.21) | collective-permute-done | bytes 245792 | tf_op jit(solution)/shard_map/ppermute | solution.py:26
  64.4 0.1 collective-permute-start.22
  64.6 1.6 %collective-permute-start.23 = (bf16[96,1280]{1,0:T(8,128)(2,1)S(1)}, bf16[96,1280]{1,0:T(8,128)(2,1)S(1)}, u32[]{:S(2)}, u32[]{:S(2)}) collective-permute-start(bf16[96,1280]{1,0:T(8,128)(2,1)S(1)} %add_convert_fusion.1), channel_id=1, source_target_pairs={{0,8},{8,0},{16,24},{24,16},{1,9},{9,1},{17,25},{25,17},{2,10},{10... | collective-permute-start | bytes 737288 | tf_op jit(solution)/shard_map/ppermute | solution.py:30
  66.2 0.6 shard_map.80
  66.8 1.6 %collective-permute-start.33 = (bf16[320,1280]{1,0:T(8,128)(2,1)S(1)}, bf16[320,1280]{1,0:T(8,128)(2,1)S(1)}, u32[]{:S(2)}, u32[]{:S(2)}) collective-permute-start(bf16[320,1280]{1,0:T(8,128)(2,1)S(1)} %shard_map.80), channel_id=1, source_target_pairs={{0,24},{24,0},{8,16},{16,8},{1,25},{25,1},{9,17},{17,9},{2,26},{26... | collective-permute-start | bytes 2457608 | tf_op jit(solution)/shard_map/ppermute | solution.py:34
  68.3 0.6 shard_map.79
  69.0 0.1 convert_element_type.66
  69.1 0.2 fusion.6
  69.4 2.1 %collective-permute-start.27 = (bf16[64,1280]{1,0:T(8,128)(2,1)S(1)}, bf16[64,1280]{1,0:T(8,128)(2,1)S(1)}, u32[]{:S(2)}, u32[]{:S(2)}) collective-permute-start(bf16[64,1280]{1,0:T(8,128)(2,1)S(1)} %pad_maximum_fusion.3), channel_id=1, source_target_pairs={{0,224},{32,0},{64,32},{96,64},{128,96},{160,128},{192,160},{224,1... | collective-permute-start | bytes 491528 | tf_op jit(solution)/shard_map/ppermute | solution.py:26
  71.5 0.1 collective-permute-start.26
  71.6 1.9 %collective-permute-start.29 = (bf16[64,1280]{1,0:T(8,128)(2,1)S(1)}, bf16[64,1280]{1,0:T(8,128)(2,1)S(1)}, u32[]{:S(2)}, u32[]{:S(2)}) collective-permute-start(bf16[64,1280]{1,0:T(8,128)(2,1)S(1)} %slice.132), channel_id=1, source_target_pairs={{0,8},{8,0},{16,24},{24,16},{1,9},{9,1},{17,25},{25,17},{2,10},{10... | collective-permute-start | bytes 491528 | tf_op jit(solution)/shard_map/ppermute | solution.py:30
  73.5 0.1 add_convert_fusion
  73.6 3.2 %collective-permute-start.31 = (bf16[32,1280]{1,0:T(8,128)(2,1)S(1)}, bf16[32,1280]{1,0:T(8,128)(2,1)S(1)}, u32[]{:S(2)}, u32[]{:S(2)}) collective-permute-start(bf16[32,1280]{1,0:T(8,128)(2,1)S(1)} %get-tuple-element.80), channel_id=1, source_target_pairs={{0,224},{32,0},{64,32},{96,64},{128,96},{160,128},{192,160},{224,1... | collective-permute-start | bytes 245768 | tf_op jit(solution)/shard_map/ppermute | solution.py:26
  76.9 1.5 %collective-permute-done.26 = bf16[64,1280]{1,0:T(8,128)(2,1)S(1)} collective-permute-done((bf16[64,1280]{1,0:T(8,128)(2,1)S(1)}, bf16[64,1280]{1,0:T(8,128)(2,1)S(1)}, u32[]{:S(2)}, u32[]{:S(2)}) %collective-permute-start.26) | collective-permute-done | bytes 163872 | tf_op jit(solution)/shard_map/ppermute | solution.py:26
  78.5 1.9 %collective-permute-start.28 = (bf16[32,1280]{1,0:T(8,128)(2,1)S(1)}, bf16[32,1280]{1,0:T(8,128)(2,1)S(1)}, u32[]{:S(2)}, u32[]{:S(2)}) collective-permute-start(bf16[32,1280]{1,0:T(8,128)(2,1)S(1)} %fusion.5), channel_id=1, source_target_pairs={{0,8},{8,0},{16,24},{24,16},{1,9},{9,1},{17,25},{25,17},{2,10},{10... | collective-permute-start | bytes 245768 | tf_op jit(solution)/shard_map/ppermute | solution.py:30
  80.5 2.1 %collective-permute-done.25 = bf16[32,1280]{1,0:T(8,128)(2,1)S(1)} collective-permute-done((bf16[32,1280]{1,0:T(8,128)(2,1)S(1)}, bf16[32,1280]{1,0:T(8,128)(2,1)S(1)}, u32[]{:S(2)}, u32[]{:S(2)}) %collective-permute-start.25) | collective-permute-done | bytes 81952 | tf_op jit(solution)/shard_map/ppermute | solution.py:26
  82.6 3.4 %collective-permute-done.24 = bf16[32,1280]{1,0:T(8,128)(2,1)S(1)} collective-permute-done((bf16[32,1280]{1,0:T(8,128)(2,1)S(1)}, bf16[32,1280]{1,0:T(8,128)(2,1)S(1)}, u32[]{:S(2)}, u32[]{:S(2)}) %collective-permute-start.24) | collective-permute-done | bytes 81952 | tf_op jit(solution)/shard_map/ppermute | solution.py:26
  86.0 0.1 fusion
  86.1 0.7 collective-permute-start.32
  86.8 2.3 %collective-permute-start.30 = (bf16[32,1280]{1,0:T(8,128)(2,1)S(1)}, bf16[32,1280]{1,0:T(8,128)(2,1)S(1)}, u32[]{:S(2)}, u32[]{:S(2)}) collective-permute-start(bf16[32,1280]{1,0:T(8,128)(2,1)S(1)} %get-tuple-element.75), channel_id=1, source_target_pairs={{0,64},{32,96},{64,128},{96,160},{128,192},{160,224},{192,0},{224,... | collective-permute-start | bytes 245768 | tf_op jit(solution)/shard_map/ppermute | solution.py:26
  89.1 1.3 %convert_add_fusion = (f32[160,1280]{1,0:T(8,128)}, f32[1280,160]{0,1:T(8,128)}) fusion(f32[160,1280]{1,0:T(8,128)S(1)} %get-tuple-element.55, bf16[320,1280]{1,0:T(8,128)(2,1)S(1)} %collective-permute-done.33, f32[160,1280]{1,0:T(8,128)S(1)} %get-tuple-element.64), kind=kLoop, calls=%fused_computation.1 | loop fusion | flops 819200 | bytes 4096000 | tf_op jit(solution)/shard_map/add | solution.py:226
  90.4 1.2 %collective-permute-done.32 = bf16[32,1280]{1,0:T(8,128)(2,1)S(1)} collective-permute-done((bf16[32,1280]{1,0:T(8,128)(2,1)S(1)}, bf16[32,1280]{1,0:T(8,128)(2,1)S(1)}, u32[]{:S(2)}, u32[]{:S(2)}) %collective-permute-start.32) | collective-permute-done | bytes 81952 | tf_op jit(solution)/shard_map/ppermute | solution.py:26
  91.6 1.8 %collective-permute-done.30 = bf16[32,1280]{1,0:T(8,128)(2,1)S(1)} collective-permute-done((bf16[32,1280]{1,0:T(8,128)(2,1)S(1)}, bf16[32,1280]{1,0:T(8,128)(2,1)S(1)}, u32[]{:S(2)}, u32[]{:S(2)}) %collective-permute-start.30) | collective-permute-done | bytes 81952 | tf_op jit(solution)/shard_map/ppermute | solution.py:26
  93.4 0.1 fusion.3
  93.5 0.6 fusion.11
  (47 shorter events, 0.4 us)
Async XLA Ops:
  1.5 11.8 %collective-permute-start.5 = (bf16[32,1280]{1,0:T(8,128)(2,1)S(1)}, bf16[32,1280]{1,0:T(8,128)(2,1)S(1)}, u32[]{:S(2)}, u32[]{:S(2)}) collective-permute-start(bf16[32,1280]{1,0:T(8,128)(2,1)S(1)} %pad_select_fusion), channel_id=1, source_target_pairs={{0,64},{32,96},{64,128},{96,160},{128,192},{160,224},{192,0},{224,... | collective-permute-start | bytes 245768 | tf_op jit(solution)/shard_map/ppermute | solution.py:26
  4.9 8.4 %collective-permute-start.1 = (bf16[32,1280]{1,0:T(8,128)(2,1)S(1)}, bf16[32,1280]{1,0:T(8,128)(2,1)S(1)}, u32[]{:S(2)}, u32[]{:S(2)}) collective-permute-start(bf16[32,1280]{1,0:T(8,128)(2,1)S(1)} %pad_select_fusion), channel_id=1, source_target_pairs={{0,192},{32,224},{64,0},{96,32},{128,64},{160,96},{192,128},{224,1... | collective-permute-start | bytes 245768 | tf_op jit(solution)/shard_map/ppermute | solution.py:26
  8.0 10.3 %collective-permute-start = (bf16[32,1280]{1,0:T(8,128)(2,1)S(1)}, bf16[32,1280]{1,0:T(8,128)(2,1)S(1)}, u32[]{:S(2)}, u32[]{:S(2)}) collective-permute-start(bf16[32,1280]{1,0:T(8,128)(2,1)S(1)} %pad_select_fusion), channel_id=1, source_target_pairs={{0,8},{8,0},{16,24},{24,16},{1,9},{9,1},{17,25},{25,17},{2,10},{10... | collective-permute-start | bytes 245768 | tf_op jit(solution)/shard_map/ppermute | solution.py:30
  9.7 25.4 %copy-start = (bf16[1280,160]{0,1:T(8,128)(2,1)S(1)}, bf16[1280,160]{0,1:T(8,128)(2,1)}, u32[]{:S(2)}) copy-start(bf16[1280,160]{0,1:T(8,128)(2,1)} %param.5) | copy-start | bytes 1228804
  9.7 25.4 %copy-start.1 = (bf16[160,1280]{1,0:T(8,128)(2,1)S(1)}, bf16[160,1280]{1,0:T(8,128)(2,1)}, u32[]{:S(2)}) copy-start(bf16[160,1280]{1,0:T(8,128)(2,1)} %refs_9_.1) | copy-start | bytes 1228804
  9.7 23.5 %collective-permute-start.10 = (bf16[320,1280]{1,0:T(8,128)(2,1)S(1)}, bf16[320,1280]{1,0:T(8,128)(2,1)S(1)}, u32[]{:S(2)}, u32[]{:S(2)}) collective-permute-start(bf16[320,1280]{1,0:T(8,128)(2,1)S(1)} %pad_maximum_fusion), channel_id=1, source_target_pairs={{0,24},{24,0},{8,16},{16,8},{1,25},{25,1},{9,17},{17,9},{2,26},{26... | collective-permute-start | bytes 2457608 | tf_op jit(solution)/shard_map/ppermute | solution.py:34
  13.3 16.8 %collective-permute-start.6 = (bf16[64,1280]{1,0:T(8,128)(2,1)S(1)}, bf16[64,1280]{1,0:T(8,128)(2,1)S(1)}, u32[]{:S(2)}, u32[]{:S(2)}) collective-permute-start(bf16[64,1280]{1,0:T(8,128)(2,1)S(1)} %get-tuple-element.85), channel_id=1, source_target_pairs={{0,8},{8,0},{16,24},{24,16},{1,9},{9,1},{17,25},{25,17},{2,10},{10... | collective-permute-start | bytes 491528 | tf_op jit(solution)/shard_map/ppermute | solution.py:30
  13.9 12.9 %collective-permute-start.8 = (bf16[32,1280]{1,0:T(8,128)(2,1)S(1)}, bf16[32,1280]{1,0:T(8,128)(2,1)S(1)}, u32[]{:S(2)}, u32[]{:S(2)}) collective-permute-start(bf16[32,1280]{1,0:T(8,128)(2,1)S(1)} %collective-permute-done.5), channel_id=1, source_target_pairs={{0,64},{32,96},{64,128},{96,160},{128,192},{160,224},{192,0},{224,... | collective-permute-start | bytes 245768 | tf_op jit(solution)/shard_map/ppermute | solution.py:26
  17.8 6.3 %collective-permute-start.7 = (bf16[32,1280]{1,0:T(8,128)(2,1)S(1)}, bf16[32,1280]{1,0:T(8,128)(2,1)S(1)}, u32[]{:S(2)}, u32[]{:S(2)}) collective-permute-start(bf16[32,1280]{1,0:T(8,128)(2,1)S(1)} %collective-permute-done.5), channel_id=1, source_target_pairs={{0,32},{32,64},{64,96},{96,128},{128,160},{160,192},{192,224},{224... | collective-permute-start | bytes 245768 | tf_op jit(solution)/shard_map/ppermute | solution.py:26
  18.3 4.8 %collective-permute-start.2 = (bf16[32,1280]{1,0:T(8,128)(2,1)S(1)}, bf16[32,1280]{1,0:T(8,128)(2,1)S(1)}, u32[]{:S(2)}, u32[]{:S(2)}) collective-permute-start(bf16[32,1280]{1,0:T(8,128)(2,1)S(1)} %collective-permute-done.1), channel_id=1, source_target_pairs={{0,224},{32,0},{64,32},{96,64},{128,96},{160,128},{192,160},{224,1... | collective-permute-start | bytes 245768 | tf_op jit(solution)/shard_map/ppermute | solution.py:26
  23.1 6.9 %collective-permute-start.4 = (bf16[64,1280]{1,0:T(8,128)(2,1)S(1)}, bf16[64,1280]{1,0:T(8,128)(2,1)S(1)}, u32[]{:S(2)}, u32[]{:S(2)}) collective-permute-start(bf16[64,1280]{1,0:T(8,128)(2,1)S(1)} %pad_maximum_fusion.1), channel_id=1, source_target_pairs={{0,32},{32,64},{64,96},{96,128},{128,160},{160,192},{192,224},{224... | collective-permute-start | bytes 491528 | tf_op jit(solution)/shard_map/ppermute | solution.py:26
  24.1 5.5 %collective-permute-start.3 = (bf16[64,1280]{1,0:T(8,128)(2,1)S(1)}, bf16[64,1280]{1,0:T(8,128)(2,1)S(1)}, u32[]{:S(2)}, u32[]{:S(2)}) collective-permute-start(bf16[64,1280]{1,0:T(8,128)(2,1)S(1)} %pad_maximum_fusion.1), channel_id=1, source_target_pairs={{0,224},{32,0},{64,32},{96,64},{128,96},{160,128},{192,160},{224,1... | collective-permute-start | bytes 491528 | tf_op jit(solution)/shard_map/ppermute | solution.py:26
  26.8 6.4 %collective-permute-start.9 = (bf16[96,1280]{1,0:T(8,128)(2,1)S(1)}, bf16[96,1280]{1,0:T(8,128)(2,1)}, u32[]{:S(2)}, u32[]{:S(2)}) collective-permute-start(bf16[96,1280]{1,0:T(8,128)(2,1)S(1)} %constant_dynamic-update-slice_fusion.8.refs_2_), channel_id=1, source_target_pairs={{0,8},{8,0},{16,24},{24,16},{1,9},{9,1},{17,25},{25,17},{2,10},{10... | collective-permute-start | bytes 737288 | tf_op jit(solution)/shard_map/ppermute | solution.py:30
  30.0 3.3 %collective-permute-start.11 = (bf16[192,1280]{1,0:T(8,128)(2,1)S(1)}, bf16[192,1280]{1,0:T(8,128)(2,1)S(1)}, u32[]{:S(2)}, u32[]{:S(2)}) collective-permute-start(bf16[192,1280]{1,0:T(8,128)(2,1)S(1)} %constant_dynamic-update-slice_fusion.refs_0_), channel_id=1, source_target_pairs={{0,1},{1,0},{2,3},{3,2},{4,5},{5,4},{6,7},{7,6},{8,9},{9,8},{10,11... | collective-permute-start | bytes 1474568 | tf_op jit(solution)/shard_map/ppermute | solution.py:26
  30.1 3.1 %collective-permute-start.12 = (bf16[128,1280]{1,0:T(8,128)(2,1)S(1)}, bf16[128,1280]{1,0:T(8,128)(2,1)S(1)}, u32[]{:S(2)}, u32[]{:S(2)}) collective-permute-start(bf16[128,1280]{1,0:T(8,128)(2,1)S(1)} %constant_dynamic-update-slice_fusion.5.refs_1_), channel_id=1, source_target_pairs={{0,1},{1,0},{2,3},{3,2},{4,5},{5,4},{6,7},{7,6},{8,9},{9,8},{10,11... | collective-permute-start | bytes 983048 | tf_op jit(solution)/shard_map/ppermute | solution.py:26
  30.7 2.5 %collective-permute-start.13 = (bf16[96,1280]{1,0:T(8,128)(2,1)S(1)}, bf16[96,1280]{1,0:T(8,128)(2,1)}, u32[]{:S(2)}, u32[]{:S(2)}) collective-permute-start(bf16[96,1280]{1,0:T(8,128)(2,1)S(1)} %constant_dynamic-update-slice_fusion.8.refs_2_), channel_id=1, source_target_pairs={{0,1},{1,0},{2,3},{3,2},{4,5},{5,4},{6,7},{7,6},{8,9},{9,8},{10,11... | collective-permute-start | bytes 737288 | tf_op jit(solution)/shard_map/ppermute | solution.py:26
  33.2 1.9 %collective-permute-start.14 = (bf16[96,1280]{1,0:T(8,128)(2,1)}, bf16[96,1280]{1,0:T(8,128)(2,1)}, u32[]{:S(2)}, u32[]{:S(2)}) collective-permute-start(bf16[96,1280]{1,0:T(8,128)(2,1)} %collective-permute-done.9.refs_3_), channel_id=1, source_target_pairs={{0,1},{1,0},{2,3},{3,2},{4,5},{5,4},{6,7},{7,6},{8,9},{9,8},{10,11... | collective-permute-start | bytes 737288 | tf_op jit(solution)/shard_map/ppermute | solution.py:26
  37.9 8.5 %collective-permute-start.15 = (bf16[2,320,128]{2,1,0:T(8,128)(2,1)S(1)}, bf16[2,320,128]{2,1,0:T(8,128)(2,1)S(1)}, u32[]{:S(2)}, u32[]{:S(2)}) collective-permute-start(bf16[2,320,128]{2,1,0:T(8,128)(2,1)S(1)} %get-tuple-element.40), channel_id=1, source_target_pairs={{0,4},{2,6},{4,0},{6,2},{1,5},{3,7},{5,1},{7,3},{8,12},{10,14},{12... | collective-permute-start | bytes 491528 | tf_op jit(solution)/shard_map/ppermute | solution.py:26
  41.7 7.8 %collective-permute-start.16 = (bf16[2,320,128]{2,1,0:T(8,128)(2,1)S(1)}, bf16[2,320,128]{2,1,0:T(8,128)(2,1)S(1)}, u32[]{:S(2)}, u32[]{:S(2)}) collective-permute-start(bf16[2,320,128]{2,1,0:T(8,128)(2,1)S(1)} %get-tuple-element.46), channel_id=1, source_target_pairs={{0,2},{2,4},{4,6},{6,0},{1,3},{3,5},{5,7},{7,1},{8,10},{10,12},{12... | collective-permute-start | bytes 491528 | tf_op jit(solution)/shard_map/ppermute | solution.py:26
  42.7 6.9 %collective-permute-start.17 = (bf16[2,320,128]{2,1,0:T(8,128)(2,1)S(1)}, bf16[2,320,128]{2,1,0:T(8,128)(2,1)S(1)}, u32[]{:S(2)}, u32[]{:S(2)}) collective-permute-start(bf16[2,320,128]{2,1,0:T(8,128)(2,1)S(1)} %get-tuple-element.47), channel_id=1, source_target_pairs={{0,6},{2,0},{4,2},{6,4},{1,7},{3,1},{5,3},{7,5},{8,14},{10,8},{12,... | collective-permute-start | bytes 491528 | tf_op jit(solution)/shard_map/ppermute | solution.py:26
  49.7 7.3 %collective-permute-start.20 = (bf16[2,320,128]{2,1,0:T(8,128)(2,1)S(1)}, bf16[2,320,128]{2,1,0:T(8,128)(2,1)S(1)}, u32[]{:S(2)}, u32[]{:S(2)}) collective-permute-start(bf16[2,320,128]{2,1,0:T(8,128)(2,1)S(1)} %shard_map.77.c0), channel_id=1, source_target_pairs={{0,2},{2,4},{4,6},{6,0},{1,3},{3,5},{5,7},{7,1},{8,10},{10,12},{12... | collective-permute-start | bytes 491528 | tf_op jit(solution)/shard_map/ppermute | solution.py:26
  51.2 7.1 %collective-permute-start.19 = (bf16[2,320,128]{2,1,0:T(8,128)(2,1)S(1)}, bf16[2,320,128]{2,1,0:T(8,128)(2,1)S(1)}, u32[]{:S(2)}, u32[]{:S(2)}) collective-permute-start(bf16[2,320,128]{2,1,0:T(8,128)(2,1)S(1)} %shard_map.77.c0), channel_id=1, source_target_pairs={{0,6},{2,0},{4,2},{6,4},{1,7},{3,1},{5,3},{7,5},{8,14},{10,8},{12,... | collective-permute-start | bytes 491528 | tf_op jit(solution)/shard_map/ppermute | solution.py:26
  53.0 8.1 %collective-permute-start.18 = (bf16[2,320,128]{2,1,0:T(8,128)(2,1)S(1)}, bf16[2,320,128]{2,1,0:T(8,128)(2,1)S(1)}, u32[]{:S(2)}, u32[]{:S(2)}) collective-permute-start(bf16[2,320,128]{2,1,0:T(8,128)(2,1)S(1)} %shard_map.77.c0), channel_id=1, source_target_pairs={{0,4},{2,6},{4,0},{6,2},{1,5},{3,7},{5,1},{7,3},{8,12},{10,14},{12... | collective-permute-start | bytes 491528 | tf_op jit(solution)/shard_map/ppermute | solution.py:26
  62.8 1.6 %collective-permute-start.21 = (bf16[96,1280]{1,0:T(8,128)(2,1)S(1)}, bf16[96,1280]{1,0:T(8,128)(2,1)S(1)}, u32[]{:S(2)}, u32[]{:S(2)}) collective-permute-start(bf16[96,1280]{1,0:T(8,128)(2,1)S(1)} %get-tuple-element.50), channel_id=1, source_target_pairs={{0,1},{1,0},{2,3},{3,2},{4,5},{5,4},{6,7},{7,6},{8,9},{9,8},{10,11... | collective-permute-start | bytes 737288 | tf_op jit(solution)/shard_map/ppermute | solution.py:26
  64.4 4.6 %collective-permute-start.22 = (bf16[416,1280]{1,0:T(8,128)(2,1)S(1)}, bf16[416,1280]{1,0:T(8,128)(2,1)S(1)}, u32[]{:S(2)}, u32[]{:S(2)}) collective-permute-start(bf16[416,1280]{1,0:T(8,128)(2,1)S(1)} %get-tuple-element.51), channel_id=1, source_target_pairs={{0,1},{1,0},{2,3},{3,2},{4,5},{5,4},{6,7},{7,6},{8,9},{9,8},{10,11... | collective-permute-start | bytes 3194888 | tf_op jit(solution)/shard_map/ppermute | solution.py:26
  64.6 8.9 %collective-permute-start.23 = (bf16[96,1280]{1,0:T(8,128)(2,1)S(1)}, bf16[96,1280]{1,0:T(8,128)(2,1)S(1)}, u32[]{:S(2)}, u32[]{:S(2)}) collective-permute-start(bf16[96,1280]{1,0:T(8,128)(2,1)S(1)} %add_convert_fusion.1), channel_id=1, source_target_pairs={{0,8},{8,0},{16,24},{24,16},{1,9},{9,1},{17,25},{25,17},{2,10},{10... | collective-permute-start | bytes 737288 | tf_op jit(solution)/shard_map/ppermute | solution.py:30
  66.8 22.3 %collective-permute-start.33 = (bf16[320,1280]{1,0:T(8,128)(2,1)S(1)}, bf16[320,1280]{1,0:T(8,128)(2,1)S(1)}, u32[]{:S(2)}, u32[]{:S(2)}) collective-permute-start(bf16[320,1280]{1,0:T(8,128)(2,1)S(1)} %shard_map.80), channel_id=1, source_target_pairs={{0,24},{24,0},{8,16},{16,8},{1,25},{25,1},{9,17},{17,9},{2,26},{26... | collective-permute-start | bytes 2457608 | tf_op jit(solution)/shard_map/ppermute | solution.py:34
  69.4 7.5 %collective-permute-start.27 = (bf16[64,1280]{1,0:T(8,128)(2,1)S(1)}, bf16[64,1280]{1,0:T(8,128)(2,1)S(1)}, u32[]{:S(2)}, u32[]{:S(2)}) collective-permute-start(bf16[64,1280]{1,0:T(8,128)(2,1)S(1)} %pad_maximum_fusion.3), channel_id=1, source_target_pairs={{0,224},{32,0},{64,32},{96,64},{128,96},{160,128},{192,160},{224,1... | collective-permute-start | bytes 491528 | tf_op jit(solution)/shard_map/ppermute | solution.py:26
  71.5 6.9 %collective-permute-start.26 = (bf16[64,1280]{1,0:T(8,128)(2,1)S(1)}, bf16[64,1280]{1,0:T(8,128)(2,1)S(1)}, u32[]{:S(2)}, u32[]{:S(2)}) collective-permute-start(bf16[64,1280]{1,0:T(8,128)(2,1)S(1)} %pad_maximum_fusion.2), channel_id=1, source_target_pairs={{0,32},{32,64},{64,96},{96,128},{128,160},{160,192},{192,224},{224... | collective-permute-start | bytes 491528 | tf_op jit(solution)/shard_map/ppermute | solution.py:26
  71.6 6.9 %collective-permute-start.29 = (bf16[64,1280]{1,0:T(8,128)(2,1)S(1)}, bf16[64,1280]{1,0:T(8,128)(2,1)S(1)}, u32[]{:S(2)}, u32[]{:S(2)}) collective-permute-start(bf16[64,1280]{1,0:T(8,128)(2,1)S(1)} %slice.132), channel_id=1, source_target_pairs={{0,8},{8,0},{16,24},{24,16},{1,9},{9,1},{17,25},{25,17},{2,10},{10... | collective-permute-start | bytes 491528 | tf_op jit(solution)/shard_map/ppermute | solution.py:30
  73.6 6.8 %collective-permute-start.31 = (bf16[32,1280]{1,0:T(8,128)(2,1)S(1)}, bf16[32,1280]{1,0:T(8,128)(2,1)S(1)}, u32[]{:S(2)}, u32[]{:S(2)}) collective-permute-start(bf16[32,1280]{1,0:T(8,128)(2,1)S(1)} %get-tuple-element.80), channel_id=1, source_target_pairs={{0,224},{32,0},{64,32},{96,64},{128,96},{160,128},{192,160},{224,1... | collective-permute-start | bytes 245768 | tf_op jit(solution)/shard_map/ppermute | solution.py:26
  76.9 5.7 %collective-permute-start.25 = (bf16[32,1280]{1,0:T(8,128)(2,1)S(1)}, bf16[32,1280]{1,0:T(8,128)(2,1)S(1)}, u32[]{:S(2)}, u32[]{:S(2)}) collective-permute-start(bf16[32,1280]{1,0:T(8,128)(2,1)S(1)} %get-tuple-element.81), channel_id=1, source_target_pairs={{0,32},{32,64},{64,96},{96,128},{128,160},{160,192},{192,224},{224... | collective-permute-start | bytes 245768 | tf_op jit(solution)/shard_map/ppermute | solution.py:26
  78.4 7.6 %collective-permute-start.24 = (bf16[32,1280]{1,0:T(8,128)(2,1)S(1)}, bf16[32,1280]{1,0:T(8,128)(2,1)S(1)}, u32[]{:S(2)}, u32[]{:S(2)}) collective-permute-start(bf16[32,1280]{1,0:T(8,128)(2,1)S(1)} %get-tuple-element.82), channel_id=1, source_target_pairs={{0,64},{32,96},{64,128},{96,160},{128,192},{160,224},{192,0},{224,... | collective-permute-start | bytes 245768 | tf_op jit(solution)/shard_map/ppermute | solution.py:26
  78.5 11.9 %collective-permute-start.28 = (bf16[32,1280]{1,0:T(8,128)(2,1)S(1)}, bf16[32,1280]{1,0:T(8,128)(2,1)S(1)}, u32[]{:S(2)}, u32[]{:S(2)}) collective-permute-start(bf16[32,1280]{1,0:T(8,128)(2,1)S(1)} %fusion.5), channel_id=1, source_target_pairs={{0,8},{8,0},{16,24},{24,16},{1,9},{9,1},{17,25},{25,17},{2,10},{10... | collective-permute-start | bytes 245768 | tf_op jit(solution)/shard_map/ppermute | solution.py:30
  86.1 5.5 %collective-permute-start.32 = (bf16[32,1280]{1,0:T(8,128)(2,1)S(1)}, bf16[32,1280]{1,0:T(8,128)(2,1)S(1)}, u32[]{:S(2)}, u32[]{:S(2)}) collective-permute-start(bf16[32,1280]{1,0:T(8,128)(2,1)S(1)} %get-tuple-element.74), channel_id=1, source_target_pairs={{0,192},{32,224},{64,0},{96,32},{128,64},{160,96},{192,128},{224,1... | collective-permute-start | bytes 245768 | tf_op jit(solution)/shard_map/ppermute | solution.py:26
  86.8 6.7 %collective-permute-start.30 = (bf16[32,1280]{1,0:T(8,128)(2,1)S(1)}, bf16[32,1280]{1,0:T(8,128)(2,1)S(1)}, u32[]{:S(2)}, u32[]{:S(2)}) collective-permute-start(bf16[32,1280]{1,0:T(8,128)(2,1)S(1)} %get-tuple-element.75), channel_id=1, source_target_pairs={{0,64},{32,96},{64,128},{96,160},{128,192},{160,224},{192,0},{224,... | collective-permute-start | bytes 245768 | tf_op jit(solution)/shard_map/ppermute | solution.py:26

commit v14 on v8

--- a/solution.py
+++ b/solution.py
@@ -151,7 +151,10 @@
     shape = jax.ShapeDtypeStruct
     flops = 2 * 1024 * d * h
 
-    base = cat([tokens, cotangent])
+    top = lax.broadcasted_iota(jnp.int32, (32, d), 0) < 16
+    base = jnp.where(
+        top, jnp.pad(tokens, ((0, 16), (0, 0))), jnp.pad(cotangent, ((16, 0), (0, 0)))
+    )
     z = {2: send(base, "z", -2), 6: send(base, "z", 2)}
     both = cat([base, token_pair(base)])
     w_in_t = w_in.T

time: 94.4 us -> 93.6 us (level)
  local copies, waits for them, and re-layouts: 2.47 us -> 0.84 us
where the time goes in v14:
time: 93.6 us; the launch traced here: 93.4 us
  starting transfers between devices  47.1 us (50%)
  waiting for transfers between devices  34.1 us (36%)
  Pallas kernels  6.3 us (7%)
  other arithmetic  4.11 us (4%)
  between operations  0.99 us (1%)
    ppermute x26, starting transfers between devices, send(): lax.ppermute(value, axis, [(i, (i + shift) % size) for i in range(size)])  35.8 us
    ppermute x26, waiting for transfers between devices, send(): lax.ppermute(value, axis, [(i, (i + shift) % size) for i in range(size)])  29.6 us
    ppermute x6, starting transfers between devices, token_pair(): return lax.ppermute(value, 'x', [(0, 1), (1, 0), (2, 3), (3, 2)])  7.62 us
    pallas_call x6, Pallas kernels, call(): return list(kernel(*args))  6.3 us
    ppermute x6, waiting for transfers between devices, token_pair(): return lax.ppermute(value, 'x', [(0, 1), (1, 0), (2, 3), (3, 2)])  4.46 us
    ppermute x2, starting transfers between devices, weight_pair(): return lax.ppermute(value, 'x', [(0, 3), (3, 0), (1, 2), (2, 1)])  3.72 us
  transfers between devices with their start and end apart: 34, of which 17 were waited for; matrix products, arithmetic and copies ran while one was open for 4% of the time, Pallas kernels for 1%

profile of v14, /device:TPU:2, one launch (start us, length us, event | category | flops | bytes accessed | tf_op | source)
XLA Modules:
  0.0 93.4 jit_solution(1174892699971004021)
XLA Ops:
  0.6 0.9 pad_select_fusion
  1.5 6.4 %collective-permute-start.1 = (bf16[32,1280]{1,0:T(8,128)(2,1)S(1)}, bf16[32,1280]{1,0:T(8,128)(2,1)S(1)}, u32[]{:S(2)}, u32[]{:S(2)}) collective-permute-start(bf16[32,1280]{1,0:T(8,128)(2,1)S(1)} %pad_select_fusion), channel_id=1, source_target_pairs={{0,192},{32,224},{64,0},{96,32},{128,64},{160,96},{192,128},{224,1... | collective-permute-start | bytes 245768 | tf_op jit(solution)/shard_map/ppermute | solution.py:26
  7.9 0.5 collective-permute-start
  8.4 1.2 %pad_maximum_fusion = bf16[320,1280]{1,0:T(8,128)(2,1)S(1)} fusion(bf16[160,1280]{1,0:T(8,128)(2,1)} %wo.3, bf16[160,1280]{1,0:T(8,128)(2,1)} %bitcast.4), kind=kLoop, calls=%fused_computation | loop fusion | flops 1638400 | bytes 1638400 | tf_op jit(solution)/shard_map/concatenate | solution.py:59
  9.6 2.2 %collective-permute-start.10 = (bf16[320,1280]{1,0:T(8,128)(2,1)S(1)}, bf16[320,1280]{1,0:T(8,128)(2,1)S(1)}, u32[]{:S(2)}, u32[]{:S(2)}) collective-permute-start(bf16[320,1280]{1,0:T(8,128)(2,1)S(1)} %pad_maximum_fusion), channel_id=1, source_target_pairs={{0,24},{24,0},{8,16},{16,8},{1,25},{25,1},{9,17},{17,9},{2,26},{26... | collective-permute-start | bytes 2457608 | tf_op jit(solution)/shard_map/ppermute | solution.py:34
  11.9 3.2 %collective-permute-done.5 = bf16[32,1280]{1,0:T(8,128)(2,1)S(1)} collective-permute-done((bf16[32,1280]{1,0:T(8,128)(2,1)S(1)}, bf16[32,1280]{1,0:T(8,128)(2,1)S(1)}, u32[]{:S(2)}, u32[]{:S(2)}) %collective-permute-start.5) | collective-permute-done | bytes 81952 | tf_op jit(solution)/shard_map/ppermute | solution.py:26
  15.1 0.6 collective-permute-start.6
  15.8 4.2 %collective-permute-start.2 = (bf16[32,1280]{1,0:T(8,128)(2,1)S(1)}, bf16[32,1280]{1,0:T(8,128)(2,1)S(1)}, u32[]{:S(2)}, u32[]{:S(2)}) collective-permute-start(bf16[32,1280]{1,0:T(8,128)(2,1)S(1)} %collective-permute-done.1), channel_id=1, source_target_pairs={{0,224},{32,0},{64,32},{96,64},{128,96},{160,128},{192,160},{224,1... | collective-permute-start | bytes 245768 | tf_op jit(solution)/shard_map/ppermute | solution.py:26
  20.0 2.0 %collective-permute-done.2 = bf16[32,1280]{1,0:T(8,128)(2,1)S(1)} collective-permute-done((bf16[32,1280]{1,0:T(8,128)(2,1)S(1)}, bf16[32,1280]{1,0:T(8,128)(2,1)S(1)}, u32[]{:S(2)}, u32[]{:S(2)}) %collective-permute-start.2) | collective-permute-done | bytes 81952 | tf_op jit(solution)/shard_map/ppermute | solution.py:26
  22.1 3.7 %collective-permute-start.3 = (bf16[64,1280]{1,0:T(8,128)(2,1)S(1)}, bf16[64,1280]{1,0:T(8,128)(2,1)S(1)}, u32[]{:S(2)}, u32[]{:S(2)}) collective-permute-start(bf16[64,1280]{1,0:T(8,128)(2,1)S(1)} %pad_maximum_fusion.1), channel_id=1, source_target_pairs={{0,224},{32,0},{64,32},{96,64},{128,96},{160,128},{192,160},{224,1... | collective-permute-start | bytes 491528 | tf_op jit(solution)/shard_map/ppermute | solution.py:26
  25.8 0.1 collective-permute-start.4
  25.9 1.6 %collective-permute-start.9 = (bf16[96,1280]{1,0:T(8,128)(2,1)S(1)}, bf16[96,1280]{1,0:T(8,128)(2,1)}, u32[]{:S(2)}, u32[]{:S(2)}) collective-permute-start(bf16[96,1280]{1,0:T(8,128)(2,1)S(1)} %constant_dynamic-update-slice_fusion.8.refs_2_), channel_id=1, source_target_pairs={{0,8},{8,0},{16,24},{24,16},{1,9},{9,1},{17,25},{25,17},{2,10},{10... | collective-permute-start | bytes 737288 | tf_op jit(solution)/shard_map/ppermute | solution.py:30
  27.5 1.1 %collective-permute-done.3 = bf16[64,1280]{1,0:T(8,128)(2,1)S(1)} collective-permute-done((bf16[64,1280]{1,0:T(8,128)(2,1)S(1)}, bf16[64,1280]{1,0:T(8,128)(2,1)S(1)}, u32[]{:S(2)}, u32[]{:S(2)}) %collective-permute-start.3) | collective-permute-done | bytes 163872 | tf_op jit(solution)/shard_map/ppermute | solution.py:26
  28.6 3.8 %collective-permute-done.4 = bf16[64,1280]{1,0:T(8,128)(2,1)S(1)} collective-permute-done((bf16[64,1280]{1,0:T(8,128)(2,1)S(1)}, bf16[64,1280]{1,0:T(8,128)(2,1)S(1)}, u32[]{:S(2)}, u32[]{:S(2)}) %collective-permute-start.4) | collective-permute-done | bytes 163872 | tf_op jit(solution)/shard_map/ppermute | solution.py:26
  32.4 0.1 collective-permute-start.11
  32.5 0.6 collective-permute-start.12
  33.1 0.1 collective-permute-start.13
  33.2 0.4 collective-permute-start.14
  33.6 1.7 %collective-permute-done.13.refs_6_ = bf16[96,1280]{1,0:T(8,128)(2,1)} collective-permute-done((bf16[96,1280]{1,0:T(8,128)(2,1)S(1)}, bf16[96,1280]{1,0:T(8,128)(2,1)}, u32[]{:S(2)}, u32[]{:S(2)}) %collective-permute-start.13) | collective-permute-done | bytes 245792 | tf_op jit(solution)/shard_map/ppermute | solution.py:26
  35.3 0.6 collective-permute-done.14.refs_7_
  35.9 2.7 %shard_map.75 = (bf16[512,1280]{1,0:T(8,128)(2,1)S(1)}, bf16[512,1280]{1,0:T(8,128)(2,1)S(1)}, bf16[2,320,128]{2,1,0:T(8,128)(2,1)S(1)}, bf16[2,320,128]{2,1,0:T(8,128)(2,1)S(1)}, bf16[2,320,128]{2,1,0:T(8,128)(2,1)S(1)}) custom-call(s32[1]{0:T(128)} %bitcast.me, bf16[192,1280]{1,0:T(8,128)(2,1)S(1)} %constant_dynamic-update-slice_fusion.refs_0_, ...), custom_call_target="tpu_custom_call" | custom-call | flops 419430400 | bytes 1048576 | tf_op jit(solution)/shard_map/pallas_call | solution.py:55
  38.6 3.3 %collective-permute-start.15 = (bf16[2,320,128]{2,1,0:T(8,128)(2,1)S(1)}, bf16[2,320,128]{2,1,0:T(8,128)(2,1)S(1)}, u32[]{:S(2)}, u32[]{:S(2)}) collective-permute-start(bf16[2,320,128]{2,1,0:T(8,128)(2,1)S(1)} %get-tuple-element.36), channel_id=1, source_target_pairs={{0,4},{2,6},{4,0},{6,2},{1,5},{3,7},{5,1},{7,3},{8,12},{10,14},{12... | collective-permute-start | bytes 491528 | tf_op jit(solution)/shard_map/ppermute | solution.py:26
  41.9 0.7 collective-permute-start.16
  42.5 2.6 %collective-permute-start.17 = (bf16[2,320,128]{2,1,0:T(8,128)(2,1)S(1)}, bf16[2,320,128]{2,1,0:T(8,128)(2,1)S(1)}, u32[]{:S(2)}, u32[]{:S(2)}) collective-permute-start(bf16[2,320,128]{2,1,0:T(8,128)(2,1)S(1)} %get-tuple-element.40), channel_id=1, source_target_pairs={{0,6},{2,0},{4,2},{6,4},{1,7},{3,1},{5,3},{7,5},{8,14},{10,8},{12,... | collective-permute-start | bytes 491528 | tf_op jit(solution)/shard_map/ppermute | solution.py:26
  45.1 0.6 shard_map.76.p0
  45.7 1.5 %collective-permute-done.15.p1 = bf16[2,320,128]{2,1,0:T(8,128)(2,1)S(1)} collective-permute-done((bf16[2,320,128]{2,1,0:T(8,128)(2,1)S(1)}, bf16[2,320,128]{2,1,0:T(8,128)(2,1)S(1)}, u32[]{:S(2)}, u32[]{:S(2)}) %collective-permute-start.15) | collective-permute-done | bytes 163872 | tf_op jit(solution)/shard_map/ppermute | solution.py:26
  47.2 2.7 %collective-permute-done.16.p2 = bf16[2,320,128]{2,1,0:T(8,128)(2,1)S(1)} collective-permute-done((bf16[2,320,128]{2,1,0:T(8,128)(2,1)S(1)}, bf16[2,320,128]{2,1,0:T(8,128)(2,1)S(1)}, u32[]{:S(2)}, u32[]{:S(2)}) %collective-permute-start.16) | collective-permute-done | bytes 163872 | tf_op jit(solution)/shard_map/ppermute | solution.py:26
  49.9 0.3 collective-permute-done.17.p3
  50.2 0.2 shard_map.77.b0
  50.4 2.2 %collective-permute-start.18 = (bf16[2,320,128]{2,1,0:T(8,128)(2,1)S(1)}, bf16[2,320,128]{2,1,0:T(8,128)(2,1)S(1)}, u32[]{:S(2)}, u32[]{:S(2)}) collective-permute-start(bf16[2,320,128]{2,1,0:T(8,128)(2,1)S(1)} %shard_map.77.b0), channel_id=1, source_target_pairs={{0,4},{2,6},{4,0},{6,2},{1,5},{3,7},{5,1},{7,3},{8,12},{10,14},{12... | collective-permute-start | bytes 491528 | tf_op jit(solution)/shard_map/ppermute | solution.py:26
  52.6 2.0 %collective-permute-start.19 = (bf16[2,320,128]{2,1,0:T(8,128)(2,1)S(1)}, bf16[2,320,128]{2,1,0:T(8,128)(2,1)S(1)}, u32[]{:S(2)}, u32[]{:S(2)}) collective-permute-start(bf16[2,320,128]{2,1,0:T(8,128)(2,1)S(1)} %shard_map.77.b0), channel_id=1, source_target_pairs={{0,6},{2,0},{4,2},{6,4},{1,7},{3,1},{5,3},{7,5},{8,14},{10,8},{12,... | collective-permute-start | bytes 491528 | tf_op jit(solution)/shard_map/ppermute | solution.py:26
  54.6 4.0 %collective-permute-done.18.b2 = bf16[2,320,128]{2,1,0:T(8,128)(2,1)S(1)} collective-permute-done((bf16[2,320,128]{2,1,0:T(8,128)(2,1)S(1)}, bf16[2,320,128]{2,1,0:T(8,128)(2,1)S(1)}, u32[]{:S(2)}, u32[]{:S(2)}) %collective-permute-start.18) | collective-permute-done | bytes 163872 | tf_op jit(solution)/shard_map/ppermute | solution.py:26
  58.6 2.4 %collective-permute-done.19.b1 = bf16[2,320,128]{2,1,0:T(8,128)(2,1)S(1)} collective-permute-done((bf16[2,320,128]{2,1,0:T(8,128)(2,1)S(1)}, bf16[2,320,128]{2,1,0:T(8,128)(2,1)S(1)}, u32[]{:S(2)}, u32[]{:S(2)}) %collective-permute-start.19) | collective-permute-done | bytes 163872 | tf_op jit(solution)/shard_map/ppermute | solution.py:26
  61.0 0.6 collective-permute-done.20.b3
  61.7 0.7 shard_map.78
  62.4 1.6 %shard_map.79 = (f32[256,1280]{1,0:T(8,128)S(1)}, f32[256,1280]{1,0:T(8,128)S(1)}, bf16[320,1280]{1,0:T(8,128)(2,1)S(1)}, bf16[192,1280]{1,0:T(8,128)(2,1)S(1)}) custom-call(s32[1]{0:T(128)} %bitcast.me, bf16[2,320,512]{2,1,0:T(8,128)(2,1)S(1)} %get-tuple-element.41.full, bf16[160,1280]{1,0:T(8,128)(2,1)S(1)} %bitcast.7, bf16[160,1280]{1,0:T(8,128)(2,1)S(1)} %copy-done.1, ...), custom_call_target="tpu_custom_call" | custom-call | flops 838860800 | bytes 1048576 | tf_op jit(solution)/shard_map/pallas_call | solution.py:55
  63.9 0.1 collective-permute-start.21
  64.0 1.9 %collective-permute-done.21 = bf16[192,1280]{1,0:T(8,128)(2,1)S(1)} collective-permute-done((bf16[192,1280]{1,0:T(8,128)(2,1)S(1)}, bf16[192,1280]{1,0:T(8,128)(2,1)S(1)}, u32[]{:S(2)}, u32[]{:S(2)}) %collective-permute-start.21) | collective-permute-done | bytes 491552 | tf_op jit(solution)/shard_map/ppermute | solution.py:26
  65.9 0.1 collective-permute-start.22
  66.0 0.1 convert_element_type.67
  66.1 0.1 fusion.2
  66.2 1.7 %collective-permute-start.23 = (bf16[96,1280]{1,0:T(8,128)(2,1)S(1)}, bf16[96,1280]{1,0:T(8,128)(2,1)S(1)}, u32[]{:S(2)}, u32[]{:S(2)}) collective-permute-start(bf16[96,1280]{1,0:T(8,128)(2,1)S(1)} %fusion.2), channel_id=1, source_target_pairs={{0,8},{8,0},{16,24},{24,16},{1,9},{9,1},{17,25},{25,17},{2,10},{10... | collective-permute-start | bytes 737288 | tf_op jit(solution)/shard_map/ppermute | solution.py:30
  67.8 1.5 %collective-permute-start.33 = (bf16[320,1280]{1,0:T(8,128)(2,1)S(1)}, bf16[320,1280]{1,0:T(8,128)(2,1)S(1)}, u32[]{:S(2)}, u32[]{:S(2)}) collective-permute-start(bf16[320,1280]{1,0:T(8,128)(2,1)S(1)} %get-tuple-element.57), channel_id=1, source_target_pairs={{0,24},{24,0},{8,16},{16,8},{1,25},{25,1},{9,17},{17,9},{2,26},{26... | collective-permute-start | bytes 2457608 | tf_op jit(solution)/shard_map/ppermute | solution.py:34
  69.3 0.6 shard_map.80
  69.9 0.1 convert_element_type.66
  70.0 0.2 fusion.9
  70.3 0.1 collective-permute-start.26
  70.4 3.3 %collective-permute-start.27 = (bf16[64,1280]{1,0:T(8,128)(2,1)S(1)}, bf16[64,1280]{1,0:T(8,128)(2,1)S(1)}, u32[]{:S(2)}, u32[]{:S(2)}) collective-permute-start(bf16[64,1280]{1,0:T(8,128)(2,1)S(1)} %pad_maximum_fusion.3), channel_id=1, source_target_pairs={{0,224},{32,0},{64,32},{96,64},{128,96},{160,128},{192,160},{224,1... | collective-permute-start | bytes 491528 | tf_op jit(solution)/shard_map/ppermute | solution.py:26
  73.7 0.8 collective-permute-done.23
  74.5 0.1 fusion.1
  74.6 0.1 collective-permute-start.24
  74.7 0.8 collective-permute-start.25
  75.6 1.9 %collective-permute-done.26 = bf16[64,1280]{1,0:T(8,128)(2,1)S(1)} collective-permute-done((bf16[64,1280]{1,0:T(8,128)(2,1)S(1)}, bf16[64,1280]{1,0:T(8,128)(2,1)S(1)}, u32[]{:S(2)}, u32[]{:S(2)}) %collective-permute-start.26) | collective-permute-done | bytes 163872 | tf_op jit(solution)/shard_map/ppermute | solution.py:26
  77.5 0.8 collective-permute-start.31
  78.3 1.7 %collective-permute-start.29 = (bf16[64,1280]{1,0:T(8,128)(2,1)S(1)}, bf16[64,1280]{1,0:T(8,128)(2,1)S(1)}, u32[]{:S(2)}, u32[]{:S(2)}) collective-permute-start(bf16[64,1280]{1,0:T(8,128)(2,1)S(1)} %slice.144), channel_id=1, source_target_pairs={{0,8},{8,0},{16,24},{24,16},{1,9},{9,1},{17,25},{25,17},{2,10},{10... | collective-permute-start | bytes 491528 | tf_op jit(solution)/shard_map/ppermute | solution.py:30
  80.0 3.7 %collective-permute-done.29 = bf16[64,1280]{1,0:T(8,128)(2,1)S(1)} collective-permute-done((bf16[64,1280]{1,0:T(8,128)(2,1)S(1)}, bf16[64,1280]{1,0:T(8,128)(2,1)S(1)}, u32[]{:S(2)}, u32[]{:S(2)}) %collective-permute-start.29) | collective-permute-done | bytes 163872 | tf_op jit(solution)/shard_map/ppermute | solution.py:30
  83.7 1.6 %collective-permute-start.28 = (bf16[32,1280]{1,0:T(8,128)(2,1)S(1)}, bf16[32,1280]{1,0:T(8,128)(2,1)S(1)}, u32[]{:S(2)}, u32[]{:S(2)}) collective-permute-start(bf16[32,1280]{1,0:T(8,128)(2,1)S(1)} %fusion.8), channel_id=1, source_target_pairs={{0,8},{8,0},{16,24},{24,16},{1,9},{9,1},{17,25},{25,17},{2,10},{10... | collective-permute-start | bytes 245768 | tf_op jit(solution)/shard_map/ppermute | solution.py:30
  85.3 0.1 fusion.3
  85.4 0.8 collective-permute-start.30
  86.2 3.4 %collective-permute-start.32 = (bf16[32,1280]{1,0:T(8,128)(2,1)S(1)}, bf16[32,1280]{1,0:T(8,128)(2,1)S(1)}, u32[]{:S(2)}, u32[]{:S(2)}) collective-permute-start(bf16[32,1280]{1,0:T(8,128)(2,1)S(1)} %get-tuple-element.66), channel_id=1, source_target_pairs={{0,192},{32,224},{64,0},{96,32},{128,64},{160,96},{192,128},{224,1... | collective-permute-start | bytes 245768 | tf_op jit(solution)/shard_map/ppermute | solution.py:26
  89.6 1.3 %convert_add_fusion = (f32[160,1280]{1,0:T(8,128)}, f32[1280,160]{0,1:T(8,128)}) fusion(f32[160,1280]{1,0:T(8,128)S(1)} %get-tuple-element.48, bf16[320,1280]{1,0:T(8,128)(2,1)S(1)} %collective-permute-done.33, f32[160,1280]{1,0:T(8,128)S(1)} %get-tuple-element.55), kind=kLoop, calls=%fused_computation.1 | loop fusion | flops 819200 | bytes 4096000 | tf_op jit(solution)/shard_map/add | solution.py:226
  90.9 1.8 %collective-permute-done.30 = bf16[32,1280]{1,0:T(8,128)(2,1)S(1)} collective-permute-done((bf16[32,1280]{1,0:T(8,128)(2,1)S(1)}, bf16[32,1280]{1,0:T(8,128)(2,1)S(1)}, u32[]{:S(2)}, u32[]{:S(2)}) %collective-permute-start.30) | collective-permute-done | bytes 81952 | tf_op jit(solution)/shard_map/ppermute | solution.py:26
  92.7 0.1 fusion.6
  92.8 0.6 fusion.14
  (48 shorter events, 0.4 us)
Async XLA Ops:
  1.5 10.4 %collective-permute-start.1 = (bf16[32,1280]{1,0:T(8,128)(2,1)S(1)}, bf16[32,1280]{1,0:T(8,128)(2,1)S(1)}, u32[]{:S(2)}, u32[]{:S(2)}) collective-permute-start(bf16[32,1280]{1,0:T(8,128)(2,1)S(1)} %pad_select_fusion), channel_id=1, source_target_pairs={{0,192},{32,224},{64,0},{96,32},{128,64},{160,96},{192,128},{224,1... | collective-permute-start | bytes 245768 | tf_op jit(solution)/shard_map/ppermute | solution.py:26
  7.9 7.2 %collective-permute-start.5 = (bf16[32,1280]{1,0:T(8,128)(2,1)S(1)}, bf16[32,1280]{1,0:T(8,128)(2,1)S(1)}, u32[]{:S(2)}, u32[]{:S(2)}) collective-permute-start(bf16[32,1280]{1,0:T(8,128)(2,1)S(1)} %pad_select_fusion), channel_id=1, source_target_pairs={{0,64},{32,96},{64,128},{96,160},{128,192},{160,224},{192,0},{224,... | collective-permute-start | bytes 245768 | tf_op jit(solution)/shard_map/ppermute | solution.py:26
  7.9 12.1 %collective-permute-start = (bf16[32,1280]{1,0:T(8,128)(2,1)S(1)}, bf16[32,1280]{1,0:T(8,128)(2,1)S(1)}, u32[]{:S(2)}, u32[]{:S(2)}) collective-permute-start(bf16[32,1280]{1,0:T(8,128)(2,1)S(1)} %pad_select_fusion), channel_id=1, source_target_pairs={{0,8},{8,0},{16,24},{24,16},{1,9},{9,1},{17,25},{25,17},{2,10},{10... | collective-permute-start | bytes 245768 | tf_op jit(solution)/shard_map/ppermute | solution.py:30
  9.6 26.2 %copy-start = (bf16[1280,160]{0,1:T(8,128)(2,1)S(1)}, bf16[1280,160]{0,1:T(8,128)(2,1)}, u32[]{:S(2)}) copy-start(bf16[1280,160]{0,1:T(8,128)(2,1)} %param.5) | copy-start | bytes 1228804
  9.6 26.2 %copy-start.1 = (bf16[160,1280]{1,0:T(8,128)(2,1)S(1)}, bf16[160,1280]{1,0:T(8,128)(2,1)}, u32[]{:S(2)}) copy-start(bf16[160,1280]{1,0:T(8,128)(2,1)} %wo.3) | copy-start | bytes 1228804
  9.6 23.5 %collective-permute-start.10 = (bf16[320,1280]{1,0:T(8,128)(2,1)S(1)}, bf16[320,1280]{1,0:T(8,128)(2,1)S(1)}, u32[]{:S(2)}, u32[]{:S(2)}) collective-permute-start(bf16[320,1280]{1,0:T(8,128)(2,1)S(1)} %pad_maximum_fusion), channel_id=1, source_target_pairs={{0,24},{24,0},{8,16},{16,8},{1,25},{25,1},{9,17},{17,9},{2,26},{26... | collective-permute-start | bytes 2457608 | tf_op jit(solution)/shard_map/ppermute | solution.py:34
  15.1 17.3 %collective-permute-start.6 = (bf16[64,1280]{1,0:T(8,128)(2,1)S(1)}, bf16[64,1280]{1,0:T(8,128)(2,1)S(1)}, u32[]{:S(2)}, u32[]{:S(2)}) collective-permute-start(bf16[64,1280]{1,0:T(8,128)(2,1)S(1)} %get-tuple-element.77), channel_id=1, source_target_pairs={{0,8},{8,0},{16,24},{24,16},{1,9},{9,1},{17,25},{25,17},{2,10},{10... | collective-permute-start | bytes 491528 | tf_op jit(solution)/shard_map/ppermute | solution.py:30
  15.8 10.1 %collective-permute-start.8 = (bf16[32,1280]{1,0:T(8,128)(2,1)S(1)}, bf16[32,1280]{1,0:T(8,128)(2,1)S(1)}, u32[]{:S(2)}, u32[]{:S(2)}) collective-permute-start(bf16[32,1280]{1,0:T(8,128)(2,1)S(1)} %collective-permute-done.5), channel_id=1, source_target_pairs={{0,64},{32,96},{64,128},{96,160},{128,192},{160,224},{192,0},{224,... | collective-permute-start | bytes 245768 | tf_op jit(solution)/shard_map/ppermute | solution.py:26
  15.8 6.3 %collective-permute-start.2 = (bf16[32,1280]{1,0:T(8,128)(2,1)S(1)}, bf16[32,1280]{1,0:T(8,128)(2,1)S(1)}, u32[]{:S(2)}, u32[]{:S(2)}) collective-permute-start(bf16[32,1280]{1,0:T(8,128)(2,1)S(1)} %collective-permute-done.1), channel_id=1, source_target_pairs={{0,224},{32,0},{64,32},{96,64},{128,96},{160,128},{192,160},{224,1... | collective-permute-start | bytes 245768 | tf_op jit(solution)/shard_map/ppermute | solution.py:26
  20.0 5.8 %collective-permute-start.7 = (bf16[32,1280]{1,0:T(8,128)(2,1)S(1)}, bf16[32,1280]{1,0:T(8,128)(2,1)S(1)}, u32[]{:S(2)}, u32[]{:S(2)}) collective-permute-start(bf16[32,1280]{1,0:T(8,128)(2,1)S(1)} %collective-permute-done.5), channel_id=1, source_target_pairs={{0,32},{32,64},{64,96},{96,128},{128,160},{160,192},{192,224},{224... | collective-permute-start | bytes 245768 | tf_op jit(solution)/shard_map/ppermute | solution.py:26
  22.1 6.5 %collective-permute-start.3 = (bf16[64,1280]{1,0:T(8,128)(2,1)S(1)}, bf16[64,1280]{1,0:T(8,128)(2,1)S(1)}, u32[]{:S(2)}, u32[]{:S(2)}) collective-permute-start(bf16[64,1280]{1,0:T(8,128)(2,1)S(1)} %pad_maximum_fusion.1), channel_id=1, source_target_pairs={{0,224},{32,0},{64,32},{96,64},{128,96},{160,128},{192,160},{224,1... | collective-permute-start | bytes 491528 | tf_op jit(solution)/shard_map/ppermute | solution.py:26
  25.8 6.6 %collective-permute-start.4 = (bf16[64,1280]{1,0:T(8,128)(2,1)S(1)}, bf16[64,1280]{1,0:T(8,128)(2,1)S(1)}, u32[]{:S(2)}, u32[]{:S(2)}) collective-permute-start(bf16[64,1280]{1,0:T(8,128)(2,1)S(1)} %pad_maximum_fusion.1), channel_id=1, source_target_pairs={{0,32},{32,64},{64,96},{96,128},{128,160},{160,192},{192,224},{224... | collective-permute-start | bytes 491528 | tf_op jit(solution)/shard_map/ppermute | solution.py:26
  25.9 7.3 %collective-permute-start.9 = (bf16[96,1280]{1,0:T(8,128)(2,1)S(1)}, bf16[96,1280]{1,0:T(8,128)(2,1)}, u32[]{:S(2)}, u32[]{:S(2)}) collective-permute-start(bf16[96,1280]{1,0:T(8,128)(2,1)S(1)} %constant_dynamic-update-slice_fusion.8.refs_2_), channel_id=1, source_target_pairs={{0,8},{8,0},{16,24},{24,16},{1,9},{9,1},{17,25},{25,17},{2,10},{10... | collective-permute-start | bytes 737288 | tf_op jit(solution)/shard_map/ppermute | solution.py:30
  32.4 2.9 %collective-permute-start.11 = (bf16[192,1280]{1,0:T(8,128)(2,1)S(1)}, bf16[192,1280]{1,0:T(8,128)(2,1)S(1)}, u32[]{:S(2)}, u32[]{:S(2)}) collective-permute-start(bf16[192,1280]{1,0:T(8,128)(2,1)S(1)} %constant_dynamic-update-slice_fusion.refs_0_), channel_id=1, source_target_pairs={{0,1},{1,0},{2,3},{3,2},{4,5},{5,4},{6,7},{7,6},{8,9},{9,8},{10,11... | collective-permute-start | bytes 1474568 | tf_op jit(solution)/shard_map/ppermute | solution.py:26
  32.5 2.8 %collective-permute-start.12 = (bf16[128,1280]{1,0:T(8,128)(2,1)S(1)}, bf16[128,1280]{1,0:T(8,128)(2,1)S(1)}, u32[]{:S(2)}, u32[]{:S(2)}) collective-permute-start(bf16[128,1280]{1,0:T(8,128)(2,1)S(1)} %constant_dynamic-update-slice_fusion.5.refs_1_), channel_id=1, source_target_pairs={{0,1},{1,0},{2,3},{3,2},{4,5},{5,4},{6,7},{7,6},{8,9},{9,8},{10,11... | collective-permute-start | bytes 983048 | tf_op jit(solution)/shard_map/ppermute | solution.py:26
  33.1 2.2 %collective-permute-start.13 = (bf16[96,1280]{1,0:T(8,128)(2,1)S(1)}, bf16[96,1280]{1,0:T(8,128)(2,1)}, u32[]{:S(2)}, u32[]{:S(2)}) collective-permute-start(bf16[96,1280]{1,0:T(8,128)(2,1)S(1)} %constant_dynamic-update-slice_fusion.8.refs_2_), channel_id=1, source_target_pairs={{0,1},{1,0},{2,3},{3,2},{4,5},{5,4},{6,7},{7,6},{8,9},{9,8},{10,11... | collective-permute-start | bytes 737288 | tf_op jit(solution)/shard_map/ppermute | solution.py:26
  33.2 2.7 %collective-permute-start.14 = (bf16[96,1280]{1,0:T(8,128)(2,1)}, bf16[96,1280]{1,0:T(8,128)(2,1)}, u32[]{:S(2)}, u32[]{:S(2)}) collective-permute-start(bf16[96,1280]{1,0:T(8,128)(2,1)} %collective-permute-done.9.refs_3_), channel_id=1, source_target_pairs={{0,1},{1,0},{2,3},{3,2},{4,5},{5,4},{6,7},{7,6},{8,9},{9,8},{10,11... | collective-permute-start | bytes 737288 | tf_op jit(solution)/shard_map/ppermute | solution.py:26
  38.6 8.6 %collective-permute-start.15 = (bf16[2,320,128]{2,1,0:T(8,128)(2,1)S(1)}, bf16[2,320,128]{2,1,0:T(8,128)(2,1)S(1)}, u32[]{:S(2)}, u32[]{:S(2)}) collective-permute-start(bf16[2,320,128]{2,1,0:T(8,128)(2,1)S(1)} %get-tuple-element.36), channel_id=1, source_target_pairs={{0,4},{2,6},{4,0},{6,2},{1,5},{3,7},{5,1},{7,3},{8,12},{10,14},{12... | collective-permute-start | bytes 491528 | tf_op jit(solution)/shard_map/ppermute | solution.py:26
  41.9 8.1 %collective-permute-start.16 = (bf16[2,320,128]{2,1,0:T(8,128)(2,1)S(1)}, bf16[2,320,128]{2,1,0:T(8,128)(2,1)S(1)}, u32[]{:S(2)}, u32[]{:S(2)}) collective-permute-start(bf16[2,320,128]{2,1,0:T(8,128)(2,1)S(1)} %get-tuple-element.39), channel_id=1, source_target_pairs={{0,2},{2,4},{4,6},{6,0},{1,3},{3,5},{5,7},{7,1},{8,10},{10,12},{12... | collective-permute-start | bytes 491528 | tf_op jit(solution)/shard_map/ppermute | solution.py:26
  42.5 7.7 %collective-permute-start.17 = (bf16[2,320,128]{2,1,0:T(8,128)(2,1)S(1)}, bf16[2,320,128]{2,1,0:T(8,128)(2,1)S(1)}, u32[]{:S(2)}, u32[]{:S(2)}) collective-permute-start(bf16[2,320,128]{2,1,0:T(8,128)(2,1)S(1)} %get-tuple-element.40), channel_id=1, source_target_pairs={{0,6},{2,0},{4,2},{6,4},{1,7},{3,1},{5,3},{7,5},{8,14},{10,8},{12,... | collective-permute-start | bytes 491528 | tf_op jit(solution)/shard_map/ppermute | solution.py:26
  50.4 8.2 %collective-permute-start.18 = (bf16[2,320,128]{2,1,0:T(8,128)(2,1)S(1)}, bf16[2,320,128]{2,1,0:T(8,128)(2,1)S(1)}, u32[]{:S(2)}, u32[]{:S(2)}) collective-permute-start(bf16[2,320,128]{2,1,0:T(8,128)(2,1)S(1)} %shard_map.77.b0), channel_id=1, source_target_pairs={{0,4},{2,6},{4,0},{6,2},{1,5},{3,7},{5,1},{7,3},{8,12},{10,14},{12... | collective-permute-start | bytes 491528 | tf_op jit(solution)/shard_map/ppermute | solution.py:26
  52.6 8.5 %collective-permute-start.19 = (bf16[2,320,128]{2,1,0:T(8,128)(2,1)S(1)}, bf16[2,320,128]{2,1,0:T(8,128)(2,1)S(1)}, u32[]{:S(2)}, u32[]{:S(2)}) collective-permute-start(bf16[2,320,128]{2,1,0:T(8,128)(2,1)S(1)} %shard_map.77.b0), channel_id=1, source_target_pairs={{0,6},{2,0},{4,2},{6,4},{1,7},{3,1},{5,3},{7,5},{8,14},{10,8},{12,... | collective-permute-start | bytes 491528 | tf_op jit(solution)/shard_map/ppermute | solution.py:26
  54.6 7.1 %collective-permute-start.20 = (bf16[2,320,128]{2,1,0:T(8,128)(2,1)S(1)}, bf16[2,320,128]{2,1,0:T(8,128)(2,1)S(1)}, u32[]{:S(2)}, u32[]{:S(2)}) collective-permute-start(bf16[2,320,128]{2,1,0:T(8,128)(2,1)S(1)} %shard_map.77.b0), channel_id=1, source_target_pairs={{0,2},{2,4},{4,6},{6,0},{1,3},{3,5},{5,7},{7,1},{8,10},{10,12},{12... | collective-permute-start | bytes 491528 | tf_op jit(solution)/shard_map/ppermute | solution.py:26
  63.9 2.0 %collective-permute-start.21 = (bf16[192,1280]{1,0:T(8,128)(2,1)S(1)}, bf16[192,1280]{1,0:T(8,128)(2,1)S(1)}, u32[]{:S(2)}, u32[]{:S(2)}) collective-permute-start(bf16[192,1280]{1,0:T(8,128)(2,1)S(1)} %get-tuple-element.44), channel_id=1, source_target_pairs={{0,1},{1,0},{2,3},{3,2},{4,5},{5,4},{6,7},{7,6},{8,9},{9,8},{10,11... | collective-permute-start | bytes 1474568 | tf_op jit(solution)/shard_map/ppermute | solution.py:26
  65.9 4.0 %collective-permute-start.22 = (bf16[320,1280]{1,0:T(8,128)(2,1)S(1)}, bf16[320,1280]{1,0:T(8,128)(2,1)S(1)}, u32[]{:S(2)}, u32[]{:S(2)}) collective-permute-start(bf16[320,1280]{1,0:T(8,128)(2,1)S(1)} %get-tuple-element.45), channel_id=1, source_target_pairs={{0,1},{1,0},{2,3},{3,2},{4,5},{5,4},{6,7},{7,6},{8,9},{9,8},{10,11... | collective-permute-start | bytes 2457608 | tf_op jit(solution)/shard_map/ppermute | solution.py:26
  66.2 8.3 %collective-permute-start.23 = (bf16[96,1280]{1,0:T(8,128)(2,1)S(1)}, bf16[96,1280]{1,0:T(8,128)(2,1)S(1)}, u32[]{:S(2)}, u32[]{:S(2)}) collective-permute-start(bf16[96,1280]{1,0:T(8,128)(2,1)S(1)} %fusion.2), channel_id=1, source_target_pairs={{0,8},{8,0},{16,24},{24,16},{1,9},{9,1},{17,25},{25,17},{2,10},{10... | collective-permute-start | bytes 737288 | tf_op jit(solution)/shard_map/ppermute | solution.py:30
  67.8 21.8 %collective-permute-start.33 = (bf16[320,1280]{1,0:T(8,128)(2,1)S(1)}, bf16[320,1280]{1,0:T(8,128)(2,1)S(1)}, u32[]{:S(2)}, u32[]{:S(2)}) collective-permute-start(bf16[320,1280]{1,0:T(8,128)(2,1)S(1)} %get-tuple-element.57), channel_id=1, source_target_pairs={{0,24},{24,0},{8,16},{16,8},{1,25},{25,1},{9,17},{17,9},{2,26},{26... | collective-permute-start | bytes 2457608 | tf_op jit(solution)/shard_map/ppermute | solution.py:34
  70.3 7.2 %collective-permute-start.26 = (bf16[64,1280]{1,0:T(8,128)(2,1)S(1)}, bf16[64,1280]{1,0:T(8,128)(2,1)S(1)}, u32[]{:S(2)}, u32[]{:S(2)}) collective-permute-start(bf16[64,1280]{1,0:T(8,128)(2,1)S(1)} %pad_maximum_fusion.2), channel_id=1, source_target_pairs={{0,32},{32,64},{64,96},{96,128},{128,160},{160,192},{192,224},{224... | collective-permute-start | bytes 491528 | tf_op jit(solution)/shard_map/ppermute | solution.py:26
  70.4 7.9 %collective-permute-start.27 = (bf16[64,1280]{1,0:T(8,128)(2,1)S(1)}, bf16[64,1280]{1,0:T(8,128)(2,1)S(1)}, u32[]{:S(2)}, u32[]{:S(2)}) collective-permute-start(bf16[64,1280]{1,0:T(8,128)(2,1)S(1)} %pad_maximum_fusion.3), channel_id=1, source_target_pairs={{0,224},{32,0},{64,32},{96,64},{128,96},{160,128},{192,160},{224,1... | collective-permute-start | bytes 491528 | tf_op jit(solution)/shard_map/ppermute | solution.py:26
  74.6 10.7 %collective-permute-start.24 = (bf16[32,1280]{1,0:T(8,128)(2,1)S(1)}, bf16[32,1280]{1,0:T(8,128)(2,1)S(1)}, u32[]{:S(2)}, u32[]{:S(2)}) collective-permute-start(bf16[32,1280]{1,0:T(8,128)(2,1)S(1)} %get-tuple-element.74), channel_id=1, source_target_pairs={{0,32},{32,64},{64,96},{96,128},{128,160},{160,192},{192,224},{224... | collective-permute-start | bytes 245768 | tf_op jit(solution)/shard_map/ppermute | solution.py:26
  74.7 10.6 %collective-permute-start.25 = (bf16[32,1280]{1,0:T(8,128)(2,1)S(1)}, bf16[32,1280]{1,0:T(8,128)(2,1)S(1)}, u32[]{:S(2)}, u32[]{:S(2)}) collective-permute-start(bf16[32,1280]{1,0:T(8,128)(2,1)S(1)} %get-tuple-element.73), channel_id=1, source_target_pairs={{0,64},{32,96},{64,128},{96,160},{128,192},{160,224},{192,0},{224,... | collective-permute-start | bytes 245768 | tf_op jit(solution)/shard_map/ppermute | solution.py:26
  77.5 7.8 %collective-permute-start.31 = (bf16[32,1280]{1,0:T(8,128)(2,1)S(1)}, bf16[32,1280]{1,0:T(8,128)(2,1)S(1)}, u32[]{:S(2)}, u32[]{:S(2)}) collective-permute-start(bf16[32,1280]{1,0:T(8,128)(2,1)S(1)} %get-tuple-element.72), channel_id=1, source_target_pairs={{0,224},{32,0},{64,32},{96,64},{128,96},{160,128},{192,160},{224,1... | collective-permute-start | bytes 245768 | tf_op jit(solution)/shard_map/ppermute | solution.py:26
  78.3 5.4 %collective-permute-start.29 = (bf16[64,1280]{1,0:T(8,128)(2,1)S(1)}, bf16[64,1280]{1,0:T(8,128)(2,1)S(1)}, u32[]{:S(2)}, u32[]{:S(2)}) collective-permute-start(bf16[64,1280]{1,0:T(8,128)(2,1)S(1)} %slice.144), channel_id=1, source_target_pairs={{0,8},{8,0},{16,24},{24,16},{1,9},{9,1},{17,25},{25,17},{2,10},{10... | collective-permute-start | bytes 491528 | tf_op jit(solution)/shard_map/ppermute | solution.py:30
  83.7 7.2 %collective-permute-start.28 = (bf16[32,1280]{1,0:T(8,128)(2,1)S(1)}, bf16[32,1280]{1,0:T(8,128)(2,1)S(1)}, u32[]{:S(2)}, u32[]{:S(2)}) collective-permute-start(bf16[32,1280]{1,0:T(8,128)(2,1)S(1)} %fusion.8), channel_id=1, source_target_pairs={{0,8},{8,0},{16,24},{24,16},{1,9},{9,1},{17,25},{25,17},{2,10},{10... | collective-permute-start | bytes 245768 | tf_op jit(solution)/shard_map/ppermute | solution.py:30
  85.4 7.3 %collective-permute-start.30 = (bf16[32,1280]{1,0:T(8,128)(2,1)S(1)}, bf16[32,1280]{1,0:T(8,128)(2,1)S(1)}, u32[]{:S(2)}, u32[]{:S(2)}) collective-permute-start(bf16[32,1280]{1,0:T(8,128)(2,1)S(1)} %get-tuple-element.67), channel_id=1, source_target_pairs={{0,64},{32,96},{64,128},{96,160},{128,192},{160,224},{192,0},{224,... | collective-permute-start | bytes 245768 | tf_op jit(solution)/shard_map/ppermute | solution.py:26
  86.2 6.5 %collective-permute-start.32 = (bf16[32,1280]{1,0:T(8,128)(2,1)S(1)}, bf16[32,1280]{1,0:T(8,128)(2,1)S(1)}, u32[]{:S(2)}, u32[]{:S(2)}) collective-permute-start(bf16[32,1280]{1,0:T(8,128)(2,1)S(1)} %get-tuple-element.66), channel_id=1, source_target_pairs={{0,192},{32,224},{64,0},{96,32},{128,64},{160,96},{192,128},{224,1... | collective-permute-start | bytes 245768 | tf_op jit(solution)/shard_map/ppermute | solution.py:26
